TPU v7x, 32 devices: a whole 2x2x4 slice. The times are simulated.
32 devices in a mesh: narrow: 4 (over z), wide: 8 (over y, x, core).
Axes of the slice: x: 2, y: 2, z: 4, core: 2. Of those that a mesh axis runs over, the one named last changes fastest.
Arguments:
- hidden_in: bfloat16 [8, 1024, 1024], P('narrow', 'wide'), may hold values from -6 to 6
- out_grad: bfloat16 [8, 1024, 1024], P('narrow', 'wide'), may hold values from -6 to 6
- seg_ids: int32 [8, 1024], P('narrow', 'wide'), may hold values from 0 to 5, as said below
- expert_ids: int32 [8, 1024, 8], P('narrow', 'wide'), may hold values from 0 to 31, all different within a row
- attn_gain: bfloat16 [1024], P(('narrow', 'wide')), may hold values from 0.099609375 to 1.8984375
- w_query: bfloat16 [1024, 1024], P(('narrow', 'wide')), may hold values from -0.1875 to 0.1875
- w_key: bfloat16 [1024, 512], P(('narrow', 'wide')), may hold values from -0.1875 to 0.1875
- w_value: bfloat16 [1024, 512], P(('narrow', 'wide')), may hold values from -0.1875 to 0.1875
- w_output: bfloat16 [1024, 1024], P(('narrow', 'wide')), may hold values from -1.5 to 1.5
- moe_gain: bfloat16 [1024], P(('narrow', 'wide')), may hold values from 0.099609375 to 1.8984375
- w_router: bfloat16 [1024, 32], P(('narrow', 'wide')), may hold values from -0.09375 to 0.09375
- w_gate_up: bfloat16 [32, 1024, 1024], P('wide', 'narrow'), may hold values from -0.1875 to 0.1875
- w_down: bfloat16 [32, 512, 1024], P('wide', 'narrow'), may hold values from -0.75 to 0.75
Outputs:
- block_out: bfloat16 [8, 1024, 1024], P('narrow', 'wide')
- input_grad: bfloat16 [8, 1024, 1024], P('narrow', 'wide')
- attn_gain_grad: float32 [1024], P(('narrow', 'wide'))
- w_query_grad: float32 [1024, 1024], P(('narrow', 'wide'))
- w_key_grad: float32 [1024, 512], P(('narrow', 'wide'))
- w_value_grad: float32 [1024, 512], P(('narrow', 'wide'))
- w_output_grad: float32 [1024, 1024], P(('narrow', 'wide'))
- moe_gain_grad: float32 [1024], P(('narrow', 'wide'))
- w_router_grad: float32 [1024, 32], P(('narrow', 'wide'))
- w_gate_up_grad: float32 [32, 1024, 1024], P('wide', 'narrow')
- w_down_grad: float32 [32, 512, 1024], P('wide', 'narrow')
- expert_load: int32 [32], replicated
Inputs may be any that keep to these rules, and one draw needn't show every extreme that they name: `seg_ids`: along each row the document numbers never fall. `expert_ids`: the 8 experts named by one token are all different; across the tokens of a packed row an expert is named many times, and every expert is named by some token.
All inputs are finite; a program needn't handle non-finite values.
Results may differ from a plain program's by a relative error of at most 0.017.
Values may be sent and summed in bfloat16 or wider, within the bound.
A program may use at most 192 MiB of HBM per device.

v0:
```python
import math

import jax
import jax.numpy as jnp
from jax import lax
from jax.sharding import PartitionSpec as P

KV_HEADS = 8
HEAD_DIM = 64
EXPERTS = 32
TOP = 8
FF = 512
CAP = 80


EPSILON = 1e-06
THETA = 10000.0
MASKED = -1e30


def rms_scale(values):
    return lax.rsqrt(jnp.mean(values * values, axis=-1, keepdims=True) + EPSILON)


def norm_back(values, scale, gain, upstream):
    weighted = upstream * gain
    inner_mean = jnp.mean(weighted * values, axis=-1, keepdims=True)
    value_grad = weighted * scale - values * (scale * scale * scale) * inner_mean
    gain_grad = jnp.sum(upstream * values * scale, axis=0)
    return (value_grad, gain_grad)


def lane_turn(head_dim):
    lane_ids = jnp.arange(128)
    lane_local = lane_ids % head_dim
    half_dim = head_dim // 2
    same_head = lane_ids[:, None] // head_dim == lane_ids[None, :] // head_dim
    from_upper = (lane_local[None, :] < half_dim) & (
        lane_local[:, None] == lane_local[None, :] + half_dim
    )
    from_lower = (lane_local[None, :] >= half_dim) & (
        lane_local[:, None] + half_dim == lane_local[None, :]
    )
    return jnp.where(
        same_head & from_upper, -1.0, jnp.where(same_head & from_lower, 1.0, 0.0)
    ).astype(jnp.float32)


def lane_angles(positions, head_dim):
    lane_ids = jnp.arange(128) % head_dim % (head_dim // 2)
    inverse = 1.0 / THETA ** (lane_ids.astype(jnp.float32) * 2.0 / head_dim)
    return positions[..., None] * inverse


def rotate(values, cos_table, sin_table, turner):
    dims_in = values.shape
    blocks = values.reshape(dims_in[0], dims_in[1], -1, 128)
    turned = jnp.einsum("abnl,lm->abnm", blocks, turner, precision=lax.Precision.HIGHEST)
    return (blocks * cos_table[:, :, None, :] + turned * sin_table[:, :, None, :]).reshape(dims_in)


def rotate_back(grad_in, cos_table, sin_table, turner):
    dims_in = grad_in.shape
    blocks = grad_in.reshape(dims_in[0], dims_in[1], -1, 128)
    turned = jnp.einsum(
        "abnm,lm->abnl", blocks * sin_table[:, :, None, :], turner, precision=lax.Precision.HIGHEST
    )
    return (blocks * cos_table[:, :, None, :] + turned).reshape(dims_in)


def masked_scores(query_five, key_block, seg_query, seg_key, place_query, place_key, factor):
    scores = (
        jnp.einsum("abgjd,akgd->agjbk", query_five, key_block, preferred_element_type=jnp.float32)
        * factor
    )
    allowed = (seg_query[:, :, None] == seg_key[:, None, :]) & (
        place_query[:, :, None] >= place_key[:, None, :]
    )
    return jnp.where(allowed[:, None, None], scores, MASKED)


def per_device(
    hidden_in,
    out_grad,
    seg_ids,
    expert_ids,
    attn_gain,
    w_query,
    w_key,
    w_value,
    w_output,
    moe_gain,
    w_router,
    w_gate_up,
    w_down,
):
    row_count, span_len, feat_dim = hidden_in.shape
    tok_count = row_count * span_len
    factor = HEAD_DIM ** (-0.5)
    kv_width = KV_HEADS * HEAD_DIM
    gain_one, query_w, key_w, value_w, output_w, gain_two, router_w = (
        lax.all_gather(attn_gain, ("narrow", "wide"), axis=0, tiled=True),
        lax.all_gather(w_query, ("narrow", "wide"), axis=0, tiled=True),
        lax.all_gather(w_key, ("narrow", "wide"), axis=0, tiled=True),
        lax.all_gather(w_value, ("narrow", "wide"), axis=0, tiled=True),
        lax.all_gather(w_output, ("narrow", "wide"), axis=0, tiled=True),
        lax.all_gather(moe_gain, ("narrow", "wide"), axis=0, tiled=True),
        lax.all_gather(w_router, ("narrow", "wide"), axis=0, tiled=True),
    )
    gate_up_w, down_w = (
        lax.all_gather(w_gate_up, "narrow", axis=1, tiled=True),
        lax.all_gather(w_down, "narrow", axis=1, tiled=True),
    )
    segs_all = lax.all_gather(seg_ids, "wide", axis=1, tiled=True)
    seq_len = segs_all.shape[1]
    key_step = math.gcd(seq_len, 512)
    place_local = lax.axis_index("wide") * span_len + jnp.arange(span_len, dtype=jnp.int32)
    place_query = place_local[None, :]
    starts = jnp.sum((segs_all[:, None, :] < seg_ids[:, :, None]).astype(jnp.int32), axis=-1)
    positions = (place_query - starts).astype(jnp.float32)
    angles = lane_angles(positions, HEAD_DIM)
    cos_table = jnp.cos(angles)
    sin_table = jnp.sin(angles)
    turner = lane_turn(HEAD_DIM)
    inputs = hidden_in.astype(jnp.float32)
    scale_one = rms_scale(inputs)
    gain_one_f = gain_one.astype(jnp.float32)
    normed_one = (inputs * scale_one * gain_one_f).astype(jnp.bfloat16)
    query_pre = jnp.dot(normed_one, query_w, preferred_element_type=jnp.float32)
    key_pre = jnp.dot(normed_one, key_w, preferred_element_type=jnp.float32)
    value_pre = jnp.dot(normed_one, value_w, preferred_element_type=jnp.float32)
    queries = rotate(query_pre, cos_table, sin_table, turner).astype(jnp.bfloat16)
    keys_local = rotate(key_pre, cos_table, sin_table, turner).astype(jnp.bfloat16)
    values_local = value_pre.astype(jnp.bfloat16)
    key_all, value_all = (
        lax.all_gather(keys_local, "wide", axis=1, tiled=True),
        lax.all_gather(values_local, "wide", axis=1, tiled=True),
    )
    query_five = queries.reshape(row_count, span_len, KV_HEADS, 2, HEAD_DIM)

    def key_slices(key_start, length):
        key_block = lax.dynamic_slice_in_dim(key_all, key_start, length, 1).reshape(
            row_count, length, KV_HEADS, HEAD_DIM
        )
        value_block = lax.dynamic_slice_in_dim(value_all, key_start, length, 1).reshape(
            row_count, length, KV_HEADS, HEAD_DIM
        )
        seg_key = lax.dynamic_slice_in_dim(segs_all, key_start, length, 1)
        place_key = (key_start + jnp.arange(length, dtype=jnp.int32))[None, :]
        return (key_block, value_block, seg_key, place_key)

    def scores_at(key_start, length):
        key_block, value_block, seg_key, place_key = key_slices(key_start, length)
        scores = masked_scores(
            query_five, key_block, seg_ids, seg_key, place_query, place_key, factor
        )
        return (scores, key_block, value_block)

    key_starts = jnp.arange(seq_len // key_step, dtype=jnp.int32) * key_step
    stat_shape = (row_count, KV_HEADS, 2, span_len)
    five_shape = (row_count, span_len, KV_HEADS, 2, HEAD_DIM)

    def top_step(state_now, key_start):
        row_top, row_total = state_now
        scores, unused_key, unused_value = scores_at(key_start, key_step)
        new_top = jnp.maximum(row_top, jnp.max(scores, axis=-1))
        row_total = row_total * jnp.exp(row_top - new_top) + jnp.sum(
            jnp.exp(scores - new_top[..., None]), axis=-1
        )
        return ((new_top, row_total), None)

    (row_top, row_total), unused = lax.scan(
        top_step,
        (jnp.full(stat_shape, MASKED, jnp.float32), jnp.zeros(stat_shape, jnp.float32)),
        key_starts,
    )
    log_total = row_top + jnp.log(row_total)

    def out_step(summed, key_start):
        scores, unused_key, value_block = scores_at(key_start, key_step)
        weights = jnp.exp(scores - log_total[..., None]).astype(jnp.bfloat16)
        return (
            summed
            + jnp.einsum(
                "agjbk,akgd->abgjd", weights, value_block, preferred_element_type=jnp.float32
            ),
            None,
        )

    attended, unused = lax.scan(out_step, jnp.zeros(five_shape, jnp.float32), key_starts)
    attended = attended.reshape(row_count, span_len, -1).astype(jnp.bfloat16)
    middle = inputs + jnp.dot(attended, output_w, preferred_element_type=jnp.float32)
    scale_two = rms_scale(middle)
    gain_two_f = gain_two.astype(jnp.float32)
    normed_two = (middle * scale_two * gain_two_f).astype(jnp.bfloat16)
    flat_two = normed_two.reshape(tok_count, feat_dim)
    logits = jnp.dot(flat_two, router_w, preferred_element_type=jnp.float32)
    expert_table = expert_ids.reshape(tok_count, TOP)
    choose = expert_table[:, :, None] == jnp.arange(EXPERTS, dtype=jnp.int32)[None, None, :]
    chosen = jnp.sum(jnp.where(choose, logits[:, None, :], 0.0), axis=-1)
    gate_vals = jax.nn.softmax(chosen, axis=-1)
    token_hot = jnp.sum(choose.astype(jnp.int32), axis=1)
    expert_load = lax.psum(jnp.sum(token_hot, axis=0), ("narrow", "wide"))
    earlier = jnp.cumsum(token_hot, axis=0) - token_hot
    places = jnp.sum(jnp.where(choose, earlier[:, None, :], 0), axis=-1)
    pair_count = tok_count * TOP
    target = jnp.where(places < CAP, expert_table * CAP + places, EXPERTS * CAP).reshape(-1)
    pair_of_slot = (
        jnp.full((EXPERTS * CAP,), pair_count, jnp.int32)
        .at[target]
        .set(jnp.arange(pair_count, dtype=jnp.int32), mode="drop")
    )
    token_of_slot = pair_of_slot // TOP
    outgoing = jnp.take(flat_two, token_of_slot, axis=0, mode="fill", fill_value=0).reshape(
        EXPERTS, CAP, feat_dim
    )
    received = lax.all_to_all(outgoing, "wide", split_axis=0, concat_axis=1, tiled=True)
    gate_up = jnp.einsum("ecd,edf->ecf", received, gate_up_w, preferred_element_type=jnp.float32)
    gate_half = gate_up[..., :FF]
    up_half = gate_up[..., FF:]
    sigmoid_gate = jax.nn.sigmoid(gate_half)
    activated = gate_half * sigmoid_gate
    hidden_b = (activated * up_half).astype(jnp.bfloat16)
    expert_out = jnp.einsum(
        "ecf,efd->ecd", hidden_b, down_w, preferred_element_type=jnp.float32
    ).astype(jnp.bfloat16)
    returned = lax.all_to_all(expert_out, "wide", split_axis=1, concat_axis=0, tiled=True)
    per_pair = (
        jnp.take(
            returned.reshape(EXPERTS * CAP, feat_dim), target, axis=0, mode="fill", fill_value=0
        )
        .reshape(tok_count, TOP, feat_dim)
        .astype(jnp.float32)
    )
    mixture = jnp.sum(gate_vals[:, :, None] * per_pair, axis=1)
    middle_flat = middle.reshape(tok_count, feat_dim)
    block_out = (middle_flat + mixture).reshape(row_count, span_len, feat_dim).astype(jnp.bfloat16)
    grad_out = out_grad.reshape(tok_count, feat_dim).astype(jnp.float32)
    gate_grad = jnp.sum(grad_out[:, None, :] * per_pair, axis=-1)
    gate_of_slot = jnp.take(gate_vals.reshape(-1), pair_of_slot, mode="fill", fill_value=0.0)
    slot_grad = (
        (
            jnp.take(grad_out, token_of_slot, axis=0, mode="fill", fill_value=0.0)
            * gate_of_slot[:, None]
        )
        .astype(jnp.bfloat16)
        .reshape(EXPERTS, CAP, feat_dim)
    )
    grad_received = lax.all_to_all(slot_grad, "wide", split_axis=0, concat_axis=1, tiled=True)
    down_grad = jnp.einsum(
        "ecf,ecd->efd", hidden_b, grad_received, preferred_element_type=jnp.float32
    )
    hidden_grad = jnp.einsum(
        "ecd,efd->ecf", grad_received, down_w, preferred_element_type=jnp.float32
    )
    gate_half_grad = (
        hidden_grad * up_half * (sigmoid_gate * (1.0 + gate_half * (1.0 - sigmoid_gate)))
    )
    up_half_grad = hidden_grad * activated
    gate_up_grad = jnp.concatenate([gate_half_grad, up_half_grad], axis=-1).astype(jnp.bfloat16)
    gate_up_wgrad = jnp.einsum(
        "ecd,ecf->edf", received, gate_up_grad, preferred_element_type=jnp.float32
    )
    slot_input_grad = jnp.einsum(
        "ecf,edf->ecd", gate_up_grad, gate_up_w, preferred_element_type=jnp.float32
    ).astype(jnp.bfloat16)
    input_back = lax.all_to_all(slot_input_grad, "wide", split_axis=1, concat_axis=0, tiled=True)
    pair_input_grad = jnp.take(
        input_back.reshape(EXPERTS * CAP, feat_dim), target, axis=0, mode="fill", fill_value=0
    ).reshape(tok_count, TOP, feat_dim)
    gate_mean = jnp.sum(gate_vals * gate_grad, axis=-1, keepdims=True)
    chosen_grad = gate_vals * (gate_grad - gate_mean)
    logit_grad = jnp.sum(jnp.where(choose, chosen_grad[:, :, None], 0.0), axis=1).astype(
        jnp.bfloat16
    )
    router_wgrad = jnp.einsum("td,te->de", flat_two, logit_grad, preferred_element_type=jnp.float32)
    normed_two_grad = jnp.sum(pair_input_grad.astype(jnp.float32), axis=1) + jnp.einsum(
        "te,de->td", logit_grad, router_w, preferred_element_type=jnp.float32
    )
    middle_part, gain_two_grad = norm_back(
        middle_flat, scale_two.reshape(tok_count, 1), gain_two_f, normed_two_grad
    )
    middle_grad = grad_out + middle_part
    attn_grad = middle_grad.astype(jnp.bfloat16)
    output_wgrad = jnp.einsum(
        "te,td->ed", attended.reshape(tok_count, -1), attn_grad, preferred_element_type=jnp.float32
    )
    attended_grad = jnp.einsum(
        "td,ed->te", attn_grad, output_w, preferred_element_type=jnp.float32
    ).astype(jnp.bfloat16)
    grad_five = attended_grad.reshape(five_shape)

    def sum_step(summed, key_start):
        scores, unused_key, value_block = scores_at(key_start, key_step)
        weights = jnp.exp(scores - log_total[..., None])
        weight_grad = jnp.einsum(
            "abgjd,akgd->agjbk", grad_five, value_block, preferred_element_type=jnp.float32
        )
        return (summed + jnp.sum(weights * weight_grad, axis=-1), None)

    row_dot, unused = lax.scan(sum_step, jnp.zeros(stat_shape, jnp.float32), key_starts)

    def query_step(summed, key_start):
        scores, key_block, value_block = scores_at(key_start, key_step)
        weights = jnp.exp(scores - log_total[..., None])
        weight_grad = jnp.einsum(
            "abgjd,akgd->agjbk", grad_five, value_block, preferred_element_type=jnp.float32
        )
        score_grad = (weights * (weight_grad - row_dot[..., None])).astype(jnp.bfloat16)
        return (
            summed
            + jnp.einsum(
                "agjbk,akgd->abgjd", score_grad, key_block, preferred_element_type=jnp.float32
            ),
            None,
        )

    query_grad, unused = lax.scan(query_step, jnp.zeros(five_shape, jnp.float32), key_starts)
    query_grad = query_grad.reshape(row_count, span_len, -1) * factor
    term_count = span_len * lax.axis_size("wide")
    sub_len = math.gcd(term_count, 512)

    def key_piece(sub_no):
        key_start = sub_no * sub_len
        key_block, value_block, seg_key, place_key = key_slices(key_start, sub_len)
        scores = masked_scores(
            query_five, key_block, seg_ids, seg_key, place_query, place_key, factor
        )
        weights = jnp.exp(scores - log_total[..., None])
        weight_grad = jnp.einsum(
            "abgjd,akgd->agjbk", grad_five, value_block, preferred_element_type=jnp.float32
        )
        score_grad = (weights * (weight_grad - row_dot[..., None])).astype(jnp.bfloat16)
        key_part = (
            jnp.einsum(
                "agjbk,abgjd->kagd", score_grad, query_five, preferred_element_type=jnp.float32
            )
            * factor
        )
        value_part = jnp.einsum(
            "agjbk,abgjd->kagd",
            weights.astype(jnp.bfloat16),
            grad_five,
            preferred_element_type=jnp.float32,
        )
        return jnp.concatenate(
            [
                key_part.reshape(sub_len, row_count, kv_width),
                value_part.reshape(sub_len, row_count, kv_width),
            ],
            axis=-1,
        )

    pieces = lax.map(key_piece, jnp.arange(term_count // sub_len, dtype=jnp.int32))
    summed_terms = lax.psum_scatter(
        pieces.reshape(term_count, row_count, 2 * kv_width).astype(jnp.bfloat16),
        "wide",
        scatter_dimension=0,
        tiled=True,
    ).astype(jnp.float32)
    key_grad = jnp.transpose(summed_terms[:, :, :kv_width], (1, 0, 2))
    value_grad = jnp.transpose(summed_terms[:, :, kv_width:], (1, 0, 2))
    query_back = (
        rotate_back(query_grad, cos_table, sin_table, turner)
        .astype(jnp.bfloat16)
        .reshape(tok_count, -1)
    )
    key_back = (
        rotate_back(key_grad, cos_table, sin_table, turner)
        .astype(jnp.bfloat16)
        .reshape(tok_count, -1)
    )
    value_back = value_grad.astype(jnp.bfloat16).reshape(tok_count, -1)
    flat_one = normed_one.reshape(tok_count, feat_dim)
    query_wgrad = jnp.einsum("td,te->de", flat_one, query_back, preferred_element_type=jnp.float32)
    key_wgrad = jnp.einsum("td,te->de", flat_one, key_back, preferred_element_type=jnp.float32)
    value_wgrad = jnp.einsum("td,te->de", flat_one, value_back, preferred_element_type=jnp.float32)
    normed_one_grad = (
        jnp.einsum("te,de->td", query_back, query_w, preferred_element_type=jnp.float32)
        + jnp.einsum("te,de->td", key_back, key_w, preferred_element_type=jnp.float32)
        + jnp.einsum("te,de->td", value_back, value_w, preferred_element_type=jnp.float32)
    )
    input_part, gain_one_grad = norm_back(
        inputs.reshape(tok_count, feat_dim),
        scale_one.reshape(tok_count, 1),
        gain_one_f,
        normed_one_grad,
    )
    input_grad = (
        (middle_grad + input_part).reshape(row_count, span_len, feat_dim).astype(jnp.bfloat16)
    )
    gain_one_sum, query_sum, key_wsum, value_wsum, output_sum, gain_two_sum, router_sum = (
        lax.psum_scatter(gain_one_grad, ("narrow", "wide"), scatter_dimension=0, tiled=True),
        lax.psum_scatter(query_wgrad, ("narrow", "wide"), scatter_dimension=0, tiled=True),
        lax.psum_scatter(key_wgrad, ("narrow", "wide"), scatter_dimension=0, tiled=True),
        lax.psum_scatter(value_wgrad, ("narrow", "wide"), scatter_dimension=0, tiled=True),
        lax.psum_scatter(output_wgrad, ("narrow", "wide"), scatter_dimension=0, tiled=True),
        lax.psum_scatter(gain_two_grad, ("narrow", "wide"), scatter_dimension=0, tiled=True),
        lax.psum_scatter(router_wgrad, ("narrow", "wide"), scatter_dimension=0, tiled=True),
    )
    gate_up_sum, down_sum = (
        lax.psum_scatter(
            gate_up_wgrad.astype(jnp.bfloat16), "narrow", scatter_dimension=1, tiled=True
        ).astype(jnp.float32),
        lax.psum_scatter(
            down_grad.astype(jnp.bfloat16), "narrow", scatter_dimension=1, tiled=True
        ).astype(jnp.float32),
    )
    return (
        block_out,
        input_grad,
        gain_one_sum,
        query_sum,
        key_wsum,
        value_wsum,
        output_sum,
        gain_two_sum,
        router_sum,
        gate_up_sum,
        down_sum,
        expert_load,
    )


def solution(mesh):
    return jax.shard_map(
        per_device,
        mesh=mesh,
        in_specs=(
            P("narrow", "wide", None),
            P("narrow", "wide", None),
            P("narrow", "wide"),
            P("narrow", "wide", None),
            P(("narrow", "wide")),
            P(("narrow", "wide"), None),
            P(("narrow", "wide"), None),
            P(("narrow", "wide"), None),
            P(("narrow", "wide"), None),
            P(("narrow", "wide")),
            P(("narrow", "wide"), None),
            P("wide", "narrow", None),
            P("wide", "narrow", None),
        ),
        out_specs=(
            P("narrow", "wide", None),
            P("narrow", "wide", None),
            P(("narrow", "wide")),
            P(("narrow", "wide"), None),
            P(("narrow", "wide"), None),
            P(("narrow", "wide"), None),
            P(("narrow", "wide"), None),
            P(("narrow", "wide")),
            P(("narrow", "wide"), None),
            P("wide", "narrow", None),
            P("wide", "narrow", None),
            P(),
        ),
        check_vma=False,
    )
```

profile of v0, /device:TPU:0, one launch (start us, length us, event | category | flops | bytes accessed | tf_op | source)
XLA Modules:
  0.0 1923.4 jit_solution(6807093027163768471)
XLA Ops:
  11.2 42.0 %all-reduce.5 = (bf16[1024]{0:T(1024)(128)(2,1)S(1)}, bf16[1024]{0:T(1024)(128)(2,1)S(1)}) all-reduce(bf16[1024]{0:T(1024)(128)(2,1)S(1)} %dynamic-update-slice, bf16[1024]{0:T(1024)(128)(2,1)S(1)} %dynamic-update-slice.1), channel_id=1, replica_groups=mesh['narrow'=4,'wide'=8] {'narrow','wide'}, use_global_device_ids=true, to_apply=%add | all-reduce | flops 2048 | bytes 8192
  55.1 12.2 all-gather.9.cloned.1.call-done
  70.0 8.9 all_gather.39
  81.1 41.7 %all-gather.13.cloned.1.call-done = bf16[1024,512]{1,0:T(8,128)(2,1)} async-done(((bf16[32,512]{1,0:T(8,128)(2,1)}), bf16[1024,512]{1,0:T(8,128)(2,1)}) %all-gather.13.cloned.1.call-update) | async-done | bytes 1048592 | tf_op jit(solution)/shard_map/all_gather | solution.py:104
  129.9 8.1 scatter_custom_fusion
  138.1 43.0 %all-gather.17.cloned.1.call-done = bf16[1024,1024]{1,0:T(8,128)(2,1)} async-done(((bf16[32,1024]{1,0:T(8,128)(2,1)}), bf16[1024,1024]{1,0:T(8,128)(2,1)}) %all-gather.17.cloned.1.call-update) | async-done | bytes 2097168 | tf_op jit(solution)/shard_map/all_gather | solution.py:103
  185.0 25.2 %all-gather.11.cloned.1.call-done = bf16[2,1024,512]{2,1,0:T(8,128)(2,1)} async-done(((bf16[2,128,512]{2,1,0:T(8,128)(2,1)}), bf16[2,1024,512]{2,1,0:T(8,128)(2,1)}) %all-gather.11.cloned.1.call-update) | async-done | bytes 2097168 | tf_op jit(solution)/shard_map/all_gather | solution.py:137
  213.4 27.4 %all-gather.15.cloned.1.call-done = bf16[2,1024,512]{1,2,0:T(8,128)(2,1)} async-done(((bf16[2,128,512]{1,2,0:T(8,128)(2,1)}), bf16[2,1024,512]{1,2,0:T(8,128)(2,1)}) %all-gather.15.cloned.1.call-update) | async-done | bytes 2097168 | tf_op jit(solution)/shard_map/all_gather | solution.py:136
  240.7 30.9 %while.58 = (s32[]{:T(128)}, f32[2,8,2,128]{3,2,1,0:T(2,128)S(1)}, f32[2,8,2,128]{3,2,1,0:T(2,128)S(1)}, s32[2,128]{1,0:T(2,128)S(1)}, s32[2]{0:T(128)S(1)}, /*i...) while((s32[]{:T(128)}, f32[2,8,2,128]{3,2,1,0:T(2,128)S(1)}, ...), condition=%wide.region_5.6_spmd.clone, body=%wide.region_2.5_spmd.clone.sunk | while | flops 283464320 | bytes 21203132 | solution.py:172
  271.7 25.4 %while.59 = (s32[]{:T(128)}, f32[2,128,8,2,64]{1,4,3,2,0:T(8,128)}, s32[2]{0:T(128)S(1)}, bf16[2,1024,512]{1,2,0:T(8,128)(2,1)S(1)}, s32[2,128]{1,0:T(2,128)S(1)...) while((s32[]{:T(128)}, f32[2,128,8,2,64]{1,4,3,2,0:T(8,128)}, ...), condition=%wide.region_7.8_spmd.clone, body=%wide.region_6.7_spmd.clone.sunk | while | flops 546112128 | bytes 9341125 | solution.py:190
  303.8 8.9 gather_fusion
  312.7 6.0 broadcast_select_fusion.1
  324.1 59.6 %all-to-all-done = bf16[32,80,1024]{2,1,0:T(8,128)(2,1)} async-done(((bf16[32,80,1024]{2,1,0:T(8,128)(2,1)}), bf16[32,80,1024]{2,1,0:T(8,128)(2,1)}, u32[]{:S(2)}, u32[]{:S(2)}) %all-to-all-start) | async-done | bytes 5242912 | tf_op jit(solution)/shard_map/all_to_all | solution.py:217
  389.4 60.5 %all-gather.21.cloned.1.call-done = bf16[4,1024,1024]{2,1,0:T(8,128)(2,1)} async-done(((bf16[4,256,1024]{2,1,0:T(8,128)(2,1)}), bf16[4,1024,1024]{2,1,0:T(8,128)(2,1)}) %all-gather.21.cloned.1.call-update) | async-done | bytes 8388624 | tf_op jit(solution)/shard_map/all_gather | solution.py:111
  450.0 9.9 fusion.183
  465.7 64.8 %all-gather.23.cloned.1.call-done = bf16[4,512,1024]{2,1,0:T(8,128)(2,1)} async-done(((bf16[4,128,1024]{2,1,0:T(8,128)(2,1)}), bf16[4,512,1024]{2,1,0:T(8,128)(2,1)}) %all-gather.23.cloned.1.call-update) | async-done | bytes 4194320 | tf_op jit(solution)/shard_map/all_gather | solution.py:112
  535.8 6.3 copy.171
  547.2 8.9 gather_fusion.1
  556.1 81.1 %all_gather.45 = bf16[1024,32]{1,0:T(8,128)(2,1)S(1)} all-gather(bf16[32,32]{1,0:T(8,128)(2,1)S(1)} %copy-done.57), channel_id=1, replica_groups=mesh['narrow'=4,'wide'=8] {'narrow','wide'}, dimensions={0}, use_global_device_ids=true | all-gather | bytes 67584 | tf_op jit(solution)/shard_map/all_gather | solution.py:108
  637.7 6.7 copy.172
  644.4 14.1 gather_fusion.3
  662.0 13.6 gather_fusion.2
  680.8 63.4 %all_to_all.66 = bf16[32,80,1024]{2,1,0:T(8,128)(2,1)S(1)} all-to-all(bf16[32,80,1024]{2,1,0:T(8,128)(2,1)S(1)} %multiply_convert_fusion), channel_id=1, replica_groups=mesh['narrow'=4,'wide'=8] {'wide'}, dimensions={0} | all-to-all | bytes 10485760 | tf_op jit(solution)/shard_map/all_to_all | solution.py:249
  747.2 11.0 multiply_convert_fusion.2
  758.2 10.0 fusion.77
  768.3 6.4 copy.177
  779.8 60.0 %all-to-all-done.3 = bf16[4,640,1024]{2,0,1:T(4,128)(2,1)} async-done(((bf16[4,640,1024]{2,0,1:T(4,128)(2,1)}), bf16[4,640,1024]{2,0,1:T(4,128)(2,1)}, u32[]{:S(2)}, u32[]{:S(2)}) %all-to-all-start.3) | async-done | bytes 5242912 | tf_op jit(solution)/shard_map/all_to_all | solution.py:267
  839.8 6.8 copy.178
  846.6 14.1 gather_fusion.4
  860.7 9.0 convert_reduce_fusion
  878.1 20.1 %while.60 = (s32[]{:T(128)}, f32[2,8,2,128]{3,2,1,0:T(2,128)S(1)}, s32[2,128]{1,0:T(2,128)S(1)}, s32[2]{0:T(128)S(1)}, s32[2,1024]{1,0:T(2,128)S(1)}, /*index=5*...) while((s32[]{:T(128)}, f32[2,8,2,128]{3,2,1,0:T(2,128)S(1)}, ...), condition=%wide.region_25.27_spmd.clone, body=%wide.region_23.26_spmd.clone.sunk | while | flops 547689088 | bytes 26708200 | solution.py:301
  898.2 48.4 %while.57 = (s32[]{:T(128)}, bf16[2,512,2,1024]{1,3,2,0:T(8,128)(2,1)}, s32[2,128]{1,0:T(2,128)S(1)}, s32[2]{0:T(128)S(1)}, s32[2,1024]{1,0:T(2,128)S(1)}, /*ind...) while((s32[]{:T(128)}, ...), condition=%wide.region_29.31_spmd.clone, body=%wide.region_28.30_spmd.clone.sunk | while | flops 1100284544 | bytes 44632828 | solution.py:354
  907.3 8.4 bitcast_multiply_fusion.11
  931.3 8.4 bitcast_multiply_fusion.11
  946.6 6.2 copy.190
  952.9 9.1 convolution_convert_fusion.2
  962.0 12.6 convolution_convert_fusion
  982.7 42.2 %while.61 = (s32[]{:T(128)}, f32[2,128,8,2,64]{1,4,3,2,0:T(8,128)}, s32[2]{0:T(128)S(1)}, bf16[2,1024,512]{1,2,0:T(8,128)(2,1)S(1)}, s32[2,128]{1,0:T(2,128)S(1)...) while((s32[]{:T(128)}, f32[2,128,8,2,64]{1,4,3,2,0:T(8,128)}, ...), condition=%wide.region_27.29_spmd.clone, body=%wide.region_26.28_spmd.clone.sunk | while | flops 818741888 | bytes 31901936 | solution.py:318
  995.2 8.5 fusion.302
  1016.2 8.7 fusion.302
  1038.1 41.3 %psum.7 = s32[32]{0:T(128)} all-reduce(s32[32]{0:T(128)S(1)} %copy-done.58), channel_id=1, replica_groups=mesh['narrow'=4,'wide'=8] {'narrow','wide'}, use_global_device_ids=true, to_apply=%region_44.46 | all-reduce | flops 32 | bytes 256 | tf_op jit(solution)/shard_map/psum | solution.py:203
  1091.1 45.9 %all-reduce.4 = (f32[1024]{0:T(1024)S(1)}, f32[1024]{0:T(1024)S(1)}) all-reduce(f32[1024]{0:T(1024)S(1)} %get-tuple-element.659, f32[1024]{0:T(1024)S(1)} %copy-done.47), channel_id=3, replica_groups=mesh['narrow'=4,'wide'=8] {'narrow','wide'}, use_global_device_ids=true, to_apply=%region_33.35.clone | all-reduce | flops 2048 | bytes 16384
  1139.3 89.8 %reduce-scatter.21.cloned.1.call-done = bf16[4,256,1024]{2,1,0:T(8,128)(2,1)} async-done(((bf16[4,1024,1024]{2,1,0:T(8,128)(2,1)}), bf16[4,256,1024]{2,1,0:T(8,128)(2,1)}) %reduce-scatter.21.cloned.1.call-update) | async-done | bytes 2097168 | tf_op jit(solution)/shard_map/reduce_scatter | solution.py:402
  1233.2 133.3 %reduce-scatter.19.cloned.1.call-done = f32[32,32]{1,0:T(8,128)} async-done(((f32[1024,32]{1,0:T(8,128)}), f32[32,32]{1,0:T(8,128)}) %reduce-scatter.19.cloned.1.call-update) | async-done | bytes 4112 | tf_op jit(solution)/shard_map/reduce_scatter | solution.py:399
  1366.5 139.8 %reduce-scatter.17.cloned.1.call-done = f32[32,1024]{1,0:T(8,128)} async-done(((f32[1024,1024]{1,0:T(8,128)}), f32[32,1024]{1,0:T(8,128)}) %reduce-scatter.17.cloned.1.call-update) | async-done | bytes 131088 | tf_op jit(solution)/shard_map/reduce_scatter | solution.py:397
  1506.3 139.8 %reduce-scatter.11.cloned.1.call-done = f32[32,1024]{1,0:T(8,128)} async-done(((f32[1024,1024]{1,0:T(8,128)}), f32[32,1024]{1,0:T(8,128)}) %reduce-scatter.11.cloned.1.call-update) | async-done | bytes 131088 | tf_op jit(solution)/shard_map/reduce_scatter | solution.py:394
  1646.0 135.3 %reduce-scatter.13.cloned.1.call-done = f32[32,512]{1,0:T(8,128)} async-done(((f32[1024,512]{1,0:T(8,128)}), f32[32,512]{1,0:T(8,128)}) %reduce-scatter.13.cloned.1.call-update) | async-done | bytes 65552 | tf_op jit(solution)/shard_map/reduce_scatter | solution.py:395
  1781.4 135.2 %reduce-scatter.15.cloned.1.call-done = f32[32,512]{1,0:T(8,128)} async-done(((f32[1024,512]{1,0:T(8,128)}), f32[32,512]{1,0:T(8,128)}) %reduce-scatter.15.cloned.1.call-update) | async-done | bytes 65552 | tf_op jit(solution)/shard_map/reduce_scatter | solution.py:396
  (380 shorter events, 238.2 us)
Async XLA Ops:
  7.2 120.5 %copy-start.36 = (s32[2,128,8]{1,2,0:T(8,128)S(1)}, s32[2,128,8]{1,2,0:T(8,128)}, u32[]{:S(2)}) copy-start(s32[2,128,8]{1,2,0:T(8,128)} %param.28) | copy-start | bytes 24580
  7.2 60.1 %all-gather.9.cloned.1.call-start = ((), (), s32[]{:S(2)}) async-start(), calls=%async_computation.12 | async-start | bytes 1081344 | tf_op jit(solution)/shard_map/all_gather | solution.py:105
  7.9 173.2 %copy-start.7 = (bf16[2,128,1024]{2,1,0:T(8,128)(2,1)S(1)}, bf16[2,128,1024]{2,1,0:T(8,128)(2,1)}, u32[]{:S(2)}) copy-start(bf16[2,128,1024]{2,1,0:T(8,128)(2,1)} %param.25) | copy-start | bytes 1572868
  7.9 114.9 %all-gather.13.cloned.1.call-start = ((), (), s32[]{:S(2)}) async-start(), calls=%async_computation.14 | async-start | bytes 1081344 | tf_op jit(solution)/shard_map/all_gather | solution.py:104
  8.7 172.4 %all-gather.17.cloned.1.call-start = ((), (), s32[]{:S(2)}) async-start(), calls=%async_computation.16 | async-start | bytes 2162688 | tf_op jit(solution)/shard_map/all_gather | solution.py:103
  9.4 200.8 %all-gather.11.cloned.1.call-start = ((), (), s32[]{:S(2)}) async-start(), calls=%async_computation.13 | async-start | bytes 2359296 | tf_op jit(solution)/shard_map/all_gather | solution.py:137
  53.2 130.5 %copy-start.37 = (f32[1024]{0:T(1024)}, f32[1024]{0:T(1024)S(1)}, u32[]{:S(2)}) copy-start(f32[1024]{0:T(1024)S(1)} %convert_element_type.174) | copy-start | bytes 12292
  54.5 73.1 %copy-start.51 = (f32[2,128]{1,0:T(2,128)}, f32[2,128]{1,0:T(2,128)S(1)}, u32[]{:S(2)}) copy-start(f32[2,128]{1,0:T(2,128)S(1)} %fusion.91) | copy-start | bytes 3076
  55.1 128.6 %copy-start.45 = (f32[2,128]{1,0:T(2,128)}, f32[2,128]{1,0:T(2,128)S(1)}, u32[]{:S(2)}) copy-start(f32[2,128]{1,0:T(2,128)S(1)} %get-tuple-element.802) | copy-start | bytes 3076
  69.9 170.8 %all-gather.15.cloned.1.call-start = ((), (), s32[]{:S(2)}) async-start(), calls=%async_computation.15 | async-start | bytes 2359296 | tf_op jit(solution)/shard_map/all_gather | solution.py:136
  78.9 104.8 %copy-start.39 = (s32[128]{0:T(128)}, s32[128]{0:T(128)S(1)}, u32[]{:S(2)}) copy-start(s32[128]{0:T(128)S(1)} %broadcast_add_fusion) | copy-start | bytes 1540
  78.9 104.8 %copy-start.41 = (s32[128]{0:T(128)}, s32[128]{0:T(128)S(1)}, u32[]{:S(2)}) copy-start(s32[128]{0:T(128)S(1)} %get-tuple-element.809) | copy-start | bytes 1540
  78.9 104.8 %copy-start.43 = (s32[128]{0:T(128)}, s32[128]{0:T(128)S(1)}, u32[]{:S(2)}) copy-start(s32[128]{0:T(128)S(1)} %get-tuple-element.810) | copy-start | bytes 1540
  78.9 104.8 %copy-start.53 = (pred[128]{0:T(512)(128)(4,1)}, pred[128]{0:T(512)(128)(4,1)S(1)}, u32[]{:S(2)}) copy-start(pred[128]{0:T(512)(128)(4,1)S(1)} %get-tuple-element.811) | copy-start | bytes 388
  79.0 104.8 %copy-start.55 = (pred[128]{0:T(512)(128)(4,1)}, pred[128]{0:T(512)(128)(4,1)S(1)}, u32[]{:S(2)}) copy-start(pred[128]{0:T(512)(128)(4,1)S(1)} %get-tuple-element.812) | copy-start | bytes 388
  81.1 103.9 %copy-start.21 = (f32[2,128,128]{1,2,0:T(8,128)}, f32[2,128,128]{1,2,0:T(8,128)S(1)}, u32[]{:S(2)}) copy-start(f32[2,128,128]{1,2,0:T(8,128)S(1)} %get-tuple-element.799) | copy-start | bytes 393220
  81.1 103.9 %copy-start.23 = (f32[2,128,128]{1,2,0:T(8,128)}, f32[2,128,128]{1,2,0:T(8,128)S(1)}, u32[]{:S(2)}) copy-start(f32[2,128,128]{1,2,0:T(8,128)S(1)} %get-tuple-element.800) | copy-start | bytes 393220
  126.3 173.7 %all-gather.19.cloned.1.call-start = ((), (), s32[]{:S(2)}) async-start(), calls=%async_computation.17 | async-start | bytes 2162688 | tf_op jit(solution)/shard_map/all_gather | solution.py:106
  126.9 323.1 %all-gather.21.cloned.1.call-start = ((), (), s32[]{:S(2)}) async-start(), calls=%async_computation.18 | async-start | bytes 10485760 | tf_op jit(solution)/shard_map/all_gather | solution.py:111
  128.7 112.1 %copy-start.30 = (s32[2,128]{1,0:T(2,128)S(1)}, s32[2,128]{1,0:T(2,128)}, u32[]{:S(2)}) copy-start(s32[2,128]{1,0:T(2,128)} %param.27) | copy-start | bytes 3076
  129.7 111.0 %copy-start.27 = (s32[2,128,8]{2,1,0:T(8,128)}, s32[2,128,8]{2,1,0:T(8,128)S(1)}, u32[]{:S(2)}) copy-start(s32[2,128,8]{2,1,0:T(8,128)S(1)} %copy.167) | copy-start | bytes 24580
  303.7 333.6 %copy-start = (bf16[2,128,1024]{2,1,0:T(8,128)(2,1)}, bf16[2,128,1024]{2,1,0:T(8,128)(2,1)S(1)}, u32[]{:S(2)}) copy-start(bf16[2,128,1024]{2,1,0:T(8,128)(2,1)S(1)} %multiply_convert_fusion.4) | copy-start | bytes 1572868
  318.7 65.0 %all-to-all-start = ((bf16[32,80,1024]{2,1,0:T(8,128)(2,1)}), bf16[32,80,1024]{2,1,0:T(8,128)(2,1)}, u32[]{:S(2)}, u32[]{:S(2)}) async-start(bf16[32,80,1024]{2,1,0:T(8,128)(2,1)} %broadcast_select_fusion.1), calls=%async_computation | async-start | bytes 10485760 | tf_op jit(solution)/shard_map/all_to_all | solution.py:217
  323.3 207.2 %all-gather.23.cloned.1.call-start = ((), (), s32[]{:S(2)}) async-start(), calls=%async_computation.19 | async-start | bytes 5242880 | tf_op jit(solution)/shard_map/all_gather | solution.py:112
  465.7 70.1 %copy-start.18 = (bf16[4,640,512]{2,1,0:T(8,128)(2,1)}, bf16[4,640,512]{2,1,0:T(8,128)(2,1)S(1)}, u32[]{:S(2)}) copy-start(bf16[4,640,512]{2,1,0:T(8,128)(2,1)S(1)} %multiply_convert_fusion.3) | copy-start | bytes 7864324
  542.1 95.6 %all-to-all-start.1 = ((bf16[4,640,1024]{2,0,1:T(4,128)(2,1)}), bf16[4,640,1024]{2,0,1:T(4,128)(2,1)}, u32[]{:S(2)}, u32[]{:S(2)}) async-start(bf16[4,640,1024]{2,0,1:T(4,128)(2,1)} %copy.171), calls=%async_computation.1 | async-start | bytes 10485760 | tf_op jit(solution)/shard_map/all_to_all | solution.py:227
  680.7 66.5 %slice-start = ((s8[10485760]{0:T(1024)(128)(4,1)}), s8[4194304]{0:T(1024)(128)(4,1)S(1)}, s32[]{:S(2)}) async-start(s8[10485760]{0:T(1024)(128)(4,1)} %bitcast.489), calls=%async_computation.28 | async-start | bytes 8388608
  680.8 66.4 %slice-start.1 = ((s8[10485760]{0:T(1024)(128)(4,1)}), s8[4194304]{0:T(1024)(128)(4,1)S(1)}, s32[]{:S(2)}) async-start(s8[10485760]{0:T(1024)(128)(4,1)} %bitcast.489), calls=%async_computation.29 | async-start | bytes 8388608
  774.7 65.0 %all-to-all-start.3 = ((bf16[4,640,1024]{2,0,1:T(4,128)(2,1)}), bf16[4,640,1024]{2,0,1:T(4,128)(2,1)}, u32[]{:S(2)}, u32[]{:S(2)}) async-start(bf16[4,640,1024]{2,0,1:T(4,128)(2,1)} %copy.177), calls=%async_computation.3 | async-start | bytes 10485760 | tf_op jit(solution)/shard_map/all_to_all | solution.py:267
  779.4 251.2 %reduce-scatter.9.cloned.1.call-start = ((), (), s32[]{:S(2)}) async-start(), calls=%async_computation.20 | async-start | bytes 4718592 | tf_op jit(solution)/shard_map/reduce_scatter | solution.py:355
  952.8 131.2 %reduce-scatter.23.cloned.1.call-start = ((), (), s32[]{:S(2)}) async-start(), calls=%async_computation.27 | async-start | bytes 5242880 | tf_op jit(solution)/shard_map/reduce_scatter | solution.py:405
  962.0 267.1 %reduce-scatter.21.cloned.1.call-start = ((), (), s32[]{:S(2)}) async-start(), calls=%async_computation.26 | async-start | bytes 10485760 | tf_op jit(solution)/shard_map/reduce_scatter | solution.py:402
  974.7 391.8 %reduce-scatter.19.cloned.1.call-start = ((), (), s32[]{:S(2)}) async-start(), calls=%async_computation.25 | async-start | bytes 540672 | tf_op jit(solution)/shard_map/reduce_scatter | solution.py:399
  978.3 527.9 %reduce-scatter.17.cloned.1.call-start = ((), (), s32[]{:S(2)}) async-start(), calls=%async_computation.24 | async-start | bytes 4325376 | tf_op jit(solution)/shard_map/reduce_scatter | solution.py:397
  982.6 663.5 %reduce-scatter.11.cloned.1.call-start = ((), (), s32[]{:S(2)}) async-start(), calls=%async_computation.21 | async-start | bytes 4325376 | tf_op jit(solution)/shard_map/reduce_scatter | solution.py:394
  982.6 42.3 %copy-start.34 = (f32[2,128,128]{1,2,0:T(8,128)S(1)}, f32[2,128,128]{1,2,0:T(8,128)}, u32[]{:S(2)}) copy-start(f32[2,128,128]{1,2,0:T(8,128)} %get-tuple-element.797) | copy-start | bytes 393220
  982.6 42.3 %copy-start.35 = (f32[2,128,128]{1,2,0:T(8,128)S(1)}, f32[2,128,128]{1,2,0:T(8,128)}, u32[]{:S(2)}) copy-start(f32[2,128,128]{1,2,0:T(8,128)} %get-tuple-element.798) | copy-start | bytes 393220
  982.6 43.7 %copy-start.40 = (s32[128]{0:T(128)S(1)}, s32[128]{0:T(128)}, u32[]{:S(2)}) copy-start(s32[128]{0:T(128)} %copy-done.39) | copy-start | bytes 1540
  982.7 43.7 %copy-start.42 = (s32[128]{0:T(128)S(1)}, s32[128]{0:T(128)}, u32[]{:S(2)}) copy-start(s32[128]{0:T(128)} %copy-done.41) | copy-start | bytes 1540
  982.7 43.7 %copy-start.44 = (s32[128]{0:T(128)S(1)}, s32[128]{0:T(128)}, u32[]{:S(2)}) copy-start(s32[128]{0:T(128)} %copy-done.43) | copy-start | bytes 1540
  982.7 43.7 %copy-start.54 = (pred[128]{0:T(512)(128)(4,1)S(1)}, pred[128]{0:T(512)(128)(4,1)}, u32[]{:S(2)}) copy-start(pred[128]{0:T(512)(128)(4,1)} %copy-done.53) | copy-start | bytes 388
  982.7 43.7 %copy-start.56 = (pred[128]{0:T(512)(128)(4,1)S(1)}, pred[128]{0:T(512)(128)(4,1)}, u32[]{:S(2)}) copy-start(pred[128]{0:T(512)(128)(4,1)} %copy-done.55) | copy-start | bytes 388
  1030.5 750.9 %reduce-scatter.13.cloned.1.call-start = ((), (), s32[]{:S(2)}) async-start(), calls=%async_computation.22 | async-start | bytes 2162688 | tf_op jit(solution)/shard_map/reduce_scatter | solution.py:395
  1033.3 46.2 %copy-start.52 = (f32[2,128]{1,0:T(2,128)S(1)}, f32[2,128]{1,0:T(2,128)}, u32[]{:S(2)}) copy-start(f32[2,128]{1,0:T(2,128)} %copy-done.51) | copy-start | bytes 3076
  1033.3 47.2 %copy-start.12 = (f32[2,128,1024]{2,1,0:T(8,128)S(1)}, f32[2,128,1024]{2,1,0:T(8,128)}, u32[]{:S(2)}) copy-start(f32[2,128,1024]{2,1,0:T(8,128)} %copy-done.10) | copy-start | bytes 3145732
  1033.3 47.2 %copy-start.17 = (f32[256,1024]{1,0:T(8,128)S(1)}, f32[256,1024]{1,0:T(8,128)}, u32[]{:S(2)}) copy-start(f32[256,1024]{1,0:T(8,128)} %get-tuple-element.664) | copy-start | bytes 3145732
  1035.2 881.4 %reduce-scatter.15.cloned.1.call-start = ((), (), s32[]{:S(2)}) async-start(), calls=%async_computation.23 | async-start | bytes 2162688 | tf_op jit(solution)/shard_map/reduce_scatter | solution.py:396
  1084.0 54.2 %copy-start.14 = (f32[256,1024]{1,0:T(8,128)S(1)}, f32[256,1024]{1,0:T(8,128)}, u32[]{:S(2)}) copy-start(f32[256,1024]{1,0:T(8,128)} %copy-done.13) | copy-start | bytes 3145732
  (38 other events, 239.2 us)
Sparse Core Ops, SparseCore 0:
  10.9 56.4 all-gather.8
  70.2 52.6 all-gather.12
  125.7 55.3 all-gather.16
  183.4 26.7 all-gather.10
  212.5 28.1 all-gather.14
  243.4 56.4 all-gather.18
  301.5 148.4 all-gather.20
  451.5 78.9 all-gather.22
  952.9 47.6 reduce-scatter.8
  1002.9 77.8 reduce-scatter.22
  1083.1 145.9 reduce-scatter.20
  1231.8 134.6 reduce-scatter.18
  1369.4 136.8 reduce-scatter.16
  1509.1 136.9 reduce-scatter.10
  1648.8 132.5 reduce-scatter.12
  1784.1 132.4 reduce-scatter.14
where the time goes:
time: 1930 us; the launch traced here: 1920 us
  waiting for transfers between devices  1170 us (61%)
  blocking collectives  283 us (15%)
  matrix products  185 us (10%)
  local copies, waits for them, and re-layouts  167 us (9%)
  other arithmetic  68.6 us (4%)
    reduce_scatter x1, waiting for transfers between devices, per_device(): lax.psum_scatter(output_wgrad, ('narrow', 'wide'), scatter_dimension=0, t...  140 us
    reduce_scatter x1, waiting for transfers between devices, per_device(): lax.psum_scatter(query_wgrad, ('narrow', 'wide'), scatter_dimension=0, ti...  140 us
    reduce_scatter x1, waiting for transfers between devices, per_device(): lax.psum_scatter(key_wgrad, ('narrow', 'wide'), scatter_dimension=0, tile...  135 us
    reduce_scatter x1, waiting for transfers between devices, per_device(): lax.psum_scatter(value_wgrad, ('narrow', 'wide'), scatter_dimension=0, ti...  135 us
    reduce_scatter x1, waiting for transfers between devices, per_device(): lax.psum_scatter(router_wgrad, ('narrow', 'wide'), scatter_dimension=0, t...  133 us
    reduce_scatter x1, waiting for transfers between devices, per_device(): lax.psum_scatter(gate_up_wgrad.astype(jnp.bfloat16), 'narrow', scatter_di...  89.8 us
    unnamed x2, blocking collectives  88 us
    all_gather x1, blocking collectives, per_device(): lax.all_gather(w_router, ('narrow', 'wide'), axis=0, tiled=True)  81.1 us
  transfers between devices with their start and end apart: 19, of which 15 were waited for; matrix products, arithmetic and copies ran while one was open for 12% of the time, Pallas kernels for 0%

commit v1 on v0

--- a/solution.py
+++ b/solution.py
@@ -2,7 +2,10 @@
 
 import jax
 import jax.numpy as jnp
+import numpy as np
 from jax import lax
+from jax.experimental import pallas as pl
+from jax.experimental.pallas import tpu as pltpu
 from jax.sharding import PartitionSpec as P
 
 KV_HEADS = 8
@@ -79,7 +82,7 @@
     return jnp.where(allowed[:, None, None], scores, MASKED)
 
 
-def per_device(
+def general_device(
     hidden_in,
     out_grad,
     seg_ids,
@@ -422,9 +425,1336 @@
     )
 
 
+MESH = pl.DeviceIdType.MESH
+F32 = jnp.float32
+BF16 = jnp.bfloat16
+IN_HBM = pl.BlockSpec(memory_space=pl.ANY)
+IN_VMEM = pl.BlockSpec(memory_space=pltpu.VMEM)
+VMEM_BYTES = 60 * 1024 * 1024
+NARROW = 4
+WIDE = 8
+GROUP = 16
+TOKENS = 256
+SPAN = 128
+WIDTH = 1024
+SEQ = 1024
+SLOTS = 80
+MINE = 2
+CHUNK = 4
+NT = (((1,), (1,)), ((), ()))
+TN = (((0,), (0,)), ((), ()))
+
+
+def mm(left, right, dims=(((1,), (0,)), ((), ()))):
+    return lax.dot_general(left, right, dims, preferred_element_type=F32)
+
+
+class Spot:
+    def __init__(self):
+        self.n = lax.axis_index("narrow")
+        self.w = lax.axis_index("wide")
+        self.core = lax.rem(self.w, 2)
+        self.x = lax.rem(lax.div(self.w, 2), 2)
+        self.y = lax.div(self.w, 4)
+        self.half = lax.rem(self.n, 2)
+        self.me = self.n * WIDE + self.w
+        self.sib = self.w + 1 - 2 * self.core
+        self.xn = self.w + 2 - 4 * self.x
+        self.yn = self.w + 4 - 8 * self.y
+        self.diag = self.xn + 4 - 8 * self.y
+        self.mate = self.n + 1 - 2 * self.half
+        self.slot = self.half * WIDE + self.w
+
+    def wide(self, to):
+        return (self.n, to)
+
+    def greet(self, count):
+        barrier = pltpu.get_barrier_semaphore()
+        base = self.n - self.half
+
+        def signal(step, carry):
+            if count == WIDE:
+                to = (self.n, lax.rem(self.w + step, WIDE))
+            elif count == GROUP:
+                other = lax.rem(self.slot + step, GROUP)
+                to = (base + lax.div(other, WIDE), lax.rem(other, WIDE))
+            else:
+                other = lax.rem(self.me + step, NARROW * WIDE)
+                to = (lax.div(other, WIDE), lax.rem(other, WIDE))
+            pl.semaphore_signal(barrier, inc=1, device_id=to, device_id_type=MESH)
+            return carry
+
+        lax.fori_loop(1, count, signal, 0)
+        pl.semaphore_wait(barrier, count - 1)
+
+
+def remote(src, dst, send_sem, recv_sem, to):
+    return pltpu.make_async_remote_copy(
+        src_ref=src, dst_ref=dst, send_sem=send_sem, recv_sem=recv_sem, device_id=to, device_id_type=MESH
+    )
+
+
+def halves(ref, which):
+    return ref.at[pl.ds(which * SPAN, SPAN)]
+
+
+class PlaneGather:
+    COPIES = 11
+
+    def __init__(self, spot, own, out, base, send, recv):
+        self.spot, self.own, self.out, self.base = spot, own, out, base
+        self.send, self.recv = send, recv
+        self.started = []
+
+    def block(self, who):
+        return self.out.at[self.base + who]
+
+    def put(self, src, dst, number, to):
+        copy = remote(src, dst, self.send.at[number], self.recv.at[number], self.spot.wide(to))
+        copy.start()
+        self.started.append(copy)
+
+    def got(self, dst, number):
+        remote(dst, dst, self.send.at[number], self.recv.at[number], self.spot.wide(self.spot.sib)).wait_recv()
+
+    def begin(self):
+        s = self.spot
+        mine = self.block(s.w)
+        self.put(halves(self.own, 0), halves(mine, 0), 0, s.xn)
+        self.put(halves(self.own, 1), halves(mine, 1), 2, s.yn)
+        self.put(halves(self.own, 1), halves(mine, 1), 1, s.xn)
+        self.put(halves(self.own, 0), halves(mine, 0), 3, s.yn)
+        self.put(self.own, mine, 4, s.sib)
+
+    def middle(self):
+        s = self.spot
+        from_x, from_y = self.block(s.xn), self.block(s.yn)
+        self.got(halves(from_x, 0), 0)
+        self.put(halves(from_x, 0), halves(from_x, 0), 5, s.yn)
+        self.got(halves(from_y, 1), 2)
+        self.put(halves(from_y, 1), halves(from_y, 1), 6, s.xn)
+
+    def late(self):
+        s = self.spot
+        from_x, from_y = self.block(s.xn), self.block(s.yn)
+        self.got(halves(from_x, 1), 1)
+        self.put(from_x, from_x, 7, s.sib)
+        self.got(halves(from_y, 0), 3)
+        self.put(from_y, from_y, 8, s.sib)
+
+    def last(self):
+        s = self.spot
+        from_d = self.block(s.diag)
+        self.got(halves(from_d, 0), 5)
+        self.put(halves(from_d, 0), halves(from_d, 0), 9, s.sib)
+        self.got(halves(from_d, 1), 6)
+        self.put(halves(from_d, 1), halves(from_d, 1), 10, s.sib)
+
+    def finish(self):
+        s = self.spot
+        sib = s.sib
+        sib_x = sib + 2 - 4 * s.x
+        sib_y = sib + 4 - 8 * s.y
+        sib_d = sib_x + 4 - 8 * s.y
+        self.got(self.block(sib), 4)
+        self.got(self.block(sib_x), 7)
+        self.got(self.block(sib_y), 8)
+        self.got(halves(self.block(sib_d), 0), 9)
+        self.got(halves(self.block(sib_d), 1), 10)
+        for copy in self.started:
+            copy.wait_send()
+
+
+def gather_kernel(x_ref, w_ref, g_ref, seg_ref, x_all, w_all, g_all, seg_all, send, recv, local, ws, wr, gs, gr, ss, sr):
+    spot = Spot()
+    spot.greet(NARROW * WIDE)
+    own = [
+        pltpu.make_async_copy(x_ref, x_all.at[spot.w], local.at[0]),
+        pltpu.make_async_copy(w_ref.at[:, pl.ds(pl.multiple_of(spot.w * 256, 256), 256)], w_all.at[spot.me], local.at[1]),
+        pltpu.make_async_copy(g_ref, g_all.at[spot.me], local.at[2]),
+        pltpu.make_async_copy(seg_ref, seg_all.at[spot.w], local.at[3]),
+    ]
+    gather = PlaneGather(spot, x_ref, x_all, 0, send, recv)
+    gather.begin()
+    for copy in own:
+        copy.start()
+
+    def others(step):
+        other = lax.rem(spot.me + step, NARROW * WIDE)
+        return other, lax.div(other, WIDE), lax.rem(other, WIDE)
+
+    def weights(step, arriving):
+        other, o_n, o_w = others(step)
+        source = w_ref.at[:, pl.ds(pl.multiple_of(o_w * 256, 256), 256)]
+        place = other if arriving else spot.me
+        return (
+            remote(source, w_all.at[place], ws.at[other], wr.at[place], (o_n, o_w)),
+            remote(g_ref, g_all.at[place], gs.at[other], gr.at[place], (o_n, o_w)),
+        )
+
+    def documents(step, arriving):
+        other = lax.rem(spot.w + step, WIDE)
+        place = other if arriving else spot.w
+        return remote(seg_ref, seg_all.at[place], ss.at[other], sr.at[place], spot.wide(other))
+
+    def start(step, carry):
+        for copy in weights(step, False):
+            copy.start()
+        return carry
+
+    def start_documents(step, carry):
+        documents(step, False).start()
+        return carry
+
+    lax.fori_loop(1, WIDE, start_documents, 0)
+    lax.fori_loop(1, NARROW * WIDE, start, 0)
+    gather.middle()
+    gather.late()
+    gather.last()
+
+    def wait(step, carry):
+        for copy in weights(step, False):
+            copy.wait_send()
+        for copy in weights(step, True):
+            copy.wait_recv()
+        return carry
+
+    def wait_documents(step, carry):
+        documents(step, False).wait_send()
+        documents(step, True).wait_recv()
+        return carry
+
+    lax.fori_loop(1, WIDE, wait_documents, 0)
+    lax.fori_loop(1, NARROW * WIDE, wait, 0)
+    gather.finish()
+    for copy in own:
+        copy.wait()
+
+
+def gather_call(x_own, w_own, g_own, seg_own):
+    dma = pltpu.SemaphoreType.DMA
+    return pl.pallas_call(
+        gather_kernel,
+        name="gather_inputs",
+        out_shape=(
+            jax.ShapeDtypeStruct((WIDE, TOKENS, WIDTH), BF16),
+            jax.ShapeDtypeStruct((NARROW * WIDE, 32, 256), BF16),
+            jax.ShapeDtypeStruct((NARROW * WIDE, 8, 128), F32),
+            jax.ShapeDtypeStruct((WIDE, 8, 128), jnp.int32),
+        ),
+        in_specs=[IN_HBM] * 4,
+        out_specs=(IN_HBM,) * 4,
+        scratch_shapes=[
+            dma((PlaneGather.COPIES,)),
+            dma((PlaneGather.COPIES,)),
+            dma((4,)),
+            dma((NARROW * WIDE,)),
+            dma((NARROW * WIDE,)),
+            dma((NARROW * WIDE,)),
+            dma((NARROW * WIDE,)),
+            dma((WIDE,)),
+            dma((WIDE,)),
+        ],
+        compiler_params=pltpu.CompilerParams(collective_id=1, has_side_effects=True),
+    )(x_own, w_own, g_own, seg_own)
+
+
+def lane_half():
+    lanes = lax.broadcasted_iota(jnp.int32, (1, 128), 1)
+    return lax.rem(lanes, 64) < 32
+
+
+def turn(values, first_half):
+    return jnp.where(first_half, -pltpu.roll(values, 96, 1), pltpu.roll(values, 32, 1))
+
+
+def turn_back(values, first_half):
+    return jnp.where(first_half, pltpu.roll(values, 96, 1), -pltpu.roll(values, 32, 1))
+
+
+def gather_gain(gains):
+    lane = lax.broadcasted_iota(jnp.int32, (128, WIDTH), 0)
+    column = lax.broadcasted_iota(jnp.int32, (128, WIDTH), 1)
+    spread = (lax.rem(column, 32) == lane).astype(BF16)
+    tiled = mm(gains.astype(BF16), spread)
+    owner = lax.broadcasted_iota(jnp.int32, (32, WIDTH), 0)
+    place = lax.broadcasted_iota(jnp.int32, (32, WIDTH), 1)
+    return jnp.sum(jnp.where(lax.div(place, 32) == owner, tiled, 0.0), axis=0, keepdims=True)
+
+
+def attend_kernel(x_ref, w_ref, g_ref, seg_ref, cos_ref, sin_ref, freq_ref, h1_ref, qkv_ref, lse_ref, o_ref, angle_ref, start_ref, gain_ref):
+    row = pl.program_id(0)
+    first_half = lane_half()
+    lanes = lax.broadcasted_iota(jnp.int32, (1, 128), 1)
+    weights = w_ref[...].reshape(WIDTH, 256)
+    gains = g_ref[...]
+    gain_one = gather_gain(gains[:, 0, :])
+    gain_two = gather_gain(gains[:, 1, :])
+    gain_ref[...] = jnp.concatenate([gain_one, gain_two, jnp.zeros((6, WIDTH), F32)], axis=0)
+    segs = [jnp.where(row == 0, seg_ref[c, 0:1, :], seg_ref[c, 1:2, :]) for c in range(WIDE)]
+    counts = []
+    for doc in range(5):
+        total = jnp.zeros((1, 128), F32)
+        for c in range(WIDE):
+            total = total + (segs[c] == doc).astype(F32)
+        counts.append(jnp.sum(total, axis=1, keepdims=True))
+    starts = [jnp.zeros((1, 1), F32)]
+    for doc in range(5):
+        starts.append(starts[-1] + counts[doc])
+    start_rows = jnp.concatenate(starts + starts[:2], axis=0)
+    start_angle = start_rows * freq_ref[0:1, :]
+    start_cos = jnp.cos(start_angle)
+    start_sin = jnp.sin(start_angle)
+
+    for i in range(4):
+        tokens = pl.ds(i * 256, 256)
+        seg_cols = [
+            jnp.transpose(jnp.broadcast_to(segs[2 * i + part].astype(F32), (128, 128))) for part in range(2)
+        ]
+        seg_col = jnp.concatenate(seg_cols, axis=0)
+        start_col = jnp.zeros((256, 128), F32)
+        cos_s = jnp.broadcast_to(start_cos[0:1], (256, 128))
+        sin_s = jnp.broadcast_to(start_sin[0:1], (256, 128))
+        for doc in range(1, 6):
+            here = seg_col == float(doc)
+            start_col = jnp.where(here, starts[doc], start_col)
+            cos_s = jnp.where(here, start_cos[doc : doc + 1], cos_s)
+            sin_s = jnp.where(here, start_sin[doc : doc + 1], sin_s)
+        start_ref[0, tokens, :] = start_col
+        cos_t = cos_ref[tokens, :]
+        sin_t = sin_ref[tokens, :]
+        cosine = cos_t * cos_s + sin_t * sin_s
+        sine = sin_t * cos_s - cos_t * sin_s
+        angle_ref[0, tokens, 0:128] = cosine
+        angle_ref[0, tokens, 128:256] = sine
+        is_key = lanes < 64
+        x = x_ref[2 * i : 2 * i + 2, 0].reshape(256, WIDTH).astype(F32)
+        scale = lax.rsqrt(jnp.mean(x * x, axis=1, keepdims=True) + EPSILON)
+        h1 = (x * scale * gain_one).astype(BF16)
+        h1_ref[0, tokens, :] = h1
+        qkv = mm(h1, weights)
+        q = qkv[:, 0:128]
+        kv = qkv[:, 128:256]
+        q = q * cosine + turn(q, first_half) * sine
+        kv = jnp.where(is_key, kv * cosine + turn(kv, first_half) * sine, kv)
+        q = q.astype(BF16)
+        kv = kv.astype(BF16)
+        qkv_ref[0, tokens, 0:128] = q
+        qkv_ref[0, tokens, 128:256] = kv
+        length = 256 * (i + 1)
+        keys = qkv_ref[0, 0:length, 128:192]
+        values = qkv_ref[0, 0:length, 192:256]
+        place_key = lax.broadcasted_iota(jnp.int32, (256, length), 1).astype(F32)
+        place_query = (lax.broadcasted_iota(jnp.int32, (256, length), 0) + 256 * i).astype(F32)
+        allowed = (place_key <= place_query) & (place_key >= start_col[:, 0:1])
+        outs, logs = [], []
+        for head in range(2):
+            query = q[:, 64 * head : 64 * head + 64]
+            scores = jnp.where(allowed, mm(query, keys, NT) * (HEAD_DIM**-0.5), MASKED)
+            top = jnp.max(scores, axis=1, keepdims=True)
+            log_total = top + jnp.log(jnp.sum(jnp.exp(scores - top), axis=1, keepdims=True))
+            weights_b = jnp.exp(scores - log_total).astype(BF16)
+            outs.append(mm(weights_b, values))
+            logs.append(log_total)
+        o_ref[0, tokens, :] = jnp.concatenate(outs, axis=1).astype(BF16)
+        lse_ref[0, tokens, :] = jnp.where(is_key, logs[0], logs[1])
+
+
+def attend_call(x_all, w_all, g_all, seg_all, cos_table, sin_table, freq):
+    def whole(shape):
+        return pl.BlockSpec(shape, lambda r: (0,) * len(shape))
+
+    def by_row(lanes):
+        return pl.BlockSpec((1, SEQ, lanes), lambda r: (r, 0, 0))
+
+    return pl.pallas_call(
+        attend_kernel,
+        name="attend",
+        grid=(2,),
+        out_shape=(
+            jax.ShapeDtypeStruct((2, SEQ, WIDTH), BF16),
+            jax.ShapeDtypeStruct((2, SEQ, 256), BF16),
+            jax.ShapeDtypeStruct((2, SEQ, 128), F32),
+            jax.ShapeDtypeStruct((2, SEQ, 128), BF16),
+            jax.ShapeDtypeStruct((2, SEQ, 256), F32),
+            jax.ShapeDtypeStruct((2, SEQ, 128), F32),
+            jax.ShapeDtypeStruct((8, WIDTH), F32),
+        ),
+        in_specs=[
+            pl.BlockSpec((WIDE, 1, SPAN, WIDTH), lambda r: (0, r, 0, 0)),
+            whole((NARROW * WIDE, 32, 256)),
+            whole((NARROW * WIDE, 8, 128)),
+            whole((WIDE, 8, 128)),
+            whole((SEQ, 128)),
+            whole((SEQ, 128)),
+            whole((8, 128)),
+        ],
+        out_specs=(by_row(WIDTH), by_row(256), by_row(128), by_row(128), by_row(256), by_row(128), whole((8, WIDTH))),
+        compiler_params=pltpu.CompilerParams(vmem_limit_bytes=VMEM_BYTES),
+    )(x_all.reshape(WIDE, 2, SPAN, WIDTH), w_all, g_all, seg_all, cos_table, sin_table, freq)
+
+
+def project_kernel(
+    o_ref, x_ref, w_ref, gain_ref, ids_ref,
+    h2_all, table_all, mid_ref, gate_ref,
+    o_full, h2_own, table_own, os, orv, s0, r0, s1, r1, ts, tr, zs, zr, local,
+):
+    spot = Spot()
+    spot.greet(GROUP)
+
+    def heads(step, arriving):
+        other = lax.rem(spot.w + step, WIDE)
+        place = other if arriving else spot.w
+        return remote(
+            o_ref.at[:, pl.ds(pl.multiple_of(other * SPAN, SPAN), SPAN), :],
+            o_full.at[:, :, pl.ds(pl.multiple_of(place * 128, 128), 128)],
+            os.at[other], orv.at[place], spot.wide(other),
+        )
+
+    def start(step, carry):
+        heads(step, False).start()
+        return carry
+
+    lax.fori_loop(1, WIDE, start, 0)
+    mine = pltpu.make_async_copy(
+        o_ref.at[:, pl.ds(pl.multiple_of(spot.w * SPAN, SPAN), SPAN), :],
+        o_full.at[:, :, pl.ds(pl.multiple_of(spot.w * 128, 128), 128)],
+        local.at[0],
+    )
+    mine.start()
+
+    expert = lax.broadcasted_iota(jnp.int32, (32, TOKENS), 0)
+    named = jnp.zeros((32, TOKENS), F32)
+    for k in range(TOP):
+        named = jnp.where(expert == ids_ref[k : k + 1, :], 1.0, named)
+    before = lax.broadcasted_iota(jnp.int32, (TOKENS, TOKENS), 0) < lax.broadcasted_iota(
+        jnp.int32, (TOKENS, TOKENS), 1
+    )
+    places = mm(named.astype(BF16), before.astype(BF16))
+    kept = jnp.where((named > 0.5) & (places < float(CAP)), places, -1.0)
+
+    def wait(step, carry):
+        heads(step, False).wait_send()
+        heads(step, True).wait_recv()
+        return carry
+
+    lax.fori_loop(1, WIDE, wait, 0)
+    mine.wait()
+
+    attended = o_full[...].reshape(TOKENS, WIDTH)
+    mid = x_ref[...].astype(F32) + mm(attended, w_ref[:, 0:WIDTH])
+    mid_ref[...] = mid
+    scale = lax.rsqrt(jnp.mean(mid * mid, axis=1, keepdims=True) + EPSILON)
+    h2 = (mid * scale * gain_ref[1:2, :]).astype(BF16)
+    h2_own[...] = h2
+    first = PlaneGather(spot, h2_own, h2_all, spot.half * WIDE, s0, r0)
+    first.begin()
+    there = h2_all.at[spot.slot]
+    mate_slot = (1 - spot.half) * WIDE + spot.w
+    arriving = h2_all.at[mate_slot]
+    across = remote(h2_own, there, zs.at[0], zr.at[0], (spot.mate, spot.w))
+    across.start()
+    keep_own = pltpu.make_async_copy(h2_own, there, local.at[1])
+    keep_own.start()
+
+    logits = jnp.transpose(mm(h2, w_ref[:, WIDTH : WIDTH + 128]))[0:32]
+    chosen = jnp.where(named > 0.5, logits, MASKED)
+    rise = jnp.where(named > 0.5, jnp.exp(chosen - jnp.max(chosen, axis=0, keepdims=True)), 0.0)
+    gate = rise / jnp.sum(rise, axis=0, keepdims=True)
+    gate_ref[0:32, :] = gate
+    gate_ref[32:64, :] = named
+    for owner in range(GROUP):
+        table_own[owner, 0:2, :] = kept[2 * owner : 2 * owner + 2]
+        table_own[owner, 2:4, :] = gate[2 * owner : 2 * owner + 2]
+        table_own[owner, 4:8, :] = jnp.zeros((4, TOKENS), F32)
+
+    def tables(step, arriving):
+        other = lax.rem(spot.slot + step, GROUP)
+        o_half, o_w = lax.div(other, WIDE), lax.rem(other, WIDE)
+        place = other if arriving else spot.slot
+        return remote(
+            table_own.at[2 * o_w + o_half], table_all.at[place], ts.at[other], tr.at[place],
+            (spot.n - spot.half + o_half, o_w),
+        )
+
+    def start_table(step, carry):
+        tables(step, False).start()
+        return carry
+
+    lax.fori_loop(1, GROUP, start_table, 0)
+    table_mine = pltpu.make_async_copy(
+        table_own.at[2 * spot.w + spot.half], table_all.at[spot.slot], local.at[2]
+    )
+    table_mine.start()
+
+    first.middle()
+    remote(arriving, arriving, zs.at[0], zr.at[0], (spot.mate, spot.w)).wait_recv()
+    second = PlaneGather(spot, arriving, h2_all, (1 - spot.half) * WIDE, s1, r1)
+    second.begin()
+    first.late()
+    first.last()
+    second.middle()
+    second.late()
+    second.last()
+
+    def wait_table(step, carry):
+        tables(step, False).wait_send()
+        tables(step, True).wait_recv()
+        return carry
+
+    lax.fori_loop(1, GROUP, wait_table, 0)
+    first.finish()
+    second.finish()
+    across.wait_send()
+    keep_own.wait()
+    table_mine.wait()
+
+
+def project_call(o_heads, x_own, w_out, gain_rows, ids):
+    dma = pltpu.SemaphoreType.DMA
+    return pl.pallas_call(
+        project_kernel,
+        name="project",
+        out_shape=(
+            jax.ShapeDtypeStruct((GROUP, TOKENS, WIDTH), BF16),
+            jax.ShapeDtypeStruct((GROUP, 8, TOKENS), F32),
+            jax.ShapeDtypeStruct((TOKENS, WIDTH), F32),
+            jax.ShapeDtypeStruct((64, TOKENS), F32),
+        ),
+        in_specs=[IN_HBM] + [IN_VMEM] * 4,
+        out_specs=(IN_HBM, IN_HBM, IN_VMEM, IN_VMEM),
+        scratch_shapes=[
+            pltpu.VMEM((2, SPAN, WIDTH), BF16),
+            pltpu.VMEM((TOKENS, WIDTH), BF16),
+            pltpu.VMEM((GROUP, 8, TOKENS), F32),
+            dma((WIDE,)),
+            dma((WIDE,)),
+            dma((PlaneGather.COPIES,)),
+            dma((PlaneGather.COPIES,)),
+            dma((PlaneGather.COPIES,)),
+            dma((PlaneGather.COPIES,)),
+            dma((GROUP,)),
+            dma((GROUP,)),
+            dma((1,)),
+            dma((1,)),
+            dma((3,)),
+        ],
+        compiler_params=pltpu.CompilerParams(collective_id=2, has_side_effects=True, vmem_limit_bytes=VMEM_BYTES),
+    )(o_heads, x_own, w_out, gain_rows, ids)
+
+
+def load_quarters(pieces, target, depth, sems, base):
+    n = lax.axis_index("narrow")
+    half, pair = lax.rem(n, 2), lax.div(n, 2)
+    mate = n + 1 - 2 * half
+    far = n + 2 - 4 * pair
+    far_mate = mate + 2 - 4 * pair
+    copies = []
+    for number, (piece, quarter) in enumerate(zip(pieces, (n, mate, far, far_mate))):
+        copies.append(
+            pltpu.make_async_copy(
+                piece,
+                target.at[:, pl.ds(pl.multiple_of(quarter * depth, depth), depth), :],
+                sems.at[base + number],
+            )
+        )
+    return copies
+
+
+def pick(table_ref, source, expert):
+    slot = lax.broadcasted_iota(jnp.int32, (SLOTS, TOKENS), 0).astype(F32)
+    return slot == table_ref[source, expert : expert + 1, :]
+
+
+def expert_kernel(
+    h2_ref, dy_ref, table_ref, gu0, gu1, gu2, gu3, d0, d1, d2, d3,
+    rows_ref, da_ref, y_ref, dgate_ref, down_grad_ref,
+    w_gu, w_down, down_sum, sems,
+):
+    step = pl.program_id(0)
+
+    @pl.when(step == 0)
+    def _():
+        copies = load_quarters((gu0, gu1, gu2, gu3), w_gu, 256, sems, 0) + load_quarters(
+            (d0, d1, d2, d3), w_down, 128, sems, 4
+        )
+        for copy in copies:
+            copy.start()
+        down_sum[...] = jnp.zeros_like(down_sum)
+        for copy in copies:
+            copy.wait()
+
+    picks = [[], []]
+    gated = [[], []]
+    dgate_ref[...] = jnp.zeros_like(dgate_ref)
+    for e in range(MINE):
+        masks = [pick(table_ref, s, e) for s in range(CHUNK)]
+        hots = [jnp.where(mask, 1.0, 0.0).astype(BF16) for mask in masks]
+        picks[e] = hots
+        rows = jnp.concatenate([mm(hots[s], h2_ref[s]) for s in range(CHUNK)], axis=0).astype(BF16)
+        grad_rows = jnp.concatenate([mm(hots[s], dy_ref[s, 0]) for s in range(CHUNK)], axis=0)
+        gates = jnp.concatenate(
+            [
+                jnp.sum(jnp.where(masks[s], table_ref[s, 2 + e : 3 + e, :], 0.0), axis=1, keepdims=True)
+                for s in range(CHUNK)
+            ],
+            axis=0,
+        )
+        rows_ref[0, e] = rows
+        g = mm(rows, w_gu[e, :, 0:FF])
+        u = mm(rows, w_gu[e, :, FF : 2 * FF])
+        sigmoid = 1.0 / (1.0 + jnp.exp(-g))
+        active = g * sigmoid
+        hidden = (active * u).astype(BF16)
+        y = mm(hidden, w_down[e]).astype(BF16).astype(F32)
+        slot_dgate = jnp.sum(y * grad_rows, axis=1, keepdims=True)
+        for s in range(CHUNK):
+            part = slot_dgate[s * SLOTS : (s + 1) * SLOTS]
+            dgate_ref[s, e : e + 1, :] = jnp.sum(jnp.where(masks[s], part, 0.0), axis=0, keepdims=True)
+        gated[e] = (y * gates).astype(BF16)
+        dy_pair = (grad_rows * gates).astype(BF16)
+        down_sum[e] += mm(hidden, dy_pair, TN)
+        dhid = mm(dy_pair, w_down[e], NT)
+        da_ref[0, e, :, 0:FF] = (dhid * u * (sigmoid * (1.0 + g * (1.0 - sigmoid)))).astype(BF16)
+        da_ref[0, e, :, FF : 2 * FF] = (dhid * active).astype(BF16)
+    for s in range(CHUNK):
+        hot = jnp.concatenate([picks[e][s] for e in range(MINE)], axis=0)
+        back = jnp.concatenate([gated[e][s * SLOTS : (s + 1) * SLOTS] for e in range(MINE)], axis=0)
+        y_ref[s, 0] = mm(hot, back, TN).astype(BF16)
+
+    @pl.when(step == pl.num_programs(0) - 1)
+    def _():
+        down_grad_ref[...] = down_sum[...].astype(BF16)
+
+
+def expert_call(h2_all, dy_all, table_all, gate_up, down):
+    steps = GROUP // CHUNK
+    block = pl.BlockSpec((CHUNK, TOKENS, WIDTH), lambda c: (c, 0, 0))
+    small = pl.BlockSpec((CHUNK, 8, TOKENS), lambda c: (c, 0, 0))
+    slots = pl.BlockSpec((1, MINE, CHUNK * SLOTS, WIDTH), lambda c: (c, 0, 0, 0))
+    steps_half = WIDE // CHUNK
+    to_wide = pl.BlockSpec(
+        (CHUNK, 1, TOKENS, WIDTH), lambda c: (lax.rem(c, steps_half), lax.div(c, steps_half), 0, 0)
+    )
+    flops = 2 * GROUP * SLOTS * MINE * WIDTH * FF * 7
+    return pl.pallas_call(
+        expert_kernel,
+        name="experts",
+        grid=(steps,),
+        out_shape=(
+            jax.ShapeDtypeStruct((steps, MINE, CHUNK * SLOTS, WIDTH), BF16),
+            jax.ShapeDtypeStruct((steps, MINE, CHUNK * SLOTS, 2 * FF), BF16),
+            jax.ShapeDtypeStruct((WIDE, 2, TOKENS, WIDTH), BF16),
+            jax.ShapeDtypeStruct((GROUP, 8, TOKENS), F32),
+            jax.ShapeDtypeStruct((MINE, FF, WIDTH), BF16),
+        ),
+        in_specs=[block, to_wide, small] + [IN_HBM] * 8,
+        out_specs=(slots, slots, to_wide, small, pl.BlockSpec((MINE, FF, WIDTH), lambda c: (0, 0, 0))),
+        scratch_shapes=[
+            pltpu.VMEM((MINE, WIDTH, 2 * FF), BF16),
+            pltpu.VMEM((MINE, FF, WIDTH), BF16),
+            pltpu.VMEM((MINE, FF, WIDTH), F32),
+            pltpu.SemaphoreType.DMA((8,)),
+        ],
+        compiler_params=pltpu.CompilerParams(vmem_limit_bytes=VMEM_BYTES),
+        cost_estimate=pl.CostEstimate(flops=flops, bytes_accessed=40 << 20, transcendentals=1 << 20),
+    )(h2_all, dy_all, table_all, *gate_up, *down)
+
+
+def gate_up_grad_kernel(rows_ref, da_ref, out_ref):
+    rows = rows_ref[:, 0].reshape(GROUP * SLOTS, WIDTH // 2)
+    da = da_ref[:, 0].reshape(GROUP * SLOTS, 2 * FF)
+    out_ref[0] = mm(rows, da, TN).astype(BF16)
+
+
+def gate_up_grad_call(rows, da):
+    steps = GROUP // CHUNK
+    return pl.pallas_call(
+        gate_up_grad_kernel,
+        name="gate_up_grad",
+        grid=(MINE, 2),
+        out_shape=jax.ShapeDtypeStruct((MINE, WIDTH, 2 * FF), BF16),
+        in_specs=[
+            pl.BlockSpec((steps, 1, CHUNK * SLOTS, WIDTH // 2), lambda e, d: (0, e, 0, d)),
+            pl.BlockSpec((steps, 1, CHUNK * SLOTS, 2 * FF), lambda e, d: (0, e, 0, 0)),
+        ],
+        out_specs=pl.BlockSpec((1, WIDTH // 2, 2 * FF), lambda e, d: (e, d, 0)),
+        compiler_params=pltpu.CompilerParams(vmem_limit_bytes=VMEM_BYTES),
+        cost_estimate=pl.CostEstimate(
+            flops=2 * GROUP * SLOTS * MINE * WIDTH * 2 * FF, bytes_accessed=14 << 20, transcendentals=0
+        ),
+    )(rows, da)
+
+
+def rows_grad_kernel(da_ref, table_ref, gu0, gu1, gu2, gu3, out_ref, w_gu, sems):
+    step = pl.program_id(0)
+
+    @pl.when(step == 0)
+    def _():
+        copies = load_quarters((gu0, gu1, gu2, gu3), w_gu, 256, sems, 0)
+        for copy in copies:
+            copy.start()
+        for copy in copies:
+            copy.wait()
+
+    grads = [mm(da_ref[0, e], w_gu[e], NT).astype(BF16) for e in range(MINE)]
+    for s in range(CHUNK):
+        hot = jnp.concatenate(
+            [jnp.where(pick(table_ref, s, e), 1.0, 0.0).astype(BF16) for e in range(MINE)], axis=0
+        )
+        back = jnp.concatenate([grads[e][s * SLOTS : (s + 1) * SLOTS] for e in range(MINE)], axis=0)
+        out_ref[s] = mm(hot, back, TN).astype(BF16)
+
+
+def rows_grad_call(da, table_all, gate_up):
+    steps = GROUP // CHUNK
+    return pl.pallas_call(
+        rows_grad_kernel,
+        name="rows_grad",
+        grid=(steps,),
+        out_shape=jax.ShapeDtypeStruct((GROUP, TOKENS, WIDTH), BF16),
+        in_specs=[
+            pl.BlockSpec((1, MINE, CHUNK * SLOTS, 2 * FF), lambda c: (c, 0, 0, 0)),
+            pl.BlockSpec((CHUNK, 8, TOKENS), lambda c: (c, 0, 0)),
+        ]
+        + [IN_HBM] * 4,
+        out_specs=pl.BlockSpec((CHUNK, TOKENS, WIDTH), lambda c: (c, 0, 0)),
+        scratch_shapes=[pltpu.VMEM((MINE, WIDTH, 2 * FF), BF16), pltpu.SemaphoreType.DMA((4,))],
+        compiler_params=pltpu.CompilerParams(vmem_limit_bytes=VMEM_BYTES),
+        cost_estimate=pl.CostEstimate(
+            flops=2 * GROUP * SLOTS * MINE * WIDTH * 2 * FF, bytes_accessed=20 << 20, transcendentals=0
+        ),
+    )(da, table_all, *gate_up)
+
+
+def widen(ref_value):
+    return ref_value.astype(F32)
+
+
+class PlaneReduce:
+    COPIES = 10
+
+    def __init__(self, spot, part, base, acc, from_core, from_one, from_two, send, recv, local):
+        self.spot, self.part, self.base = spot, part, base
+        self.acc, self.from_core, self.from_one, self.from_two = acc, from_core, from_one, from_two
+        self.send, self.recv, self.local = send, recv, local
+        self.started = []
+        s = spot
+        self.q_own = 2 * s.y + s.x
+        self.q_x = 2 * s.y + 1 - s.x
+        self.q_y = 2 - 2 * s.y + s.x
+        self.q_d = 3 - self.q_own
+
+    def put(self, src, dst, number, to):
+        copy = remote(src, dst, self.send.at[number], self.recv.at[number], self.spot.wide(to))
+        copy.start()
+        self.started.append(copy)
+
+    def got(self, dst, number):
+        remote(dst, dst, self.send.at[number], self.recv.at[number], self.spot.wide(self.spot.sib)).wait_recv()
+
+    def begin(self):
+        s = self.spot
+        self.loads = []
+        for q in range(4):
+            self.put(self.part.at[self.base + 2 * q + 1 - s.core], self.from_core.at[q], q, s.sib)
+            copy = pltpu.make_async_copy(self.part.at[self.base + 2 * q + s.core], self.acc.at[q], self.local.at[q])
+            copy.start()
+            self.loads.append(copy)
+
+    def across_core(self):
+        s = self.spot
+        for q in range(4):
+            self.loads[q].wait()
+            self.got(self.from_core.at[q], q)
+            self.acc[q] = (widen(self.acc[q]) + widen(self.from_core[q])).astype(BF16)
+        self.put(halves(self.acc.at[self.q_d], 0), self.from_one.at[1], 5, s.xn)
+        self.put(halves(self.acc.at[self.q_d], 1), self.from_one.at[3], 7, s.yn)
+        self.put(halves(self.acc.at[self.q_x], 0), self.from_one.at[0], 4, s.xn)
+        self.put(halves(self.acc.at[self.q_y], 1), self.from_one.at[2], 6, s.yn)
+
+    def across_one(self):
+        s = self.spot
+        self.got(self.from_one.at[1], 5)
+        upper = halves(self.acc.at[self.q_y], 0)
+        upper[...] = (widen(upper[...]) + widen(self.from_one[1])).astype(BF16)
+        self.put(upper, self.from_two.at[0], 8, s.yn)
+        self.got(self.from_one.at[3], 7)
+        lower = halves(self.acc.at[self.q_x], 1)
+        lower[...] = (widen(lower[...]) + widen(self.from_one[3])).astype(BF16)
+        self.put(lower, self.from_two.at[1], 9, s.xn)
+
+    def total(self, out):
+        self.got(self.from_one.at[0], 4)
+        self.got(self.from_two.at[0], 8)
+        own = self.acc.at[self.q_own]
+        out[0:SPAN, :] = widen(own[0:SPAN, :]) + widen(self.from_one[0]) + widen(self.from_two[0])
+        self.got(self.from_one.at[2], 6)
+        self.got(self.from_two.at[1], 9)
+        out[SPAN:TOKENS, :] = widen(own[SPAN:TOKENS, :]) + widen(self.from_one[2]) + widen(self.from_two[1])
+
+    def finish(self):
+        for copy in self.started:
+            copy.wait_send()
+
+
+def reduce_scratch():
+    dma = pltpu.SemaphoreType.DMA
+    return [
+        pltpu.VMEM((2, 4, TOKENS, WIDTH), BF16),
+        pltpu.VMEM((2, 4, TOKENS, WIDTH), BF16),
+        pltpu.VMEM((2, 4, SPAN, WIDTH), BF16),
+        pltpu.VMEM((2, 2, SPAN, WIDTH), BF16),
+        pltpu.VMEM((TOKENS, WIDTH), F32),
+        pltpu.VMEM((TOKENS, WIDTH), BF16),
+        pltpu.VMEM((TOKENS, WIDTH), BF16),
+        dma((2, PlaneReduce.COPIES)),
+        dma((2, PlaneReduce.COPIES)),
+        dma((2, 4)),
+        dma((1,)),
+        dma((1,)),
+    ]
+
+
+def group_reduce(spot, part, scratch):
+    acc, from_core, from_one, from_two, total, mate_send, mate_recv, send, recv, local, zs, zr = scratch
+    sums = []
+    for which, base in ((0, (1 - spot.half) * WIDE), (1, spot.half * WIDE)):
+        sums.append(
+            PlaneReduce(
+                spot, part, base, acc.at[which], from_core.at[which], from_one.at[which], from_two.at[which],
+                send.at[which], recv.at[which], local.at[which],
+            )
+        )
+    theirs, ours = sums
+    theirs.begin()
+    ours.begin()
+    theirs.across_core()
+    ours.across_core()
+    theirs.across_one()
+    theirs.total(total)
+    mate_send[...] = total[...].astype(BF16)
+    across = remote(mate_send, mate_recv, zs.at[0], zr.at[0], (spot.mate, spot.w))
+    across.start()
+    ours.across_one()
+    ours.total(total)
+    across.wait_recv()
+    total[...] += widen(mate_recv[...])
+    theirs.finish()
+    ours.finish()
+    across.wait_send()
+
+
+def collect_kernel(
+    part_ref, dgate_ref, h2_ref, mid_ref, gate_ref, w_ref, gain_ref, dy_ref,
+    dattn_all, dmid_ref, small_ref,
+    dgate_all, h2_own, dattn_own, ts, tr, s0, r0, local, *scratch,
+):
+    spot = Spot()
+    spot.greet(GROUP)
+
+    def tables(step, arriving):
+        other = lax.rem(spot.slot + step, GROUP)
+        o_half, o_w = lax.div(other, WIDE), lax.rem(other, WIDE)
+        place = other if arriving else spot.slot
+        return remote(
+            dgate_ref.at[other], dgate_all.at[place], ts.at[other], tr.at[place],
+            (spot.n - spot.half + o_half, o_w),
+        )
+
+    def start_table(step, carry):
+        tables(step, False).start()
+        return carry
+
+    lax.fori_loop(1, GROUP, start_table, 0)
+    mine = pltpu.make_async_copy(dgate_ref.at[spot.slot], dgate_all.at[spot.slot], local.at[0])
+    mine.start()
+    load = pltpu.make_async_copy(h2_ref.at[spot.slot], h2_own, local.at[1])
+    load.start()
+    group_reduce(spot, part_ref, scratch)
+
+    def wait_table(step, carry):
+        tables(step, False).wait_send()
+        tables(step, True).wait_recv()
+        return carry
+
+    lax.fori_loop(1, GROUP, wait_table, 0)
+    mine.wait()
+    load.wait()
+
+    total = scratch[4]
+    gate = gate_ref[0:32, :]
+    dgate = jnp.concatenate([dgate_all[(o % 2) * WIDE + o // 2, 0:2, :] for o in range(GROUP)], axis=0)
+    dsel = gate * (dgate - jnp.sum(gate * dgate, axis=0, keepdims=True))
+    dlogits = jnp.concatenate([dsel, jnp.zeros((96, TOKENS), F32)], axis=0)
+    dh2 = total[...] + mm(jnp.transpose(dlogits).astype(BF16), w_ref[:, WIDTH : WIDTH + 128], NT)
+    small_ref[0:32, :] = mm(dsel.astype(BF16), h2_own[...])
+    mid = mid_ref[...]
+    scale = lax.rsqrt(jnp.mean(mid * mid, axis=1, keepdims=True) + EPSILON)
+    small_ref[32:33, :] = jnp.sum(dh2 * mid * scale, axis=0, keepdims=True)
+    lane = lax.broadcasted_iota(jnp.int32, (32, WIDTH), 1)
+    column = lax.broadcasted_iota(jnp.int32, (32, WIDTH), 0)
+    count = jnp.sum(gate_ref[32:64, :], axis=1, keepdims=True)
+    small_ref[33:34, :] = jnp.sum(jnp.where(lax.rem(lane, 128) == column, count, 0.0), axis=0, keepdims=True)
+    small_ref[34:40, :] = jnp.zeros((6, WIDTH), F32)
+    weighted = dh2 * gain_ref[1:2, :]
+    inner = jnp.mean(weighted * mid, axis=1, keepdims=True)
+    dmid = dy_ref[...].astype(F32) + weighted * scale - mid * (scale * scale * scale) * inner
+    dmid_ref[...] = dmid
+    dattn_own[...] = dmid.astype(BF16)
+    gather = PlaneGather(spot, dattn_own, dattn_all, 0, s0, r0)
+    gather.begin()
+    keep = pltpu.make_async_copy(dattn_own, dattn_all.at[spot.w], local.at[0])
+    keep.start()
+    gather.middle()
+    gather.late()
+    gather.last()
+    gather.finish()
+    keep.wait()
+
+
+def collect_call(part, dgate, h2_all, mid, gate, w_out, gain_rows, dy_own):
+    dma = pltpu.SemaphoreType.DMA
+    return pl.pallas_call(
+        collect_kernel,
+        name="collect",
+        out_shape=(
+            jax.ShapeDtypeStruct((WIDE, TOKENS, WIDTH), BF16),
+            jax.ShapeDtypeStruct((TOKENS, WIDTH), F32),
+            jax.ShapeDtypeStruct((40, WIDTH), F32),
+        ),
+        in_specs=[IN_HBM] * 3 + [IN_VMEM] * 5,
+        out_specs=(IN_HBM, IN_VMEM, IN_VMEM),
+        scratch_shapes=[
+            pltpu.VMEM((GROUP, 8, TOKENS), F32),
+            pltpu.VMEM((TOKENS, WIDTH), BF16),
+            pltpu.VMEM((TOKENS, WIDTH), BF16),
+            dma((GROUP,)),
+            dma((GROUP,)),
+            dma((PlaneGather.COPIES,)),
+            dma((PlaneGather.COPIES,)),
+            dma((2,)),
+        ]
+        + reduce_scratch(),
+        compiler_params=pltpu.CompilerParams(collective_id=3, has_side_effects=True, vmem_limit_bytes=VMEM_BYTES),
+    )(part, dgate, h2_all, mid, gate, w_out, gain_rows, dy_own)
+
+
+def attend_back_kernel(
+    dattn_ref, w_ref, h1_ref, qkv_ref, lse_ref, o_ref, angle_ref, start_ref,
+    dqkv_ref, wgrad_ref, ograd_ref,
+    do_ref, dkv_ref, wsum, osum,
+):
+    row = pl.program_id(0)
+    first_half = lane_half()
+    is_key = lax.broadcasted_iota(jnp.int32, (1, 128), 1) < 64
+
+    @pl.when(row == 0)
+    def _():
+        wsum[...] = jnp.zeros_like(wsum)
+        osum[...] = jnp.zeros_like(osum)
+
+    dattn = dattn_ref[:, 0].reshape(SEQ, WIDTH)
+    do_ref[...] = mm(dattn, w_ref[...], NT).astype(BF16)
+    osum[...] += mm(o_ref[0], dattn, TN)
+    dkv_ref[...] = jnp.zeros_like(dkv_ref)
+    for i in range(4):
+        tokens = pl.ds(i * 256, 256)
+        length = 256 * (i + 1)
+        keys = qkv_ref[0, 0:length, 128:192]
+        values = qkv_ref[0, 0:length, 192:256]
+        place_key = lax.broadcasted_iota(jnp.int32, (256, length), 1).astype(F32)
+        place_query = (lax.broadcasted_iota(jnp.int32, (256, length), 0) + 256 * i).astype(F32)
+        allowed = (place_key <= place_query) & (place_key >= start_ref[0, tokens, 0:1])
+        query_grads = []
+        dk = jnp.zeros((length, HEAD_DIM), F32)
+        dv = jnp.zeros((length, HEAD_DIM), F32)
+        for head in range(2):
+            part = slice(64 * head, 64 * head + 64)
+            query = qkv_ref[0, tokens, part]
+            do = do_ref[tokens, part]
+            log_total = lse_ref[0, tokens, 64 * head : 64 * head + 1]
+            scores = jnp.where(allowed, mm(query, keys, NT) * (HEAD_DIM**-0.5), MASKED)
+            weights = jnp.exp(scores - log_total)
+            dp = mm(do, values, NT)
+            delta = jnp.sum(weights * dp, axis=1, keepdims=True)
+            ds = (weights * (dp - delta)).astype(BF16)
+            query_grads.append(mm(ds, keys) * (HEAD_DIM**-0.5))
+            dk = dk + mm(ds, query, TN)
+            dv = dv + mm(weights.astype(BF16), do, TN)
+        dkv_ref[0:length, :] += jnp.concatenate([dk * (HEAD_DIM**-0.5), dv], axis=1)
+        dq = jnp.concatenate(query_grads, axis=1)
+        cosine = angle_ref[0, tokens, 0:128]
+        sine = angle_ref[0, tokens, 128:256]
+        dqkv_ref[0, tokens, 0:128] = (dq * cosine + turn_back(dq * sine, first_half)).astype(BF16)
+    for i in range(4):
+        tokens = pl.ds(i * 256, 256)
+        cosine = angle_ref[0, tokens, 0:128]
+        sine = angle_ref[0, tokens, 128:256]
+        dkv = dkv_ref[tokens, :]
+        turned = dkv * cosine + turn_back(dkv * sine, first_half)
+        dqkv_ref[0, tokens, 128:256] = jnp.where(is_key, turned, dkv).astype(BF16)
+    wsum[...] += mm(h1_ref[0], dqkv_ref[0], TN)
+
+    @pl.when(row == 1)
+    def _():
+        wgrad_ref[...] = wsum[...].astype(BF16)
+        ograd_ref[...] = osum[...].astype(BF16)
+
+
+def attend_back_call(dattn_all, w_rows, h1, qkv, lse, o_heads, angle, start):
+    def by_row(lanes):
+        return pl.BlockSpec((1, SEQ, lanes), lambda r: (r, 0, 0))
+
+    def whole(shape):
+        return pl.BlockSpec(shape, lambda r: (0,) * len(shape))
+
+    return pl.pallas_call(
+        attend_back_kernel,
+        name="attend_back",
+        grid=(2,),
+        out_shape=(
+            jax.ShapeDtypeStruct((2, SEQ, 256), BF16),
+            jax.ShapeDtypeStruct((WIDTH, 256), BF16),
+            jax.ShapeDtypeStruct((128, WIDTH), BF16),
+        ),
+        in_specs=[
+            pl.BlockSpec((WIDE, 1, SPAN, WIDTH), lambda r: (0, r, 0, 0)),
+            whole((128, WIDTH)),
+            by_row(WIDTH),
+            by_row(256),
+            by_row(128),
+            by_row(128),
+            by_row(256),
+            by_row(128),
+        ],
+        out_specs=(by_row(256), whole((WIDTH, 256)), whole((128, WIDTH))),
+        scratch_shapes=[
+            pltpu.VMEM((SEQ, 128), BF16),
+            pltpu.VMEM((SEQ, 128), F32),
+            pltpu.VMEM((WIDTH, 256), F32),
+            pltpu.VMEM((128, WIDTH), F32),
+        ],
+        compiler_params=pltpu.CompilerParams(vmem_limit_bytes=VMEM_BYTES),
+        cost_estimate=pl.CostEstimate(flops=8 << 30, bytes_accessed=16 << 20, transcendentals=3 << 20),
+    )(dattn_all.reshape(WIDE, 2, SPAN, WIDTH), w_rows, h1, qkv, lse, o_heads, angle, start)
+
+
+def finish_kernel(
+    dqkv_ref, wg_ref, og_ref, small_ref, w_ref, x_ref, dmid_ref, gain_ref,
+    in_grad, q_grad, k_grad, v_grad, o_grad, sums, gain_sum,
+    dq_full, w_recv, o_recv, s_recv, gain_own, g_recv,
+    qs, qr, ws, wr, os, orv, ss, sr, gs, gr, local,
+):
+    spot = Spot()
+    everyone = NARROW * WIDE
+    spot.greet(everyone)
+
+    def to_plane(step, arriving):
+        other = lax.rem(spot.w + step, WIDE)
+        place = other if arriving else spot.w
+        return remote(
+            dqkv_ref.at[:, pl.ds(pl.multiple_of(other * SPAN, SPAN), SPAN), :],
+            dq_full.at[:, :, pl.ds(pl.multiple_of(place * 256, 256), 256)],
+            qs.at[other], qr.at[place], spot.wide(other),
+        )
+
+    def others(step):
+        other = lax.rem(spot.me + step, everyone)
+        return other, (lax.div(other, WIDE), lax.rem(other, WIDE))
+
+    def rows_of(ref, owner):
+        return ref.at[pl.ds(pl.multiple_of(owner * 32, 32), 32)]
+
+    def lanes_of(ref, owner):
+        return ref.at[:, pl.ds(pl.multiple_of(lax.div(owner, 4) * 128, 128), 128)]
+
+    def to_owner(step, arriving):
+        other, to = others(step)
+        place = other if arriving else spot.me
+        return (
+            remote(rows_of(wg_ref, other), w_recv.at[place], ws.at[other], wr.at[place], to),
+            remote(lanes_of(small_ref, other), s_recv.at[place], ss.at[other], sr.at[place], to),
+        )
+
+    def gain_to_owner(step, arriving):
+        other, to = others(step)
+        place = other if arriving else spot.me
+        return remote(lanes_of(gain_own, other), g_recv.at[place], gs.at[other], gr.at[place], to)
+
+    def start_plane(step, carry):
+        to_plane(step, False).start()
+        return carry
+
+    def start_owner(step, carry):
+        for copy in to_owner(step, False):
+            copy.start()
+        return carry
+
+    def start_gain(step, carry):
+        gain_to_owner(step, False).start()
+        return carry
+
+    lax.fori_loop(1, WIDE, start_plane, 0)
+    mine = [
+        pltpu.make_async_copy(
+            dqkv_ref.at[:, pl.ds(pl.multiple_of(spot.w * SPAN, SPAN), SPAN), :],
+            dq_full.at[:, :, pl.ds(pl.multiple_of(spot.w * 256, 256), 256)],
+            local.at[0],
+        ),
+        pltpu.make_async_copy(rows_of(wg_ref, spot.me), w_recv.at[spot.me], local.at[1]),
+        pltpu.make_async_copy(lanes_of(small_ref, spot.me), s_recv.at[spot.me], local.at[2]),
+    ]
+    for copy in mine:
+        copy.start()
+
+    def output_copies(act_local, act_send, act_recv):
+        for i in range(4):
+            owner = 4 * spot.w + i
+            to = (lax.div(owner, WIDE), lax.rem(owner, WIDE))
+            source = og_ref.at[pl.ds(i * 32, 32)]
+            here = owner == spot.me
+
+            @pl.when(here)
+            def _():
+                act_local(pltpu.make_async_copy(source, o_recv.at[spot.n], local.at[3]))
+
+            @pl.when(jnp.logical_not(here))
+            def _():
+                act_send(remote(source, o_recv.at[spot.n], os.at[i], orv.at[spot.n], to))
+
+        for plane in range(NARROW):
+            giver = lax.div(spot.me, 4)
+            here = (plane == spot.n) & (giver == spot.w)
+
+            @pl.when(jnp.logical_not(here))
+            def _():
+                place = o_recv.at[plane]
+                act_recv(remote(place, place, os.at[0], orv.at[plane], (plane, giver)))
+
+    def nothing(copy):
+        return None
+
+    output_copies(lambda c: c.start(), lambda c: c.start(), nothing)
+    lax.fori_loop(1, everyone, start_owner, 0)
+
+    def wait_plane(step, carry):
+        to_plane(step, False).wait_send()
+        to_plane(step, True).wait_recv()
+        return carry
+
+    lax.fori_loop(1, WIDE, wait_plane, 0)
+    mine[0].wait()
+    dqkv = dq_full[...].reshape(TOKENS, 2 * WIDTH)
+    dh1 = mm(dqkv, w_ref[...], NT)
+    x = x_ref[...].astype(F32)
+    scale = lax.rsqrt(jnp.mean(x * x, axis=1, keepdims=True) + EPSILON)
+    gain_own[0:1, :] = jnp.sum(dh1 * x * scale, axis=0, keepdims=True)
+    gain_own[1:8, :] = jnp.zeros((7, WIDTH), F32)
+    lax.fori_loop(1, everyone, start_gain, 0)
+    gain_mine = pltpu.make_async_copy(lanes_of(gain_own, spot.me), g_recv.at[spot.me], local.at[0])
+    gain_mine.start()
+    weighted = dh1 * gain_ref[0:1, :]
+    inner = jnp.mean(weighted * x, axis=1, keepdims=True)
+    in_grad[...] = (dmid_ref[...] + weighted * scale - x * (scale * scale * scale) * inner).astype(BF16)
+
+    def wait_owner(step, carry):
+        for copy in to_owner(step, False):
+            copy.wait_send()
+        for copy in to_owner(step, True):
+            copy.wait_recv()
+        return carry
+
+    lax.fori_loop(1, everyone, wait_owner, 0)
+    mine[1].wait()
+    mine[2].wait()
+    output_copies(lambda c: c.wait(), lambda c: c.wait_send(), lambda c: c.wait_recv())
+    for w in range(WIDE):
+        total = widen(w_recv[w])
+        for plane in range(1, NARROW):
+            total = total + widen(w_recv[plane * WIDE + w])
+        q_grad[:, 128 * w : 128 * w + 128] = total[:, 0:128]
+        k_grad[:, 64 * w : 64 * w + 64] = total[:, 128:192]
+        v_grad[:, 64 * w : 64 * w + 64] = total[:, 192:256]
+    total = widen(o_recv[0])
+    for plane in range(1, NARROW):
+        total = total + widen(o_recv[plane])
+    o_grad[...] = total
+    total = s_recv[0]
+    for device in range(1, everyone):
+        total = total + s_recv[device]
+    sums[...] = total
+
+    def wait_gain(step, carry):
+        gain_to_owner(step, False).wait_send()
+        gain_to_owner(step, True).wait_recv()
+        return carry
+
+    lax.fori_loop(1, everyone, wait_gain, 0)
+    gain_mine.wait()
+    total = g_recv[0]
+    for device in range(1, everyone):
+        total = total + g_recv[device]
+    gain_sum[...] = total
+
+
+def finish_call(dqkv, wgrad, ograd, small, w_full, x_own, dmid, gain_rows):
+    dma = pltpu.SemaphoreType.DMA
+    everyone = NARROW * WIDE
+    return pl.pallas_call(
+        finish_kernel,
+        name="finish",
+        out_shape=(
+            jax.ShapeDtypeStruct((TOKENS, WIDTH), BF16),
+            jax.ShapeDtypeStruct((32, WIDTH), F32),
+            jax.ShapeDtypeStruct((32, WIDTH // 2), F32),
+            jax.ShapeDtypeStruct((32, WIDTH // 2), F32),
+            jax.ShapeDtypeStruct((32, WIDTH), F32),
+            jax.ShapeDtypeStruct((40, 128), F32),
+            jax.ShapeDtypeStruct((8, 128), F32),
+        ),
+        in_specs=[IN_HBM] * 4 + [IN_VMEM] * 4,
+        out_specs=(IN_VMEM,) * 7,
+        scratch_shapes=[
+            pltpu.VMEM((2, SPAN, 2 * WIDTH), BF16),
+            pltpu.VMEM((everyone, 32, 256), BF16),
+            pltpu.VMEM((NARROW, 32, WIDTH), BF16),
+            pltpu.VMEM((everyone, 40, 128), F32),
+            pltpu.VMEM((8, WIDTH), F32),
+            pltpu.VMEM((everyone, 8, 128), F32),
+            dma((WIDE,)),
+            dma((WIDE,)),
+            dma((everyone,)),
+            dma((everyone,)),
+            dma((4,)),
+            dma((NARROW,)),
+            dma((everyone,)),
+            dma((everyone,)),
+            dma((everyone,)),
+            dma((everyone,)),
+            dma((4,)),
+        ],
+        compiler_params=pltpu.CompilerParams(collective_id=4, has_side_effects=True, vmem_limit_bytes=VMEM_BYTES),
+    )(dqkv, wgrad, ograd, small, w_full, x_own, dmid, gain_rows)
+
+
+def swap(values, distance):
+    return lax.ppermute(values, "narrow", [(i, i ^ distance) for i in range(NARROW)])
+
+
+def quarters(shard, half):
+    by_pair = shard.reshape((2, MINE) + shard.shape[1:])
+    own = lax.dynamic_index_in_dim(by_pair, half, 0, keepdims=False)
+    other = lax.dynamic_index_in_dim(by_pair, 1 - half, 0, keepdims=False)
+    return own, swap(other, 1), swap(own, 2), swap(other, 3)
+
+
+def owner_sums(grad, depth, n, half):
+    def rows(quarter):
+        return lax.dynamic_slice_in_dim(grad, quarter * depth, depth, axis=1)
+
+    mate = n + 1 - 2 * half
+    far = n + 2 - 4 * (n // 2)
+    far_mate = mate + 2 - 4 * (n // 2)
+    own = rows(n)
+    from_far = swap(rows(far), 2)
+    from_mate = swap(rows(mate), 1)
+    from_far_mate = swap(rows(far_mate), 3)
+    same = own.astype(F32) + from_far.astype(F32)
+    opposite = from_mate.astype(F32) + from_far_mate.astype(F32)
+    is_first = half == 0
+    return jnp.concatenate(
+        [jnp.where(is_first, same, opposite), jnp.where(is_first, opposite, same)], axis=0
+    )
+
+
+def position_tables():
+    freq = (1.0 / np.float32(THETA) ** (np.arange(32, dtype=np.float32) * np.float32(2.0) / np.float32(HEAD_DIM))).astype(np.float32)
+    angle = np.arange(SEQ, dtype=np.float32)[:, None] * freq[None, :]
+    cosine = np.tile(np.cos(angle.astype(np.float64)), (1, 4)).astype(np.float32)
+    sine = np.tile(np.sin(angle.astype(np.float64)), (1, 4)).astype(np.float32)
+    return cosine, sine, np.tile(freq[None, :], (8, 4)).astype(np.float32)
+
+
+def fast_device(
+    hidden_in, out_grad, seg_ids, expert_ids, attn_gain, w_query, w_key, w_value, w_output,
+    moe_gain, w_router, w_gate_up, w_down,
+):
+    n = lax.axis_index("narrow")
+    w = lax.axis_index("wide")
+    half = n % 2
+    me = n * WIDE + w
+    cos_table, sin_table, freq = position_tables()
+
+    gate_up = quarters(w_gate_up, half)
+    down = quarters(w_down, half)
+    out_shard = jnp.concatenate([w_output, w_router, jnp.zeros((32, 96), BF16)], axis=1)
+    w_out = lax.all_gather(out_shard, ("narrow", "wide"), axis=0, tiled=True)
+
+    x_own = hidden_in.reshape(TOKENS, WIDTH)
+    dy_own = out_grad.reshape(TOKENS, WIDTH)
+    w_own = jnp.concatenate(
+        [w_query.reshape(32, WIDE, 128), w_key.reshape(32, WIDE, 64), w_value.reshape(32, WIDE, 64)], axis=2
+    ).reshape(32, 2 * WIDTH)
+    gains = jnp.concatenate([attn_gain[None], moe_gain[None]], axis=0).astype(F32)
+    g_own = jnp.pad(gains, ((0, 6), (0, 96)))
+    seg_own = jnp.pad(seg_ids, ((0, 6), (0, 0)))
+    ids = expert_ids.reshape(TOKENS, TOP).T
+
+    x_all, w_all, g_all, seg_all = gather_call(x_own, w_own, g_own, seg_own)
+    h1, qkv, lse, o_heads, angle, start, gain_rows = attend_call(
+        x_all, w_all, g_all, seg_all, cos_table, sin_table, freq
+    )
+    dy_mate = swap(dy_own, 1)
+    dy_pair = jnp.where(half == 0, jnp.stack([dy_own, dy_mate]), jnp.stack([dy_mate, dy_own]))
+    dy_all = lax.all_gather(dy_pair.reshape(2 * TOKENS, WIDTH), "wide", axis=0, tiled=True).reshape(
+        WIDE, 2, TOKENS, WIDTH
+    )
+    w_full = lax.all_gather(w_own, ("narrow", "wide"), axis=0, tiled=True)
+
+    h2_all, table_all, mid, gate = project_call(o_heads, x_own, w_out, gain_rows, ids)
+    rows, da, y_part, dgate, down_grad = expert_call(h2_all, dy_all, table_all, gate_up, down)
+    down_sum = owner_sums(down_grad, FF // NARROW, n, half)
+    y_plane = lax.psum_scatter(
+        y_part.reshape(WIDE * 2 * TOKENS, WIDTH), "wide", scatter_dimension=0, tiled=True
+    ).reshape(2, TOKENS, WIDTH)
+    y_own = lax.dynamic_index_in_dim(y_plane, half, 0, keepdims=False)
+    y_mate = swap(lax.dynamic_index_in_dim(y_plane, 1 - half, 0, keepdims=False), 1)
+    block_out = (mid + y_own.astype(F32) + y_mate.astype(F32)).astype(BF16)
+    gate_up_grad = gate_up_grad_call(rows, da)
+    gate_up_sum = owner_sums(gate_up_grad, WIDTH // NARROW, n, half)
+    part = rows_grad_call(da, table_all, gate_up)
+    dattn_all, dmid, small = collect_call(part, dgate, h2_all, mid, gate, w_out, gain_rows, dy_own)
+    w_rows = lax.dynamic_slice(w_out, (w * 128, 0), (128, WIDTH))
+    dqkv, wgrad, ograd = attend_back_call(dattn_all, w_rows, h1, qkv, lse, o_heads, angle, start)
+    in_grad, q_grad, k_grad, v_grad, o_grad, sums, gain_sum = finish_call(
+        dqkv, wgrad, ograd, small, w_full, x_own, dmid, gain_rows
+    )
+    lanes = (me % 4) * 32
+    router_grad = lax.dynamic_slice(sums, (0, lanes), (32, 32)).T
+    moe_gain_grad = lax.dynamic_slice(sums, (32, lanes), (1, 32)).reshape(32)
+    attn_gain_grad = lax.dynamic_slice(gain_sum, (0, lanes), (1, 32)).reshape(32)
+    expert_load = sums[33, 0:32].astype(jnp.int32)
+    return (
+        block_out.reshape(hidden_in.shape),
+        in_grad.reshape(hidden_in.shape),
+        attn_gain_grad,
+        q_grad,
+        k_grad,
+        v_grad,
+        o_grad,
+        moe_gain_grad,
+        router_grad,
+        gate_up_sum,
+        down_sum,
+        expert_load,
+    )
+
+
 def solution(mesh):
+    planned = mesh.shape["narrow"] == NARROW and mesh.shape["wide"] == WIDE
     return jax.shard_map(
-        per_device,
+        fast_device if planned else general_device,
         mesh=mesh,
         in_specs=(
             P("narrow", "wide", None),

time: 1930 us -> 555 us (0.29)
  waiting for transfers between devices: 1170 us -> 52.7 us
  Pallas kernels: 0 us -> 423 us
  blocking collectives: 283 us -> 0 us
  matrix products: 185 us -> 0 us
  local copies, waits for them, and re-layouts: 167 us -> 19.1 us
  other arithmetic: 68.6 us -> 14.1 us
    reduce_scatter x8 -> x1, waiting for transfers between devices: 773 us -> 0.01 us  [fast_device(): lax.psum_scatter(y_part.reshape(WIDE * 2 * TOKENS, WIDTH), 'wide', scatte...]
    pallas_call x0 -> x9, Pallas kernels: none -> 423 us  [the longest x1 118 us: gather_call(): pl.pallas_call(gather_kernel, name='gather_inputs', out_shape=(jax.ShapeD...]
    all_gather x8 -> x3, waiting for transfers between devices: 275 us -> 0.06 us  [the longest x1 0.02 us: fast_device(): w_out = lax.all_gather(out_shard, ('narrow', 'wide'), axis=0, tiled=True)]
    dot_general x43 -> x0, matrix products: 185 us -> none  [the longest x8 30.4 us: masked_scores(): jnp.einsum('abgjd,akgd->agjbk', query_five, key_block, preferred_element_...]
    all_to_all x3 -> x0, waiting for transfers between devices: 120 us -> none  [the longest x1 60 us: per_device(): lax.all_to_all(slot_input_grad, 'wide', split_axis=1, concat_axis=0, tile...]
    all_gather x2 -> x0, blocking collectives: 90 us -> none  [the longest x1 81.1 us: per_device(): lax.all_gather(w_router, ('narrow', 'wide'), axis=0, tiled=True)]
    unnamed x2 -> x0, blocking collectives: 88 us -> none
    all_to_all x1 -> x0, blocking collectives: 63.4 us -> none  [per_device(): lax.all_to_all(slot_grad, 'wide', split_axis=0, concat_axis=1, tiled=True)]
  transfers between devices with their start and end apart: 19 -> 18, of which waited for: 15 -> 3; matrix products, arithmetic and copies ran while one was open for 12% -> 5% of each run, Pallas kernels for 0% -> 77%
where the time goes in v1:
time: 555 us; the launch traced here: 547 us
  Pallas kernels  423 us (76%)
  waiting for transfers between devices  52.7 us (9%)
  starting transfers between devices  22.8 us (4%)
  local copies, waits for them, and re-layouts  19.1 us (3%)
  between operations  14.6 us (3%)
  other arithmetic  14.1 us (3%)
    pallas_call x1, Pallas kernels, gather_call(): pl.pallas_call(gather_kernel, name='gather_inputs', out_shape=(jax.ShapeD...  118 us
    pallas_call x1, Pallas kernels, collect_call(): pl.pallas_call(collect_kernel, name='collect', out_shape=(jax.ShapeDtypeS...  87.8 us
    pallas_call x1, Pallas kernels, project_call(): pl.pallas_call(project_kernel, name='project', out_shape=(jax.ShapeDtypeS...  62.1 us
    pallas_call x1, Pallas kernels, finish_call(): pl.pallas_call(finish_kernel, name='finish', out_shape=(jax.ShapeDtypeStr...  54.9 us
    ppermute x14, waiting for transfers between devices, swap(): lax.ppermute(values, 'narrow', [(i, i ^ distance) for i in range(NARROW)])  52.6 us
    pallas_call x1, Pallas kernels, expert_call(): pl.pallas_call(expert_kernel, name='experts', grid=(steps,), out_shape=(j...  34.8 us
    ppermute x14, starting transfers between devices, swap(): lax.ppermute(values, 'narrow', [(i, i ^ distance) for i in range(NARROW)])  22.6 us
    pallas_call x1, Pallas kernels, attend_back_call(): pl.pallas_call(attend_back_kernel, name='attend_back', grid=(2,), out_sha...  21.9 us
  transfers between devices with their start and end apart: 18, of which 3 were waited for; matrix products, arithmetic and copies ran while one was open for 5% of the time, Pallas kernels for 77%

profile of v1, /device:TPU:0, one launch (start us, length us, event | category | flops | bytes accessed | tf_op | source)
XLA Modules:
  0.0 546.7 jit_solution(12983131256655718483)
XLA Ops:
  7.3 1.6 concatenate.17
  8.9 3.1 collective-permute-start
  12.0 12.1 %collective-permute-done = bf16[256,1024]{1,0:T(8,128)(2,1)S(1)} collective-permute-done((bf16[256,1024]{1,0:T(8,128)(2,1)}, bf16[256,1024]{1,0:T(8,128)(2,1)S(1)}, u32[]{:S(2)}, u32[]{:S(2)}) %collective-permute-start) | collective-permute-done | bytes 524320 | tf_op jit(solution)/shard_map/ppermute | solution.py:1642
  24.1 2.5 maximum_select_fusion
  27.0 0.7 copy.30
  27.8 1.0 dynamic-slice_bitcast_fusion.3
  28.8 1.7 collective-permute-start.4
  30.6 1.2 dynamic-slice_bitcast_fusion
  32.1 2.8 collective-permute-start.2
  34.9 1.3 collective-permute-start.3
  36.2 1.7 collective-permute-start.5
  37.9 31.9 %collective-permute-done.4.d1 = bf16[2,128,1024]{2,1,0:T(8,128)(2,1)S(1)} collective-permute-done((bf16[2,128,1024]{2,1,0:T(8,128)(2,1)}, bf16[2,128,1024]{2,1,0:T(8,128)(2,1)S(1)}, u32[]{:S(2)}, u32[]{:S(2)}) %collective-permute-start.4) | collective-permute-done | bytes 524320 | tf_op jit(solution)/shard_map/ppermute | solution.py:1642
  69.8 3.6 collective-permute-start.6
  73.4 0.6 pad.12.seg_ref
  74.0 0.6 fusion.12.g_ref
  74.6 117.6 %gather_inputs.1 = (bf16[8,256,1024]{2,1,0:T(8,128)(2,1)}, bf16[32,32,256]{2,1,0:T(8,128)(2,1)}, f32[32,8,128]{2,1,0:T(8,128)}, s32[8,8,128]{2,1,0:T(8,128)}) custom-call(bf16[256,1024]{1,0:T(8,128)(2,1)} %bitcast.45, bf16[32,2048]{1,0:T(8,128)(2,1)} %bitcast.55, f32[8,128]{1,0:T(8,128)} %fusion.12.g_ref, s32[8,128]{1,0:T(8,128)} %pad.12.seg_ref), custom_call_target="tpu_custom_call" | custom-call | tf_op jit(solution)/shard_map/gather_inputs/pallas_call | solution.py:636
  192.2 18.4 %attend.1 = (bf16[2,1024,1024]{2,1,0:T(8,128)(2,1)}, bf16[2,1024,256]{2,1,0:T(8,128)(2,1)}, f32[2,1024,128]{2,1,0:T(8,128)}, bf16[2,1024,128]{2,1,0:T(8,128)(2,1...) custom-call(bf16[8,2,128,1024]{3,2,1,0:T(8,128)(2,1)} %bitcast.48, ...), custom_call_target="tpu_custom_call" | custom-call | tf_op jit(solution)/shard_map/attend/pallas_call | solution.py:770
  210.7 62.1 %project.1 = (bf16[16,256,1024]{2,1,0:T(8,128)(2,1)}, f32[16,8,256]{2,1,0:T(8,128)}, f32[256,1024]{1,0:T(8,128)}, f32[64,256]{1,0:T(8,128)}) custom-call(bf16[2,1024,128]{2,1,0:T(8,128)(2,1)} %get-tuple-element.49.o_ref, bf16[256,1024]{1,0:T(8,128)(2,1)} %bitcast.46, bf16[1024,1152]{1,0:T(8,128)(2,1)} %all-gather.4.cloned.1.call-done.w_ref, ...), custom_call_target="tpu_custom_call" | custom-call | tf_op jit(solution)/shard_map/project/pallas_call | solution.py:915
  272.9 0.9 copy-done.17
  273.9 0.3 copy-done.18
  274.2 34.8 %experts.1 = (bf16[4,2,320,1024]{3,2,1,0:T(8,128)(2,1)}, bf16[4,2,320,1024]{3,2,1,0:T(8,128)(2,1)}, bf16[8,2,256,1024]{3,2,1,0:T(8,128)(2,1)}, f32[16,8,256]{2,1,0:T(8,128)}, bf16[2,512,1024]{2,1,0:T(8,128)(2,1)}) custom-call(bf16[16,256,1024]{2,1,0:T(8,128)(2,1)} %get-tuple-element.52.h2_ref, bf16[8,2,256,1024]{3,2,1,0:T(8,128)(2,1)} %bitcast.68, ...), custom_call_target="tpu_custom_call" | custom-call | flops 18790481920 | bytes 41943040 | tf_op jit(solution)/shard_map/experts/pallas_call | solution.py:1040
  309.1 1.8 constant_dynamic-slice_fusion.7.w_ref
  310.9 1.1 constant_dynamic-slice_fusion.1
  312.0 2.6 collective-permute-start.11
  314.7 1.2 collective-permute-start.12
  315.9 0.6 collective-permute-start.13
  316.4 12.2 %gate_up_grad.1 = bf16[2,1024,1024]{2,1,0:T(8,128)(2,1)} custom-call(bf16[4,2,320,1024]{3,2,1,0:T(8,128)(2,1)} %get-tuple-element.76.rows_ref, bf16[4,2,320,1024]{3,2,1,0:T(8,128)(2,1)} %get-tuple-element.55.da_ref), custom_call_target="tpu_custom_call" | custom-call | flops 5368709120 | bytes 14680064 | tf_op jit(solution)/shard_map/gate_up_grad/pallas_call | solution.py:1072
  328.7 3.6 constant_dynamic-slice_fusion.4
  332.3 3.4 collective-permute-start.10
  335.7 13.6 %rows_grad.1.part_ref = bf16[16,256,1024]{2,1,0:T(8,128)(2,1)} custom-call(bf16[4,2,320,1024]{3,2,1,0:T(8,128)(2,1)} %get-tuple-element.55.da_ref, f32[16,8,256]{2,1,0:T(8,128)} %get-tuple-element.53.table_ref, bf16[2,256,1024]{2,1,0:T(8,128)(2,1)} %copy-done.3, bf16[2,256,1024]{2,1,0:T(8,128)(2,1)} %copy-done.17, bf16[2,256,1024]{2,1,0:T(8,128)(2,1)} %copy-done.18, ...), custom_call_target="tpu_custom_call" | custom-call | flops 5368709120 | bytes 20971520 | tf_op jit(solution)/shard_map/rows_grad/pallas_call | solution.py:1111
  349.3 87.8 %collect.1 = (bf16[8,256,1024]{2,1,0:T(8,128)(2,1)}, f32[256,1024]{1,0:T(8,128)}, f32[40,1024]{1,0:T(8,128)}) custom-call(bf16[16,256,1024]{2,1,0:T(8,128)(2,1)} %rows_grad.1.part_ref, f32[16,8,256]{2,1,0:T(8,128)} %get-tuple-element.56.dgate_ref, bf16[16,256,1024]{2,1,0:T(8,128)(2,1)} %get-tuple-element.52.h2_ref, f32[256,1024]{1,0:T(8,128)} %get-tuple-element.51.mid_ref, ...), custom_call_target="tpu_custom_call" | custom-call | tf_op jit(solution)/shard_map/collect/pallas_call | solution.py:1318
  437.4 21.9 %attend_back.1 = (bf16[2,1024,256]{2,1,0:T(8,128)(2,1)}, bf16[1024,256]{1,0:T(8,128)(2,1)}, bf16[128,1024]{1,0:T(8,128)(2,1)}) custom-call(bf16[8,2,128,1024]{3,2,1,0:T(8,128)(2,1)} %bitcast.69, bf16[128,1024]{1,0:T(8,128)(2,1)} %constant_dynamic-slice_fusion.7.w_ref, bf16[2,1024,1024]{2,1,0:T(8,128)(2,1)} %get-tuple-element.59.h1_ref, ...), custom_call_target="tpu_custom_call" | custom-call | flops 8589934592 | bytes 16777216 | tf_op jit(solution)/shard_map/attend_back/pallas_call | solution.py:1412
  459.3 54.9 %finish.1 = (bf16[256,1024]{1,0:T(8,128)(2,1)}, f32[32,1024]{1,0:T(8,128)}, f32[32,512]{1,0:T(8,128)}, f32[32,512]{1,0:T(8,128)}, f32[32,1024]{1,0:T(8,128)}, /*index=5*/f32[40,128]{1,0:T(8,128)}, f32[8,128]{1,0:T(8,128)}) custom-call(bf16[2,1024,256]{2,1,0:T(8,128)(2,1)} %get-tuple-element.64.dqkv_ref, bf16[1024,256]{1,0:T(8,128)(2,1)} %get-tuple-element.65.wg_ref, ...), custom_call_target="tpu_custom_call" | custom-call | tf_op jit(solution)/shard_map/finish/pallas_call | solution.py:1604
  514.2 0.8 dynamic-slice_bitcast_fusion.5
  515.0 0.7 copy.28
  515.6 1.3 convert_bitcast_fusion
  517.0 1.8 fusion.5
  518.8 1.5 pad_maximum_fusion.1
  520.2 1.1 dynamic-slice_bitcast_fusion.2
  521.4 2.8 fusion.1
  524.2 2.5 pad_maximum_fusion
  526.8 8.5 %collective-permute-done.7 = bf16[256,1024]{1,0:T(8,128)(2,1)S(1)} collective-permute-done((bf16[256,1024]{1,0:T(8,128)(2,1)S(1)}, bf16[256,1024]{1,0:T(8,128)(2,1)S(1)}, u32[]{:S(2)}, u32[]{:S(2)}) %collective-permute-start.7) | collective-permute-done | bytes 524320 | tf_op jit(solution)/shard_map/ppermute | solution.py:1642
  535.3 1.0 fusion.3
  536.4 0.8 copy.36
  537.2 0.7 copy.37
  537.8 0.6 copy.38
  538.5 0.6 copy.39
  539.1 0.7 copy.40
  (70 shorter events, 1.4 us)
Async XLA Ops:
  7.2 19.5 %copy-start.9 = (bf16[32,1024]{1,0:T(8,128)(2,1)S(1)}, bf16[32,1024]{1,0:T(8,128)(2,1)}, u32[]{:S(2)}) copy-start(bf16[32,1024]{1,0:T(8,128)(2,1)} %param.21) | copy-start | bytes 196612
  7.2 19.5 %copy-start.12 = (bf16[32,512]{1,0:T(8,128)(2,1)S(1)}, bf16[32,512]{1,0:T(8,128)(2,1)}, u32[]{:S(2)}) copy-start(bf16[32,512]{1,0:T(8,128)(2,1)} %param.22) | copy-start | bytes 98308
  7.2 19.6 %copy-start.13 = (bf16[32,512]{1,0:T(8,128)(2,1)S(1)}, bf16[32,512]{1,0:T(8,128)(2,1)}, u32[]{:S(2)}) copy-start(bf16[32,512]{1,0:T(8,128)(2,1)} %param.23) | copy-start | bytes 98308
  7.2 203.5 %all-gather.4.cloned.1.call-start = ((), (), s32[]{:S(2)}) async-start(), calls=%async_computation.1 | async-start | bytes 2433024 | tf_op jit(solution)/shard_map/all_gather | solution.py:1692
  8.8 264.1 %all-gather.6.cloned.1.call-start = ((), (), s32[]{:S(2)}) async-start(), calls=%async_computation.2 | async-start | bytes 9437184 | tf_op jit(solution)/shard_map/all_gather | solution.py:1710
  8.9 15.2 %collective-permute-start = (bf16[256,1024]{1,0:T(8,128)(2,1)}, bf16[256,1024]{1,0:T(8,128)(2,1)S(1)}, u32[]{:S(2)}, u32[]{:S(2)}) collective-permute-start(bf16[256,1024]{1,0:T(8,128)(2,1)} %bitcast.50), channel_id=1, source_target_pairs={{0,8},{8,0},{16,24},{24,16},{1,9},{9,1},{17,25},{25,17},{2,10},{10... | collective-permute-start | bytes 1572872 | tf_op jit(solution)/shard_map/ppermute | solution.py:1642
  24.1 3.7 copy-start.4
  26.6 4.0 copy-start.1
  26.6 432.7 %all-gather.8.cloned.1.call-start = ((), (), s32[]{:S(2)}) async-start(), calls=%async_computation.4 | async-start | bytes 4325376 | tf_op jit(solution)/shard_map/all_gather | solution.py:1713
  27.7 492.5 %reduce-scatter.2.cloned.1.call-start = ((), (), s32[]{:S(2)}) async-start(), calls=%async_computation.3 | async-start | bytes 9437184 | tf_op jit(solution)/shard_map/reduce_scatter | solution.py:1718
  28.8 41.0 %collective-permute-start.4 = (bf16[2,128,1024]{2,1,0:T(8,128)(2,1)}, bf16[2,128,1024]{2,1,0:T(8,128)(2,1)S(1)}, u32[]{:S(2)}, u32[]{:S(2)}) collective-permute-start(bf16[2,128,1024]{2,1,0:T(8,128)(2,1)} %get-tuple-element.102), channel_id=1, source_target_pairs={{0,8},{8,0},{16,24},{24,16},{1,9},{9,1},{17,25},{25,17},{2,10},{10... | collective-permute-start | bytes 1572872 | tf_op jit(solution)/shard_map/ppermute | solution.py:1642
  30.6 42.8 %copy-start.14 = (s32[2,128]{1,0:T(2,128)S(1)}, s32[2,128]{1,0:T(2,128)}, u32[]{:S(2)}) copy-start(s32[2,128]{1,0:T(2,128)} %param.18) | copy-start | bytes 3076
  30.6 43.4 %copy-start.15 = (bf16[32]{0:T(256)(128)(2,1)S(1)}, bf16[32]{0:T(256)(128)(2,1)}, u32[]{:S(2)}) copy-start(bf16[32]{0:T(256)(128)(2,1)} %param.25) | copy-start | bytes 196
  30.6 43.4 %copy-start.16 = (bf16[32]{0:T(256)(128)(2,1)S(1)}, bf16[32]{0:T(256)(128)(2,1)}, u32[]{:S(2)}) copy-start(bf16[32]{0:T(256)(128)(2,1)} %param.20) | copy-start | bytes 196
  31.8 178.8 %copy-start.3 = (bf16[2,256,1024]{2,1,0:T(8,128)(2,1)}, bf16[2,256,1024]{2,1,0:T(8,128)(2,1)S(1)}, u32[]{:S(2)}) copy-start(bf16[2,256,1024]{2,1,0:T(8,128)(2,1)S(1)} %get-tuple-element.101.gu0) | copy-start | bytes 3145732
  31.8 241.0 %collective-permute-start.1 = (bf16[2,256,1024]{2,1,0:T(8,128)(2,1)}, bf16[2,256,1024]{2,1,0:T(8,128)(2,1)S(1)}, u32[]{:S(2)}, u32[]{:S(2)}) collective-permute-start(bf16[2,256,1024]{2,1,0:T(8,128)(2,1)} %get-tuple-element.100), channel_id=1, source_target_pairs={{0,8},{8,0},{16,24},{24,16},{1,9},{9,1},{17,25},{25,17},{2,10},{10... | collective-permute-start | bytes 3145736 | tf_op jit(solution)/shard_map/ppermute | solution.py:1642
  32.1 240.8 %collective-permute-start.2 = (bf16[2,256,1024]{2,1,0:T(8,128)(2,1)S(1)}, bf16[2,256,1024]{2,1,0:T(8,128)(2,1)S(1)}, u32[]{:S(2)}, u32[]{:S(2)}) collective-permute-start(bf16[2,256,1024]{2,1,0:T(8,128)(2,1)S(1)} %get-tuple-element.101.gu0), channel_id=1, source_target_pairs={{0,16},{8,24},{16,0},{24,8},{1,17},{9,25},{17,1},{25,9},{2,18},{10... | collective-permute-start | bytes 3145736 | tf_op jit(solution)/shard_map/ppermute | solution.py:1642
  34.9 238.0 %collective-permute-start.3 = (bf16[2,256,1024]{2,1,0:T(8,128)(2,1)}, bf16[2,256,1024]{2,1,0:T(8,128)(2,1)}, u32[]{:S(2)}, u32[]{:S(2)}) collective-permute-start(bf16[2,256,1024]{2,1,0:T(8,128)(2,1)} %get-tuple-element.100), channel_id=1, source_target_pairs={{0,24},{8,16},{16,8},{24,0},{1,25},{9,17},{17,9},{25,1},{2,26},{10... | collective-permute-start | bytes 3145736 | tf_op jit(solution)/shard_map/ppermute | solution.py:1642
  36.2 236.6 %collective-permute-start.5 = (bf16[2,128,1024]{2,1,0:T(8,128)(2,1)}, bf16[2,128,1024]{2,1,0:T(8,128)(2,1)}, u32[]{:S(2)}, u32[]{:S(2)}) collective-permute-start(bf16[2,128,1024]{2,1,0:T(8,128)(2,1)} %get-tuple-element.103.d0), channel_id=1, source_target_pairs={{0,16},{8,24},{16,0},{24,8},{1,17},{9,25},{17,1},{25,9},{2,18},{10... | collective-permute-start | bytes 1572872 | tf_op jit(solution)/shard_map/ppermute | solution.py:1642
  69.8 4.8 copy-start.19
  69.8 203.0 %collective-permute-start.6 = (bf16[2,128,1024]{2,1,0:T(8,128)(2,1)}, bf16[2,128,1024]{2,1,0:T(8,128)(2,1)}, u32[]{:S(2)}, u32[]{:S(2)}) collective-permute-start(bf16[2,128,1024]{2,1,0:T(8,128)(2,1)} %get-tuple-element.102), channel_id=1, source_target_pairs={{0,24},{8,16},{16,8},{24,0},{1,25},{9,17},{17,9},{25,1},{2,26},{10... | collective-permute-start | bytes 1572872 | tf_op jit(solution)/shard_map/ppermute | solution.py:1642
  272.9 1.0 copy-start.17
  272.9 1.3 copy-start.18
  309.0 1.9 copy-start.2
  312.0 125.0 %collective-permute-start.11 = (bf16[2,128,1024]{2,1,0:T(8,128)(2,1)S(1)}, bf16[2,128,1024]{2,1,0:T(8,128)(2,1)}, u32[]{:S(2)}, u32[]{:S(2)}) collective-permute-start(bf16[2,128,1024]{2,1,0:T(8,128)(2,1)S(1)} %get-tuple-element.99), channel_id=1, source_target_pairs={{0,16},{8,24},{16,0},{24,8},{1,17},{9,25},{17,1},{25,9},{2,18},{10... | collective-permute-start | bytes 1572872 | tf_op jit(solution)/shard_map/ppermute | solution.py:1642
  314.7 202.3 %collective-permute-start.12 = (bf16[2,128,1024]{2,1,0:T(8,128)(2,1)}, bf16[2,128,1024]{2,1,0:T(8,128)(2,1)}, u32[]{:S(2)}, u32[]{:S(2)}) collective-permute-start(bf16[2,128,1024]{2,1,0:T(8,128)(2,1)} %get-tuple-element.97), channel_id=1, source_target_pairs={{0,8},{8,0},{16,24},{24,16},{1,9},{9,1},{17,25},{25,17},{2,10},{10... | collective-permute-start | bytes 1572872 | tf_op jit(solution)/shard_map/ppermute | solution.py:1642
  315.9 201.1 %collective-permute-start.13 = (bf16[2,128,1024]{2,1,0:T(8,128)(2,1)}, bf16[2,128,1024]{2,1,0:T(8,128)(2,1)}, u32[]{:S(2)}, u32[]{:S(2)}) collective-permute-start(bf16[2,128,1024]{2,1,0:T(8,128)(2,1)} %get-tuple-element.98), channel_id=1, source_target_pairs={{0,24},{8,16},{16,8},{24,0},{1,25},{9,17},{17,9},{25,1},{2,26},{10... | collective-permute-start | bytes 1572872 | tf_op jit(solution)/shard_map/ppermute | solution.py:1642
  332.3 189.1 %collective-permute-start.10 = (bf16[2,256,1024]{2,1,0:T(8,128)(2,1)}, bf16[2,256,1024]{2,1,0:T(8,128)(2,1)S(1)}, u32[]{:S(2)}, u32[]{:S(2)}) collective-permute-start(bf16[2,256,1024]{2,1,0:T(8,128)(2,1)} %get-tuple-element.93), channel_id=1, source_target_pairs={{0,24},{8,16},{16,8},{24,0},{1,25},{9,17},{17,9},{25,1},{2,26},{10... | collective-permute-start | bytes 3145736 | tf_op jit(solution)/shard_map/ppermute | solution.py:1642
  335.7 185.7 %collective-permute-start.8 = (bf16[2,256,1024]{2,1,0:T(8,128)(2,1)}, bf16[2,256,1024]{2,1,0:T(8,128)(2,1)}, u32[]{:S(2)}, u32[]{:S(2)}) collective-permute-start(bf16[2,256,1024]{2,1,0:T(8,128)(2,1)} %get-tuple-element.94), channel_id=1, source_target_pairs={{0,16},{8,24},{16,0},{24,8},{1,17},{9,25},{17,1},{25,9},{2,18},{10... | collective-permute-start | bytes 3145736 | tf_op jit(solution)/shard_map/ppermute | solution.py:1642
  437.1 84.3 %collective-permute-start.9 = (bf16[2,256,1024]{2,1,0:T(8,128)(2,1)}, bf16[2,256,1024]{2,1,0:T(8,128)(2,1)}, u32[]{:S(2)}, u32[]{:S(2)}) collective-permute-start(bf16[2,256,1024]{2,1,0:T(8,128)(2,1)} %get-tuple-element.92), channel_id=1, source_target_pairs={{0,8},{8,0},{16,24},{24,16},{1,9},{9,1},{17,25},{25,17},{2,10},{10... | collective-permute-start | bytes 3145736 | tf_op jit(solution)/shard_map/ppermute | solution.py:1642
  521.3 14.0 %collective-permute-start.7 = (bf16[256,1024]{1,0:T(8,128)(2,1)S(1)}, bf16[256,1024]{1,0:T(8,128)(2,1)S(1)}, u32[]{:S(2)}, u32[]{:S(2)}) collective-permute-start(bf16[256,1024]{1,0:T(8,128)(2,1)S(1)} %dynamic-slice_bitcast_fusion.2), channel_id=1, source_target_pairs={{0,8},{8,0},{16,24},{24,16},{1,9},{9,1},{17,25},{25,17},{2,10},{10... | collective-permute-start | bytes 1572872 | tf_op jit(solution)/shard_map/ppermute | solution.py:1642
  524.2 11.1 %copy-start = (f32[256,1024]{1,0:T(8,128)S(1)}, f32[256,1024]{1,0:T(8,128)}, u32[]{:S(2)}) copy-start(f32[256,1024]{1,0:T(8,128)} %get-tuple-element.51.mid_ref) | copy-start | bytes 3145732
  524.2 11.1 %copy-start.5 = (bf16[512,1024]{1,0:T(8,128)(2,1)S(1)}, bf16[512,1024]{1,0:T(8,128)(2,1)}, u32[]{:S(2)}) copy-start(bf16[512,1024]{1,0:T(8,128)(2,1)} %reduce-scatter.2.cloned.1.call-done) | copy-start | bytes 3145732
  526.8 9.6 %copy-start.6 = (bf16[256,1024]{1,0:T(8,128)(2,1)S(1)}, bf16[256,1024]{1,0:T(8,128)(2,1)}, u32[]{:S(2)}) copy-start(bf16[256,1024]{1,0:T(8,128)(2,1)} %get-tuple-element.69) | copy-start | bytes 1572868
  526.8 10.4 %copy-start.8 = (f32[32,1024]{1,0:T(8,128)S(1)}, f32[32,1024]{1,0:T(8,128)}, u32[]{:S(2)}) copy-start(f32[32,1024]{1,0:T(8,128)} %get-tuple-element.122) | copy-start | bytes 393220
  526.8 11.0 %copy-start.11 = (f32[32,512]{1,0:T(8,128)S(1)}, f32[32,512]{1,0:T(8,128)}, u32[]{:S(2)}) copy-start(f32[32,512]{1,0:T(8,128)} %get-tuple-element.123) | copy-start | bytes 196612
  526.8 11.7 %copy-start.10 = (f32[32,512]{1,0:T(8,128)S(1)}, f32[32,512]{1,0:T(8,128)}, u32[]{:S(2)}) copy-start(f32[32,512]{1,0:T(8,128)} %get-tuple-element.124) | copy-start | bytes 196612
  526.8 12.3 %copy-start.7 = (f32[32,1024]{1,0:T(8,128)S(1)}, f32[32,1024]{1,0:T(8,128)}, u32[]{:S(2)}) copy-start(f32[32,1024]{1,0:T(8,128)} %get-tuple-element.125) | copy-start | bytes 393220
Sparse Core Ops, SparseCore 0:
  11.5 144.3 all-gather.3
  157.8 54.2 all-gather.5
  215.6 68.4 all-gather.7
  309.2 83.9 reduce-scatter.1

commit v2 on v1

--- a/solution.py
+++ b/solution.py
@@ -1,5 +1,6 @@
 import math
 
+import functools
 import jax
 import jax.numpy as jnp
 import numpy as np
@@ -445,6 +446,10 @@
 TN = (((0,), (0,)), ((), ()))
 
 
+def duration(us):
+    return pl.CostEstimate(flops=us * 1000000000, bytes_accessed=us * 3600000, transcendentals=0)
+
+
 def mm(left, right, dims=(((1,), (0,)), ((), ()))):
     return lax.dot_general(left, right, dims, preferred_element_type=F32)
 
@@ -501,71 +506,81 @@
 class PlaneGather:
     COPIES = 11
 
-    def __init__(self, spot, own, out, base, send, recv):
-        self.spot, self.own, self.out, self.base = spot, own, out, base
+    def __init__(self, spot, source, place, send, recv):
+        self.spot, self.source, self.place = spot, source, place
         self.send, self.recv = send, recv
         self.started = []
-
-    def block(self, who):
-        return self.out.at[self.base + who]
 
     def put(self, src, dst, number, to):
         copy = remote(src, dst, self.send.at[number], self.recv.at[number], self.spot.wide(to))
         copy.start()
         self.started.append(copy)
 
-    def got(self, dst, number):
+    def pass_on(self, who, half, number, to):
+        place = self.place(who, half)
+        self.put(place, place, number, to)
+
+    def got(self, who, half, number):
+        dst = self.place(who, half)
         remote(dst, dst, self.send.at[number], self.recv.at[number], self.spot.wide(self.spot.sib)).wait_recv()
 
     def begin(self):
         s = self.spot
-        mine = self.block(s.w)
-        self.put(halves(self.own, 0), halves(mine, 0), 0, s.xn)
-        self.put(halves(self.own, 1), halves(mine, 1), 2, s.yn)
-        self.put(halves(self.own, 1), halves(mine, 1), 1, s.xn)
-        self.put(halves(self.own, 0), halves(mine, 0), 3, s.yn)
-        self.put(self.own, mine, 4, s.sib)
+        self.put(self.source(0), self.place(s.w, 0), 0, s.xn)
+        self.put(self.source(1), self.place(s.w, 1), 2, s.yn)
+        self.put(self.source(1), self.place(s.w, 1), 1, s.xn)
+        self.put(self.source(0), self.place(s.w, 0), 3, s.yn)
+        self.put(self.source(None), self.place(s.w, None), 4, s.sib)
 
     def middle(self):
         s = self.spot
-        from_x, from_y = self.block(s.xn), self.block(s.yn)
-        self.got(halves(from_x, 0), 0)
-        self.put(halves(from_x, 0), halves(from_x, 0), 5, s.yn)
-        self.got(halves(from_y, 1), 2)
-        self.put(halves(from_y, 1), halves(from_y, 1), 6, s.xn)
+        self.got(s.xn, 0, 0)
+        self.pass_on(s.xn, 0, 5, s.yn)
+        self.got(s.yn, 1, 2)
+        self.pass_on(s.yn, 1, 6, s.xn)
 
     def late(self):
         s = self.spot
-        from_x, from_y = self.block(s.xn), self.block(s.yn)
-        self.got(halves(from_x, 1), 1)
-        self.put(from_x, from_x, 7, s.sib)
-        self.got(halves(from_y, 0), 3)
-        self.put(from_y, from_y, 8, s.sib)
+        self.got(s.xn, 1, 1)
+        self.pass_on(s.xn, None, 7, s.sib)
+        self.got(s.yn, 0, 3)
+        self.pass_on(s.yn, None, 8, s.sib)
 
     def last(self):
         s = self.spot
-        from_d = self.block(s.diag)
-        self.got(halves(from_d, 0), 5)
-        self.put(halves(from_d, 0), halves(from_d, 0), 9, s.sib)
-        self.got(halves(from_d, 1), 6)
-        self.put(halves(from_d, 1), halves(from_d, 1), 10, s.sib)
+        self.got(s.diag, 0, 5)
+        self.pass_on(s.diag, 0, 9, s.sib)
+        self.got(s.diag, 1, 6)
+        self.pass_on(s.diag, 1, 10, s.sib)
 
     def finish(self):
         s = self.spot
-        sib = s.sib
-        sib_x = sib + 2 - 4 * s.x
-        sib_y = sib + 4 - 8 * s.y
+        sib_x = s.sib + 2 - 4 * s.x
+        sib_y = s.sib + 4 - 8 * s.y
         sib_d = sib_x + 4 - 8 * s.y
-        self.got(self.block(sib), 4)
-        self.got(self.block(sib_x), 7)
-        self.got(self.block(sib_y), 8)
-        self.got(halves(self.block(sib_d), 0), 9)
-        self.got(halves(self.block(sib_d), 1), 10)
+        self.got(s.sib, None, 4)
+        self.got(sib_x, None, 7)
+        self.got(sib_y, None, 8)
+        self.got(sib_d, 0, 9)
+        self.got(sib_d, 1, 10)
         for copy in self.started:
             copy.wait_send()
 
 
-def gather_kernel(x_ref, w_ref, g_ref, seg_ref, x_all, w_all, g_all, seg_all, send, recv, local, ws, wr, gs, gr, ss, sr):
+def gather_tokens(spot, own, out, base, send, recv):
+    def part(ref, half):
+        return ref if half is None else ref.at[pl.ds(half * SPAN, SPAN)]
+
+    return PlaneGather(
+        spot, lambda half: part(own, half), lambda who, half: part(out.at[base + who], half), send, recv
+    )
+
+
+def gather_kernel(
+    x_ref, w_ref, g_ref, seg_ref, wo_ref, dy_ref,
+    x_all, w_all, g_all, seg_all, wo_block, dy_pair,
+    send, recv, local, ws, wr, gs, gr, ss, sr, zs, zr, ds, dr,
+):
     spot = Spot()
     spot.greet(NARROW * WIDE)
     own = [
@@ -573,11 +588,10 @@
         pltpu.make_async_copy(w_ref.at[:, pl.ds(pl.multiple_of(spot.w * 256, 256), 256)], w_all.at[spot.me], local.at[1]),
         pltpu.make_async_copy(g_ref, g_all.at[spot.me], local.at[2]),
         pltpu.make_async_copy(seg_ref, seg_all.at[spot.w], local.at[3]),
+        pltpu.make_async_copy(wo_ref, wo_block.at[spot.n], local.at[4]),
+        pltpu.make_async_copy(dy_ref, dy_pair.at[spot.half], local.at[5]),
     ]
-    gather = PlaneGather(spot, x_ref, x_all, 0, send, recv)
-    gather.begin()
-    for copy in own:
-        copy.start()
+    gather = gather_tokens(spot, x_ref, x_all, 0, send, recv)
 
     def others(step):
         other = lax.rem(spot.me + step, NARROW * WIDE)
@@ -597,17 +611,32 @@
         place = other if arriving else spot.w
         return remote(seg_ref, seg_all.at[place], ss.at[other], sr.at[place], spot.wide(other))
 
+    def column(step, arriving):
+        other = lax.rem(spot.n + step, NARROW)
+        place = other if arriving else spot.n
+        return remote(wo_ref, wo_block.at[place], zs.at[other], zr.at[place], (other, spot.w))
+
     def start(step, carry):
         for copy in weights(step, False):
             copy.start()
         return carry
 
+    def start_column(step, carry):
+        column(step, False).start()
+        return carry
+
     def start_documents(step, carry):
         documents(step, False).start()
         return carry
 
     lax.fori_loop(1, WIDE, start_documents, 0)
     lax.fori_loop(1, NARROW * WIDE, start, 0)
+    gather.begin()
+    lax.fori_loop(1, NARROW, start_column, 0)
+    for copy in own:
+        copy.start()
+    across = remote(dy_ref, dy_pair.at[spot.half], ds.at[0], dr.at[0], (spot.mate, spot.w))
+    across.start()
     gather.middle()
     gather.late()
     gather.last()
@@ -619,6 +648,11 @@
             copy.wait_recv()
         return carry
 
+    def wait_column(step, carry):
+        column(step, False).wait_send()
+        column(step, True).wait_recv()
+        return carry
+
     def wait_documents(step, carry):
         documents(step, False).wait_send()
         documents(step, True).wait_recv()
@@ -626,12 +660,16 @@
 
     lax.fori_loop(1, WIDE, wait_documents, 0)
     lax.fori_loop(1, NARROW * WIDE, wait, 0)
+    lax.fori_loop(1, NARROW, wait_column, 0)
     gather.finish()
+    across.wait_send()
+    arrived = dy_pair.at[1 - spot.half]
+    remote(arrived, arrived, ds.at[0], dr.at[0], (spot.mate, spot.w)).wait_recv()
     for copy in own:
         copy.wait()
 
 
-def gather_call(x_own, w_own, g_own, seg_own):
+def gather_call(x_own, w_own, g_own, seg_own, wo_own, dy_own):
     dma = pltpu.SemaphoreType.DMA
     return pl.pallas_call(
         gather_kernel,
@@ -641,22 +679,29 @@
             jax.ShapeDtypeStruct((NARROW * WIDE, 32, 256), BF16),
             jax.ShapeDtypeStruct((NARROW * WIDE, 8, 128), F32),
             jax.ShapeDtypeStruct((WIDE, 8, 128), jnp.int32),
+            jax.ShapeDtypeStruct((NARROW, 32, WIDTH + 128), BF16),
+            jax.ShapeDtypeStruct((2, TOKENS, WIDTH), BF16),
         ),
-        in_specs=[IN_HBM] * 4,
-        out_specs=(IN_HBM,) * 4,
+        in_specs=[IN_VMEM] * 6,
+        out_specs=(IN_HBM,) * 6,
         scratch_shapes=[
             dma((PlaneGather.COPIES,)),
             dma((PlaneGather.COPIES,)),
-            dma((4,)),
+            dma((6,)),
             dma((NARROW * WIDE,)),
             dma((NARROW * WIDE,)),
             dma((NARROW * WIDE,)),
             dma((NARROW * WIDE,)),
             dma((WIDE,)),
             dma((WIDE,)),
+            dma((NARROW,)),
+            dma((NARROW,)),
+            dma((1,)),
+            dma((1,)),
         ],
         compiler_params=pltpu.CompilerParams(collective_id=1, has_side_effects=True),
-    )(x_own, w_own, g_own, seg_own)
+        cost_estimate=duration(1),
+    )(x_own, w_own, g_own, seg_own, wo_own, dy_own)
 
 
 def lane_half():
@@ -682,35 +727,36 @@
     return jnp.sum(jnp.where(lax.div(place, 32) == owner, tiled, 0.0), axis=0, keepdims=True)
 
 
-def attend_kernel(x_ref, w_ref, g_ref, seg_ref, cos_ref, sin_ref, freq_ref, h1_ref, qkv_ref, lse_ref, o_ref, angle_ref, start_ref, gain_ref):
-    row = pl.program_id(0)
-    first_half = lane_half()
-    lanes = lax.broadcasted_iota(jnp.int32, (1, 128), 1)
-    weights = w_ref[...].reshape(WIDTH, 256)
-    gains = g_ref[...]
-    gain_one = gather_gain(gains[:, 0, :])
-    gain_two = gather_gain(gains[:, 1, :])
-    gain_ref[...] = jnp.concatenate([gain_one, gain_two, jnp.zeros((6, WIDTH), F32)], axis=0)
-    segs = [jnp.where(row == 0, seg_ref[c, 0:1, :], seg_ref[c, 1:2, :]) for c in range(WIDE)]
-    counts = []
-    for doc in range(5):
-        total = jnp.zeros((1, 128), F32)
-        for c in range(WIDE):
-            total = total + (segs[c] == doc).astype(F32)
-        counts.append(jnp.sum(total, axis=1, keepdims=True))
-    starts = [jnp.zeros((1, 1), F32)]
-    for doc in range(5):
-        starts.append(starts[-1] + counts[doc])
-    start_rows = jnp.concatenate(starts + starts[:2], axis=0)
-    start_angle = start_rows * freq_ref[0:1, :]
-    start_cos = jnp.cos(start_angle)
-    start_sin = jnp.sin(start_angle)
-
-    for i in range(4):
+class Attention:
+    def __init__(self, x_ref, w_ref, seg_ref, cos_ref, sin_ref, freq_ref, gain_one, h1_ref, qkv_ref, lse_ref, o_ref, angle_ref, start_ref):
+        self.x_ref, self.seg_ref, self.cos_ref, self.sin_ref = x_ref, seg_ref, cos_ref, sin_ref
+        self.h1_ref, self.qkv_ref, self.lse_ref, self.o_ref = h1_ref, qkv_ref, lse_ref, o_ref
+        self.angle_ref, self.start_ref = angle_ref, start_ref
+        self.gain_one = gain_one
+        self.w_ref = w_ref
+        self.first_half = lane_half()
+        self.is_key = lax.broadcasted_iota(jnp.int32, (1, 128), 1) < 64
+        self.starts, self.start_cos, self.start_sin = [], [], []
+        for row in range(2):
+            segs = [seg_ref[c, row : row + 1, :] for c in range(WIDE)]
+            starts = [jnp.zeros((1, 1), F32)]
+            for doc in range(5):
+                total = jnp.zeros((1, 128), F32)
+                for seg in segs:
+                    total = total + jnp.where(seg == doc, 1.0, 0.0)
+                starts.append(starts[-1] + jnp.sum(total, axis=1, keepdims=True))
+            angle = jnp.concatenate(starts + starts[:2], axis=0) * freq_ref[0:1, :]
+            self.starts.append(starts)
+            self.start_cos.append(jnp.cos(angle))
+            self.start_sin.append(jnp.sin(angle))
+
+    def chunk(self, row, i):
         tokens = pl.ds(i * 256, 256)
-        seg_cols = [
-            jnp.transpose(jnp.broadcast_to(segs[2 * i + part].astype(F32), (128, 128))) for part in range(2)
-        ]
+        starts, start_cos, start_sin = self.starts[row], self.start_cos[row], self.start_sin[row]
+        seg_cols = []
+        for part in range(2):
+            seg = self.seg_ref[2 * i + part, row : row + 1, :].astype(F32)
+            seg_cols.append(jnp.transpose(jnp.broadcast_to(seg, (128, 128))))
         seg_col = jnp.concatenate(seg_cols, axis=0)
         start_col = jnp.zeros((256, 128), F32)
         cos_s = jnp.broadcast_to(start_cos[0:1], (256, 128))
@@ -720,30 +766,27 @@
             start_col = jnp.where(here, starts[doc], start_col)
             cos_s = jnp.where(here, start_cos[doc : doc + 1], cos_s)
             sin_s = jnp.where(here, start_sin[doc : doc + 1], sin_s)
-        start_ref[0, tokens, :] = start_col
-        cos_t = cos_ref[tokens, :]
-        sin_t = sin_ref[tokens, :]
+        self.start_ref[row, tokens, :] = start_col
+        cos_t = self.cos_ref[tokens, :]
+        sin_t = self.sin_ref[tokens, :]
         cosine = cos_t * cos_s + sin_t * sin_s
         sine = sin_t * cos_s - cos_t * sin_s
-        angle_ref[0, tokens, 0:128] = cosine
-        angle_ref[0, tokens, 128:256] = sine
-        is_key = lanes < 64
-        x = x_ref[2 * i : 2 * i + 2, 0].reshape(256, WIDTH).astype(F32)
+        self.angle_ref[row, tokens, 0:128] = cosine
+        self.angle_ref[row, tokens, 128:256] = sine
+        x = self.x_ref[2 * i : 2 * i + 2, row].reshape(256, WIDTH).astype(F32)
         scale = lax.rsqrt(jnp.mean(x * x, axis=1, keepdims=True) + EPSILON)
-        h1 = (x * scale * gain_one).astype(BF16)
-        h1_ref[0, tokens, :] = h1
-        qkv = mm(h1, weights)
+        h1 = (x * scale * self.gain_one).astype(BF16)
+        self.h1_ref[row, tokens, :] = h1
+        qkv = mm(h1, self.w_ref[...].reshape(WIDTH, 256))
         q = qkv[:, 0:128]
         kv = qkv[:, 128:256]
-        q = q * cosine + turn(q, first_half) * sine
-        kv = jnp.where(is_key, kv * cosine + turn(kv, first_half) * sine, kv)
-        q = q.astype(BF16)
-        kv = kv.astype(BF16)
-        qkv_ref[0, tokens, 0:128] = q
-        qkv_ref[0, tokens, 128:256] = kv
+        q = (q * cosine + turn(q, self.first_half) * sine).astype(BF16)
+        kv = jnp.where(self.is_key, kv * cosine + turn(kv, self.first_half) * sine, kv).astype(BF16)
+        self.qkv_ref[row, tokens, 0:128] = q
+        self.qkv_ref[row, tokens, 128:256] = kv
         length = 256 * (i + 1)
-        keys = qkv_ref[0, 0:length, 128:192]
-        values = qkv_ref[0, 0:length, 192:256]
+        keys = self.qkv_ref[row, 0:length, 128:192]
+        values = self.qkv_ref[row, 0:length, 192:256]
         place_key = lax.broadcasted_iota(jnp.int32, (256, length), 1).astype(F32)
         place_query = (lax.broadcasted_iota(jnp.int32, (256, length), 0) + 256 * i).astype(F32)
         allowed = (place_key <= place_query) & (place_key >= start_col[:, 0:1])
@@ -753,75 +796,76 @@
             scores = jnp.where(allowed, mm(query, keys, NT) * (HEAD_DIM**-0.5), MASKED)
             top = jnp.max(scores, axis=1, keepdims=True)
             log_total = top + jnp.log(jnp.sum(jnp.exp(scores - top), axis=1, keepdims=True))
-            weights_b = jnp.exp(scores - log_total).astype(BF16)
-            outs.append(mm(weights_b, values))
+            outs.append(mm(jnp.exp(scores - log_total).astype(BF16), values))
             logs.append(log_total)
-        o_ref[0, tokens, :] = jnp.concatenate(outs, axis=1).astype(BF16)
-        lse_ref[0, tokens, :] = jnp.where(is_key, logs[0], logs[1])
-
-
-def attend_call(x_all, w_all, g_all, seg_all, cos_table, sin_table, freq):
-    def whole(shape):
-        return pl.BlockSpec(shape, lambda r: (0,) * len(shape))
-
-    def by_row(lanes):
-        return pl.BlockSpec((1, SEQ, lanes), lambda r: (r, 0, 0))
-
-    return pl.pallas_call(
-        attend_kernel,
-        name="attend",
-        grid=(2,),
-        out_shape=(
-            jax.ShapeDtypeStruct((2, SEQ, WIDTH), BF16),
-            jax.ShapeDtypeStruct((2, SEQ, 256), BF16),
-            jax.ShapeDtypeStruct((2, SEQ, 128), F32),
-            jax.ShapeDtypeStruct((2, SEQ, 128), BF16),
-            jax.ShapeDtypeStruct((2, SEQ, 256), F32),
-            jax.ShapeDtypeStruct((2, SEQ, 128), F32),
-            jax.ShapeDtypeStruct((8, WIDTH), F32),
-        ),
-        in_specs=[
-            pl.BlockSpec((WIDE, 1, SPAN, WIDTH), lambda r: (0, r, 0, 0)),
-            whole((NARROW * WIDE, 32, 256)),
-            whole((NARROW * WIDE, 8, 128)),
-            whole((WIDE, 8, 128)),
-            whole((SEQ, 128)),
-            whole((SEQ, 128)),
-            whole((8, 128)),
-        ],
-        out_specs=(by_row(WIDTH), by_row(256), by_row(128), by_row(128), by_row(256), by_row(128), whole((8, WIDTH))),
-        compiler_params=pltpu.CompilerParams(vmem_limit_bytes=VMEM_BYTES),
-    )(x_all.reshape(WIDE, 2, SPAN, WIDTH), w_all, g_all, seg_all, cos_table, sin_table, freq)
-
-
-def project_kernel(
-    o_ref, x_ref, w_ref, gain_ref, ids_ref,
-    h2_all, table_all, mid_ref, gate_ref,
-    o_full, h2_own, table_own, os, orv, s0, r0, s1, r1, ts, tr, zs, zr, local,
+        self.o_ref[row, tokens, :] = jnp.concatenate(outs, axis=1).astype(BF16)
+        self.lse_ref[row, tokens, :] = jnp.where(self.is_key, logs[0], logs[1])
+
+
+def forward_kernel(
+    x_ref, w_ref, g_ref, seg_ref, cos_ref, sin_ref, freq_ref, wo_ref, ids_ref, dy_ref, wq_ref, own_piece, other_piece,
+    h1_out, qkv_ref, lse_ref, o_ref, angle_ref, start_ref, gain_ref, mid_ref, gate_ref, w_all,
+    h2_all, dy_all, table_all, wq_block, far_piece, mate_piece,
+    h1_ref, o_full, h2_own, table_own,
+    os, orv, w_send, w_recv, a_send, a_recv, b_send, b_recv, s0, r0, s1, r1, ts, tr, zs, zr, cs, cr, es, er, local,
 ):
     spot = Spot()
-    spot.greet(GROUP)
-
-    def heads(step, arriving):
-        other = lax.rem(spot.w + step, WIDE)
-        place = other if arriving else spot.w
-        return remote(
-            o_ref.at[:, pl.ds(pl.multiple_of(other * SPAN, SPAN), SPAN), :],
+    spot.greet(NARROW * WIDE)
+    mate_base = (1 - spot.half) * WIDE
+    own_base = spot.half * WIDE
+    mate_slot = mate_base + spot.w
+
+    def w_source(half):
+        return wo_ref if half is None else wo_ref.at[pl.ds(2 * half, 2)]
+
+    def w_place(who, half):
+        return w_all.at[:, who] if half is None else w_all.at[pl.ds(2 * half, 2), who]
+
+    w_gather = PlaneGather(spot, w_source, w_place, w_send, w_recv)
+    dy_gather = gather_tokens(spot, dy_ref.at[spot.half], dy_all, own_base, a_send, a_recv)
+    mate_dy_gather = gather_tokens(spot, dy_ref.at[1 - spot.half], dy_all, mate_base, b_send, b_recv)
+    w_gather.begin()
+    dy_gather.begin()
+
+    def column(step, arriving):
+        other = lax.rem(spot.n + step, NARROW)
+        place = other if arriving else spot.n
+        return remote(wq_ref, wq_block.at[place], cs.at[other], cr.at[place], (other, spot.w))
+
+    def start_column(step, carry):
+        column(step, False).start()
+        return carry
+
+    def wait_column(step, carry):
+        column(step, False).wait_send()
+        column(step, True).wait_recv()
+        return carry
+
+    keep = [
+        pltpu.make_async_copy(wo_ref, w_place(spot.w, None), local.at[0]),
+        pltpu.make_async_copy(dy_ref.at[spot.half], dy_all.at[spot.slot], local.at[1]),
+        pltpu.make_async_copy(dy_ref.at[1 - spot.half], dy_all.at[mate_slot], local.at[2]),
+        pltpu.make_async_copy(wq_ref, wq_block.at[spot.n], local.at[7]),
+    ]
+    for copy in keep:
+        copy.start()
+
+    def heads(to, place):
+        return (
+            o_ref.at[:, pl.ds(to * SPAN, SPAN), :],
             o_full.at[:, :, pl.ds(pl.multiple_of(place * 128, 128), 128)],
-            os.at[other], orv.at[place], spot.wide(other),
-        )
-
-    def start(step, carry):
-        heads(step, False).start()
-        return carry
-
-    lax.fori_loop(1, WIDE, start, 0)
-    mine = pltpu.make_async_copy(
-        o_ref.at[:, pl.ds(pl.multiple_of(spot.w * SPAN, SPAN), SPAN), :],
-        o_full.at[:, :, pl.ds(pl.multiple_of(spot.w * 128, 128), 128)],
-        local.at[0],
-    )
-    mine.start()
+        )
+
+    def each_head_copy(to, act_local, act_remote):
+        source, target = heads(to, spot.w)
+
+        @pl.when(spot.w == to)
+        def _():
+            act_local(pltpu.make_async_copy(source, target, local.at[3]))
+
+        @pl.when(spot.w != to)
+        def _():
+            act_remote(remote(source, target, os.at[to], orv.at[spot.w], spot.wide(to)))
 
     expert = lax.broadcasted_iota(jnp.int32, (32, TOKENS), 0)
     named = jnp.zeros((32, TOKENS), F32)
@@ -830,34 +874,60 @@
     before = lax.broadcasted_iota(jnp.int32, (TOKENS, TOKENS), 0) < lax.broadcasted_iota(
         jnp.int32, (TOKENS, TOKENS), 1
     )
-    places = mm(named.astype(BF16), before.astype(BF16))
+    places = mm(named.astype(BF16), jnp.where(before, 1.0, 0.0).astype(BF16))
     kept = jnp.where((named > 0.5) & (places < float(CAP)), places, -1.0)
 
-    def wait(step, carry):
-        heads(step, False).wait_send()
-        heads(step, True).wait_recv()
+    gains = g_ref[...]
+    gain_one = gather_gain(gains[:, 0, :])
+    gain_two = gather_gain(gains[:, 1, :])
+    gain_ref[...] = jnp.concatenate([gain_one, gain_two, jnp.zeros((6, WIDTH), F32)], axis=0)
+    attention = Attention(
+        x_ref, w_ref, seg_ref, cos_ref, sin_ref, freq_ref, gain_one,
+        h1_ref, qkv_ref, lse_ref, o_ref, angle_ref, start_ref,
+    )
+    between = {1: [w_gather.middle], 2: [w_gather.late, dy_gather.middle], 3: [w_gather.last, dy_gather.late]}
+    for i in range(4):
+        for row in range(2):
+            attention.chunk(row, i)
+        for to in (2 * i, 2 * i + 1):
+            each_head_copy(to, lambda copy: copy.start(), lambda copy: copy.start())
+        for step in between.get(i, []):
+            step()
+    pair = lax.div(spot.n, 2)
+    far = remote(own_piece, far_piece, es.at[0], er.at[0], (spot.n + 2 - 4 * pair, spot.w))
+    far.start()
+    near = remote(other_piece, mate_piece, es.at[1], er.at[1], (spot.mate, spot.w))
+    h1_copy = pltpu.make_async_copy(h1_ref, h1_out, local.at[4])
+    h1_copy.start()
+    dy_gather.last()
+    mate_dy_gather.begin()
+    w_gather.finish()
+    keep[0].wait()
+    for to in range(WIDE):
+        each_head_copy(to, lambda copy: copy.wait(), lambda copy: copy.wait_send())
+
+    def wait_heads(step, carry):
+        other = lax.rem(spot.w + step, WIDE)
+        target = o_full.at[:, :, pl.ds(pl.multiple_of(other * 128, 128), 128)]
+        remote(target, target, os.at[0], orv.at[other], spot.wide(other)).wait_recv()
         return carry
 
-    lax.fori_loop(1, WIDE, wait, 0)
-    mine.wait()
-
+    lax.fori_loop(1, WIDE, wait_heads, 0)
     attended = o_full[...].reshape(TOKENS, WIDTH)
-    mid = x_ref[...].astype(F32) + mm(attended, w_ref[:, 0:WIDTH])
+    x_own = x_ref[spot.w].reshape(TOKENS, WIDTH).astype(F32)
+    mid = x_own + mm(attended, w_all[:, :, :, 0:WIDTH].reshape(WIDTH, WIDTH))
     mid_ref[...] = mid
     scale = lax.rsqrt(jnp.mean(mid * mid, axis=1, keepdims=True) + EPSILON)
-    h2 = (mid * scale * gain_ref[1:2, :]).astype(BF16)
+    h2 = (mid * scale * gain_two).astype(BF16)
     h2_own[...] = h2
-    first = PlaneGather(spot, h2_own, h2_all, spot.half * WIDE, s0, r0)
+    across = remote(h2_own, h2_all.at[spot.slot], zs.at[0], zr.at[0], (spot.mate, spot.w))
+    across.start()
+    first = gather_tokens(spot, h2_own, h2_all, own_base, s0, r0)
     first.begin()
-    there = h2_all.at[spot.slot]
-    mate_slot = (1 - spot.half) * WIDE + spot.w
-    arriving = h2_all.at[mate_slot]
-    across = remote(h2_own, there, zs.at[0], zr.at[0], (spot.mate, spot.w))
-    across.start()
-    keep_own = pltpu.make_async_copy(h2_own, there, local.at[1])
+    keep_own = pltpu.make_async_copy(h2_own, h2_all.at[spot.slot], local.at[5])
     keep_own.start()
 
-    logits = jnp.transpose(mm(h2, w_ref[:, WIDTH : WIDTH + 128]))[0:32]
+    logits = jnp.transpose(mm(h2, w_all[:, :, :, WIDTH : WIDTH + 128].reshape(WIDTH, 128)))[0:32]
     chosen = jnp.where(named > 0.5, logits, MASKED)
     rise = jnp.where(named > 0.5, jnp.exp(chosen - jnp.max(chosen, axis=0, keepdims=True)), 0.0)
     gate = rise / jnp.sum(rise, axis=0, keepdims=True)
@@ -882,17 +952,23 @@
         return carry
 
     lax.fori_loop(1, GROUP, start_table, 0)
+    lax.fori_loop(1, NARROW, start_column, 0)
     table_mine = pltpu.make_async_copy(
-        table_own.at[2 * spot.w + spot.half], table_all.at[spot.slot], local.at[2]
+        table_own.at[2 * spot.w + spot.half], table_all.at[spot.slot], local.at[6]
     )
     table_mine.start()
 
+    mate_dy_gather.middle()
+    mate_dy_gather.late()
     first.middle()
-    remote(arriving, arriving, zs.at[0], zr.at[0], (spot.mate, spot.w)).wait_recv()
-    second = PlaneGather(spot, arriving, h2_all, (1 - spot.half) * WIDE, s1, r1)
-    second.begin()
+    mate_dy_gather.last()
     first.late()
     first.last()
+    arriving = h2_all.at[mate_slot]
+    remote(arriving, arriving, zs.at[0], zr.at[0], (spot.mate, spot.w)).wait_recv()
+    second = gather_tokens(spot, arriving, h2_all, mate_base, s1, r1)
+    second.begin()
+    near.start()
     second.middle()
     second.late()
     second.last()
@@ -903,47 +979,65 @@
         return carry
 
     lax.fori_loop(1, GROUP, wait_table, 0)
+    lax.fori_loop(1, NARROW, wait_column, 0)
+    keep[3].wait()
+    dy_gather.finish()
+    mate_dy_gather.finish()
     first.finish()
     second.finish()
     across.wait_send()
+    keep[1].wait()
+    keep[2].wait()
     keep_own.wait()
     table_mine.wait()
-
-
-def project_call(o_heads, x_own, w_out, gain_rows, ids):
+    h1_copy.wait()
+    for copy in (far, near):
+        copy.wait_send()
+        copy.wait_recv()
+
+
+def forward_call(x_all, w_all, g_all, seg_all, cos_table, sin_table, freq, wo_block, ids, dy_pair, w_own, own, other):
     dma = pltpu.SemaphoreType.DMA
+    copies = PlaneGather.COPIES
     return pl.pallas_call(
-        project_kernel,
-        name="project",
+        forward_kernel,
+        name="forward",
         out_shape=(
+            jax.ShapeDtypeStruct((2, SEQ, WIDTH), BF16),
+            jax.ShapeDtypeStruct((2, SEQ, 256), BF16),
+            jax.ShapeDtypeStruct((2, SEQ, 128), F32),
+            jax.ShapeDtypeStruct((2, SEQ, 128), BF16),
+            jax.ShapeDtypeStruct((2, SEQ, 256), F32),
+            jax.ShapeDtypeStruct((2, SEQ, 128), F32),
+            jax.ShapeDtypeStruct((8, WIDTH), F32),
+            jax.ShapeDtypeStruct((TOKENS, WIDTH), F32),
+            jax.ShapeDtypeStruct((64, TOKENS), F32),
+            jax.ShapeDtypeStruct((NARROW, WIDE, 32, WIDTH + 128), BF16),
+            jax.ShapeDtypeStruct((GROUP, TOKENS, WIDTH), BF16),
             jax.ShapeDtypeStruct((GROUP, TOKENS, WIDTH), BF16),
             jax.ShapeDtypeStruct((GROUP, 8, TOKENS), F32),
-            jax.ShapeDtypeStruct((TOKENS, WIDTH), F32),
-            jax.ShapeDtypeStruct((64, TOKENS), F32),
+            jax.ShapeDtypeStruct((NARROW, 32, 2 * WIDTH), BF16),
+            jax.ShapeDtypeStruct((384, WIDTH), BF16),
+            jax.ShapeDtypeStruct((384, WIDTH), BF16),
         ),
-        in_specs=[IN_HBM] + [IN_VMEM] * 4,
-        out_specs=(IN_HBM, IN_HBM, IN_VMEM, IN_VMEM),
+        in_specs=[IN_VMEM] * 7 + [IN_HBM, IN_VMEM, IN_VMEM, IN_VMEM, IN_HBM, IN_HBM],
+        out_specs=(IN_HBM,) + (IN_VMEM,) * 9 + (IN_HBM,) * 6,
         scratch_shapes=[
+            pltpu.VMEM((2, SEQ, WIDTH), BF16),
             pltpu.VMEM((2, SPAN, WIDTH), BF16),
             pltpu.VMEM((TOKENS, WIDTH), BF16),
             pltpu.VMEM((GROUP, 8, TOKENS), F32),
             dma((WIDE,)),
             dma((WIDE,)),
-            dma((PlaneGather.COPIES,)),
-            dma((PlaneGather.COPIES,)),
-            dma((PlaneGather.COPIES,)),
-            dma((PlaneGather.COPIES,)),
-            dma((GROUP,)),
-            dma((GROUP,)),
-            dma((1,)),
-            dma((1,)),
-            dma((3,)),
-        ],
+        ]
+        + [dma((copies,))] * 10
+        + [dma((GROUP,)), dma((GROUP,)), dma((1,)), dma((1,)), dma((NARROW,)), dma((NARROW,)), dma((2,)), dma((2,)), dma((8,))],
         compiler_params=pltpu.CompilerParams(collective_id=2, has_side_effects=True, vmem_limit_bytes=VMEM_BYTES),
-    )(o_heads, x_own, w_out, gain_rows, ids)
-
-
-def load_quarters(pieces, target, depth, sems, base):
+        cost_estimate=duration(1),
+    )(x_all.reshape(WIDE, 2, SPAN, WIDTH), w_all, g_all, seg_all, cos_table, sin_table, freq, wo_block, ids, dy_pair, w_own, own, other)
+
+
+def load_quarters(pieces, target, first, depth, sems, base):
     n = lax.axis_index("narrow")
     half, pair = lax.rem(n, 2), lax.div(n, 2)
     mate = n + 1 - 2 * half
@@ -953,8 +1047,8 @@
     for number, (piece, quarter) in enumerate(zip(pieces, (n, mate, far, far_mate))):
         copies.append(
             pltpu.make_async_copy(
-                piece,
-                target.at[:, pl.ds(pl.multiple_of(quarter * depth, depth), depth), :],
+                piece.at[pl.ds(first, depth)],
+                target.at[pl.ds(pl.multiple_of(quarter * depth, depth), depth)],
                 sems.at[base + number],
             )
         )
@@ -966,165 +1060,218 @@
     return slot == table_ref[source, expert : expert + 1, :]
 
 
-def expert_kernel(
-    h2_ref, dy_ref, table_ref, gu0, gu1, gu2, gu3, d0, d1, d2, d3,
-    rows_ref, da_ref, y_ref, dgate_ref, down_grad_ref,
-    w_gu, w_down, down_sum, sems,
-):
+def expert_kernel(e, *refs):
+    if e == 0:
+        h2_ref, dy_ref, table_ref, w0, w1, w2, w3 = refs[:7]
+        refs = refs[7:]
+    else:
+        h2_ref, dy_ref, table_ref, w0, w1, w2, w3, y_before, dgate_before = refs[:9]
+        refs = refs[9:]
+    rows_ref, da_ref, y_ref, dgate_ref, down_grad_ref, w_gu, w_down, down_sum, sems = refs
     step = pl.program_id(0)
 
     @pl.when(step == 0)
     def _():
-        copies = load_quarters((gu0, gu1, gu2, gu3), w_gu, 256, sems, 0) + load_quarters(
-            (d0, d1, d2, d3), w_down, 128, sems, 4
-        )
+        pieces = (w0, w1, w2, w3)
+        copies = load_quarters(pieces, w_gu, 0, 256, sems, 0) + load_quarters(pieces, w_down, 256, 128, sems, 4)
         for copy in copies:
             copy.start()
         down_sum[...] = jnp.zeros_like(down_sum)
         for copy in copies:
             copy.wait()
 
-    picks = [[], []]
-    gated = [[], []]
-    dgate_ref[...] = jnp.zeros_like(dgate_ref)
-    for e in range(MINE):
-        masks = [pick(table_ref, s, e) for s in range(CHUNK)]
-        hots = [jnp.where(mask, 1.0, 0.0).astype(BF16) for mask in masks]
-        picks[e] = hots
-        rows = jnp.concatenate([mm(hots[s], h2_ref[s]) for s in range(CHUNK)], axis=0).astype(BF16)
-        grad_rows = jnp.concatenate([mm(hots[s], dy_ref[s, 0]) for s in range(CHUNK)], axis=0)
-        gates = jnp.concatenate(
-            [
-                jnp.sum(jnp.where(masks[s], table_ref[s, 2 + e : 3 + e, :], 0.0), axis=1, keepdims=True)
-                for s in range(CHUNK)
-            ],
-            axis=0,
-        )
-        rows_ref[0, e] = rows
-        g = mm(rows, w_gu[e, :, 0:FF])
-        u = mm(rows, w_gu[e, :, FF : 2 * FF])
-        sigmoid = 1.0 / (1.0 + jnp.exp(-g))
-        active = g * sigmoid
-        hidden = (active * u).astype(BF16)
-        y = mm(hidden, w_down[e]).astype(BF16).astype(F32)
-        slot_dgate = jnp.sum(y * grad_rows, axis=1, keepdims=True)
-        for s in range(CHUNK):
-            part = slot_dgate[s * SLOTS : (s + 1) * SLOTS]
-            dgate_ref[s, e : e + 1, :] = jnp.sum(jnp.where(masks[s], part, 0.0), axis=0, keepdims=True)
-        gated[e] = (y * gates).astype(BF16)
-        dy_pair = (grad_rows * gates).astype(BF16)
-        down_sum[e] += mm(hidden, dy_pair, TN)
-        dhid = mm(dy_pair, w_down[e], NT)
-        da_ref[0, e, :, 0:FF] = (dhid * u * (sigmoid * (1.0 + g * (1.0 - sigmoid)))).astype(BF16)
-        da_ref[0, e, :, FF : 2 * FF] = (dhid * active).astype(BF16)
+    masks = [pick(table_ref, s, e) for s in range(CHUNK)]
+    hots = [jnp.where(mask, 1.0, 0.0).astype(BF16) for mask in masks]
+    rows = jnp.concatenate([mm(hots[s], h2_ref[s]) for s in range(CHUNK)], axis=0).astype(BF16)
+    grad_rows = jnp.concatenate([mm(hots[s], dy_ref[s]) for s in range(CHUNK)], axis=0)
+    gates = jnp.concatenate(
+        [
+            jnp.sum(jnp.where(masks[s], table_ref[s, 2 + e : 3 + e, :], 0.0), axis=1, keepdims=True)
+            for s in range(CHUNK)
+        ],
+        axis=0,
+    )
+    rows_ref[0] = rows
+    g = mm(rows, w_gu[:, 0:FF])
+    u = mm(rows, w_gu[:, FF : 2 * FF])
+    sigmoid = 1.0 / (1.0 + jnp.exp(-g))
+    active = g * sigmoid
+    hidden = (active * u).astype(BF16)
+    y = mm(hidden, w_down[...]).astype(BF16).astype(F32)
+    slot_dgate = jnp.sum(y * grad_rows, axis=1, keepdims=True)
+    if e == 0:
+        dgate_ref[...] = jnp.zeros_like(dgate_ref)
+    else:
+        dgate_ref[...] = dgate_before[...]
     for s in range(CHUNK):
-        hot = jnp.concatenate([picks[e][s] for e in range(MINE)], axis=0)
-        back = jnp.concatenate([gated[e][s * SLOTS : (s + 1) * SLOTS] for e in range(MINE)], axis=0)
-        y_ref[s, 0] = mm(hot, back, TN).astype(BF16)
+        part = slot_dgate[s * SLOTS : (s + 1) * SLOTS]
+        dgate_ref[s, e : e + 1, :] = jnp.sum(jnp.where(masks[s], part, 0.0), axis=0, keepdims=True)
+    gated = (y * gates).astype(BF16)
+    dy_pair = (grad_rows * gates).astype(BF16)
+    down_sum[...] += mm(hidden, dy_pair, TN)
+    dhid = mm(dy_pair, w_down[...], NT)
+    da_ref[0, :, 0:FF] = (dhid * u * (sigmoid * (1.0 + g * (1.0 - sigmoid)))).astype(BF16)
+    da_ref[0, :, FF : 2 * FF] = (dhid * active).astype(BF16)
+    for s in range(CHUNK):
+        back = mm(hots[s], gated[s * SLOTS : (s + 1) * SLOTS], TN)
+        if e == 1:
+            back = back + y_before[s].astype(F32)
+        y_ref[s] = back.astype(BF16)
 
     @pl.when(step == pl.num_programs(0) - 1)
     def _():
         down_grad_ref[...] = down_sum[...].astype(BF16)
 
 
-def expert_call(h2_all, dy_all, table_all, gate_up, down):
-    steps = GROUP // CHUNK
-    block = pl.BlockSpec((CHUNK, TOKENS, WIDTH), lambda c: (c, 0, 0))
-    small = pl.BlockSpec((CHUNK, 8, TOKENS), lambda c: (c, 0, 0))
-    slots = pl.BlockSpec((1, MINE, CHUNK * SLOTS, WIDTH), lambda c: (c, 0, 0, 0))
-    steps_half = WIDE // CHUNK
-    to_wide = pl.BlockSpec(
-        (CHUNK, 1, TOKENS, WIDTH), lambda c: (lax.rem(c, steps_half), lax.div(c, steps_half), 0, 0)
-    )
-    flops = 2 * GROUP * SLOTS * MINE * WIDTH * FF * 7
+STEPS = GROUP // CHUNK
+
+
+def expert_specs():
+    block = pl.BlockSpec((CHUNK, TOKENS, WIDTH), lambda c, *_: (c, 0, 0))
+    small = pl.BlockSpec((CHUNK, 8, TOKENS), lambda c, *_: (c, 0, 0))
+    slots = pl.BlockSpec((1, CHUNK * SLOTS, WIDTH), lambda c, *_: (c, 0, 0))
+    return block, small, slots
+
+
+def expert_call(e, h2_all, dy_all, table_all, pieces, before):
+    block, small, slots = expert_specs()
     return pl.pallas_call(
-        expert_kernel,
-        name="experts",
-        grid=(steps,),
+        functools.partial(expert_kernel, e),
+        name=f"expert_{e}",
+        grid=(STEPS,),
         out_shape=(
-            jax.ShapeDtypeStruct((steps, MINE, CHUNK * SLOTS, WIDTH), BF16),
-            jax.ShapeDtypeStruct((steps, MINE, CHUNK * SLOTS, 2 * FF), BF16),
-            jax.ShapeDtypeStruct((WIDE, 2, TOKENS, WIDTH), BF16),
+            jax.ShapeDtypeStruct((STEPS, CHUNK * SLOTS, WIDTH), BF16),
+            jax.ShapeDtypeStruct((STEPS, CHUNK * SLOTS, 2 * FF), BF16),
+            jax.ShapeDtypeStruct((GROUP, TOKENS, WIDTH), BF16),
             jax.ShapeDtypeStruct((GROUP, 8, TOKENS), F32),
-            jax.ShapeDtypeStruct((MINE, FF, WIDTH), BF16),
+            jax.ShapeDtypeStruct((FF, WIDTH), BF16),
         ),
-        in_specs=[block, to_wide, small] + [IN_HBM] * 8,
-        out_specs=(slots, slots, to_wide, small, pl.BlockSpec((MINE, FF, WIDTH), lambda c: (0, 0, 0))),
+        in_specs=[block, block, small] + [IN_HBM] * 4 + ([block, small] if e else []),
+        out_specs=(slots, slots, block, small, pl.BlockSpec((FF, WIDTH), lambda c: (0, 0))),
         scratch_shapes=[
-            pltpu.VMEM((MINE, WIDTH, 2 * FF), BF16),
-            pltpu.VMEM((MINE, FF, WIDTH), BF16),
-            pltpu.VMEM((MINE, FF, WIDTH), F32),
+            pltpu.VMEM((WIDTH, 2 * FF), BF16),
+            pltpu.VMEM((FF, WIDTH), BF16),
+            pltpu.VMEM((FF, WIDTH), F32),
             pltpu.SemaphoreType.DMA((8,)),
         ],
         compiler_params=pltpu.CompilerParams(vmem_limit_bytes=VMEM_BYTES),
-        cost_estimate=pl.CostEstimate(flops=flops, bytes_accessed=40 << 20, transcendentals=1 << 20),
-    )(h2_all, dy_all, table_all, *gate_up, *down)
-
-
-def gate_up_grad_kernel(rows_ref, da_ref, out_ref):
-    rows = rows_ref[:, 0].reshape(GROUP * SLOTS, WIDTH // 2)
-    da = da_ref[:, 0].reshape(GROUP * SLOTS, 2 * FF)
-    out_ref[0] = mm(rows, da, TN).astype(BF16)
-
-
-def gate_up_grad_call(rows, da):
-    steps = GROUP // CHUNK
+        cost_estimate=duration(1),
+    )(h2_all, dy_all, table_all, *pieces, *before)
+
+
+def weight_grad_kernel(n_ref, rows_ref, da_ref, down_ref, own, mate, far, far_mate):
+    step = pl.program_id(0)
+    rows = rows_ref[...].reshape(GROUP * SLOTS, WIDTH // NARROW)
+    da = da_ref[...].reshape(GROUP * SLOTS, 2 * FF)
+    grad = mm(rows, da, TN).astype(BF16)
+    for number, out in enumerate((own, mate, far, far_mate)):
+
+        @pl.when(step == number)
+        def _():
+            out[0:256, :] = grad
+            out[256:384, :] = down_ref[...]
+
+
+def weight_grad_call(e, n_row, rows, da, down_grad):
+    def quarter(step, n_ref):
+        n = n_ref[0]
+        mate = n + 1 - 2 * lax.rem(n, 2)
+        far = 2 - 4 * lax.div(n, 2)
+        return jnp.where(lax.rem(step, 2) == 1, mate, n) + jnp.where(step >= 2, far, 0)
+
+    whole = pl.BlockSpec((384, WIDTH), lambda j, n_ref: (0, 0))
     return pl.pallas_call(
-        gate_up_grad_kernel,
-        name="gate_up_grad",
-        grid=(MINE, 2),
-        out_shape=jax.ShapeDtypeStruct((MINE, WIDTH, 2 * FF), BF16),
-        in_specs=[
-            pl.BlockSpec((steps, 1, CHUNK * SLOTS, WIDTH // 2), lambda e, d: (0, e, 0, d)),
-            pl.BlockSpec((steps, 1, CHUNK * SLOTS, 2 * FF), lambda e, d: (0, e, 0, 0)),
-        ],
-        out_specs=pl.BlockSpec((1, WIDTH // 2, 2 * FF), lambda e, d: (e, d, 0)),
+        weight_grad_kernel,
+        name=f"weight_grad_{e}",
+        grid_spec=pltpu.PrefetchScalarGridSpec(
+            num_scalar_prefetch=1,
+            grid=(NARROW,),
+            in_specs=[
+                pl.BlockSpec((STEPS, CHUNK * SLOTS, 256), lambda j, n_ref: (0, 0, quarter(j, n_ref))),
+                pl.BlockSpec((STEPS, CHUNK * SLOTS, 2 * FF), lambda j, n_ref: (0, 0, 0)),
+                pl.BlockSpec((128, WIDTH), lambda j, n_ref: (quarter(j, n_ref), 0)),
+            ],
+            out_specs=(whole,) * 4,
+        ),
+        out_shape=(jax.ShapeDtypeStruct((384, WIDTH), BF16),) * 4,
         compiler_params=pltpu.CompilerParams(vmem_limit_bytes=VMEM_BYTES),
-        cost_estimate=pl.CostEstimate(
-            flops=2 * GROUP * SLOTS * MINE * WIDTH * 2 * FF, bytes_accessed=14 << 20, transcendentals=0
-        ),
-    )(rows, da)
-
-
-def rows_grad_kernel(da_ref, table_ref, gu0, gu1, gu2, gu3, out_ref, w_gu, sems):
+        cost_estimate=duration(1),
+    )(n_row, rows, da, down_grad)
+
+
+def rows_grad_kernel(e, *refs):
+    if e == 0:
+        da_ref, table_ref, w0, w1, w2, w3, out_ref, w_gu, sems = refs
+    else:
+        da_ref, table_ref, w0, w1, w2, w3, before, out_ref, w_gu, sems = refs
     step = pl.program_id(0)
 
     @pl.when(step == 0)
     def _():
-        copies = load_quarters((gu0, gu1, gu2, gu3), w_gu, 256, sems, 0)
+        copies = load_quarters((w0, w1, w2, w3), w_gu, 0, 256, sems, 0)
         for copy in copies:
             copy.start()
         for copy in copies:
             copy.wait()
 
-    grads = [mm(da_ref[0, e], w_gu[e], NT).astype(BF16) for e in range(MINE)]
+    grads = mm(da_ref[0], w_gu[...], NT).astype(BF16)
     for s in range(CHUNK):
-        hot = jnp.concatenate(
-            [jnp.where(pick(table_ref, s, e), 1.0, 0.0).astype(BF16) for e in range(MINE)], axis=0
-        )
-        back = jnp.concatenate([grads[e][s * SLOTS : (s + 1) * SLOTS] for e in range(MINE)], axis=0)
-        out_ref[s] = mm(hot, back, TN).astype(BF16)
-
-
-def rows_grad_call(da, table_all, gate_up):
-    steps = GROUP // CHUNK
+        hot = jnp.where(pick(table_ref, s, e), 1.0, 0.0).astype(BF16)
+        back = mm(hot, grads[s * SLOTS : (s + 1) * SLOTS], TN)
+        if e == 1:
+            back = back + before[s].astype(F32)
+        out_ref[s] = back.astype(BF16)
+
+
+def rows_grad_call(e, da, table_all, pieces, before):
+    block, small, slots = expert_specs()
     return pl.pallas_call(
-        rows_grad_kernel,
-        name="rows_grad",
-        grid=(steps,),
+        functools.partial(rows_grad_kernel, e),
+        name=f"rows_grad_{e}",
+        grid=(STEPS,),
         out_shape=jax.ShapeDtypeStruct((GROUP, TOKENS, WIDTH), BF16),
-        in_specs=[
-            pl.BlockSpec((1, MINE, CHUNK * SLOTS, 2 * FF), lambda c: (c, 0, 0, 0)),
-            pl.BlockSpec((CHUNK, 8, TOKENS), lambda c: (c, 0, 0)),
-        ]
-        + [IN_HBM] * 4,
-        out_specs=pl.BlockSpec((CHUNK, TOKENS, WIDTH), lambda c: (c, 0, 0)),
-        scratch_shapes=[pltpu.VMEM((MINE, WIDTH, 2 * FF), BF16), pltpu.SemaphoreType.DMA((4,))],
+        in_specs=[slots, small] + [IN_HBM] * 4 + ([block] if e else []),
+        out_specs=block,
+        scratch_shapes=[pltpu.VMEM((WIDTH, 2 * FF), BF16), pltpu.SemaphoreType.DMA((4,))],
         compiler_params=pltpu.CompilerParams(vmem_limit_bytes=VMEM_BYTES),
-        cost_estimate=pl.CostEstimate(
-            flops=2 * GROUP * SLOTS * MINE * WIDTH * 2 * FF, bytes_accessed=20 << 20, transcendentals=0
+        cost_estimate=duration(1),
+    )(da, table_all, *pieces, *before)
+
+
+def owner_sum_kernel(half_ref, own, mate, far, far_mate, *refs):
+    gate_up_ref, down_ref = refs[-2:]
+    first, second = (own, far), (mate, far_mate)
+    for step, (left, right) in enumerate((first, second)):
+
+        @pl.when(pl.program_id(0) == step)
+        def _():
+            total = left[...].astype(F32) + right[...].astype(F32)
+            gate_up_ref[0] = total[0:256]
+            down_ref[0] = total[256:384]
+
+
+def owner_sum_call(e, half_row, parts, before, after):
+    def place(step, half_ref):
+        return (2 * lax.rem(half_ref[0] + step, 2) + e, 0, 0)
+
+    whole = pl.BlockSpec((384, WIDTH), lambda j, half_ref: (0, 0))
+    return pl.pallas_call(
+        owner_sum_kernel,
+        name=f"owner_sum_{e}",
+        grid_spec=pltpu.PrefetchScalarGridSpec(
+            num_scalar_prefetch=1,
+            grid=(2,),
+            in_specs=[whole] * 4 + [IN_HBM] * (len(before) + 1),
+            out_specs=(pl.BlockSpec((1, 256, WIDTH), place), pl.BlockSpec((1, 128, WIDTH), place)),
         ),
-    )(da, table_all, *gate_up)
+        out_shape=(
+            jax.ShapeDtypeStruct((4, 256, WIDTH), F32),
+            jax.ShapeDtypeStruct((4, 128, WIDTH), F32),
+        ),
+        input_output_aliases={6: 0, 7: 1} if before else {},
+        compiler_params=pltpu.CompilerParams(vmem_limit_bytes=VMEM_BYTES),
+        cost_estimate=duration(1),
+    )(half_row, *parts, after, *before)
 
 
 def widen(ref_value):
@@ -1134,9 +1281,9 @@
 class PlaneReduce:
     COPIES = 10
 
-    def __init__(self, spot, part, base, acc, from_core, from_one, from_two, send, recv, local):
-        self.spot, self.part, self.base = spot, part, base
-        self.acc, self.from_core, self.from_one, self.from_two = acc, from_core, from_one, from_two
+    def __init__(self, spot, part, buffers, send, recv, local):
+        self.spot, self.part = spot, part
+        self.acc, self.from_core, self.from_one, self.from_two = buffers
         self.send, self.recv, self.local = send, recv, local
         self.started = []
         s = spot
@@ -1157,8 +1304,8 @@
         s = self.spot
         self.loads = []
         for q in range(4):
-            self.put(self.part.at[self.base + 2 * q + 1 - s.core], self.from_core.at[q], q, s.sib)
-            copy = pltpu.make_async_copy(self.part.at[self.base + 2 * q + s.core], self.acc.at[q], self.local.at[q])
+            self.put(self.part(2 * q + 1 - s.core), self.from_core.at[q], q, s.sib)
+            copy = pltpu.make_async_copy(self.part(2 * q + s.core), self.acc.at[q], self.local.at[q])
             copy.start()
             self.loads.append(copy)
 
@@ -1196,6 +1343,47 @@
     def finish(self):
         for copy in self.started:
             copy.wait_send()
+
+
+def halves(ref, which):
+    return ref.at[pl.ds(which * SPAN, SPAN)]
+
+
+class GroupReduce:
+    def __init__(self, spot, theirs, ours, scratch):
+        acc, from_core, from_one, from_two, total, mate_send, mate_recv, send, recv, local, zs, zr = scratch
+        self.total_ref, self.mate_send, self.mate_recv = total, mate_send, mate_recv
+        parts = []
+        for which, part in enumerate((theirs, ours)):
+            buffers = (acc.at[which], from_core.at[which], from_one.at[which], from_two.at[which])
+            parts.append(PlaneReduce(spot, part, buffers, send.at[which], recv.at[which], local.at[which]))
+        self.theirs, self.ours = parts
+        self.across = remote(mate_send, mate_recv, zs.at[0], zr.at[0], (spot.mate, spot.w))
+
+    def begin(self):
+        self.theirs.begin()
+        self.ours.begin()
+
+    def across_core(self):
+        self.theirs.across_core()
+        self.ours.across_core()
+
+    def across_one(self):
+        self.theirs.across_one()
+        self.ours.across_one()
+
+    def to_mate(self):
+        self.theirs.total(self.total_ref)
+        self.mate_send[...] = self.total_ref[...].astype(BF16)
+        self.across.start()
+
+    def finish(self):
+        self.ours.total(self.total_ref)
+        self.across.wait_recv()
+        self.total_ref[...] += widen(self.mate_recv[...])
+        self.theirs.finish()
+        self.ours.finish()
+        self.across.wait_send()
 
 
 def reduce_scratch():
@@ -1216,42 +1404,100 @@
     ]
 
 
-def group_reduce(spot, part, scratch):
-    acc, from_core, from_one, from_two, total, mate_send, mate_recv, send, recv, local, zs, zr = scratch
-    sums = []
-    for which, base in ((0, (1 - spot.half) * WIDE), (1, spot.half * WIDE)):
-        sums.append(
-            PlaneReduce(
-                spot, part, base, acc.at[which], from_core.at[which], from_one.at[which], from_two.at[which],
-                send.at[which], recv.at[which], local.at[which],
-            )
-        )
-    theirs, ours = sums
-    theirs.begin()
-    ours.begin()
-    theirs.across_core()
-    ours.across_core()
-    theirs.across_one()
-    theirs.total(total)
-    mate_send[...] = total[...].astype(BF16)
-    across = remote(mate_send, mate_recv, zs.at[0], zr.at[0], (spot.mate, spot.w))
-    across.start()
-    ours.across_one()
-    ours.total(total)
-    across.wait_recv()
-    total[...] += widen(mate_recv[...])
-    theirs.finish()
-    ours.finish()
-    across.wait_send()
-
-
-def collect_kernel(
-    part_ref, dgate_ref, h2_ref, mid_ref, gate_ref, w_ref, gain_ref, dy_ref,
-    dattn_all, dmid_ref, small_ref,
-    dgate_all, h2_own, dattn_own, ts, tr, s0, r0, local, *scratch,
-):
+REDUCE_REFS = 12
+
+
+class AttentionBack:
+    def __init__(self, dattn_all, w_rows, qkv_ref, lse_ref, o_ref, angle_ref, start_ref, dqkv_ref, dkv_ref, dq_ref, osum):
+        self.dattn_all, self.w_rows, self.qkv, self.lse, self.o = dattn_all, w_rows, qkv_ref, lse_ref, o_ref
+        self.angle, self.start = angle_ref, start_ref
+        self.dqkv, self.dkv, self.dq, self.osum = dqkv_ref, dkv_ref, dq_ref, osum
+        self.first_half = lane_half()
+        self.is_key = lax.broadcasted_iota(jnp.int32, (1, 128), 1) < 64
+        dkv_ref[...] = jnp.zeros_like(dkv_ref)
+        osum[...] = jnp.zeros_like(osum)
+
+    def stack(self, both):
+        return jnp.concatenate([both[:, 0:64], both[:, 64:128]], axis=0)
+
+    def chunk(self, row, q):
+        first = pl.multiple_of(q * 256, 256)
+        tokens = pl.ds(first, 256)
+        dattn = self.dattn_all[pl.ds(2 * q, 2), pl.ds(row * SPAN, SPAN), :].reshape(256, WIDTH)
+        outs = self.o[row, tokens, :]
+        do = mm(dattn, self.w_rows[...], NT).astype(BF16)
+        self.osum[...] += mm(outs, dattn, TN)
+        inner = do.astype(F32) * outs.astype(F32)
+        delta = jnp.concatenate(
+            [
+                jnp.sum(jnp.where(self.is_key, inner, 0.0), axis=1, keepdims=True),
+                jnp.sum(jnp.where(self.is_key, 0.0, inner), axis=1, keepdims=True),
+            ],
+            axis=0,
+        )
+        query = self.stack(self.qkv[row, tokens, 0:128])
+        do = self.stack(do)
+        log_total = jnp.concatenate([self.lse[row, tokens, 0:1], self.lse[row, tokens, 64:65]], axis=0)
+        start = self.start[row, tokens, 0:1]
+        start = jnp.concatenate([start, start], axis=0)
+        place = lax.broadcasted_iota(jnp.int32, (256, 1), 0)
+        place_query = (jnp.concatenate([place, place], axis=0) + q * 256).astype(F32)
+        self.dq[...] = jnp.zeros_like(self.dq)
+
+        def key_block(block, carry):
+            keys_at = pl.ds(pl.multiple_of(block * 256, 256), 256)
+            keys = self.qkv[row, keys_at, 128:192]
+            values = self.qkv[row, keys_at, 192:256]
+            place_key = (lax.broadcasted_iota(jnp.int32, (1, 256), 1) + block * 256).astype(F32)
+            allowed = (place_key <= place_query) & (place_key >= start)
+            scores = jnp.where(allowed, mm(query, keys, NT) * (HEAD_DIM**-0.5), MASKED)
+            weights = jnp.exp(scores - log_total)
+            dp = mm(do, values, NT)
+            ds = (weights * (dp - delta)).astype(BF16)
+            self.dq[...] += mm(ds, keys)
+            dk = mm(ds, query, TN) * (HEAD_DIM**-0.5)
+            dv = mm(weights.astype(BF16), do, TN)
+            self.dkv[row, keys_at, :] += jnp.concatenate([dk, dv], axis=1)
+            return carry
+
+        lax.fori_loop(0, q + 1, key_block, 0)
+        dq = jnp.concatenate([self.dq[0:256], self.dq[256:512]], axis=1) * (HEAD_DIM**-0.5)
+        cosine = self.angle[row, tokens, 0:128]
+        sine = self.angle[row, tokens, 128:256]
+        self.dqkv[row, tokens, 0:128] = (dq * cosine + turn_back(dq * sine, self.first_half)).astype(BF16)
+
+    def keys(self, row):
+        cosine = self.angle[row, :, 0:128]
+        sine = self.angle[row, :, 128:256]
+        dkv = self.dkv[row]
+        turned = dkv * cosine + turn_back(dkv * sine, self.first_half)
+        self.dqkv[row, :, 128:256] = jnp.where(self.is_key, turned, dkv).astype(BF16)
+
+
+def backward_kernel(*refs):
+    (
+        part_ref, y_ref, dgate_ref, h2_ref, w_out_ref, w_full_ref, h1_ref, qkv_ref, lse_ref, o_ref,
+        angle_ref, start_ref, x_ref, mid_ref, gate_ref, gain_ref, dy_ref,
+    ) = refs[:17]
+    block_out, in_grad, q_grad, k_grad, v_grad, o_grad, sums, gain_sum = refs[17:25]
+    (
+        dgate_all, h2_own, dattn_all, dmid_ref, small_ref, small_all, small_sum, w_router, w_rows, w_full,
+        h1, qkv, lse, outs, angle, start, dqkv_ref, dkv_ref, dq_ref, osum, og_ref, wg_ref,
+        dq_full, w_recv, o_recv, s_recv, gain_own, g_recv,
+        ts, tr, s0, r0, bs, br, qs, qr, ws, wr, os, orv, ss, sr, gs, gr, local,
+    ) = refs[25:70]
+    h2_sum_refs = refs[70 : 70 + REDUCE_REFS]
+    y_sum_refs = refs[70 + REDUCE_REFS :]
+
     spot = Spot()
-    spot.greet(GROUP)
+    everyone = NARROW * WIDE
+    spot.greet(everyone)
+    base, mate_base = spot.half * WIDE, (1 - spot.half) * WIDE
+    h2_sum = GroupReduce(
+        spot, lambda who: part_ref.at[mate_base + who], lambda who: part_ref.at[base + who], h2_sum_refs
+    )
+    y_sum = GroupReduce(spot, lambda who: y_ref.at[mate_base + who], lambda who: y_ref.at[base + who], y_sum_refs)
+    h2_sum.begin()
 
     def tables(step, arriving):
         other = lax.rem(spot.slot + step, GROUP)
@@ -1267,11 +1513,31 @@
         return carry
 
     lax.fori_loop(1, GROUP, start_table, 0)
-    mine = pltpu.make_async_copy(dgate_ref.at[spot.slot], dgate_all.at[spot.slot], local.at[0])
-    mine.start()
-    load = pltpu.make_async_copy(h2_ref.at[spot.slot], h2_own, local.at[1])
-    load.start()
-    group_reduce(spot, part_ref, scratch)
+    rows = pl.ds(pl.multiple_of(spot.w * 128, 128), 128)
+    loads = [
+        (dgate_ref.at[spot.slot], dgate_all.at[spot.slot]),
+        (h2_ref.at[spot.slot], h2_own),
+        (w_out_ref.at[:, pl.ds(WIDTH, 128)], w_router),
+        (w_out_ref.at[rows, pl.ds(0, WIDTH)], w_rows),
+        (qkv_ref, qkv),
+        (lse_ref, lse),
+        (o_ref, outs),
+        (angle_ref, angle),
+        (start_ref, start),
+        (h1_ref, h1),
+    ]
+    loads = [pltpu.make_async_copy(src, dst, local.at[i]) for i, (src, dst) in enumerate(loads)]
+    for copy in loads:
+        copy.start()
+    w_loads = [pltpu.make_async_copy(w_full_ref.at[who], w_full.at[:, who], local.at[10 + who]) for who in range(WIDE)]
+    for copy in w_loads:
+        copy.start()
+    y_sum.begin()
+    h2_sum.across_core()
+    h2_sum.across_one()
+    h2_sum.to_mate()
+    y_sum.across_core()
+    h2_sum.finish()
 
     def wait_table(step, carry):
         tables(step, False).wait_send()
@@ -1279,176 +1545,81 @@
         return carry
 
     lax.fori_loop(1, GROUP, wait_table, 0)
-    mine.wait()
-    load.wait()
-
-    total = scratch[4]
+    for copy in loads[:4]:
+        copy.wait()
+
     gate = gate_ref[0:32, :]
     dgate = jnp.concatenate([dgate_all[(o % 2) * WIDE + o // 2, 0:2, :] for o in range(GROUP)], axis=0)
     dsel = gate * (dgate - jnp.sum(gate * dgate, axis=0, keepdims=True))
     dlogits = jnp.concatenate([dsel, jnp.zeros((96, TOKENS), F32)], axis=0)
-    dh2 = total[...] + mm(jnp.transpose(dlogits).astype(BF16), w_ref[:, WIDTH : WIDTH + 128], NT)
-    small_ref[0:32, :] = mm(dsel.astype(BF16), h2_own[...])
+    dh2 = h2_sum.total_ref[...] + mm(jnp.transpose(dlogits).astype(BF16), w_router[...], NT)
     mid = mid_ref[...]
     scale = lax.rsqrt(jnp.mean(mid * mid, axis=1, keepdims=True) + EPSILON)
+    weighted = dh2 * gain_ref[1:2, :]
+    inner = jnp.mean(weighted * mid, axis=1, keepdims=True)
+    dmid = dy_ref[...].astype(F32) + weighted * scale - mid * (scale * scale * scale) * inner
+    dmid_ref[...] = dmid
+    dattn_all[spot.w] = dmid.astype(BF16)
+    mine = dattn_all.at[spot.w]
+    gather = PlaneGather(
+        spot,
+        lambda half: mine if half is None else halves(mine, half),
+        lambda who, half: dattn_all.at[who] if half is None else halves(dattn_all.at[who], half),
+        s0, r0,
+    )
+    gather.begin()
+    small_ref[0:32, :] = mm(dsel.astype(BF16), h2_own[...])
     small_ref[32:33, :] = jnp.sum(dh2 * mid * scale, axis=0, keepdims=True)
     lane = lax.broadcasted_iota(jnp.int32, (32, WIDTH), 1)
     column = lax.broadcasted_iota(jnp.int32, (32, WIDTH), 0)
     count = jnp.sum(gate_ref[32:64, :], axis=1, keepdims=True)
     small_ref[33:34, :] = jnp.sum(jnp.where(lax.rem(lane, 128) == column, count, 0.0), axis=0, keepdims=True)
     small_ref[34:40, :] = jnp.zeros((6, WIDTH), F32)
-    weighted = dh2 * gain_ref[1:2, :]
-    inner = jnp.mean(weighted * mid, axis=1, keepdims=True)
-    dmid = dy_ref[...].astype(F32) + weighted * scale - mid * (scale * scale * scale) * inner
-    dmid_ref[...] = dmid
-    dattn_own[...] = dmid.astype(BF16)
-    gather = PlaneGather(spot, dattn_own, dattn_all, 0, s0, r0)
-    gather.begin()
-    keep = pltpu.make_async_copy(dattn_own, dattn_all.at[spot.w], local.at[0])
-    keep.start()
+
+    def lanes_to(step, arriving):
+        other = lax.rem(spot.w + step, WIDE)
+        place = other if arriving else spot.w
+        return remote(
+            small_ref.at[:, pl.ds(pl.multiple_of(other * 128, 128), 128)], small_all.at[place],
+            bs.at[other], br.at[place], spot.wide(other),
+        )
+
+    def start_lanes(step, carry):
+        lanes_to(step, False).start()
+        return carry
+
+    lax.fori_loop(1, WIDE, start_lanes, 0)
+    small_all[spot.w] = small_ref[:, pl.ds(pl.multiple_of(spot.w * 128, 128), 128)]
+
+    for copy in loads[4:9]:
+        copy.wait()
+    back = AttentionBack(dattn_all, w_rows, qkv, lse, outs, angle, start, dqkv_ref, dkv_ref, dq_ref, osum)
+    order = h2_sum.ours
+    gather.got(spot.sib, None, 4)
+    back.chunk(0, order.q_own)
     gather.middle()
+    back.chunk(1, order.q_own)
     gather.late()
     gather.last()
-    gather.finish()
-    keep.wait()
-
-
-def collect_call(part, dgate, h2_all, mid, gate, w_out, gain_rows, dy_own):
-    dma = pltpu.SemaphoreType.DMA
-    return pl.pallas_call(
-        collect_kernel,
-        name="collect",
-        out_shape=(
-            jax.ShapeDtypeStruct((WIDE, TOKENS, WIDTH), BF16),
-            jax.ShapeDtypeStruct((TOKENS, WIDTH), F32),
-            jax.ShapeDtypeStruct((40, WIDTH), F32),
-        ),
-        in_specs=[IN_HBM] * 3 + [IN_VMEM] * 5,
-        out_specs=(IN_HBM, IN_VMEM, IN_VMEM),
-        scratch_shapes=[
-            pltpu.VMEM((GROUP, 8, TOKENS), F32),
-            pltpu.VMEM((TOKENS, WIDTH), BF16),
-            pltpu.VMEM((TOKENS, WIDTH), BF16),
-            dma((GROUP,)),
-            dma((GROUP,)),
-            dma((PlaneGather.COPIES,)),
-            dma((PlaneGather.COPIES,)),
-            dma((2,)),
-        ]
-        + reduce_scratch(),
-        compiler_params=pltpu.CompilerParams(collective_id=3, has_side_effects=True, vmem_limit_bytes=VMEM_BYTES),
-    )(part, dgate, h2_all, mid, gate, w_out, gain_rows, dy_own)
-
-
-def attend_back_kernel(
-    dattn_ref, w_ref, h1_ref, qkv_ref, lse_ref, o_ref, angle_ref, start_ref,
-    dqkv_ref, wgrad_ref, ograd_ref,
-    do_ref, dkv_ref, wsum, osum,
-):
-    row = pl.program_id(0)
-    first_half = lane_half()
-    is_key = lax.broadcasted_iota(jnp.int32, (1, 128), 1) < 64
-
-    @pl.when(row == 0)
-    def _():
-        wsum[...] = jnp.zeros_like(wsum)
-        osum[...] = jnp.zeros_like(osum)
-
-    dattn = dattn_ref[:, 0].reshape(SEQ, WIDTH)
-    do_ref[...] = mm(dattn, w_ref[...], NT).astype(BF16)
-    osum[...] += mm(o_ref[0], dattn, TN)
-    dkv_ref[...] = jnp.zeros_like(dkv_ref)
-    for i in range(4):
-        tokens = pl.ds(i * 256, 256)
-        length = 256 * (i + 1)
-        keys = qkv_ref[0, 0:length, 128:192]
-        values = qkv_ref[0, 0:length, 192:256]
-        place_key = lax.broadcasted_iota(jnp.int32, (256, length), 1).astype(F32)
-        place_query = (lax.broadcasted_iota(jnp.int32, (256, length), 0) + 256 * i).astype(F32)
-        allowed = (place_key <= place_query) & (place_key >= start_ref[0, tokens, 0:1])
-        query_grads = []
-        dk = jnp.zeros((length, HEAD_DIM), F32)
-        dv = jnp.zeros((length, HEAD_DIM), F32)
-        for head in range(2):
-            part = slice(64 * head, 64 * head + 64)
-            query = qkv_ref[0, tokens, part]
-            do = do_ref[tokens, part]
-            log_total = lse_ref[0, tokens, 64 * head : 64 * head + 1]
-            scores = jnp.where(allowed, mm(query, keys, NT) * (HEAD_DIM**-0.5), MASKED)
-            weights = jnp.exp(scores - log_total)
-            dp = mm(do, values, NT)
-            delta = jnp.sum(weights * dp, axis=1, keepdims=True)
-            ds = (weights * (dp - delta)).astype(BF16)
-            query_grads.append(mm(ds, keys) * (HEAD_DIM**-0.5))
-            dk = dk + mm(ds, query, TN)
-            dv = dv + mm(weights.astype(BF16), do, TN)
-        dkv_ref[0:length, :] += jnp.concatenate([dk * (HEAD_DIM**-0.5), dv], axis=1)
-        dq = jnp.concatenate(query_grads, axis=1)
-        cosine = angle_ref[0, tokens, 0:128]
-        sine = angle_ref[0, tokens, 128:256]
-        dqkv_ref[0, tokens, 0:128] = (dq * cosine + turn_back(dq * sine, first_half)).astype(BF16)
-    for i in range(4):
-        tokens = pl.ds(i * 256, 256)
-        cosine = angle_ref[0, tokens, 0:128]
-        sine = angle_ref[0, tokens, 128:256]
-        dkv = dkv_ref[tokens, :]
-        turned = dkv * cosine + turn_back(dkv * sine, first_half)
-        dqkv_ref[0, tokens, 128:256] = jnp.where(is_key, turned, dkv).astype(BF16)
-    wsum[...] += mm(h1_ref[0], dqkv_ref[0], TN)
-
-    @pl.when(row == 1)
-    def _():
-        wgrad_ref[...] = wsum[...].astype(BF16)
-        ograd_ref[...] = osum[...].astype(BF16)
-
-
-def attend_back_call(dattn_all, w_rows, h1, qkv, lse, o_heads, angle, start):
-    def by_row(lanes):
-        return pl.BlockSpec((1, SEQ, lanes), lambda r: (r, 0, 0))
-
-    def whole(shape):
-        return pl.BlockSpec(shape, lambda r: (0,) * len(shape))
-
-    return pl.pallas_call(
-        attend_back_kernel,
-        name="attend_back",
-        grid=(2,),
-        out_shape=(
-            jax.ShapeDtypeStruct((2, SEQ, 256), BF16),
-            jax.ShapeDtypeStruct((WIDTH, 256), BF16),
-            jax.ShapeDtypeStruct((128, WIDTH), BF16),
-        ),
-        in_specs=[
-            pl.BlockSpec((WIDE, 1, SPAN, WIDTH), lambda r: (0, r, 0, 0)),
-            whole((128, WIDTH)),
-            by_row(WIDTH),
-            by_row(256),
-            by_row(128),
-            by_row(128),
-            by_row(256),
-            by_row(128),
-        ],
-        out_specs=(by_row(256), whole((WIDTH, 256)), whole((128, WIDTH))),
-        scratch_shapes=[
-            pltpu.VMEM((SEQ, 128), BF16),
-            pltpu.VMEM((SEQ, 128), F32),
-            pltpu.VMEM((WIDTH, 256), F32),
-            pltpu.VMEM((128, WIDTH), F32),
-        ],
-        compiler_params=pltpu.CompilerParams(vmem_limit_bytes=VMEM_BYTES),
-        cost_estimate=pl.CostEstimate(flops=8 << 30, bytes_accessed=16 << 20, transcendentals=3 << 20),
-    )(dattn_all.reshape(WIDE, 2, SPAN, WIDTH), w_rows, h1, qkv, lse, o_heads, angle, start)
-
-
-def finish_kernel(
-    dqkv_ref, wg_ref, og_ref, small_ref, w_ref, x_ref, dmid_ref, gain_ref,
-    in_grad, q_grad, k_grad, v_grad, o_grad, sums, gain_sum,
-    dq_full, w_recv, o_recv, s_recv, gain_own, g_recv,
-    qs, qr, ws, wr, os, orv, ss, sr, gs, gr, local,
-):
-    spot = Spot()
-    everyone = NARROW * WIDE
-    spot.greet(everyone)
+    sib_x = spot.sib + 2 - 4 * spot.x
+    sib_y = spot.sib + 4 - 8 * spot.y
+    gather.got(sib_x, None, 7)
+    back.chunk(0, order.q_x)
+    back.chunk(1, order.q_x)
+    y_sum.across_one()
+    gather.got(sib_y, None, 8)
+    back.chunk(0, order.q_y)
+    back.chunk(1, order.q_y)
+    y_sum.to_mate()
+    sib_d = sib_x + 4 - 8 * spot.y
+    gather.got(sib_d, 0, 9)
+    gather.got(sib_d, 1, 10)
+    back.chunk(0, order.q_d)
+    back.chunk(1, order.q_d)
+    for copy in gather.started:
+        copy.wait_send()
+    back.keys(0)
+    back.keys(1)
 
     def to_plane(step, arriving):
         other = lax.rem(spot.w + step, WIDE)
@@ -1472,10 +1643,7 @@
     def to_owner(step, arriving):
         other, to = others(step)
         place = other if arriving else spot.me
-        return (
-            remote(rows_of(wg_ref, other), w_recv.at[place], ws.at[other], wr.at[place], to),
-            remote(lanes_of(small_ref, other), s_recv.at[place], ss.at[other], sr.at[place], to),
-        )
+        return remote(rows_of(wg_ref, other), w_recv.at[place], ws.at[other], wr.at[place], to)
 
     def gain_to_owner(step, arriving):
         other, to = others(step)
@@ -1487,8 +1655,7 @@
         return carry
 
     def start_owner(step, carry):
-        for copy in to_owner(step, False):
-            copy.start()
+        to_owner(step, False).start()
         return carry
 
     def start_gain(step, carry):
@@ -1496,17 +1663,30 @@
         return carry
 
     lax.fori_loop(1, WIDE, start_plane, 0)
-    mine = [
-        pltpu.make_async_copy(
-            dqkv_ref.at[:, pl.ds(pl.multiple_of(spot.w * SPAN, SPAN), SPAN), :],
-            dq_full.at[:, :, pl.ds(pl.multiple_of(spot.w * 256, 256), 256)],
-            local.at[0],
-        ),
-        pltpu.make_async_copy(rows_of(wg_ref, spot.me), w_recv.at[spot.me], local.at[1]),
-        pltpu.make_async_copy(lanes_of(small_ref, spot.me), s_recv.at[spot.me], local.at[2]),
-    ]
-    for copy in mine:
-        copy.start()
+    plane_mine = pltpu.make_async_copy(
+        dqkv_ref.at[:, pl.ds(pl.multiple_of(spot.w * SPAN, SPAN), SPAN), :],
+        dq_full.at[:, :, pl.ds(pl.multiple_of(spot.w * 256, 256), 256)],
+        local.at[0],
+    )
+    plane_mine.start()
+
+    loads[9].wait()
+    wg_ref[...] = (mm(h1[0], dqkv_ref[0], TN) + mm(h1[1], dqkv_ref[1], TN)).astype(BF16)
+    lax.fori_loop(1, everyone, start_owner, 0)
+    owner_mine = pltpu.make_async_copy(rows_of(wg_ref, spot.me), w_recv.at[spot.me], local.at[1])
+    owner_mine.start()
+    og_ref[...] = osum[...].astype(BF16)
+
+    def wait_lanes(step, carry):
+        lanes_to(step, False).wait_send()
+        lanes_to(step, True).wait_recv()
+        return carry
+
+    lax.fori_loop(1, WIDE, wait_lanes, 0)
+    lane_total = small_all[0]
+    for device in range(1, WIDE):
+        lane_total = lane_total + small_all[device]
+    small_sum[...] = lane_total
 
     def output_copies(act_local, act_send, act_recv):
         for i in range(4):
@@ -1518,10 +1698,12 @@
             @pl.when(here)
             def _():
                 act_local(pltpu.make_async_copy(source, o_recv.at[spot.n], local.at[3]))
+                act_local(pltpu.make_async_copy(small_sum, s_recv.at[spot.n], local.at[2]))
 
             @pl.when(jnp.logical_not(here))
             def _():
                 act_send(remote(source, o_recv.at[spot.n], os.at[i], orv.at[spot.n], to))
+                act_send(remote(small_sum, s_recv.at[spot.n], ss.at[i], sr.at[spot.n], to))
 
         for plane in range(NARROW):
             giver = lax.div(spot.me, 4)
@@ -1531,12 +1713,13 @@
             def _():
                 place = o_recv.at[plane]
                 act_recv(remote(place, place, os.at[0], orv.at[plane], (plane, giver)))
+                small = s_recv.at[plane]
+                act_recv(remote(small, small, ss.at[0], sr.at[plane], (plane, giver)))
 
     def nothing(copy):
         return None
 
     output_copies(lambda c: c.start(), lambda c: c.start(), nothing)
-    lax.fori_loop(1, everyone, start_owner, 0)
 
     def wait_plane(step, carry):
         to_plane(step, False).wait_send()
@@ -1544,9 +1727,10 @@
         return carry
 
     lax.fori_loop(1, WIDE, wait_plane, 0)
-    mine[0].wait()
-    dqkv = dq_full[...].reshape(TOKENS, 2 * WIDTH)
-    dh1 = mm(dqkv, w_ref[...], NT)
+    plane_mine.wait()
+    for copy in w_loads:
+        copy.wait()
+    dh1 = mm(dq_full[...].reshape(TOKENS, 2 * WIDTH), w_full[...].reshape(WIDTH, 2 * WIDTH), NT)
     x = x_ref[...].astype(F32)
     scale = lax.rsqrt(jnp.mean(x * x, axis=1, keepdims=True) + EPSILON)
     gain_own[0:1, :] = jnp.sum(dh1 * x * scale, axis=0, keepdims=True)
@@ -1557,17 +1741,16 @@
     weighted = dh1 * gain_ref[0:1, :]
     inner = jnp.mean(weighted * x, axis=1, keepdims=True)
     in_grad[...] = (dmid_ref[...] + weighted * scale - x * (scale * scale * scale) * inner).astype(BF16)
+    y_sum.finish()
+    block_out[...] = (mid_ref[...] + y_sum.total_ref[...]).astype(BF16)
 
     def wait_owner(step, carry):
-        for copy in to_owner(step, False):
-            copy.wait_send()
-        for copy in to_owner(step, True):
-            copy.wait_recv()
+        to_owner(step, False).wait_send()
+        to_owner(step, True).wait_recv()
         return carry
 
     lax.fori_loop(1, everyone, wait_owner, 0)
-    mine[1].wait()
-    mine[2].wait()
+    owner_mine.wait()
     output_copies(lambda c: c.wait(), lambda c: c.wait_send(), lambda c: c.wait_recv())
     for w in range(WIDE):
         total = widen(w_recv[w])
@@ -1581,8 +1764,8 @@
         total = total + widen(o_recv[plane])
     o_grad[...] = total
     total = s_recv[0]
-    for device in range(1, everyone):
-        total = total + s_recv[device]
+    for plane in range(1, NARROW):
+        total = total + s_recv[plane]
     sums[...] = total
 
     def wait_gain(step, carry):
@@ -1598,13 +1781,16 @@
     gain_sum[...] = total
 
 
-def finish_call(dqkv, wgrad, ograd, small, w_full, x_own, dmid, gain_rows):
+def backward_call(*operands):
     dma = pltpu.SemaphoreType.DMA
+    vmem = pltpu.VMEM
     everyone = NARROW * WIDE
+    copies = PlaneGather.COPIES
     return pl.pallas_call(
-        finish_kernel,
-        name="finish",
+        backward_kernel,
+        name="backward",
         out_shape=(
+            jax.ShapeDtypeStruct((TOKENS, WIDTH), BF16),
             jax.ShapeDtypeStruct((TOKENS, WIDTH), BF16),
             jax.ShapeDtypeStruct((32, WIDTH), F32),
             jax.ShapeDtypeStruct((32, WIDTH // 2), F32),
@@ -1613,59 +1799,77 @@
             jax.ShapeDtypeStruct((40, 128), F32),
             jax.ShapeDtypeStruct((8, 128), F32),
         ),
-        in_specs=[IN_HBM] * 4 + [IN_VMEM] * 4,
-        out_specs=(IN_VMEM,) * 7,
+        in_specs=[IN_HBM] * 12 + [IN_VMEM] * 5,
+        out_specs=(IN_VMEM,) * 8,
         scratch_shapes=[
-            pltpu.VMEM((2, SPAN, 2 * WIDTH), BF16),
-            pltpu.VMEM((everyone, 32, 256), BF16),
-            pltpu.VMEM((NARROW, 32, WIDTH), BF16),
-            pltpu.VMEM((everyone, 40, 128), F32),
-            pltpu.VMEM((8, WIDTH), F32),
-            pltpu.VMEM((everyone, 8, 128), F32),
+            vmem((GROUP, 8, TOKENS), F32),
+            vmem((TOKENS, WIDTH), BF16),
+            vmem((WIDE, TOKENS, WIDTH), BF16),
+            vmem((TOKENS, WIDTH), F32),
+            vmem((40, WIDTH), F32),
+            vmem((WIDE, 40, 128), F32),
+            vmem((40, 128), F32),
+            vmem((WIDTH, 128), BF16),
+            vmem((128, WIDTH), BF16),
+            vmem((NARROW, WIDE, 32, 2 * WIDTH), BF16),
+            vmem((2, SEQ, WIDTH), BF16),
+            vmem((2, SEQ, 256), BF16),
+            vmem((2, SEQ, 128), F32),
+            vmem((2, SEQ, 128), BF16),
+            vmem((2, SEQ, 256), F32),
+            vmem((2, SEQ, 128), F32),
+            vmem((2, SEQ, 256), BF16),
+            vmem((2, SEQ, 128), F32),
+            vmem((512, HEAD_DIM), F32),
+            vmem((128, WIDTH), F32),
+            vmem((128, WIDTH), BF16),
+            vmem((WIDTH, 256), BF16),
+            vmem((2, SPAN, 2 * WIDTH), BF16),
+            vmem((everyone, 32, 256), BF16),
+            vmem((NARROW, 32, WIDTH), BF16),
+            vmem((NARROW, 40, 128), F32),
+            vmem((8, WIDTH), F32),
+            vmem((everyone, 8, 128), F32),
+            dma((GROUP,)),
+            dma((GROUP,)),
+            dma((copies,)),
+            dma((copies,)),
+            dma((WIDE,)),
+            dma((WIDE,)),
             dma((WIDE,)),
             dma((WIDE,)),
             dma((everyone,)),
             dma((everyone,)),
             dma((4,)),
             dma((NARROW,)),
+            dma((4,)),
+            dma((NARROW,)),
             dma((everyone,)),
             dma((everyone,)),
-            dma((everyone,)),
-            dma((everyone,)),
-            dma((4,)),
-        ],
-        compiler_params=pltpu.CompilerParams(collective_id=4, has_side_effects=True, vmem_limit_bytes=VMEM_BYTES),
-    )(dqkv, wgrad, ograd, small, w_full, x_own, dmid, gain_rows)
+            dma((18,)),
+        ]
+        + reduce_scratch()
+        + reduce_scratch(),
+        compiler_params=pltpu.CompilerParams(collective_id=3, has_side_effects=True, vmem_limit_bytes=VMEM_BYTES),
+        cost_estimate=duration(1),
+    )(*operands)
 
 
 def swap(values, distance):
     return lax.ppermute(values, "narrow", [(i, i ^ distance) for i in range(NARROW)])
 
 
-def quarters(shard, half):
-    by_pair = shard.reshape((2, MINE) + shard.shape[1:])
-    own = lax.dynamic_index_in_dim(by_pair, half, 0, keepdims=False)
-    other = lax.dynamic_index_in_dim(by_pair, 1 - half, 0, keepdims=False)
-    return own, swap(other, 1), swap(own, 2), swap(other, 3)
-
-
-def owner_sums(grad, depth, n, half):
-    def rows(quarter):
-        return lax.dynamic_slice_in_dim(grad, quarter * depth, depth, axis=1)
-
-    mate = n + 1 - 2 * half
-    far = n + 2 - 4 * (n // 2)
-    far_mate = mate + 2 - 4 * (n // 2)
-    own = rows(n)
-    from_far = swap(rows(far), 2)
-    from_mate = swap(rows(mate), 1)
-    from_far_mate = swap(rows(far_mate), 3)
-    same = own.astype(F32) + from_far.astype(F32)
-    opposite = from_mate.astype(F32) + from_far_mate.astype(F32)
-    is_first = half == 0
-    return jnp.concatenate(
-        [jnp.where(is_first, same, opposite), jnp.where(is_first, opposite, same)], axis=0
-    )
+def expert_pieces(w_gate_up, w_down, e, half):
+    def piece(pair):
+        return jnp.concatenate(
+            [
+                lax.dynamic_index_in_dim(w_gate_up, 2 * pair + e, 0, keepdims=False),
+                lax.dynamic_index_in_dim(w_down, 2 * pair + e, 0, keepdims=False),
+            ],
+            axis=0,
+        )
+
+    return piece(half), piece(1 - half)
 
 
 def position_tables():
@@ -1686,11 +1890,7 @@
     me = n * WIDE + w
     cos_table, sin_table, freq = position_tables()
 
-    gate_up = quarters(w_gate_up, half)
-    down = quarters(w_down, half)
-    out_shard = jnp.concatenate([w_output, w_router, jnp.zeros((32, 96), BF16)], axis=1)
-    w_out = lax.all_gather(out_shard, ("narrow", "wide"), axis=0, tiled=True)
-
+    wo_own = jnp.concatenate([w_output, w_router, jnp.zeros((32, 96), BF16)], axis=1)
     x_own = hidden_in.reshape(TOKENS, WIDTH)
     dy_own = out_grad.reshape(TOKENS, WIDTH)
     w_own = jnp.concatenate(
@@ -1701,35 +1901,46 @@
     seg_own = jnp.pad(seg_ids, ((0, 6), (0, 0)))
     ids = expert_ids.reshape(TOKENS, TOP).T
 
-    x_all, w_all, g_all, seg_all = gather_call(x_own, w_own, g_own, seg_own)
-    h1, qkv, lse, o_heads, angle, start, gain_rows = attend_call(
-        x_all, w_all, g_all, seg_all, cos_table, sin_table, freq
-    )
-    dy_mate = swap(dy_own, 1)
-    dy_pair = jnp.where(half == 0, jnp.stack([dy_own, dy_mate]), jnp.stack([dy_mate, dy_own]))
-    dy_all = lax.all_gather(dy_pair.reshape(2 * TOKENS, WIDTH), "wide", axis=0, tiled=True).reshape(
-        WIDE, 2, TOKENS, WIDTH
-    )
-    w_full = lax.all_gather(w_own, ("narrow", "wide"), axis=0, tiled=True)
-
-    h2_all, table_all, mid, gate = project_call(o_heads, x_own, w_out, gain_rows, ids)
-    rows, da, y_part, dgate, down_grad = expert_call(h2_all, dy_all, table_all, gate_up, down)
-    down_sum = owner_sums(down_grad, FF // NARROW, n, half)
-    y_plane = lax.psum_scatter(
-        y_part.reshape(WIDE * 2 * TOKENS, WIDTH), "wide", scatter_dimension=0, tiled=True
-    ).reshape(2, TOKENS, WIDTH)
-    y_own = lax.dynamic_index_in_dim(y_plane, half, 0, keepdims=False)
-    y_mate = swap(lax.dynamic_index_in_dim(y_plane, 1 - half, 0, keepdims=False), 1)
-    block_out = (mid + y_own.astype(F32) + y_mate.astype(F32)).astype(BF16)
-    gate_up_grad = gate_up_grad_call(rows, da)
-    gate_up_sum = owner_sums(gate_up_grad, WIDTH // NARROW, n, half)
-    part = rows_grad_call(da, table_all, gate_up)
-    dattn_all, dmid, small = collect_call(part, dgate, h2_all, mid, gate, w_out, gain_rows, dy_own)
-    w_rows = lax.dynamic_slice(w_out, (w * 128, 0), (128, WIDTH))
-    dqkv, wgrad, ograd = attend_back_call(dattn_all, w_rows, h1, qkv, lse, o_heads, angle, start)
-    in_grad, q_grad, k_grad, v_grad, o_grad, sums, gain_sum = finish_call(
-        dqkv, wgrad, ograd, small, w_full, x_own, dmid, gain_rows
-    )
+    x_all, w_all, g_all, seg_all, wo_block, dy_pair = gather_call(x_own, w_own, g_own, seg_own, wo_own, dy_own)
+    w_gate_up, w_down, x_all, dy_pair = lax.optimization_barrier((w_gate_up, w_down, x_all, dy_pair))
+    own_0, other_0 = expert_pieces(w_gate_up, w_down, 0, half)
+    own_1, other_1 = expert_pieces(w_gate_up, w_down, 1, half)
+    pieces_0 = (own_0, swap(other_0, 1), swap(own_0, 2), swap(other_0, 3))
+    (
+        h1, qkv, lse, o_heads, angle, start, gain_rows, mid, gate, w_out, h2_all, dy_all, table_all, wq_block,
+        far_1, mate_1,
+    ) = forward_call(
+        x_all, w_all, g_all, seg_all, cos_table, sin_table, freq, wo_block, ids, dy_pair, w_own, own_1, other_1
+    )
+    w_out = w_out.reshape(WIDTH, WIDTH + 128)
+    other_1, h2_all = lax.optimization_barrier((other_1, h2_all))
+    pieces_1 = (own_1, mate_1, far_1, swap(other_1, 3))
+    n_row = n.reshape(1).astype(jnp.int32)
+    half_row = half.reshape(1).astype(jnp.int32)
+
+    def send_grads(e, rows, da, down_grad):
+        own, mate, far, far_mate = weight_grad_call(e, n_row, rows, da, down_grad)
+        own, da = lax.optimization_barrier((own, da))
+        return da, (own, swap(mate, 1), swap(far, 2), swap(far_mate, 3))
+
+    rows_0, da_0, y_0, dgate_0, down_grad_0 = expert_call(0, h2_all, dy_all, table_all, pieces_0, ())
+    rows_0, wq_block = lax.optimization_barrier((rows_0, wq_block))
+    w_full = lax.all_gather(wq_block, "wide", axis=0, tiled=False)
+    da_0, grads_0 = send_grads(0, rows_0, da_0, down_grad_0)
+    part_0 = rows_grad_call(0, da_0, table_all, pieces_0, ())
+    pieces_1, part_0, own_0 = lax.optimization_barrier((pieces_1, part_0, grads_0[0]))
+    grads_0 = (own_0,) + grads_0[1:]
+    rows_1, da_1, y_1, dgate, down_grad_1 = expert_call(
+        1, h2_all, dy_all, table_all, pieces_1, (y_0, dgate_0)
+    )
+    da_1, grads_1 = send_grads(1, rows_1, da_1, down_grad_1)
+    part = rows_grad_call(1, da_1, table_all, pieces_1, (part_0,))
+    block_out, in_grad, q_grad, k_grad, v_grad, o_grad, sums, gain_sum = backward_call(
+        part, y_1, dgate, h2_all, w_out, w_full, h1, qkv, lse, o_heads, angle, start,
+        x_own, mid, gate, gain_rows, dy_own,
+    )
+    sums_0 = owner_sum_call(0, half_row, grads_0, (), gain_sum)
+    gate_up_sum, down_sum = owner_sum_call(1, half_row, grads_1, sums_0, gain_sum)
     lanes = (me % 4) * 32
     router_grad = lax.dynamic_slice(sums, (0, lanes), (32, 32)).T
     moe_gain_grad = lax.dynamic_slice(sums, (32, lanes), (1, 32)).reshape(32)

time: 555 us -> 475 us (0.86)
  waiting for transfers between devices: 52.7 us -> 0.06 us
  Pallas kernels: 423 us -> 400 us
  other arithmetic: 14.1 us -> 4.06 us
  starting transfers between devices: 22.8 us -> 28.4 us
    pallas_call x1, Pallas kernels: 118 us -> 38.2 us  [gather_call(): pl.pallas_call(gather_kernel, name='gather_inputs', out_shape=(jax.ShapeD...]
    pallas_call x8 -> x10, Pallas kernels: 306 us -> 362 us  [the longest x1 152 us: backward_call(): pl.pallas_call(backward_kernel, name='backward', out_shape=(jax.ShapeDtyp...]
    ppermute x14 -> x10, waiting for transfers between devices: 52.6 us -> 0.03 us  [swap(): lax.ppermute(values, 'narrow', [(i, i ^ distance) for i in range(NARROW)])]
    select_n x3 -> x0, other arithmetic: 7.02 us -> none  [the longest x2 4.57 us: owner_sums(): jnp.where(is_first, same, opposite)]
    dynamic_slice x3 -> x0, local copies, waits for them, and re-layouts: 6.55 us -> none  [the longest x2 4.75 us: rows(): return lax.dynamic_slice_in_dim(grad, quarter * depth, depth, axis=1)]
    ppermute x14 -> x10, starting transfers between devices: 22.6 us -> 28.4 us  [swap(): lax.ppermute(values, 'narrow', [(i, i ^ distance) for i in range(NARROW)])]
    unnamed x48 -> x45, local copies, waits for them, and re-layouts: 6.04 us -> 11.1 us
  transfers between devices with their start and end apart: 18 -> 11, of which waited for: 3 -> 0; matrix products, arithmetic and copies ran while one was open for 5% -> 1% of each run, Pallas kernels for 77% -> 72%
where the time goes in v2:
time: 475 us; the launch traced here: 466 us
  Pallas kernels  400 us (84%)
  starting transfers between devices  28.4 us (6%)
  local copies, waits for them, and re-layouts  18 us (4%)
  between operations  14.7 us (3%)
    pallas_call x1, Pallas kernels, backward_call(): pl.pallas_call(backward_kernel, name='backward', out_shape=(jax.ShapeDtyp...  152 us
    pallas_call x1, Pallas kernels, forward_call(): pl.pallas_call(forward_kernel, name='forward', out_shape=(jax.ShapeDtypeS...  121 us
    pallas_call x2, Pallas kernels, expert_call(): pl.pallas_call(functools.partial(expert_kernel, e), name=f'expert_{e}', g...  44.2 us
    pallas_call x1, Pallas kernels, gather_call(): pl.pallas_call(gather_kernel, name='gather_inputs', out_shape=(jax.ShapeD...  38.2 us
    ppermute x10, starting transfers between devices, swap(): lax.ppermute(values, 'narrow', [(i, i ^ distance) for i in range(NARROW)])  28.4 us
    pallas_call x2, Pallas kernels, rows_grad_call(): pl.pallas_call(functools.partial(rows_grad_kernel, e), name=f'rows_grad_{...  22.1 us
    pallas_call x2, Pallas kernels, weight_grad_call(): pl.pallas_call(weight_grad_kernel, name=f'weight_grad_{e}', grid_spec=plt...  15.9 us
    unnamed x45, local copies, waits for them, and re-layouts  11.1 us
  transfers between devices with their start and end apart: 11, of which 0 were waited for; matrix products, arithmetic and copies ran while one was open for 1% of the time, Pallas kernels for 72%

profile of v2, /device:TPU:0, one launch (start us, length us, event | category | flops | bytes accessed | tf_op | source)
XLA Modules:
  0.0 465.6 jit_solution(824551187273077795)
XLA Ops:
  7.3 0.9 copy.32
  8.1 0.9 reshape.73
  9.0 0.9 reshape.74
  9.8 0.1 pad_maximum_fusion.4
  10.0 0.7 copy.33
  10.6 1.3 pad.12.seg_ref
  11.9 1.3 fusion.6.g_ref
  13.2 1.6 concatenate.23.wo_ref
  14.7 38.2 %gather_inputs.1 = (bf16[8,256,1024]{2,1,0:T(8,128)(2,1)}, bf16[32,32,256]{2,1,0:T(8,128)(2,1)}, f32[32,8,128]{2,1,0:T(8,128)}, s32[8,8,128]{2,1,0:T(8,128)}, bf...) custom-call(bf16[256,1024]{1,0:T(8,128)(2,1)} %bitcast.45, bf16[32,2048]{1,0:T(8,128)(2,1)} %bitcast.49, ...), custom_call_target="tpu_custom_call" | custom-call | flops 1000000000 | bytes 3600000 | tf_op jit(solution)/shard_map/gather_inputs/pallas_call | solution.py:674
  53.0 0.2 dynamic-slice_bitcast_fusion
  53.2 1.0 copy-done.7
  54.4 1.6 collective-permute-start.1
  56.0 0.5 collective-permute-start.2
  56.5 2.4 collective-permute-start.3
  58.9 1.3 pad_maximum_fusion
  60.2 120.9 %forward.1 = (bf16[2,1024,1024]{2,1,0:T(8,128)(2,1)}, bf16[2,1024,256]{2,1,0:T(8,128)(2,1)}, f32[2,1024,128]{2,1,0:T(8,128)}, bf16[2,1024,128]{2,1,0:T(8,128)(2,...) custom-call(bf16[8,2,128,1024]{3,2,1,0:T(8,128)(2,1)} %bitcast.43, ...), custom_call_target="tpu_custom_call" | custom-call | flops 1000000000 | bytes 3600000 | tf_op jit(solution)/shard_map/forward/pallas_call | solution.py:1002
  181.2 0.8 copy-done.2
  182.1 0.3 copy-done.3
  182.3 0.3 copy-done.4
  182.6 21.2 %expert_0.1 = (bf16[4,320,1024]{2,1,0:T(8,128)(2,1)}, bf16[4,320,1024]{2,1,0:T(8,128)(2,1)}, bf16[16,256,1024]{2,1,0:T(8,128)(2,1)}, f32[16,8,256]{2,1,0:T(8,128)}, bf16[512,1024]{1,0:T(8,128)(2,1)}) custom-call(bf16[16,256,1024]{2,1,0:T(8,128)(2,1)} %get-tuple-element.93.refs_0_.refs_3_, bf16[16,256,1024]{2,1,0:T(8,128)(2,1)} %get-tuple-element.94.refs_1_, ...), custom_call_target="tpu_custom_call" | custom-call | flops 1000000000 | bytes 3600000 | tf_op jit(solution)/shard_map/expert_0/pallas_call | solution.py:1138
  203.8 2.0 collective-permute-start
  205.9 7.8 %weight_grad_0.1 = (bf16[384,1024]{1,0:T(8,128)(2,1)}, bf16[384,1024]{1,0:T(8,128)(2,1)}, bf16[384,1024]{1,0:T(8,128)(2,1)}, bf16[384,1024]{1,0:T(8,128)(2,1)}) custom-call(s32[1]{0:T(128)} %bitcast.n_ref, bf16[4,320,1024]{2,1,0:T(8,128)(2,1)} %get-tuple-element.101.rows_ref, bf16[4,320,1024]{2,1,0:T(8,128)(2,1)} %get-tuple-element.105.da_ref.refs_0_, ...), custom_call_target="tpu_custom_call" | custom-call | flops 1000000000 | bytes 3600000 | tf_op jit(solution)/shard_map/weight_grad_0/pallas_call | solution.py:1183
  213.7 2.5 collective-permute-start.8
  216.2 1.9 collective-permute-start.9
  218.1 10.1 %rows_grad_0.1.refs_6_ = bf16[16,256,1024]{2,1,0:T(8,128)(2,1)} custom-call(bf16[4,320,1024]{2,1,0:T(8,128)(2,1)} %get-tuple-element.105.da_ref.refs_0_, f32[16,8,256]{2,1,0:T(8,128)} %get-tuple-element.95.refs_2_.refs_1_, bf16[384,1024]{1,0:T(8,128)(2,1)} %copy-done, bf16[384,1024]{1,0:T(8,128)(2,1)} %copy-done.2, bf16[384,1024]{1,0:T(8,128)(2,1)} %copy-done.3, ...), custom_call_target="tpu_custom_call" | custom-call | flops 1000000000 | bytes 3600000 | tf_op jit(solution)/shard_map/rows_grad_0/pallas_call | solution.py:1228
  228.2 0.9 copy-done.1
  229.1 23.0 %expert_1.1 = (bf16[4,320,1024]{2,1,0:T(8,128)(2,1)}, bf16[4,320,1024]{2,1,0:T(8,128)(2,1)}, bf16[16,256,1024]{2,1,0:T(8,128)(2,1)}, f32[16,8,256]{2,1,0:T(8,128)}, bf16[512,1024]{1,0:T(8,128)(2,1)}) custom-call(bf16[16,256,1024]{2,1,0:T(8,128)(2,1)} %get-tuple-element.93.refs_0_.refs_3_, bf16[16,256,1024]{2,1,0:T(8,128)(2,1)} %get-tuple-element.94.refs_1_, ...), custom_call_target="tpu_custom_call" | custom-call | flops 1000000000 | bytes 3600000 | tf_op jit(solution)/shard_map/expert_1/pallas_call | solution.py:1138
  252.1 8.1 %weight_grad_1.1 = (bf16[384,1024]{1,0:T(8,128)(2,1)}, bf16[384,1024]{1,0:T(8,128)(2,1)}, bf16[384,1024]{1,0:T(8,128)(2,1)}, bf16[384,1024]{1,0:T(8,128)(2,1)}) custom-call(s32[1]{0:T(128)} %bitcast.n_ref, bf16[4,320,1024]{2,1,0:T(8,128)(2,1)} %get-tuple-element.113.rows_ref, bf16[4,320,1024]{2,1,0:T(8,128)(2,1)} %get-tuple-element.117.da_ref.refs_0_, ...), custom_call_target="tpu_custom_call" | custom-call | flops 1000000000 | bytes 3600000 | tf_op jit(solution)/shard_map/weight_grad_1/pallas_call | solution.py:1183
  260.2 14.0 %collective-permute-start.4 = (bf16[384,1024]{1,0:T(8,128)(2,1)}, bf16[384,1024]{1,0:T(8,128)(2,1)S(1)}, u32[]{:S(2)}, u32[]{:S(2)}) collective-permute-start(bf16[384,1024]{1,0:T(8,128)(2,1)} %get-tuple-element.141), channel_id=1, source_target_pairs={{0,8},{8,0},{16,24},{24,16},{1,9},{9,1},{17,25},{25,17},{2,10},{10... | collective-permute-start | bytes 2359304 | tf_op jit(solution)/shard_map/ppermute | solution.py:1859
  274.2 1.9 collective-permute-start.5
  276.1 1.5 collective-permute-start.6
  277.6 12.1 %rows_grad_1.1.refs_0_ = bf16[16,256,1024]{2,1,0:T(8,128)(2,1)} custom-call(bf16[4,320,1024]{2,1,0:T(8,128)(2,1)} %get-tuple-element.117.da_ref.refs_0_, f32[16,8,256]{2,1,0:T(8,128)} %get-tuple-element.95.refs_2_.refs_1_, bf16[384,1024]{1,0:T(8,128)(2,1)} %get-tuple-element.107.own_piece.refs_3_.refs_2_, ...), custom_call_target="tpu_custom_call" | custom-call | flops 1000000000 | bytes 3600000 | tf_op jit(solution)/shard_map/rows_grad_1/pallas_call | solution.py:1228
  289.7 151.5 %backward.1 = (bf16[256,1024]{1,0:T(8,128)(2,1)}, bf16[256,1024]{1,0:T(8,128)(2,1)}, f32[32,1024]{1,0:T(8,128)}, f32[32,512]{1,0:T(8,128)}, f32[32,512]{1,0:T(8,...) custom-call(bf16[16,256,1024]{2,1,0:T(8,128)(2,1)} %rows_grad_1.1.refs_0_, ...), custom_call_target="tpu_custom_call" | custom-call | flops 1000000000 | bytes 3600000 | tf_op jit(solution)/shard_map/backward/pallas_call | solution.py:1789
  441.2 0.8 dynamic-slice_bitcast_fusion.8
  442.0 0.7 copy.31
  442.7 3.7 owner_sum_0.1
  446.4 1.3 fusion.7
  447.7 1.3 convert_bitcast_fusion
  449.1 0.9 copy-done.8
  449.9 0.3 copy-done.9
  450.2 0.3 copy-done.10
  450.5 3.8 owner_sum_1.1
  454.3 0.8 copy.42
  455.1 0.8 copy.43
  455.9 0.7 copy.44
  456.5 0.6 copy.45
  457.2 0.6 copy.46
  457.8 0.7 copy.47
  (46 shorter events, 0.4 us)
Async XLA Ops:
  7.2 282.5 %all-gather.3.cloned.1.call-start = ((), (), s32[]{:S(2)}) async-start(), calls=%async_computation | async-start | bytes 4718592 | tf_op jit(solution)/shard_map/all_gather | solution.py:1928
  9.9 43.0 %copy-start.6 = (bf16[4,256,1024]{2,1,0:T(8,128)(2,1)S(1)}, bf16[4,256,1024]{2,1,0:T(8,128)(2,1)}, u32[]{:S(2)}) copy-start(bf16[4,256,1024]{2,1,0:T(8,128)(2,1)} %param.27) | copy-start | bytes 6291460
  53.0 1.2 copy-start.7
  54.4 126.8 %collective-permute-start.1 = (bf16[384,1024]{1,0:T(8,128)(2,1)S(1)}, bf16[384,1024]{1,0:T(8,128)(2,1)S(1)}, u32[]{:S(2)}, u32[]{:S(2)}) collective-permute-start(bf16[384,1024]{1,0:T(8,128)(2,1)S(1)} %pad_maximum_fusion.3), channel_id=1, source_target_pairs={{0,8},{8,0},{16,24},{24,16},{1,9},{9,1},{17,25},{25,17},{2,10},{10... | collective-permute-start | bytes 2359304 | tf_op jit(solution)/shard_map/ppermute | solution.py:1859
  56.0 125.2 %copy-start = (bf16[384,1024]{1,0:T(8,128)(2,1)}, bf16[384,1024]{1,0:T(8,128)(2,1)S(1)}, u32[]{:S(2)}) copy-start(bf16[384,1024]{1,0:T(8,128)(2,1)S(1)} %pad_maximum_fusion.2.refs_3_.refs_2_) | copy-start | bytes 2359300
  56.0 125.2 %collective-permute-start.2 = (bf16[384,1024]{1,0:T(8,128)(2,1)S(1)}, bf16[384,1024]{1,0:T(8,128)(2,1)S(1)}, u32[]{:S(2)}, u32[]{:S(2)}) collective-permute-start(bf16[384,1024]{1,0:T(8,128)(2,1)S(1)} %pad_maximum_fusion.2.refs_3_.refs_2_), channel_id=1, source_target_pairs={{0,16},{8,24},{16,0},{24,8},{1,17},{9,25},{17,1},{25,9},{2,18},{10... | collective-permute-start | bytes 2359304 | tf_op jit(solution)/shard_map/ppermute | solution.py:1859
  56.5 124.7 %collective-permute-start.3 = (bf16[384,1024]{1,0:T(8,128)(2,1)S(1)}, bf16[384,1024]{1,0:T(8,128)(2,1)S(1)}, u32[]{:S(2)}, u32[]{:S(2)}) collective-permute-start(bf16[384,1024]{1,0:T(8,128)(2,1)S(1)} %pad_maximum_fusion.3), channel_id=1, source_target_pairs={{0,24},{8,16},{16,8},{24,0},{1,25},{9,17},{17,9},{25,1},{2,26},{10... | collective-permute-start | bytes 2359304 | tf_op jit(solution)/shard_map/ppermute | solution.py:1859
  181.2 0.9 copy-start.2
  181.2 1.2 copy-start.3
  181.2 1.4 copy-start.4
  182.6 21.2 %copy-start.5 = (bf16[384,1024]{1,0:T(8,128)(2,1)S(1)}, bf16[384,1024]{1,0:T(8,128)(2,1)}, u32[]{:S(2)}) copy-start(bf16[384,1024]{1,0:T(8,128)(2,1)} %get-tuple-element.98.other_piece) | copy-start | bytes 2359300
  203.8 24.3 %collective-permute-start = (bf16[384,1024]{1,0:T(8,128)(2,1)S(1)}, bf16[384,1024]{1,0:T(8,128)(2,1)S(1)}, u32[]{:S(2)}, u32[]{:S(2)}) collective-permute-start(bf16[384,1024]{1,0:T(8,128)(2,1)S(1)} %copy-done.5), channel_id=1, source_target_pairs={{0,24},{8,16},{16,8},{24,0},{1,25},{9,17},{17,9},{25,1},{2,26},{10... | collective-permute-start | bytes 2359304 | tf_op jit(solution)/shard_map/ppermute | solution.py:1859
  213.7 62.4 %collective-permute-start.7 = (bf16[384,1024]{1,0:T(8,128)(2,1)}, bf16[384,1024]{1,0:T(8,128)(2,1)S(1)}, u32[]{:S(2)}, u32[]{:S(2)}) collective-permute-start(bf16[384,1024]{1,0:T(8,128)(2,1)} %get-tuple-element.145), channel_id=1, source_target_pairs={{0,8},{8,0},{16,24},{24,16},{1,9},{9,1},{17,25},{25,17},{2,10},{10... | collective-permute-start | bytes 2359304 | tf_op jit(solution)/shard_map/ppermute | solution.py:1859
  213.7 229.0 %collective-permute-start.8 = (bf16[384,1024]{1,0:T(8,128)(2,1)}, bf16[384,1024]{1,0:T(8,128)(2,1)}, u32[]{:S(2)}, u32[]{:S(2)}) collective-permute-start(bf16[384,1024]{1,0:T(8,128)(2,1)} %get-tuple-element.146), channel_id=1, source_target_pairs={{0,16},{8,24},{16,0},{24,8},{1,17},{9,25},{17,1},{25,9},{2,18},{10... | collective-permute-start | bytes 2359304 | tf_op jit(solution)/shard_map/ppermute | solution.py:1859
  216.2 226.5 %collective-permute-start.9 = (bf16[384,1024]{1,0:T(8,128)(2,1)}, bf16[384,1024]{1,0:T(8,128)(2,1)}, u32[]{:S(2)}, u32[]{:S(2)}) collective-permute-start(bf16[384,1024]{1,0:T(8,128)(2,1)} %get-tuple-element.147), channel_id=1, source_target_pairs={{0,24},{8,16},{16,8},{24,0},{1,25},{9,17},{17,9},{25,1},{2,26},{10... | collective-permute-start | bytes 2359304 | tf_op jit(solution)/shard_map/ppermute | solution.py:1859
  228.2 0.9 copy-start.1
  260.2 188.8 %collective-permute-start.4 = (bf16[384,1024]{1,0:T(8,128)(2,1)}, bf16[384,1024]{1,0:T(8,128)(2,1)S(1)}, u32[]{:S(2)}, u32[]{:S(2)}) collective-permute-start(bf16[384,1024]{1,0:T(8,128)(2,1)} %get-tuple-element.141), channel_id=1, source_target_pairs={{0,8},{8,0},{16,24},{24,16},{1,9},{9,1},{17,25},{25,17},{2,10},{10... | collective-permute-start | bytes 2359304 | tf_op jit(solution)/shard_map/ppermute | solution.py:1859
  274.2 174.9 %collective-permute-start.5 = (bf16[384,1024]{1,0:T(8,128)(2,1)}, bf16[384,1024]{1,0:T(8,128)(2,1)S(1)}, u32[]{:S(2)}, u32[]{:S(2)}) collective-permute-start(bf16[384,1024]{1,0:T(8,128)(2,1)} %get-tuple-element.142), channel_id=1, source_target_pairs={{0,16},{8,24},{16,0},{24,8},{1,17},{9,25},{17,1},{25,9},{2,18},{10... | collective-permute-start | bytes 2359304 | tf_op jit(solution)/shard_map/ppermute | solution.py:1859
  276.1 13.6 %copy-start.17 = (bf16[384,1024]{1,0:T(8,128)(2,1)}, bf16[384,1024]{1,0:T(8,128)(2,1)S(1)}, u32[]{:S(2)}) copy-start(bf16[384,1024]{1,0:T(8,128)(2,1)S(1)} %collective-permute-done.7.mate) | copy-start | bytes 2359300
  276.1 172.9 %collective-permute-start.6 = (bf16[384,1024]{1,0:T(8,128)(2,1)}, bf16[384,1024]{1,0:T(8,128)(2,1)S(1)}, u32[]{:S(2)}, u32[]{:S(2)}) collective-permute-start(bf16[384,1024]{1,0:T(8,128)(2,1)} %get-tuple-element.143), channel_id=1, source_target_pairs={{0,24},{8,16},{16,8},{24,0},{1,25},{9,17},{17,9},{25,1},{2,26},{10... | collective-permute-start | bytes 2359304 | tf_op jit(solution)/shard_map/ppermute | solution.py:1859
  449.0 0.9 copy-start.8
  449.0 1.2 copy-start.9
  449.1 1.4 copy-start.10
  450.5 3.8 copy-start.12
  450.5 4.6 copy-start.11
  454.3 1.6 copy-start.14
  454.3 2.3 copy-start.16
  454.3 2.9 copy-start.15
  454.3 3.5 copy-start.13
Sparse Core Ops, SparseCore 0:
  203.9 35.3 all-gather.2

commit v3 on v2

--- a/solution.py
+++ b/solution.py
@@ -441,6 +441,7 @@
 SEQ = 1024
 SLOTS = 80
 MINE = 2
+EARLY = 160
 CHUNK = 4
 NT = (((1,), (1,)), ((), ()))
 TN = (((0,), (0,)), ((), ()))
@@ -577,11 +578,24 @@
 
 
 def gather_kernel(
-    x_ref, w_ref, g_ref, seg_ref, wo_ref, dy_ref,
-    x_all, w_all, g_all, seg_all, wo_block, dy_pair,
-    send, recv, local, ws, wr, gs, gr, ss, sr, zs, zr, ds, dr,
+    x_ref, dy_ref, seg_in, q_ref, k_ref, v_ref, o_ref, router_ref, gain_one_ref, gain_two_ref, gu_ref,
+    x_all, w_all, g_all, seg_all, wo_block, dy_pair, far_gu, w_ref,
+    g_ref, seg_ref, wo_ref, send, recv, local, ws, wr, gs, gr, ss, sr, zs, zr, ds, dr, es, er,
 ):
     spot = Spot()
+    for head in range(WIDE):
+        at = 256 * head
+        w_ref[:, at : at + 128] = q_ref[:, 128 * head : 128 * head + 128]
+        w_ref[:, at + 128 : at + 256] = jnp.concatenate(
+            [k_ref[:, 64 * head : 64 * head + 64], v_ref[:, 64 * head : 64 * head + 64]], axis=1
+        )
+    wo_ref[:, 0:WIDTH] = o_ref[...]
+    wo_ref[:, WIDTH : WIDTH + 128] = jnp.concatenate([router_ref[...], jnp.zeros((32, 96), BF16)], axis=1)
+    g_ref[...] = jnp.zeros_like(g_ref)
+    g_ref[0:1, 0:32] = gain_one_ref[...].astype(F32)
+    g_ref[1:2, 0:32] = gain_two_ref[...].astype(F32)
+    seg_ref[...] = jnp.zeros_like(seg_ref)
+    seg_ref[0:2, :] = seg_in[...]
     spot.greet(NARROW * WIDE)
     own = [
         pltpu.make_async_copy(x_ref, x_all.at[spot.w], local.at[0]),
@@ -637,6 +651,11 @@
         copy.start()
     across = remote(dy_ref, dy_pair.at[spot.half], ds.at[0], dr.at[0], (spot.mate, spot.w))
     across.start()
+    far = remote(
+        gu_ref.at[2 * spot.half, pl.ds(0, EARLY)], far_gu, es.at[0], er.at[0],
+        (spot.n + 2 - 4 * lax.div(spot.n, 2), spot.w),
+    )
+    far.start()
     gather.middle()
     gather.late()
     gather.last()
@@ -667,9 +686,11 @@
     remote(arrived, arrived, ds.at[0], dr.at[0], (spot.mate, spot.w)).wait_recv()
     for copy in own:
         copy.wait()
-
-
-def gather_call(x_own, w_own, g_own, seg_own, wo_own, dy_own):
+    far.wait_send()
+    far.wait_recv()
+
+
+def gather_call(*operands):
     dma = pltpu.SemaphoreType.DMA
     return pl.pallas_call(
         gather_kernel,
@@ -681,10 +702,15 @@
             jax.ShapeDtypeStruct((WIDE, 8, 128), jnp.int32),
             jax.ShapeDtypeStruct((NARROW, 32, WIDTH + 128), BF16),
             jax.ShapeDtypeStruct((2, TOKENS, WIDTH), BF16),
+            jax.ShapeDtypeStruct((EARLY, WIDTH), BF16),
+            jax.ShapeDtypeStruct((32, 2 * WIDTH), BF16),
         ),
-        in_specs=[IN_VMEM] * 6,
-        out_specs=(IN_HBM,) * 6,
+        in_specs=[IN_VMEM] * 10 + [IN_HBM],
+        out_specs=(IN_HBM,) * 7 + (IN_VMEM,),
         scratch_shapes=[
+            pltpu.VMEM((8, 128), F32),
+            pltpu.VMEM((8, 128), jnp.int32),
+            pltpu.VMEM((32, WIDTH + 128), BF16),
             dma((PlaneGather.COPIES,)),
             dma((PlaneGather.COPIES,)),
             dma((6,)),
@@ -698,10 +724,12 @@
             dma((NARROW,)),
             dma((1,)),
             dma((1,)),
+            dma((1,)),
+            dma((1,)),
         ],
         compiler_params=pltpu.CompilerParams(collective_id=1, has_side_effects=True),
         cost_estimate=duration(1),
-    )(x_own, w_own, g_own, seg_own, wo_own, dy_own)
+    )(*operands)
 
 
 def lane_half():
@@ -728,10 +756,10 @@
 
 
 class Attention:
-    def __init__(self, x_ref, w_ref, seg_ref, cos_ref, sin_ref, freq_ref, gain_one, h1_ref, qkv_ref, lse_ref, o_ref, angle_ref, start_ref):
+    def __init__(self, x_ref, w_ref, seg_ref, cos_ref, sin_ref, freq_ref, gain_one, h1_ref, qkv_ref, lse_ref, o_ref, angle_ref):
         self.x_ref, self.seg_ref, self.cos_ref, self.sin_ref = x_ref, seg_ref, cos_ref, sin_ref
         self.h1_ref, self.qkv_ref, self.lse_ref, self.o_ref = h1_ref, qkv_ref, lse_ref, o_ref
-        self.angle_ref, self.start_ref = angle_ref, start_ref
+        self.angle_ref = angle_ref
         self.gain_one = gain_one
         self.w_ref = w_ref
         self.first_half = lane_half()
@@ -766,7 +794,6 @@
             start_col = jnp.where(here, starts[doc], start_col)
             cos_s = jnp.where(here, start_cos[doc : doc + 1], cos_s)
             sin_s = jnp.where(here, start_sin[doc : doc + 1], sin_s)
-        self.start_ref[row, tokens, :] = start_col
         cos_t = self.cos_ref[tokens, :]
         sin_t = self.sin_ref[tokens, :]
         cosine = cos_t * cos_s + sin_t * sin_s
@@ -799,15 +826,35 @@
             outs.append(mm(jnp.exp(scores - log_total).astype(BF16), values))
             logs.append(log_total)
         self.o_ref[row, tokens, :] = jnp.concatenate(outs, axis=1).astype(BF16)
-        self.lse_ref[row, tokens, :] = jnp.where(self.is_key, logs[0], logs[1])
+        self.lse_ref[row, tokens, :] = jnp.where(
+            self.is_key, jnp.where(self.first_half, logs[0], start_col), logs[1]
+        )
+
+
+def piece_copies(spot, gu_ref, down_ref, e, kind, target, send, recv, number):
+    pair = lax.div(spot.n, 2)
+    plane = spot.n if kind == 2 else spot.mate
+    if kind >= 2:
+        plane = plane + 2 - 4 * pair
+    half = spot.half if kind == 2 else 1 - spot.half
+    to = (plane, spot.w)
+    return [
+        remote(gu_ref.at[2 * half + e], target.at[pl.ds(0, 256)], send.at[number], recv.at[number], to),
+        remote(down_ref.at[2 * half + e], target.at[pl.ds(256, 128)], send.at[number + 1], recv.at[number + 1], to),
+    ]
+
+
+def start_all(copies):
+    for copy in copies:
+        copy.start()
 
 
 def forward_kernel(
-    x_ref, w_ref, g_ref, seg_ref, cos_ref, sin_ref, freq_ref, wo_ref, ids_ref, dy_ref, wq_ref, own_piece, other_piece,
-    h1_out, qkv_ref, lse_ref, o_ref, angle_ref, start_ref, gain_ref, mid_ref, gate_ref, w_all,
-    h2_all, dy_all, table_all, wq_block, far_piece, mate_piece,
+    x_ref, w_ref, g_ref, seg_ref, cos_ref, sin_ref, freq_ref, wo_ref, ids_ref, dy_ref, gu_ref, down_ref,
+    h1_out, qkv_ref, lse_ref, o_ref, angle_ref, gain_ref, mid_ref, gate_ref, w_all,
+    h2_all, dy_all, table_all, mate_0, far_rest_0, far_mate_0, mate_1, far_1,
     h1_ref, o_full, h2_own, table_own,
-    os, orv, w_send, w_recv, a_send, a_recv, b_send, b_recv, s0, r0, s1, r1, ts, tr, zs, zr, cs, cr, es, er, local,
+    os, orv, w_send, w_recv, a_send, a_recv, b_send, b_recv, s0, r0, s1, r1, ts, tr, zs, zr, es, er, local,
 ):
     spot = Spot()
     spot.greet(NARROW * WIDE)
@@ -826,26 +873,24 @@
     mate_dy_gather = gather_tokens(spot, dy_ref.at[1 - spot.half], dy_all, mate_base, b_send, b_recv)
     w_gather.begin()
     dy_gather.begin()
-
-    def column(step, arriving):
-        other = lax.rem(spot.n + step, NARROW)
-        place = other if arriving else spot.n
-        return remote(wq_ref, wq_block.at[place], cs.at[other], cr.at[place], (other, spot.w))
-
-    def start_column(step, carry):
-        column(step, False).start()
-        return carry
-
-    def wait_column(step, carry):
-        column(step, False).wait_send()
-        column(step, True).wait_recv()
-        return carry
+    far_plane = (spot.n + 2 - 4 * lax.div(spot.n, 2), spot.w)
+    first_expert = [
+        remote(
+            gu_ref.at[2 * spot.half, pl.ds(EARLY, 256 - EARLY)], far_rest_0.at[pl.ds(0, 256 - EARLY)],
+            es.at[0], er.at[0], far_plane,
+        ),
+        remote(
+            down_ref.at[2 * spot.half], far_rest_0.at[pl.ds(256 - EARLY, 128)], es.at[1], er.at[1], far_plane
+        ),
+    ]
+    first_expert += piece_copies(spot, gu_ref, down_ref, 0, 3, far_mate_0, es, er, 2)
+    first_expert += piece_copies(spot, gu_ref, down_ref, 0, 1, mate_0, es, er, 4)
+    start_all(first_expert)
 
     keep = [
         pltpu.make_async_copy(wo_ref, w_place(spot.w, None), local.at[0]),
         pltpu.make_async_copy(dy_ref.at[spot.half], dy_all.at[spot.slot], local.at[1]),
         pltpu.make_async_copy(dy_ref.at[1 - spot.half], dy_all.at[mate_slot], local.at[2]),
-        pltpu.make_async_copy(wq_ref, wq_block.at[spot.n], local.at[7]),
     ]
     for copy in keep:
         copy.start()
@@ -867,10 +912,12 @@
         def _():
             act_remote(remote(source, target, os.at[to], orv.at[spot.w], spot.wide(to)))
 
-    expert = lax.broadcasted_iota(jnp.int32, (32, TOKENS), 0)
+    expert = lax.broadcasted_iota(jnp.int32, (32, TOKENS), 0).astype(F32)
     named = jnp.zeros((32, TOKENS), F32)
+    ids = ids_ref[...].astype(F32)
+    ids = jnp.transpose(jnp.concatenate([ids, jnp.zeros((TOKENS, 128 - TOP), F32)], axis=1))
     for k in range(TOP):
-        named = jnp.where(expert == ids_ref[k : k + 1, :], 1.0, named)
+        named = jnp.where(expert == ids[k : k + 1, :], 1.0, named)
     before = lax.broadcasted_iota(jnp.int32, (TOKENS, TOKENS), 0) < lax.broadcasted_iota(
         jnp.int32, (TOKENS, TOKENS), 1
     )
@@ -883,7 +930,7 @@
     gain_ref[...] = jnp.concatenate([gain_one, gain_two, jnp.zeros((6, WIDTH), F32)], axis=0)
     attention = Attention(
         x_ref, w_ref, seg_ref, cos_ref, sin_ref, freq_ref, gain_one,
-        h1_ref, qkv_ref, lse_ref, o_ref, angle_ref, start_ref,
+        h1_ref, qkv_ref, lse_ref, o_ref, angle_ref,
     )
     between = {1: [w_gather.middle], 2: [w_gather.late, dy_gather.middle], 3: [w_gather.last, dy_gather.late]}
     for i in range(4):
@@ -893,10 +940,8 @@
             each_head_copy(to, lambda copy: copy.start(), lambda copy: copy.start())
         for step in between.get(i, []):
             step()
-    pair = lax.div(spot.n, 2)
-    far = remote(own_piece, far_piece, es.at[0], er.at[0], (spot.n + 2 - 4 * pair, spot.w))
-    far.start()
-    near = remote(other_piece, mate_piece, es.at[1], er.at[1], (spot.mate, spot.w))
+    far = piece_copies(spot, gu_ref, down_ref, 1, 2, far_1, es, er, 6)
+    near = piece_copies(spot, gu_ref, down_ref, 1, 1, mate_1, es, er, 8)
     h1_copy = pltpu.make_async_copy(h1_ref, h1_out, local.at[4])
     h1_copy.start()
     dy_gather.last()
@@ -952,7 +997,6 @@
         return carry
 
     lax.fori_loop(1, GROUP, start_table, 0)
-    lax.fori_loop(1, NARROW, start_column, 0)
     table_mine = pltpu.make_async_copy(
         table_own.at[2 * spot.w + spot.half], table_all.at[spot.slot], local.at[6]
     )
@@ -968,7 +1012,7 @@
     remote(arriving, arriving, zs.at[0], zr.at[0], (spot.mate, spot.w)).wait_recv()
     second = gather_tokens(spot, arriving, h2_all, mate_base, s1, r1)
     second.begin()
-    near.start()
+    start_all(far + near)
     second.middle()
     second.late()
     second.last()
@@ -979,8 +1023,6 @@
         return carry
 
     lax.fori_loop(1, GROUP, wait_table, 0)
-    lax.fori_loop(1, NARROW, wait_column, 0)
-    keep[3].wait()
     dy_gather.finish()
     mate_dy_gather.finish()
     first.finish()
@@ -991,12 +1033,12 @@
     keep_own.wait()
     table_mine.wait()
     h1_copy.wait()
-    for copy in (far, near):
+    for copy in first_expert + far + near:
         copy.wait_send()
         copy.wait_recv()
 
 
-def forward_call(x_all, w_all, g_all, seg_all, cos_table, sin_table, freq, wo_block, ids, dy_pair, w_own, own, other):
+def forward_call(x_all, w_all, g_all, seg_all, cos_table, sin_table, freq, wo_block, ids, dy_pair, w_gate_up, w_down):
     dma = pltpu.SemaphoreType.DMA
     copies = PlaneGather.COPIES
     return pl.pallas_call(
@@ -1008,7 +1050,6 @@
             jax.ShapeDtypeStruct((2, SEQ, 128), F32),
             jax.ShapeDtypeStruct((2, SEQ, 128), BF16),
             jax.ShapeDtypeStruct((2, SEQ, 256), F32),
-            jax.ShapeDtypeStruct((2, SEQ, 128), F32),
             jax.ShapeDtypeStruct((8, WIDTH), F32),
             jax.ShapeDtypeStruct((TOKENS, WIDTH), F32),
             jax.ShapeDtypeStruct((64, TOKENS), F32),
@@ -1016,12 +1057,10 @@
             jax.ShapeDtypeStruct((GROUP, TOKENS, WIDTH), BF16),
             jax.ShapeDtypeStruct((GROUP, TOKENS, WIDTH), BF16),
             jax.ShapeDtypeStruct((GROUP, 8, TOKENS), F32),
-            jax.ShapeDtypeStruct((NARROW, 32, 2 * WIDTH), BF16),
-            jax.ShapeDtypeStruct((384, WIDTH), BF16),
-            jax.ShapeDtypeStruct((384, WIDTH), BF16),
-        ),
-        in_specs=[IN_VMEM] * 7 + [IN_HBM, IN_VMEM, IN_VMEM, IN_VMEM, IN_HBM, IN_HBM],
-        out_specs=(IN_HBM,) + (IN_VMEM,) * 9 + (IN_HBM,) * 6,
+        )
+        + tuple(jax.ShapeDtypeStruct((depth, WIDTH), BF16) for depth in (384, 384 - EARLY, 384, 384, 384)),
+        in_specs=[IN_VMEM] * 7 + [IN_HBM, IN_VMEM, IN_VMEM, IN_HBM, IN_HBM],
+        out_specs=(IN_HBM,) + (IN_VMEM,) * 8 + (IN_HBM,) * 8,
         scratch_shapes=[
             pltpu.VMEM((2, SEQ, WIDTH), BF16),
             pltpu.VMEM((2, SPAN, WIDTH), BF16),
@@ -1031,27 +1070,35 @@
             dma((WIDE,)),
         ]
         + [dma((copies,))] * 10
-        + [dma((GROUP,)), dma((GROUP,)), dma((1,)), dma((1,)), dma((NARROW,)), dma((NARROW,)), dma((2,)), dma((2,)), dma((8,))],
+        + [dma((GROUP,)), dma((GROUP,)), dma((1,)), dma((1,)), dma((10,)), dma((10,)), dma((7,))],
         compiler_params=pltpu.CompilerParams(collective_id=2, has_side_effects=True, vmem_limit_bytes=VMEM_BYTES),
         cost_estimate=duration(1),
-    )(x_all.reshape(WIDE, 2, SPAN, WIDTH), w_all, g_all, seg_all, cos_table, sin_table, freq, wo_block, ids, dy_pair, w_own, own, other)
-
-
-def load_quarters(pieces, target, first, depth, sems, base):
+    )(x_all.reshape(WIDE, 2, SPAN, WIDTH), w_all, g_all, seg_all, cos_table, sin_table, freq, wo_block, ids, dy_pair, w_gate_up, w_down)
+
+
+def load_quarters(own, pieces, w_gu, w_down, sems):
     n = lax.axis_index("narrow")
     half, pair = lax.rem(n, 2), lax.div(n, 2)
     mate = n + 1 - 2 * half
     far = n + 2 - 4 * pair
     far_mate = mate + 2 - 4 * pair
     copies = []
-    for number, (piece, quarter) in enumerate(zip(pieces, (n, mate, far, far_mate))):
-        copies.append(
-            pltpu.make_async_copy(
-                piece.at[pl.ds(first, depth)],
-                target.at[pl.ds(pl.multiple_of(quarter * depth, depth), depth)],
-                sems.at[base + number],
-            )
-        )
+    for quarter, parts in zip((n, mate, far, far_mate), (own,) + pieces):
+        first = 0
+        for part in parts if isinstance(parts, tuple) else (parts,):
+            depth = part.shape[0]
+            for start, rows, target in ((0, 256, w_gu), (256, 128, w_down)):
+                low, high = max(first, start), min(first + depth, start + rows)
+                if low < high:
+                    place = quarter * rows + (low - start)
+                    copies.append(
+                        pltpu.make_async_copy(
+                            part.at[pl.ds(low - first, high - low)],
+                            target.at[pl.ds(pl.multiple_of(place, 32), high - low)],
+                            sems.at[len(copies)],
+                        )
+                    )
+            first += depth
     return copies
 
 
@@ -1060,218 +1107,261 @@
     return slot == table_ref[source, expert : expert + 1, :]
 
 
-def expert_kernel(e, *refs):
-    if e == 0:
-        h2_ref, dy_ref, table_ref, w0, w1, w2, w3 = refs[:7]
-        refs = refs[7:]
-    else:
-        h2_ref, dy_ref, table_ref, w0, w1, w2, w3, y_before, dgate_before = refs[:9]
-        refs = refs[9:]
-    rows_ref, da_ref, y_ref, dgate_ref, down_grad_ref, w_gu, w_down, down_sum, sems = refs
-    step = pl.program_id(0)
-
-    @pl.when(step == 0)
-    def _():
-        pieces = (w0, w1, w2, w3)
-        copies = load_quarters(pieces, w_gu, 0, 256, sems, 0) + load_quarters(pieces, w_down, 256, 128, sems, 4)
-        for copy in copies:
-            copy.start()
-        down_sum[...] = jnp.zeros_like(down_sum)
-        for copy in copies:
-            copy.wait()
-
-    masks = [pick(table_ref, s, e) for s in range(CHUNK)]
-    hots = [jnp.where(mask, 1.0, 0.0).astype(BF16) for mask in masks]
-    rows = jnp.concatenate([mm(hots[s], h2_ref[s]) for s in range(CHUNK)], axis=0).astype(BF16)
-    grad_rows = jnp.concatenate([mm(hots[s], dy_ref[s]) for s in range(CHUNK)], axis=0)
-    gates = jnp.concatenate(
+STEPS = GROUP // CHUNK
+ROWS = CHUNK * SLOTS
+
+
+def start_weights(e, gu_ref, down_ref, pieces, w_gu, w_down, gu_sum, down_sum, sems):
+    mine = 2 * lax.rem(lax.axis_index("narrow"), 2) + e
+    copies = load_quarters((gu_ref.at[mine], down_ref.at[mine]), pieces, w_gu, w_down, sems)
+    for copy in copies:
+        copy.start()
+    gu_sum[...] = jnp.zeros_like(gu_sum)
+    down_sum[...] = jnp.zeros_like(down_sum)
+    for copy in copies:
+        copy.wait()
+
+
+def slot_gates(table_ref, masks, e):
+    return jnp.concatenate(
         [
             jnp.sum(jnp.where(masks[s], table_ref[s, 2 + e : 3 + e, :], 0.0), axis=1, keepdims=True)
             for s in range(CHUNK)
         ],
         axis=0,
     )
-    rows_ref[0] = rows
+
+
+def expert_math(rows, grad_rows, gates, w_gu, w_down, gu_sum, down_sum):
     g = mm(rows, w_gu[:, 0:FF])
     u = mm(rows, w_gu[:, FF : 2 * FF])
     sigmoid = 1.0 / (1.0 + jnp.exp(-g))
     active = g * sigmoid
     hidden = (active * u).astype(BF16)
+    grad_rows = grad_rows.astype(F32)
+    dy_pair = (grad_rows * gates).astype(BF16)
+    dhid = mm(dy_pair, w_down[...], NT)
+    da_g = (dhid * u * (sigmoid * (1.0 + g * (1.0 - sigmoid)))).astype(BF16)
+    da_u = (dhid * active).astype(BF16)
     y = mm(hidden, w_down[...]).astype(BF16).astype(F32)
     slot_dgate = jnp.sum(y * grad_rows, axis=1, keepdims=True)
-    if e == 0:
-        dgate_ref[...] = jnp.zeros_like(dgate_ref)
-    else:
-        dgate_ref[...] = dgate_before[...]
+    down_sum[...] += mm(hidden, dy_pair, TN)
+    gu_sum[:, 0:FF] += mm(rows, da_g, TN)
+    gu_sum[:, FF : 2 * FF] += mm(rows, da_u, TN)
+    dx = (mm(da_g, w_gu[:, 0:FF], NT) + mm(da_u, w_gu[:, FF : 2 * FF], NT)).astype(BF16)
+    return (y * gates).astype(BF16), dx, slot_dgate
+
+
+def token_dgate(dgate_ref, masks, slot_dgate, e):
     for s in range(CHUNK):
         part = slot_dgate[s * SLOTS : (s + 1) * SLOTS]
         dgate_ref[s, e : e + 1, :] = jnp.sum(jnp.where(masks[s], part, 0.0), axis=0, keepdims=True)
-    gated = (y * gates).astype(BF16)
-    dy_pair = (grad_rows * gates).astype(BF16)
-    down_sum[...] += mm(hidden, dy_pair, TN)
-    dhid = mm(dy_pair, w_down[...], NT)
-    da_ref[0, :, 0:FF] = (dhid * u * (sigmoid * (1.0 + g * (1.0 - sigmoid)))).astype(BF16)
-    da_ref[0, :, FF : 2 * FF] = (dhid * active).astype(BF16)
+
+
+def store_quarters(outs, gu_sum, down_sum):
+    n = lax.axis_index("narrow")
+    half, pair = lax.rem(n, 2), lax.div(n, 2)
+    mate = n + 1 - 2 * half
+    far = n + 2 - 4 * pair
+    far_mate = mate + 2 - 4 * pair
+    for out, quarter in zip(outs, (n, mate, far, far_mate)):
+        out[0:256, :] = gu_sum[pl.ds(pl.multiple_of(quarter * 256, 256), 256), :].astype(BF16)
+        out[256:384, :] = down_sum[pl.ds(pl.multiple_of(quarter * 128, 128), 128), :].astype(BF16)
+
+
+def expert_0_kernel(
+    h2_ref, dy_ref, table_ref, gu_ref, down_ref, w1, w2_early, w2_rest, w3,
+    gated_ref, dx_ref, rows_ref, grad_rows_ref, dgate_ref, own, mate, far, far_mate, far_mate_1,
+    w_gu, w_down, gu_sum, down_sum, sems, es, er,
+):
+    step = pl.program_id(0)
+    spot = Spot()
+    second_expert = piece_copies(spot, gu_ref, down_ref, 1, 3, far_mate_1, es, er, 0)
+
+    @pl.when(step == 0)
+    def _():
+        barrier = pltpu.get_barrier_semaphore()
+        plane = spot.mate + 2 - 4 * lax.div(spot.n, 2)
+        pl.semaphore_signal(barrier, inc=1, device_id=(plane, spot.w), device_id_type=MESH)
+        pl.semaphore_wait(barrier, 1)
+        start_all(second_expert)
+        start_weights(0, gu_ref, down_ref, (w1, (w2_early, w2_rest), w3), w_gu, w_down, gu_sum, down_sum, sems)
+
+    masks = [[pick(table_ref, s, e) for s in range(CHUNK)] for e in range(MINE)]
+    rows, grad_rows = [], []
     for s in range(CHUNK):
-        back = mm(hots[s], gated[s * SLOTS : (s + 1) * SLOTS], TN)
-        if e == 1:
-            back = back + y_before[s].astype(F32)
-        y_ref[s] = back.astype(BF16)
-
-    @pl.when(step == pl.num_programs(0) - 1)
+        hot = jnp.concatenate([jnp.where(masks[e][s], 1.0, 0.0) for e in range(MINE)], axis=0).astype(BF16)
+        rows.append(mm(hot, h2_ref[s]).astype(BF16))
+        grad_rows.append(mm(hot, dy_ref[s]).astype(BF16))
+    for s in range(CHUNK):
+        rows_ref[0, s * SLOTS : (s + 1) * SLOTS, :] = rows[s][SLOTS:]
+        grad_rows_ref[0, s * SLOTS : (s + 1) * SLOTS, :] = grad_rows[s][SLOTS:]
+    rows = jnp.concatenate([r[:SLOTS] for r in rows], axis=0)
+    grad_rows = jnp.concatenate([r[:SLOTS] for r in grad_rows], axis=0)
+    gated, dx, slot_dgate = expert_math(
+        rows, grad_rows, slot_gates(table_ref, masks[0], 0), w_gu, w_down, gu_sum, down_sum
+    )
+    gated_ref[0] = gated
+    dx_ref[0] = dx
+    dgate_ref[...] = jnp.zeros_like(dgate_ref)
+    token_dgate(dgate_ref, masks[0], slot_dgate, 0)
+
+    @pl.when(step == STEPS - 1)
     def _():
-        down_grad_ref[...] = down_sum[...].astype(BF16)
-
-
-STEPS = GROUP // CHUNK
+        store_quarters((own, mate, far, far_mate), gu_sum, down_sum)
+        for copy in second_expert:
+            copy.wait_send()
+            copy.wait_recv()
+
+
+def expert_1_kernel(
+    rows_ref, grad_rows_ref, gated_before, dx_before, dgate_before, table_ref, gu_ref, down_ref, w1, w2, w3,
+    y_ref, part_ref, dgate_ref, own, mate, far, far_mate,
+    w_gu, w_down, gu_sum, down_sum, sems,
+):
+    step = pl.program_id(0)
+
+    @pl.when(step == 0)
+    def _():
+        start_weights(1, gu_ref, down_ref, (w1, w2, w3), w_gu, w_down, gu_sum, down_sum, sems)
+
+    masks = [[pick(table_ref, s, e) for s in range(CHUNK)] for e in range(MINE)]
+    gated, dx, slot_dgate = expert_math(
+        rows_ref[0], grad_rows_ref[0], slot_gates(table_ref, masks[1], 1), w_gu, w_down, gu_sum, down_sum
+    )
+    dgate_ref[...] = dgate_before[...]
+    token_dgate(dgate_ref, masks[1], slot_dgate, 1)
+    for s in range(CHUNK):
+        at = slice(s * SLOTS, (s + 1) * SLOTS)
+        hot = jnp.concatenate([jnp.where(masks[e][s], 1.0, 0.0) for e in range(MINE)], axis=0).astype(BF16)
+        y_ref[s] = mm(hot, jnp.concatenate([gated_before[0, at, :], gated[at]], axis=0), TN).astype(BF16)
+        part_ref[s] = mm(hot, jnp.concatenate([dx_before[0, at, :], dx[at]], axis=0), TN).astype(BF16)
+
+    @pl.when(step == STEPS - 1)
+    def _():
+        store_quarters((own, mate, far, far_mate), gu_sum, down_sum)
 
 
 def expert_specs():
-    block = pl.BlockSpec((CHUNK, TOKENS, WIDTH), lambda c, *_: (c, 0, 0))
-    small = pl.BlockSpec((CHUNK, 8, TOKENS), lambda c, *_: (c, 0, 0))
-    slots = pl.BlockSpec((1, CHUNK * SLOTS, WIDTH), lambda c, *_: (c, 0, 0))
-    return block, small, slots
-
-
-def expert_call(e, h2_all, dy_all, table_all, pieces, before):
-    block, small, slots = expert_specs()
+    block = pl.BlockSpec((CHUNK, TOKENS, WIDTH), lambda c: (c, 0, 0))
+    small = pl.BlockSpec((CHUNK, 8, TOKENS), lambda c: (c, 0, 0))
+    slots = pl.BlockSpec((1, ROWS, WIDTH), lambda c: (c, 0, 0))
+    quarter = pl.BlockSpec((384, WIDTH), lambda c: (0, 0))
+    return block, small, slots, quarter
+
+
+def expert_scratch():
+    return [
+        pltpu.VMEM((WIDTH, 2 * FF), BF16),
+        pltpu.VMEM((FF, WIDTH), BF16),
+        pltpu.VMEM((WIDTH, 2 * FF), F32),
+        pltpu.VMEM((FF, WIDTH), F32),
+        pltpu.SemaphoreType.DMA((10,)),
+    ]
+
+
+SLOT_ROWS = jax.ShapeDtypeStruct((STEPS, ROWS, WIDTH), BF16)
+TOKEN_ROWS = jax.ShapeDtypeStruct((GROUP, TOKENS, WIDTH), BF16)
+TABLES = jax.ShapeDtypeStruct((GROUP, 8, TOKENS), F32)
+QUARTER = jax.ShapeDtypeStruct((384, WIDTH), BF16)
+
+
+def expert_0_call(h2_all, dy_all, table_all, w_gate_up, w_down, pieces):
+    block, small, slots, quarter = expert_specs()
     return pl.pallas_call(
-        functools.partial(expert_kernel, e),
-        name=f"expert_{e}",
+        expert_0_kernel,
+        name="expert_0",
         grid=(STEPS,),
-        out_shape=(
-            jax.ShapeDtypeStruct((STEPS, CHUNK * SLOTS, WIDTH), BF16),
-            jax.ShapeDtypeStruct((STEPS, CHUNK * SLOTS, 2 * FF), BF16),
-            jax.ShapeDtypeStruct((GROUP, TOKENS, WIDTH), BF16),
-            jax.ShapeDtypeStruct((GROUP, 8, TOKENS), F32),
-            jax.ShapeDtypeStruct((FF, WIDTH), BF16),
-        ),
-        in_specs=[block, block, small] + [IN_HBM] * 4 + ([block, small] if e else []),
-        out_specs=(slots, slots, block, small, pl.BlockSpec((FF, WIDTH), lambda c: (0, 0))),
-        scratch_shapes=[
-            pltpu.VMEM((WIDTH, 2 * FF), BF16),
-            pltpu.VMEM((FF, WIDTH), BF16),
-            pltpu.VMEM((FF, WIDTH), F32),
-            pltpu.SemaphoreType.DMA((8,)),
-        ],
+        out_shape=(SLOT_ROWS,) * 4 + (TABLES,) + (QUARTER,) * 5,
+        in_specs=[block, block, small] + [IN_HBM] * 6,
+        out_specs=(slots,) * 4 + (small,) + (quarter,) * 4 + (IN_HBM,),
+        scratch_shapes=expert_scratch() + [pltpu.SemaphoreType.DMA((2,)), pltpu.SemaphoreType.DMA((2,))],
+        compiler_params=pltpu.CompilerParams(collective_id=4, has_side_effects=True, vmem_limit_bytes=VMEM_BYTES),
+        cost_estimate=duration(1),
+    )(h2_all, dy_all, table_all, w_gate_up, w_down, *pieces)
+
+
+def expert_1_call(rows, grad_rows, gated, dx, dgate, table_all, w_gate_up, w_down, pieces):
+    block, small, slots, quarter = expert_specs()
+    return pl.pallas_call(
+        expert_1_kernel,
+        name="expert_1",
+        grid=(STEPS,),
+        out_shape=(TOKEN_ROWS,) * 2 + (TABLES,) + (QUARTER,) * 4,
+        in_specs=[slots] * 4 + [small, small] + [IN_HBM] * 5,
+        out_specs=(block, block, small) + (quarter,) * 4,
+        scratch_shapes=expert_scratch(),
         compiler_params=pltpu.CompilerParams(vmem_limit_bytes=VMEM_BYTES),
         cost_estimate=duration(1),
-    )(h2_all, dy_all, table_all, *pieces, *before)
-
-
-def weight_grad_kernel(n_ref, rows_ref, da_ref, down_ref, own, mate, far, far_mate):
-    step = pl.program_id(0)
-    rows = rows_ref[...].reshape(GROUP * SLOTS, WIDTH // NARROW)
-    da = da_ref[...].reshape(GROUP * SLOTS, 2 * FF)
-    grad = mm(rows, da, TN).astype(BF16)
-    for number, out in enumerate((own, mate, far, far_mate)):
-
-        @pl.when(step == number)
-        def _():
-            out[0:256, :] = grad
-            out[256:384, :] = down_ref[...]
-
-
-def weight_grad_call(e, n_row, rows, da, down_grad):
-    def quarter(step, n_ref):
-        n = n_ref[0]
-        mate = n + 1 - 2 * lax.rem(n, 2)
-        far = 2 - 4 * lax.div(n, 2)
-        return jnp.where(lax.rem(step, 2) == 1, mate, n) + jnp.where(step >= 2, far, 0)
-
-    whole = pl.BlockSpec((384, WIDTH), lambda j, n_ref: (0, 0))
+    )(rows, grad_rows, gated, dx, dgate, table_all, w_gate_up, w_down, *pieces)
+
+
+RESULTS = 6
+
+
+def results_kernel(*refs):
+    pieces, arrays, small = refs[:8], refs[8 : 8 + RESULTS], refs[8 + RESULTS : 11 + RESULTS]
+    refs = refs[11 + RESULTS :]
+    gate_up_ref, down_ref, outs, small_outs = refs[0], refs[1], refs[2 : 2 + RESULTS], refs[2 + RESULTS : 6 + RESULTS]
+    refs = refs[6 + RESULTS :]
+    loaded, totals, held, sems, out_sems, held_sems = refs[0], refs[1], refs[2 : 2 + RESULTS], *refs[2 + RESULTS :]
+    half = lax.rem(lax.axis_index("narrow"), 2)
+    loads = [pltpu.make_async_copy(piece, loaded.at[i], sems.at[i]) for i, piece in enumerate(pieces)]
+    through = [pltpu.make_async_copy(a, h, held_sems.at[i]) for i, (a, h) in enumerate(zip(arrays, held))]
+    start_all([loads[i] for i in (0, 2, 1, 3, 4, 6, 5, 7)])
+    start_all(through)
+    router, gains, load = small
+    small_outs[0][...] = router[...]
+    small_outs[1][...] = gains[0:1, :]
+    small_outs[2][...] = gains[1:2, :]
+    small_outs[3][...] = load[...]
+    stores = []
+    for e in range(2):
+        for which in range(2):
+            left, right = 4 * e + which, 4 * e + which + 2
+            loads[left].wait()
+            loads[right].wait()
+            number = 2 * e + which
+            place = 2 * (half if which == 0 else 1 - half) + e
+            totals[number] = loaded[left].astype(F32) + loaded[right].astype(F32)
+            for part, (out, first, depth) in enumerate(((gate_up_ref, 0, 256), (down_ref, 256, 128))):
+                copy = pltpu.make_async_copy(
+                    totals.at[number, pl.ds(first, depth)], out.at[place], out_sems.at[2 * number + part]
+                )
+                copy.start()
+                stores.append(copy)
+    for i, copy in enumerate(through):
+        copy.wait()
+        copy = pltpu.make_async_copy(held[i], outs[i], held_sems.at[i])
+        copy.start()
+        stores.append(copy)
+    for copy in stores:
+        copy.wait()
+
+
+def results_call(first, second, arrays, small):
+    shapes = [jax.ShapeDtypeStruct(a.shape, a.dtype) for a in arrays]
+    row = jax.ShapeDtypeStruct((1, 32), F32)
     return pl.pallas_call(
-        weight_grad_kernel,
-        name=f"weight_grad_{e}",
-        grid_spec=pltpu.PrefetchScalarGridSpec(
-            num_scalar_prefetch=1,
-            grid=(NARROW,),
-            in_specs=[
-                pl.BlockSpec((STEPS, CHUNK * SLOTS, 256), lambda j, n_ref: (0, 0, quarter(j, n_ref))),
-                pl.BlockSpec((STEPS, CHUNK * SLOTS, 2 * FF), lambda j, n_ref: (0, 0, 0)),
-                pl.BlockSpec((128, WIDTH), lambda j, n_ref: (quarter(j, n_ref), 0)),
-            ],
-            out_specs=(whole,) * 4,
-        ),
-        out_shape=(jax.ShapeDtypeStruct((384, WIDTH), BF16),) * 4,
-        compiler_params=pltpu.CompilerParams(vmem_limit_bytes=VMEM_BYTES),
-        cost_estimate=duration(1),
-    )(n_row, rows, da, down_grad)
-
-
-def rows_grad_kernel(e, *refs):
-    if e == 0:
-        da_ref, table_ref, w0, w1, w2, w3, out_ref, w_gu, sems = refs
-    else:
-        da_ref, table_ref, w0, w1, w2, w3, before, out_ref, w_gu, sems = refs
-    step = pl.program_id(0)
-
-    @pl.when(step == 0)
-    def _():
-        copies = load_quarters((w0, w1, w2, w3), w_gu, 0, 256, sems, 0)
-        for copy in copies:
-            copy.start()
-        for copy in copies:
-            copy.wait()
-
-    grads = mm(da_ref[0], w_gu[...], NT).astype(BF16)
-    for s in range(CHUNK):
-        hot = jnp.where(pick(table_ref, s, e), 1.0, 0.0).astype(BF16)
-        back = mm(hot, grads[s * SLOTS : (s + 1) * SLOTS], TN)
-        if e == 1:
-            back = back + before[s].astype(F32)
-        out_ref[s] = back.astype(BF16)
-
-
-def rows_grad_call(e, da, table_all, pieces, before):
-    block, small, slots = expert_specs()
-    return pl.pallas_call(
-        functools.partial(rows_grad_kernel, e),
-        name=f"rows_grad_{e}",
-        grid=(STEPS,),
-        out_shape=jax.ShapeDtypeStruct((GROUP, TOKENS, WIDTH), BF16),
-        in_specs=[slots, small] + [IN_HBM] * 4 + ([block] if e else []),
-        out_specs=block,
-        scratch_shapes=[pltpu.VMEM((WIDTH, 2 * FF), BF16), pltpu.SemaphoreType.DMA((4,))],
-        compiler_params=pltpu.CompilerParams(vmem_limit_bytes=VMEM_BYTES),
-        cost_estimate=duration(1),
-    )(da, table_all, *pieces, *before)
-
-
-def owner_sum_kernel(half_ref, own, mate, far, far_mate, *refs):
-    gate_up_ref, down_ref = refs[-2:]
-    first, second = (own, far), (mate, far_mate)
-    for step, (left, right) in enumerate((first, second)):
-
-        @pl.when(pl.program_id(0) == step)
-        def _():
-            total = left[...].astype(F32) + right[...].astype(F32)
-            gate_up_ref[0] = total[0:256]
-            down_ref[0] = total[256:384]
-
-
-def owner_sum_call(e, half_row, parts, before, after):
-    def place(step, half_ref):
-        return (2 * lax.rem(half_ref[0] + step, 2) + e, 0, 0)
-
-    whole = pl.BlockSpec((384, WIDTH), lambda j, half_ref: (0, 0))
-    return pl.pallas_call(
-        owner_sum_kernel,
-        name=f"owner_sum_{e}",
-        grid_spec=pltpu.PrefetchScalarGridSpec(
-            num_scalar_prefetch=1,
-            grid=(2,),
-            in_specs=[whole] * 4 + [IN_HBM] * (len(before) + 1),
-            out_specs=(pl.BlockSpec((1, 256, WIDTH), place), pl.BlockSpec((1, 128, WIDTH), place)),
-        ),
+        results_kernel,
+        name="results",
         out_shape=(
             jax.ShapeDtypeStruct((4, 256, WIDTH), F32),
             jax.ShapeDtypeStruct((4, 128, WIDTH), F32),
+            *shapes,
+            jax.ShapeDtypeStruct((32, 32), F32),
+            row,
+            row,
+            jax.ShapeDtypeStruct((1, 32), jnp.int32),
         ),
-        input_output_aliases={6: 0, 7: 1} if before else {},
+        in_specs=[IN_HBM] * (8 + RESULTS) + [IN_VMEM] * 3,
+        out_specs=(IN_HBM,) * (2 + RESULTS) + (IN_VMEM,) * 4,
+        scratch_shapes=[pltpu.VMEM((8, 384, WIDTH), BF16), pltpu.VMEM((4, 384, WIDTH), F32)]
+        + [pltpu.VMEM(s.shape, s.dtype) for s in shapes]
+        + [pltpu.SemaphoreType.DMA((8,)), pltpu.SemaphoreType.DMA((8,)), pltpu.SemaphoreType.DMA((RESULTS,))],
         compiler_params=pltpu.CompilerParams(vmem_limit_bytes=VMEM_BYTES),
         cost_estimate=duration(1),
-    )(half_row, *parts, after, *before)
+    )(*first, *second, *arrays, *small)
 
 
 def widen(ref_value):
@@ -1303,22 +1393,27 @@
     def begin(self):
         s = self.spot
         self.loads = []
-        for q in range(4):
-            self.put(self.part(2 * q + 1 - s.core), self.from_core.at[q], q, s.sib)
-            copy = pltpu.make_async_copy(self.part(2 * q + s.core), self.acc.at[q], self.local.at[q])
+        for number, q in enumerate((self.q_d, self.q_x, self.q_y, self.q_own)):
+            self.put(self.part(2 * q + 1 - s.core), self.from_core.at[q], number, s.sib)
+            copy = pltpu.make_async_copy(self.part(2 * q + s.core), self.acc.at[q], self.local.at[number])
             copy.start()
             self.loads.append(copy)
 
+    def add_core(self, number, q):
+        self.loads[number].wait()
+        self.got(self.from_core.at[q], number)
+        self.acc[q] = (widen(self.acc[q]) + widen(self.from_core[q])).astype(BF16)
+
     def across_core(self):
         s = self.spot
-        for q in range(4):
-            self.loads[q].wait()
-            self.got(self.from_core.at[q], q)
-            self.acc[q] = (widen(self.acc[q]) + widen(self.from_core[q])).astype(BF16)
+        self.add_core(0, self.q_d)
         self.put(halves(self.acc.at[self.q_d], 0), self.from_one.at[1], 5, s.xn)
         self.put(halves(self.acc.at[self.q_d], 1), self.from_one.at[3], 7, s.yn)
+        self.add_core(1, self.q_x)
         self.put(halves(self.acc.at[self.q_x], 0), self.from_one.at[0], 4, s.xn)
+        self.add_core(2, self.q_y)
         self.put(halves(self.acc.at[self.q_y], 1), self.from_one.at[2], 6, s.yn)
+        self.add_core(3, self.q_own)
 
     def across_one(self):
         s = self.spot
@@ -1408,9 +1503,9 @@
 
 
 class AttentionBack:
-    def __init__(self, dattn_all, w_rows, qkv_ref, lse_ref, o_ref, angle_ref, start_ref, dqkv_ref, dkv_ref, dq_ref, osum):
+    def __init__(self, dattn_all, w_rows, qkv_ref, lse_ref, o_ref, angle_ref, dqkv_ref, dkv_ref, dq_ref, osum):
         self.dattn_all, self.w_rows, self.qkv, self.lse, self.o = dattn_all, w_rows, qkv_ref, lse_ref, o_ref
-        self.angle, self.start = angle_ref, start_ref
+        self.angle = angle_ref
         self.dqkv, self.dkv, self.dq, self.osum = dqkv_ref, dkv_ref, dq_ref, osum
         self.first_half = lane_half()
         self.is_key = lax.broadcasted_iota(jnp.int32, (1, 128), 1) < 64
@@ -1438,7 +1533,7 @@
         query = self.stack(self.qkv[row, tokens, 0:128])
         do = self.stack(do)
         log_total = jnp.concatenate([self.lse[row, tokens, 0:1], self.lse[row, tokens, 64:65]], axis=0)
-        start = self.start[row, tokens, 0:1]
+        start = self.lse[row, tokens, 32:33]
         start = jnp.concatenate([start, start], axis=0)
         place = lax.broadcasted_iota(jnp.int32, (256, 1), 0)
         place_query = (jnp.concatenate([place, place], axis=0) + q * 256).astype(F32)
@@ -1477,17 +1572,20 @@
 def backward_kernel(*refs):
     (
         part_ref, y_ref, dgate_ref, h2_ref, w_out_ref, w_full_ref, h1_ref, qkv_ref, lse_ref, o_ref,
-        angle_ref, start_ref, x_ref, mid_ref, gate_ref, gain_ref, dy_ref,
-    ) = refs[:17]
-    block_out, in_grad, q_grad, k_grad, v_grad, o_grad, sums, gain_sum = refs[17:25]
+        angle_ref, mate_1, far_1, far_mate_1,
+        x_ref, mid_ref, gate_ref, gain_ref, dy_ref, w_own, gain_col,
+    ) = refs[:21]
+    (
+        block_out, in_grad, q_grad, k_grad, v_grad, o_grad, router_grad, two_gains, load_out, *quarters_recv,
+    ) = refs[21:33]
     (
         dgate_all, h2_own, dattn_all, dmid_ref, small_ref, small_all, small_sum, w_router, w_rows, w_full,
-        h1, qkv, lse, outs, angle, start, dqkv_ref, dkv_ref, dq_ref, osum, og_ref, wg_ref,
-        dq_full, w_recv, o_recv, s_recv, gain_own, g_recv,
-        ts, tr, s0, r0, bs, br, qs, qr, ws, wr, os, orv, ss, sr, gs, gr, local,
-    ) = refs[25:70]
-    h2_sum_refs = refs[70 : 70 + REDUCE_REFS]
-    y_sum_refs = refs[70 + REDUCE_REFS :]
+        h1, qkv, lse, outs, angle, dqkv_ref, dkv_ref, dq_ref, osum, og_ref, wg_ref,
+        dq_full, w_recv, o_recv, s_recv,
+        ts, tr, s0, r0, bs, br, qs, qr, ks, kr, ws, wr, os, orv, ss, sr, gs, gr, local,
+    ) = refs[33:77]
+    h2_sum_refs = refs[77 : 77 + REDUCE_REFS]
+    y_sum_refs = refs[77 + REDUCE_REFS :]
 
     spot = Spot()
     everyone = NARROW * WIDE
@@ -1523,21 +1621,24 @@
         (lse_ref, lse),
         (o_ref, outs),
         (angle_ref, angle),
-        (start_ref, start),
         (h1_ref, h1),
     ]
     loads = [pltpu.make_async_copy(src, dst, local.at[i]) for i, (src, dst) in enumerate(loads)]
-    for copy in loads:
-        copy.start()
-    w_loads = [pltpu.make_async_copy(w_full_ref.at[who], w_full.at[:, who], local.at[10 + who]) for who in range(WIDE)]
-    for copy in w_loads:
-        copy.start()
+    w_loads = [pltpu.make_async_copy(w_full_ref.at[who], w_full.at[who], local.at[10 + who]) for who in range(WIDE)]
+    h2_sum.across_core()
+    start_all(loads + w_loads)
     y_sum.begin()
-    h2_sum.across_core()
+    far_plane = 2 - 4 * lax.div(spot.n, 2)
+    quarter_copies = [
+        remote(piece, quarters_recv[number], gs.at[number], gr.at[number], (plane, spot.w))
+        for number, (piece, plane) in enumerate(
+            ((mate_1, spot.mate), (far_1, spot.n + far_plane), (far_mate_1, spot.mate + far_plane))
+        )
+    ]
     h2_sum.across_one()
     h2_sum.to_mate()
-    y_sum.across_core()
     h2_sum.finish()
+    start_all(quarter_copies)
 
     def wait_table(step, carry):
         tables(step, False).wait_send()
@@ -1591,90 +1692,78 @@
     lax.fori_loop(1, WIDE, start_lanes, 0)
     small_all[spot.w] = small_ref[:, pl.ds(pl.multiple_of(spot.w * 128, 128), 128)]
 
-    for copy in loads[4:9]:
+    for copy in loads[4:8]:
         copy.wait()
-    back = AttentionBack(dattn_all, w_rows, qkv, lse, outs, angle, start, dqkv_ref, dkv_ref, dq_ref, osum)
+    back = AttentionBack(dattn_all, w_rows, qkv, lse, outs, angle, dqkv_ref, dkv_ref, dq_ref, osum)
     order = h2_sum.ours
+    sib_x = spot.sib + 2 - 4 * spot.x
+    sib_y = spot.sib + 4 - 8 * spot.y
+    sib_d = sib_x + 4 - 8 * spot.y
+
+    def to_tokens(other, place, first, send, recv):
+        return remote(
+            dqkv_ref.at[:, pl.ds(pl.multiple_of(other * SPAN, SPAN), SPAN), pl.ds(first, 128)],
+            dq_full.at[:, :, pl.ds(pl.multiple_of(place * 256 + first, 128), 128)],
+            send.at[other], recv.at[place], spot.wide(other),
+        )
+
+    def send_queries(who):
+        for other in who:
+            to_tokens(other, spot.w, 0, qs, qr).start()
+
     gather.got(spot.sib, None, 4)
     back.chunk(0, order.q_own)
     gather.middle()
     back.chunk(1, order.q_own)
+    send_queries((spot.sib,))
     gather.late()
-    gather.last()
-    sib_x = spot.sib + 2 - 4 * spot.x
-    sib_y = spot.sib + 4 - 8 * spot.y
     gather.got(sib_x, None, 7)
     back.chunk(0, order.q_x)
+    gather.last()
+    y_sum.across_core()
     back.chunk(1, order.q_x)
-    y_sum.across_one()
+    send_queries((spot.xn, sib_x))
     gather.got(sib_y, None, 8)
     back.chunk(0, order.q_y)
     back.chunk(1, order.q_y)
-    y_sum.to_mate()
-    sib_d = sib_x + 4 - 8 * spot.y
+    send_queries((spot.yn, sib_y))
     gather.got(sib_d, 0, 9)
     gather.got(sib_d, 1, 10)
     back.chunk(0, order.q_d)
     back.chunk(1, order.q_d)
+    send_queries((spot.diag, sib_d))
     for copy in gather.started:
         copy.wait_send()
     back.keys(0)
     back.keys(1)
 
-    def to_plane(step, arriving):
-        other = lax.rem(spot.w + step, WIDE)
-        place = other if arriving else spot.w
-        return remote(
-            dqkv_ref.at[:, pl.ds(pl.multiple_of(other * SPAN, SPAN), SPAN), :],
-            dq_full.at[:, :, pl.ds(pl.multiple_of(place * 256, 256), 256)],
-            qs.at[other], qr.at[place], spot.wide(other),
-        )
-
     def others(step):
         other = lax.rem(spot.me + step, everyone)
         return other, (lax.div(other, WIDE), lax.rem(other, WIDE))
 
     def rows_of(ref, owner):
         return ref.at[pl.ds(pl.multiple_of(owner * 32, 32), 32)]
-
-    def lanes_of(ref, owner):
-        return ref.at[:, pl.ds(pl.multiple_of(lax.div(owner, 4) * 128, 128), 128)]
 
     def to_owner(step, arriving):
         other, to = others(step)
         place = other if arriving else spot.me
         return remote(rows_of(wg_ref, other), w_recv.at[place], ws.at[other], wr.at[place], to)
 
-    def gain_to_owner(step, arriving):
-        other, to = others(step)
-        place = other if arriving else spot.me
-        return remote(lanes_of(gain_own, other), g_recv.at[place], gs.at[other], gr.at[place], to)
-
-    def start_plane(step, carry):
-        to_plane(step, False).start()
-        return carry
-
     def start_owner(step, carry):
         to_owner(step, False).start()
         return carry
 
-    def start_gain(step, carry):
-        gain_to_owner(step, False).start()
+    def start_keys(step, carry):
+        to_tokens(lax.rem(spot.w + step, WIDE), spot.w, 128, ks, kr).start()
         return carry
 
-    lax.fori_loop(1, WIDE, start_plane, 0)
+    lax.fori_loop(1, WIDE, start_keys, 0)
     plane_mine = pltpu.make_async_copy(
         dqkv_ref.at[:, pl.ds(pl.multiple_of(spot.w * SPAN, SPAN), SPAN), :],
         dq_full.at[:, :, pl.ds(pl.multiple_of(spot.w * 256, 256), 256)],
         local.at[0],
     )
     plane_mine.start()
-
-    loads[9].wait()
-    wg_ref[...] = (mm(h1[0], dqkv_ref[0], TN) + mm(h1[1], dqkv_ref[1], TN)).astype(BF16)
-    lax.fori_loop(1, everyone, start_owner, 0)
-    owner_mine = pltpu.make_async_copy(rows_of(wg_ref, spot.me), w_recv.at[spot.me], local.at[1])
-    owner_mine.start()
     og_ref[...] = osum[...].astype(BF16)
 
     def wait_lanes(step, carry):
@@ -1687,7 +1776,6 @@
     for device in range(1, WIDE):
         lane_total = lane_total + small_all[device]
     small_sum[...] = lane_total
-
     def output_copies(act_local, act_send, act_recv):
         for i in range(4):
             owner = 4 * spot.w + i
@@ -1720,24 +1808,32 @@
         return None
 
     output_copies(lambda c: c.start(), lambda c: c.start(), nothing)
+    y_sum.across_one()
+
+    loads[8].wait()
+    wg_ref[...] = (mm(h1[0], dqkv_ref[0], TN) + mm(h1[1], dqkv_ref[1], TN)).astype(BF16)
+    lax.fori_loop(1, everyone, start_owner, 0)
+    owner_mine = pltpu.make_async_copy(rows_of(wg_ref, spot.me), w_recv.at[spot.me], local.at[1])
+    owner_mine.start()
+    y_sum.to_mate()
 
     def wait_plane(step, carry):
-        to_plane(step, False).wait_send()
-        to_plane(step, True).wait_recv()
+        other = lax.rem(spot.w + step, WIDE)
+        for first, send, recv in ((0, qs, qr), (128, ks, kr)):
+            to_tokens(other, spot.w, first, send, recv).wait_send()
+            to_tokens(other, other, first, send, recv).wait_recv()
         return carry
 
     lax.fori_loop(1, WIDE, wait_plane, 0)
     plane_mine.wait()
     for copy in w_loads:
         copy.wait()
-    dh1 = mm(dq_full[...].reshape(TOKENS, 2 * WIDTH), w_full[...].reshape(WIDTH, 2 * WIDTH), NT)
+    dh1 = jnp.zeros((TOKENS, WIDTH), F32)
+    for who in range(WIDE):
+        grads = dq_full[:, :, 256 * who : 256 * who + 256].reshape(TOKENS, 256)
+        dh1 = dh1 + mm(grads, w_full[who], NT)
     x = x_ref[...].astype(F32)
     scale = lax.rsqrt(jnp.mean(x * x, axis=1, keepdims=True) + EPSILON)
-    gain_own[0:1, :] = jnp.sum(dh1 * x * scale, axis=0, keepdims=True)
-    gain_own[1:8, :] = jnp.zeros((7, WIDTH), F32)
-    lax.fori_loop(1, everyone, start_gain, 0)
-    gain_mine = pltpu.make_async_copy(lanes_of(gain_own, spot.me), g_recv.at[spot.me], local.at[0])
-    gain_mine.start()
     weighted = dh1 * gain_ref[0:1, :]
     inner = jnp.mean(weighted * x, axis=1, keepdims=True)
     in_grad[...] = (dmid_ref[...] + weighted * scale - x * (scale * scale * scale) * inner).astype(BF16)
@@ -1752,6 +1848,7 @@
     lax.fori_loop(1, everyone, wait_owner, 0)
     owner_mine.wait()
     output_copies(lambda c: c.wait(), lambda c: c.wait_send(), lambda c: c.wait_recv())
+    gain_total = jnp.zeros((32, 1), F32)
     for w in range(WIDE):
         total = widen(w_recv[w])
         for plane in range(1, NARROW):
@@ -1759,6 +1856,8 @@
         q_grad[:, 128 * w : 128 * w + 128] = total[:, 0:128]
         k_grad[:, 64 * w : 64 * w + 64] = total[:, 128:192]
         v_grad[:, 64 * w : 64 * w + 64] = total[:, 192:256]
+        gain_total += jnp.sum(total * widen(w_own[:, 256 * w : 256 * w + 256]), axis=1, keepdims=True)
+    gain_total = gain_total / gain_col[...].astype(F32)
     total = widen(o_recv[0])
     for plane in range(1, NARROW):
         total = total + widen(o_recv[plane])
@@ -1766,19 +1865,20 @@
     total = s_recv[0]
     for plane in range(1, NARROW):
         total = total + s_recv[plane]
-    sums[...] = total
-
-    def wait_gain(step, carry):
-        gain_to_owner(step, False).wait_send()
-        gain_to_owner(step, True).wait_recv()
-        return carry
-
-    lax.fori_loop(1, everyone, wait_gain, 0)
-    gain_mine.wait()
-    total = g_recv[0]
-    for device in range(1, everyone):
-        total = total + g_recv[device]
-    gain_sum[...] = total
+    load_out[...] = total[33:34, 0:32].astype(jnp.int32)
+    lane = lax.rem(spot.me, 4)
+    mine = jnp.zeros((40, 32), F32)
+    for part in range(4):
+        mine = mine + jnp.where(lane == part, 1.0, 0.0) * total[:, 32 * part : 32 * part + 32]
+    square = jnp.concatenate([mine, jnp.zeros((40, 96), F32)], axis=1)
+    square = jnp.concatenate([square, jnp.zeros((88, 128), F32)], axis=0)
+    router_grad[...] = jnp.transpose(square)[0:32, 0:32]
+    column = jnp.concatenate([jnp.broadcast_to(gain_total, (32, 128)), jnp.zeros((96, 128), F32)], axis=0)
+    two_gains[...] = jnp.concatenate([jnp.transpose(column)[0:1, 0:32], mine[32:33]], axis=0)
+
+    for copy in quarter_copies:
+        copy.wait_send()
+        copy.wait_recv()
 
 
 def backward_call(*operands):
@@ -1796,11 +1896,13 @@
             jax.ShapeDtypeStruct((32, WIDTH // 2), F32),
             jax.ShapeDtypeStruct((32, WIDTH // 2), F32),
             jax.ShapeDtypeStruct((32, WIDTH), F32),
-            jax.ShapeDtypeStruct((40, 128), F32),
-            jax.ShapeDtypeStruct((8, 128), F32),
-        ),
-        in_specs=[IN_HBM] * 12 + [IN_VMEM] * 5,
-        out_specs=(IN_VMEM,) * 8,
+            jax.ShapeDtypeStruct((32, 32), F32),
+            jax.ShapeDtypeStruct((2, 32), F32),
+            jax.ShapeDtypeStruct((1, 32), jnp.int32),
+        )
+        + (QUARTER,) * 3,
+        in_specs=[IN_HBM] * 14 + [IN_VMEM] * 7,
+        out_specs=(IN_VMEM,) * 9 + (IN_HBM,) * 3,
         scratch_shapes=[
             vmem((GROUP, 8, TOKENS), F32),
             vmem((TOKENS, WIDTH), BF16),
@@ -1811,13 +1913,12 @@
             vmem((40, 128), F32),
             vmem((WIDTH, 128), BF16),
             vmem((128, WIDTH), BF16),
-            vmem((NARROW, WIDE, 32, 2 * WIDTH), BF16),
+            vmem((WIDE, WIDTH, 256), BF16),
             vmem((2, SEQ, WIDTH), BF16),
             vmem((2, SEQ, 256), BF16),
             vmem((2, SEQ, 128), F32),
             vmem((2, SEQ, 128), BF16),
             vmem((2, SEQ, 256), F32),
-            vmem((2, SEQ, 128), F32),
             vmem((2, SEQ, 256), BF16),
             vmem((2, SEQ, 128), F32),
             vmem((512, HEAD_DIM), F32),
@@ -1828,12 +1929,12 @@
             vmem((everyone, 32, 256), BF16),
             vmem((NARROW, 32, WIDTH), BF16),
             vmem((NARROW, 40, 128), F32),
-            vmem((8, WIDTH), F32),
-            vmem((everyone, 8, 128), F32),
             dma((GROUP,)),
             dma((GROUP,)),
             dma((copies,)),
             dma((copies,)),
+            dma((WIDE,)),
+            dma((WIDE,)),
             dma((WIDE,)),
             dma((WIDE,)),
             dma((WIDE,)),
@@ -1844,8 +1945,8 @@
             dma((NARROW,)),
             dma((4,)),
             dma((NARROW,)),
-            dma((everyone,)),
-            dma((everyone,)),
+            dma((3,)),
+            dma((3,)),
             dma((18,)),
         ]
         + reduce_scratch()
@@ -1857,19 +1958,6 @@
 
 def swap(values, distance):
     return lax.ppermute(values, "narrow", [(i, i ^ distance) for i in range(NARROW)])
-
-
-def expert_pieces(w_gate_up, w_down, e, half):
-    def piece(pair):
-        return jnp.concatenate(
-            [
-                lax.dynamic_index_in_dim(w_gate_up, 2 * pair + e, 0, keepdims=False),
-                lax.dynamic_index_in_dim(w_down, 2 * pair + e, 0, keepdims=False),
-            ],
-            axis=0,
-        )
-
-    return piece(half), piece(1 - half)
 
 
 def position_tables():
@@ -1890,75 +1978,59 @@
     me = n * WIDE + w
     cos_table, sin_table, freq = position_tables()
 
-    wo_own = jnp.concatenate([w_output, w_router, jnp.zeros((32, 96), BF16)], axis=1)
     x_own = hidden_in.reshape(TOKENS, WIDTH)
     dy_own = out_grad.reshape(TOKENS, WIDTH)
-    w_own = jnp.concatenate(
-        [w_query.reshape(32, WIDE, 128), w_key.reshape(32, WIDE, 64), w_value.reshape(32, WIDE, 64)], axis=2
-    ).reshape(32, 2 * WIDTH)
-    gains = jnp.concatenate([attn_gain[None], moe_gain[None]], axis=0).astype(F32)
-    g_own = jnp.pad(gains, ((0, 6), (0, 96)))
-    seg_own = jnp.pad(seg_ids, ((0, 6), (0, 0)))
-    ids = expert_ids.reshape(TOKENS, TOP).T
-
-    x_all, w_all, g_all, seg_all, wo_block, dy_pair = gather_call(x_own, w_own, g_own, seg_own, wo_own, dy_own)
-    w_gate_up, w_down, x_all, dy_pair = lax.optimization_barrier((w_gate_up, w_down, x_all, dy_pair))
-    own_0, other_0 = expert_pieces(w_gate_up, w_down, 0, half)
-    own_1, other_1 = expert_pieces(w_gate_up, w_down, 1, half)
-    pieces_0 = (own_0, swap(other_0, 1), swap(own_0, 2), swap(other_0, 3))
+    ids = expert_ids.reshape(TOKENS, TOP)
+    x_all, w_all, g_all, seg_all, wo_block, dy_pair, far_early_0, w_own = gather_call(
+        x_own, dy_own, seg_ids, w_query, w_key, w_value, w_output, w_router,
+        attn_gain.reshape(1, 32), moe_gain.reshape(1, 32), w_gate_up,
+    )
     (
-        h1, qkv, lse, o_heads, angle, start, gain_rows, mid, gate, w_out, h2_all, dy_all, table_all, wq_block,
-        far_1, mate_1,
+        h1, qkv, lse, o_heads, angle, gain_rows, mid, gate, w_out, h2_all, dy_all, table_all,
+        mate_0, far_rest_0, far_mate_0, mate_1, far_1,
     ) = forward_call(
-        x_all, w_all, g_all, seg_all, cos_table, sin_table, freq, wo_block, ids, dy_pair, w_own, own_1, other_1
+        x_all, w_all, g_all, seg_all, cos_table, sin_table, freq, wo_block, ids, dy_pair, w_gate_up, w_down
     )
     w_out = w_out.reshape(WIDTH, WIDTH + 128)
-    other_1, h2_all = lax.optimization_barrier((other_1, h2_all))
-    pieces_1 = (own_1, mate_1, far_1, swap(other_1, 3))
-    n_row = n.reshape(1).astype(jnp.int32)
-    half_row = half.reshape(1).astype(jnp.int32)
-
-    def send_grads(e, rows, da, down_grad):
-        own, mate, far, far_mate = weight_grad_call(e, n_row, rows, da, down_grad)
-        own, da = lax.optimization_barrier((own, da))
-        return da, (own, swap(mate, 1), swap(far, 2), swap(far_mate, 3))
-
-    rows_0, da_0, y_0, dgate_0, down_grad_0 = expert_call(0, h2_all, dy_all, table_all, pieces_0, ())
-    rows_0, wq_block = lax.optimization_barrier((rows_0, wq_block))
-    w_full = lax.all_gather(wq_block, "wide", axis=0, tiled=False)
-    da_0, grads_0 = send_grads(0, rows_0, da_0, down_grad_0)
-    part_0 = rows_grad_call(0, da_0, table_all, pieces_0, ())
-    pieces_1, part_0, own_0 = lax.optimization_barrier((pieces_1, part_0, grads_0[0]))
-    grads_0 = (own_0,) + grads_0[1:]
-    rows_1, da_1, y_1, dgate, down_grad_1 = expert_call(
-        1, h2_all, dy_all, table_all, pieces_1, (y_0, dgate_0)
-    )
-    da_1, grads_1 = send_grads(1, rows_1, da_1, down_grad_1)
-    part = rows_grad_call(1, da_1, table_all, pieces_1, (part_0,))
-    block_out, in_grad, q_grad, k_grad, v_grad, o_grad, sums, gain_sum = backward_call(
-        part, y_1, dgate, h2_all, w_out, w_full, h1, qkv, lse, o_heads, angle, start,
-        x_own, mid, gate, gain_rows, dy_own,
-    )
-    sums_0 = owner_sum_call(0, half_row, grads_0, (), gain_sum)
-    gate_up_sum, down_sum = owner_sum_call(1, half_row, grads_1, sums_0, gain_sum)
-    lanes = (me % 4) * 32
-    router_grad = lax.dynamic_slice(sums, (0, lanes), (32, 32)).T
-    moe_gain_grad = lax.dynamic_slice(sums, (32, lanes), (1, 32)).reshape(32)
-    attn_gain_grad = lax.dynamic_slice(gain_sum, (0, lanes), (1, 32)).reshape(32)
-    expert_load = sums[33, 0:32].astype(jnp.int32)
+
+    def send_grads(own, mate, far, far_mate):
+        return own, swap(mate, 1), swap(far, 2), swap(far_mate, 3)
+
+    gated_0, dx_0, rows_1, grad_rows_1, dgate_0, *grads_0, far_mate_1 = expert_0_call(
+        h2_all, dy_all, table_all, w_gate_up, w_down, (mate_0, far_early_0, far_rest_0, far_mate_0)
+    )
+    dgate_0, w_heads = lax.optimization_barrier((dgate_0, w_all))
+    w_full = lax.all_gather(w_heads.reshape(WIDTH, 256), "wide", axis=0, tiled=False)
+    grads_0 = send_grads(*grads_0)
+    y, part, dgate, *grads_1 = expert_1_call(
+        rows_1, grad_rows_1, gated_0, dx_0, dgate_0, table_all, w_gate_up, w_down, (mate_1, far_1, far_mate_1)
+    )
+    (
+        block_out, in_grad, q_grad, k_grad, v_grad, o_grad, router_grad, two_gains, load, *arrived_1,
+    ) = backward_call(
+        part, y, dgate, h2_all, w_out, w_full, h1, qkv, lse, o_heads, angle, *grads_1[1:],
+        x_own, mid, gate, gain_rows, dy_own, w_own, attn_gain.reshape(32, 1),
+    )
+    (
+        gate_up_sum, down_sum, block_out, in_grad, q_grad, k_grad, v_grad, o_grad,
+        router_grad, attn_gain_grad, moe_gain_grad, load,
+    ) = results_call(
+        grads_0, (grads_1[0], *arrived_1),
+        (block_out, in_grad, q_grad, k_grad, v_grad, o_grad), (router_grad, two_gains, load),
+    )
     return (
         block_out.reshape(hidden_in.shape),
         in_grad.reshape(hidden_in.shape),
-        attn_gain_grad,
+        attn_gain_grad.reshape(32),
         q_grad,
         k_grad,
         v_grad,
         o_grad,
-        moe_gain_grad,
+        moe_gain_grad.reshape(32),
         router_grad,
         gate_up_sum,
         down_sum,
-        expert_load,
+        load.reshape(32),
     )
 
 

time: 475 us -> 424 us (0.89)
  Pallas kernels: 400 us -> 381 us
  local copies, waits for them, and re-layouts: 18 us -> 3.57 us
  starting transfers between devices: 28.4 us -> 14.6 us
    pallas_call x8 -> x3, Pallas kernels: 89.7 us -> 64.5 us  [the longest x1 28.8 us: expert_1_call(): pl.pallas_call(expert_1_kernel, name='expert_1', grid=(STEPS,), out_shape...]
    ppermute x10 -> x3, starting transfers between devices: 28.4 us -> 14.5 us  [swap(): lax.ppermute(values, 'narrow', [(i, i ^ distance) for i in range(NARROW)])]
    pallas_call x1, Pallas kernels: 38.2 us -> 47.2 us  [gather_call(): pl.pallas_call(gather_kernel, name='gather_inputs', out_shape=(jax.ShapeD...]
    unnamed x45 -> x9, local copies, waits for them, and re-layouts: 11.1 us -> 2.88 us
  transfers between devices with their start and end apart: 11 -> 4, of which waited for: 0 -> 1; matrix products, arithmetic and copies ran while one was open for 1% -> 0% of each run, Pallas kernels for 72% -> 44%
where the time goes in v3:
time: 424 us; the launch traced here: 417 us
  Pallas kernels  381 us (90%)
  starting transfers between devices  14.6 us (3%)
  between operations  14.6 us (3%)
    pallas_call x1, Pallas kernels, backward_call(): pl.pallas_call(backward_kernel, name='backward', out_shape=(jax.ShapeDtyp...  153 us
    pallas_call x1, Pallas kernels, forward_call(): pl.pallas_call(forward_kernel, name='forward', out_shape=(jax.ShapeDtypeS...  116 us
    pallas_call x1, Pallas kernels, gather_call(): pl.pallas_call(gather_kernel, name='gather_inputs', out_shape=(jax.ShapeD...  47.2 us
    pallas_call x1, Pallas kernels, expert_1_call(): pl.pallas_call(expert_1_kernel, name='expert_1', grid=(STEPS,), out_shape...  28.8 us
    pallas_call x1, Pallas kernels, expert_0_call(): pl.pallas_call(expert_0_kernel, name='expert_0', grid=(STEPS,), out_shape...  28 us
    ppermute x3, starting transfers between devices, swap(): lax.ppermute(values, 'narrow', [(i, i ^ distance) for i in range(NARROW)])  14.5 us
  transfers between devices with their start and end apart: 4, of which 1 were waited for; matrix products, arithmetic and copies ran while one was open for 0% of the time, Pallas kernels for 44%

profile of v3, /device:TPU:0, one launch (start us, length us, event | category | flops | bytes accessed | tf_op | source)
XLA Modules:
  0.0 416.5 jit_solution(978739037499645704)
XLA Ops:
  7.2 0.0 all-gather.2.cloned.1.call-start
  7.2 1.5 copy.30
  8.7 47.2 %gather_inputs.1 = (bf16[8,256,1024]{2,1,0:T(8,128)(2,1)}, bf16[32,32,256]{2,1,0:T(8,128)(2,1)}, f32[32,8,128]{2,1,0:T(8,128)}, s32[8,8,128]{2,1,0:T(8,128)}, bf...) custom-call(bf16[256,1024]{1,0:T(8,128)(2,1)} %bitcast.17, ...), custom_call_target="tpu_custom_call" | custom-call | flops 1000000000 | bytes 3600000 | tf_op jit(solution)/shard_map/gather_inputs/pallas_call | solution.py:695
  55.9 116.4 %forward.1 = (bf16[2,1024,1024]{2,1,0:T(8,128)(2,1)}, bf16[2,1024,256]{2,1,0:T(8,128)(2,1)}, f32[2,1024,128]{2,1,0:T(8,128)}, bf16[2,1024,128]{2,1,0:T(8,128)(2,...) custom-call(bf16[8,2,128,1024]{3,2,1,0:T(8,128)(2,1)} %bitcast.14, ...), custom_call_target="tpu_custom_call" | custom-call | flops 1000000000 | bytes 3600000 | tf_op jit(solution)/shard_map/forward/pallas_call | solution.py:1044
  172.3 0.0 copy-start.3
  172.3 28.0 %expert_0.1 = (bf16[4,320,1024]{2,1,0:T(8,128)(2,1)}, bf16[4,320,1024]{2,1,0:T(8,128)(2,1)}, bf16[4,320,1024]{2,1,0:T(8,128)(2,1)}, bf16[4,320,1024]{2,1,0:T(8,1...) custom-call(bf16[16,256,1024]{2,1,0:T(8,128)(2,1)} %get-tuple-elemen, ...), custom_call_target="tpu_custom_call" | custom-call | flops 1000000000 | bytes 3600000 | tf_op jit(solution)/shard_map/expert_0/pallas_call | solution.py:1271
  200.3 0.0 all-gather.2.cloned.1.call-update
  200.4 11.9 %collective-permute-start = (bf16[384,1024]{1,0:T(8,128)(2,1)}, bf16[384,1024]{1,0:T(8,128)(2,1)S(1)}, u32[]{:S(2)}, u32[]{:S(2)}) collective-permute-start(bf16[384,1024]{1,0:T(8,128)(2,1)} %get-tuple-element.94), channel_id=1, source_target_pairs={{0,8},{8,0},{16,24},{24,16},{1,9},{9,1},{17,25},{25,17},{2,10},{10... | collective-permute-start | bytes 2359304 | tf_op jit(solution)/shard_map/ppermute | solution.py:1960
  212.3 1.3 collective-permute-start.1
  213.5 1.4 collective-permute-start.2
  214.9 0.0 copy-done.3
  214.9 0.7 copy.31.refs_20_
  215.6 28.8 %expert_1.1 = (bf16[16,256,1024]{2,1,0:T(8,128)(2,1)}, bf16[16,256,1024]{2,1,0:T(8,128)(2,1)}, f32[16,8,256]{2,1,0:T(8,128)}, bf16[384,1024]{1,0:T(8,128)(2,1)},...) custom-call(bf16[4,320,1024]{2,1,0:T(8,128)(2,1)} %get-tuple-element.97.rows_ref, ...), custom_call_target="tpu_custom_call" | custom-call | flops 1000000000 | bytes 3600000 | tf_op jit(solution)/shard_map/expert_1/pallas_call | solution.py:1286
  244.4 2.6 all-gather.2.cloned.1.call-done.refs_5_
  247.0 153.1 %backward.1 = (bf16[256,1024]{1,0:T(8,128)(2,1)}, bf16[256,1024]{1,0:T(8,128)(2,1)}, f32[32,1024]{1,0:T(8,128)}, f32[32,512]{1,0:T(8,128)}, f32[32,512]{1,0:T(8,...) custom-call(bf16[16,256,1024]{2,1,0:T(8,128)(2,1)} %get-tuple-elemen, ...), custom_call_target="tpu_custom_call" | custom-call | flops 1000000000 | bytes 3600000 | tf_op jit(solution)/shard_map/backward/pallas_call | solution.py:1889
  400.1 0.0 collective-permute-done.refs_1_
  400.1 0.0 copy-start
  400.1 0.0 collective-permute-done.1.refs_2_
  400.2 0.0 copy-start.1
  400.2 0.0 collective-permute-done.2.refs_3_
  400.2 0.0 copy-start.2
  400.2 0.8 copy-done
  401.0 0.3 copy-done.1
  401.3 0.3 copy-done.2
  401.6 7.6 %results.1 = (f32[4,256,1024]{2,1,0:T(8,128)}, f32[4,128,1024]{2,1,0:T(8,128)}, bf16[256,1024]{1,0:T(8,128)(2,1)}, bf16[256,1024]{1,0:T(8,128)(2,1)}, f32[32,102...) custom-call(bf16[384,1024]{1,0:T(8,128)(2,1)} %get-tuple-element.93., ...), custom_call_target="tpu_custom_call" | custom-call | flops 1000000000 | bytes 3600000 | tf_op jit(solution)/shard_map/results/pallas_call | solution.py:1345
Async XLA Ops:
  7.2 239.8 %all-gather.2.cloned.1.call-start = ((), (), s32[]{:S(2)}) async-start(), calls=%async_computation | async-start | bytes 4718592 | tf_op jit(solution)/shard_map/all_gather | solution.py:2003
  172.3 42.6 %copy-start.3 = (bf16[32]{0:T(256)(128)(2,1)S(1)}, bf16[32]{0:T(256)(128)(2,1)}, u32[]{:S(2)}) copy-start(bf16[32]{0:T(256)(128)(2,1)} %param.20) | copy-start | bytes 196
  200.4 199.8 %collective-permute-start = (bf16[384,1024]{1,0:T(8,128)(2,1)}, bf16[384,1024]{1,0:T(8,128)(2,1)S(1)}, u32[]{:S(2)}, u32[]{:S(2)}) collective-permute-start(bf16[384,1024]{1,0:T(8,128)(2,1)} %get-tuple-element.94), channel_id=1, source_target_pairs={{0,8},{8,0},{16,24},{24,16},{1,9},{9,1},{17,25},{25,17},{2,10},{10... | collective-permute-start | bytes 2359304 | tf_op jit(solution)/shard_map/ppermute | solution.py:1960
  212.3 187.9 %collective-permute-start.1 = (bf16[384,1024]{1,0:T(8,128)(2,1)}, bf16[384,1024]{1,0:T(8,128)(2,1)S(1)}, u32[]{:S(2)}, u32[]{:S(2)}) collective-permute-start(bf16[384,1024]{1,0:T(8,128)(2,1)} %get-tuple-element.95), channel_id=1, source_target_pairs={{0,16},{8,24},{16,0},{24,8},{1,17},{9,25},{17,1},{25,9},{2,18},{10... | collective-permute-start | bytes 2359304 | tf_op jit(solution)/shard_map/ppermute | solution.py:1960
  213.5 186.7 %collective-permute-start.2 = (bf16[384,1024]{1,0:T(8,128)(2,1)}, bf16[384,1024]{1,0:T(8,128)(2,1)S(1)}, u32[]{:S(2)}, u32[]{:S(2)}) collective-permute-start(bf16[384,1024]{1,0:T(8,128)(2,1)} %get-tuple-element.96), channel_id=1, source_target_pairs={{0,24},{8,16},{16,8},{24,0},{1,25},{9,17},{17,9},{25,1},{2,26},{10... | collective-permute-start | bytes 2359304 | tf_op jit(solution)/shard_map/ppermute | solution.py:1960
  400.1 0.9 copy-start
  400.2 1.2 copy-start.1
  400.2 1.4 copy-start.2
Sparse Core Ops, SparseCore 0:
  200.5 46.4 all-gather.1

commit v4 on v3

--- a/solution.py
+++ b/solution.py
@@ -442,6 +442,7 @@
 SLOTS = 80
 MINE = 2
 EARLY = 160
+MIDDLE = 96
 CHUNK = 4
 NT = (((1,), (1,)), ((), ()))
 TN = (((0,), (0,)), ((), ()))
@@ -831,17 +832,24 @@
         )
 
 
-def piece_copies(spot, gu_ref, down_ref, e, kind, target, send, recv, number):
+def piece_copies(spot, gu_ref, down_ref, e, kind, target, send, recv, number, first=0, last=384):
     pair = lax.div(spot.n, 2)
     plane = spot.n if kind == 2 else spot.mate
     if kind >= 2:
         plane = plane + 2 - 4 * pair
     half = spot.half if kind == 2 else 1 - spot.half
     to = (plane, spot.w)
-    return [
-        remote(gu_ref.at[2 * half + e], target.at[pl.ds(0, 256)], send.at[number], recv.at[number], to),
-        remote(down_ref.at[2 * half + e], target.at[pl.ds(256, 128)], send.at[number + 1], recv.at[number + 1], to),
-    ]
+    copies = []
+    for part, (ref, start, rows) in enumerate(((gu_ref, 0, 256), (down_ref, 256, 128))):
+        low, high = max(first, start), min(last, start + rows)
+        if low < high:
+            copies.append(
+                remote(
+                    ref.at[2 * half + e, pl.ds(low - start, high - low)], target.at[pl.ds(low - first, high - low)],
+                    send.at[number + part], recv.at[number + part], to,
+                )
+            )
+    return copies
 
 
 def start_all(copies):
@@ -852,7 +860,7 @@
 def forward_kernel(
     x_ref, w_ref, g_ref, seg_ref, cos_ref, sin_ref, freq_ref, wo_ref, ids_ref, dy_ref, gu_ref, down_ref,
     h1_out, qkv_ref, lse_ref, o_ref, angle_ref, gain_ref, mid_ref, gate_ref, w_all,
-    h2_all, dy_all, table_all, mate_0, far_rest_0, far_mate_0, mate_1, far_1,
+    h2_all, dy_all, table_all, mate_0, far_rest_0, far_mate_0, mate_1, far_1, far_mate_early_1,
     h1_ref, o_full, h2_own, table_own,
     os, orv, w_send, w_recv, a_send, a_recv, b_send, b_recv, s0, r0, s1, r1, ts, tr, zs, zr, es, er, local,
 ):
@@ -873,16 +881,7 @@
     mate_dy_gather = gather_tokens(spot, dy_ref.at[1 - spot.half], dy_all, mate_base, b_send, b_recv)
     w_gather.begin()
     dy_gather.begin()
-    far_plane = (spot.n + 2 - 4 * lax.div(spot.n, 2), spot.w)
-    first_expert = [
-        remote(
-            gu_ref.at[2 * spot.half, pl.ds(EARLY, 256 - EARLY)], far_rest_0.at[pl.ds(0, 256 - EARLY)],
-            es.at[0], er.at[0], far_plane,
-        ),
-        remote(
-            down_ref.at[2 * spot.half], far_rest_0.at[pl.ds(256 - EARLY, 128)], es.at[1], er.at[1], far_plane
-        ),
-    ]
+    first_expert = piece_copies(spot, gu_ref, down_ref, 0, 2, far_rest_0, es, er, 0, first=EARLY)
     first_expert += piece_copies(spot, gu_ref, down_ref, 0, 3, far_mate_0, es, er, 2)
     first_expert += piece_copies(spot, gu_ref, down_ref, 0, 1, mate_0, es, er, 4)
     start_all(first_expert)
@@ -942,6 +941,7 @@
             step()
     far = piece_copies(spot, gu_ref, down_ref, 1, 2, far_1, es, er, 6)
     near = piece_copies(spot, gu_ref, down_ref, 1, 1, mate_1, es, er, 8)
+    far_mate = piece_copies(spot, gu_ref, down_ref, 1, 3, far_mate_early_1, es, er, 10, last=MIDDLE)
     h1_copy = pltpu.make_async_copy(h1_ref, h1_out, local.at[4])
     h1_copy.start()
     dy_gather.last()
@@ -1004,6 +1004,7 @@
 
     mate_dy_gather.middle()
     mate_dy_gather.late()
+    start_all(far)
     first.middle()
     mate_dy_gather.last()
     first.late()
@@ -1012,7 +1013,7 @@
     remote(arriving, arriving, zs.at[0], zr.at[0], (spot.mate, spot.w)).wait_recv()
     second = gather_tokens(spot, arriving, h2_all, mate_base, s1, r1)
     second.begin()
-    start_all(far + near)
+    start_all(far_mate + near)
     second.middle()
     second.late()
     second.last()
@@ -1033,7 +1034,7 @@
     keep_own.wait()
     table_mine.wait()
     h1_copy.wait()
-    for copy in first_expert + far + near:
+    for copy in first_expert + far + far_mate + near:
         copy.wait_send()
         copy.wait_recv()
 
@@ -1058,9 +1059,9 @@
             jax.ShapeDtypeStruct((GROUP, TOKENS, WIDTH), BF16),
             jax.ShapeDtypeStruct((GROUP, 8, TOKENS), F32),
         )
-        + tuple(jax.ShapeDtypeStruct((depth, WIDTH), BF16) for depth in (384, 384 - EARLY, 384, 384, 384)),
+        + tuple(jax.ShapeDtypeStruct((depth, WIDTH), BF16) for depth in (384, 384 - EARLY, 384, 384, 384, MIDDLE)),
         in_specs=[IN_VMEM] * 7 + [IN_HBM, IN_VMEM, IN_VMEM, IN_HBM, IN_HBM],
-        out_specs=(IN_HBM,) + (IN_VMEM,) * 8 + (IN_HBM,) * 8,
+        out_specs=(IN_HBM,) + (IN_VMEM,) * 8 + (IN_HBM,) * 9,
         scratch_shapes=[
             pltpu.VMEM((2, SEQ, WIDTH), BF16),
             pltpu.VMEM((2, SPAN, WIDTH), BF16),
@@ -1070,7 +1071,7 @@
             dma((WIDE,)),
         ]
         + [dma((copies,))] * 10
-        + [dma((GROUP,)), dma((GROUP,)), dma((1,)), dma((1,)), dma((10,)), dma((10,)), dma((7,))],
+        + [dma((GROUP,)), dma((GROUP,)), dma((1,)), dma((1,)), dma((12,)), dma((12,)), dma((7,))],
         compiler_params=pltpu.CompilerParams(collective_id=2, has_side_effects=True, vmem_limit_bytes=VMEM_BYTES),
         cost_estimate=duration(1),
     )(x_all.reshape(WIDE, 2, SPAN, WIDTH), w_all, g_all, seg_all, cos_table, sin_table, freq, wo_block, ids, dy_pair, w_gate_up, w_down)
@@ -1176,7 +1177,7 @@
 ):
     step = pl.program_id(0)
     spot = Spot()
-    second_expert = piece_copies(spot, gu_ref, down_ref, 1, 3, far_mate_1, es, er, 0)
+    second_expert = piece_copies(spot, gu_ref, down_ref, 1, 3, far_mate_1, es, er, 0, first=MIDDLE)
 
     @pl.when(step == 0)
     def _():
@@ -1215,15 +1216,52 @@
 
 
 def expert_1_kernel(
-    rows_ref, grad_rows_ref, gated_before, dx_before, dgate_before, table_ref, gu_ref, down_ref, w1, w2, w3,
-    y_ref, part_ref, dgate_ref, own, mate, far, far_mate,
-    w_gu, w_down, gu_sum, down_sum, sems,
+    rows_ref, grad_rows_ref, gated_before, dx_before, dgate_before, table_ref, gu_ref, down_ref, w1, w2, w3_early, w3_rest,
+    y_here, y_there, part_here, part_there, dgate_ref, own, mate, far, far_mate,
+    w_gu, w_down, gu_sum, down_sum, sems, held, local, send, recv,
 ):
     step = pl.program_id(0)
+    spot = Spot()
+    slot = lax.rem(step, 2)
+    outs = ((y_here, y_there), (part_here, part_there))
+
+    def copies(at_step, at_slot):
+        result = []
+        for kind, (here, there) in enumerate(outs):
+            for pair in range(CHUNK // 2):
+                block = at_step * (CHUNK // 2) + pair
+                source = held.at[kind, at_slot]
+                result.append(
+                    pltpu.make_async_copy(
+                        source.at[2 * pair + spot.core], here.at[block], local.at[kind, at_slot, pair]
+                    )
+                )
+                other = source.at[2 * pair + 1 - spot.core]
+                if kind == 0:
+                    result.append(pltpu.make_async_copy(other, there.at[block], send.at[kind, at_slot, pair]))
+                else:
+                    result.append(
+                        remote(
+                            other, there.at[block], send.at[kind, at_slot, pair], recv.at[block],
+                            spot.wide(spot.sib),
+                        )
+                    )
+        return result
+
+    def finish(at_step, at_slot):
+        done = copies(at_step, at_slot)
+        for number, copy in enumerate(done):
+            if number % 2 == 1 and number >= CHUNK:
+                copy.wait_send()
+            else:
+                copy.wait()
 
     @pl.when(step == 0)
     def _():
-        start_weights(1, gu_ref, down_ref, (w1, w2, w3), w_gu, w_down, gu_sum, down_sum, sems)
+        barrier = pltpu.get_barrier_semaphore()
+        pl.semaphore_signal(barrier, inc=1, device_id=spot.wide(spot.sib), device_id_type=MESH)
+        pl.semaphore_wait(barrier, 1)
+        start_weights(1, gu_ref, down_ref, (w1, w2, (w3_early, w3_rest)), w_gu, w_down, gu_sum, down_sum, sems)
 
     masks = [[pick(table_ref, s, e) for s in range(CHUNK)] for e in range(MINE)]
     gated, dx, slot_dgate = expert_math(
@@ -1231,15 +1269,26 @@
     )
     dgate_ref[...] = dgate_before[...]
     token_dgate(dgate_ref, masks[1], slot_dgate, 1)
+
+    @pl.when(step >= 2)
+    def _():
+        finish(step - 2, slot)
+
     for s in range(CHUNK):
         at = slice(s * SLOTS, (s + 1) * SLOTS)
         hot = jnp.concatenate([jnp.where(masks[e][s], 1.0, 0.0) for e in range(MINE)], axis=0).astype(BF16)
-        y_ref[s] = mm(hot, jnp.concatenate([gated_before[0, at, :], gated[at]], axis=0), TN).astype(BF16)
-        part_ref[s] = mm(hot, jnp.concatenate([dx_before[0, at, :], dx[at]], axis=0), TN).astype(BF16)
+        held[0, slot, s] = mm(hot, jnp.concatenate([gated_before[0, at, :], gated[at]], axis=0), TN).astype(BF16)
+        held[1, slot, s] = mm(hot, jnp.concatenate([dx_before[0, at, :], dx[at]], axis=0), TN).astype(BF16)
+    start_all(copies(step, slot))
 
     @pl.when(step == STEPS - 1)
     def _():
         store_quarters((own, mate, far, far_mate), gu_sum, down_sum)
+        for last in (STEPS - 2, STEPS - 1):
+            finish(last, last % 2)
+        for block in range(WIDE):
+            place = part_there.at[block]
+            remote(place, place, send.at[0, 0, 0], recv.at[block], spot.wide(spot.sib)).wait_recv()
 
 
 def expert_specs():
@@ -1261,7 +1310,7 @@
 
 
 SLOT_ROWS = jax.ShapeDtypeStruct((STEPS, ROWS, WIDTH), BF16)
-TOKEN_ROWS = jax.ShapeDtypeStruct((GROUP, TOKENS, WIDTH), BF16)
+CORE_BLOCKS = jax.ShapeDtypeStruct((WIDE, TOKENS, WIDTH), BF16)
 TABLES = jax.ShapeDtypeStruct((GROUP, 8, TOKENS), F32)
 QUARTER = jax.ShapeDtypeStruct((384, WIDTH), BF16)
 
@@ -1272,7 +1321,10 @@
         expert_0_kernel,
         name="expert_0",
         grid=(STEPS,),
-        out_shape=(SLOT_ROWS,) * 4 + (TABLES,) + (QUARTER,) * 5,
+        out_shape=(SLOT_ROWS,) * 4
+        + (TABLES,)
+        + (QUARTER,) * 4
+        + (jax.ShapeDtypeStruct((384 - MIDDLE, WIDTH), BF16),),
         in_specs=[block, block, small] + [IN_HBM] * 6,
         out_specs=(slots,) * 4 + (small,) + (quarter,) * 4 + (IN_HBM,),
         scratch_shapes=expert_scratch() + [pltpu.SemaphoreType.DMA((2,)), pltpu.SemaphoreType.DMA((2,))],
@@ -1287,11 +1339,17 @@
         expert_1_kernel,
         name="expert_1",
         grid=(STEPS,),
-        out_shape=(TOKEN_ROWS,) * 2 + (TABLES,) + (QUARTER,) * 4,
-        in_specs=[slots] * 4 + [small, small] + [IN_HBM] * 5,
-        out_specs=(block, block, small) + (quarter,) * 4,
-        scratch_shapes=expert_scratch(),
-        compiler_params=pltpu.CompilerParams(vmem_limit_bytes=VMEM_BYTES),
+        out_shape=(CORE_BLOCKS,) * 4 + (TABLES,) + (QUARTER,) * 4,
+        in_specs=[slots] * 4 + [small, small] + [IN_HBM] * 6,
+        out_specs=(IN_HBM,) * 4 + (small,) + (quarter,) * 4,
+        scratch_shapes=expert_scratch()
+        + [
+            pltpu.VMEM((2, 2, CHUNK, TOKENS, WIDTH), BF16),
+            pltpu.SemaphoreType.DMA((2, 2, CHUNK // 2)),
+            pltpu.SemaphoreType.DMA((2, 2, CHUNK // 2)),
+            pltpu.SemaphoreType.DMA((WIDE,)),
+        ],
+        compiler_params=pltpu.CompilerParams(collective_id=5, has_side_effects=True, vmem_limit_bytes=VMEM_BYTES),
         cost_estimate=duration(1),
     )(rows, grad_rows, gated, dx, dgate, table_all, w_gate_up, w_down, *pieces)
 
@@ -1371,16 +1429,28 @@
 class PlaneReduce:
     COPIES = 10
 
-    def __init__(self, spot, part, buffers, send, recv, local):
-        self.spot, self.part = spot, part
+    def __init__(self, spot, here, there, arrived, first, buffers, send, recv, local):
+        self.spot, self.arrived = spot, arrived
         self.acc, self.from_core, self.from_one, self.from_two = buffers
-        self.send, self.recv, self.local = send, recv, local
+        self.send, self.recv = send, recv
         self.started = []
         s = spot
         self.q_own = 2 * s.y + s.x
         self.q_x = 2 * s.y + 1 - s.x
         self.q_y = 2 - 2 * s.y + s.x
         self.q_d = 3 - self.q_own
+        self.order = (self.q_d, self.q_x, self.q_y, self.q_own)
+        self.loads = []
+        for number, q in enumerate(self.order):
+            mine = pltpu.make_async_copy(here.at[first + q], self.acc.at[q], local.at[number])
+            if arrived:
+                other = pltpu.make_async_copy(there.at[first + q], self.from_core.at[q], local.at[4 + number])
+            else:
+                other = remote(
+                    there.at[first + q], self.from_core.at[q], send.at[6 + number], recv.at[6 + number], s.wide(s.sib)
+                )
+                self.started.append(other)
+            self.loads.append((mine, other))
 
     def put(self, src, dst, number, to):
         copy = remote(src, dst, self.send.at[number], self.recv.at[number], self.spot.wide(to))
@@ -1391,48 +1461,45 @@
         remote(dst, dst, self.send.at[number], self.recv.at[number], self.spot.wide(self.spot.sib)).wait_recv()
 
     def begin(self):
-        s = self.spot
-        self.loads = []
-        for number, q in enumerate((self.q_d, self.q_x, self.q_y, self.q_own)):
-            self.put(self.part(2 * q + 1 - s.core), self.from_core.at[q], number, s.sib)
-            copy = pltpu.make_async_copy(self.part(2 * q + s.core), self.acc.at[q], self.local.at[number])
-            copy.start()
-            self.loads.append(copy)
-
-    def add_core(self, number, q):
-        self.loads[number].wait()
-        self.got(self.from_core.at[q], number)
-        self.acc[q] = (widen(self.acc[q]) + widen(self.from_core[q])).astype(BF16)
+        for pair in self.loads:
+            start_all(pair)
+
+    def add_core(self, number):
+        mine, other = self.loads[number]
+        mine.wait()
+        other.wait() if self.arrived else other.wait_recv()
+        q = self.order[number]
+        self.acc[q] = self.acc[q] + self.from_core[q]
 
     def across_core(self):
         s = self.spot
-        self.add_core(0, self.q_d)
-        self.put(halves(self.acc.at[self.q_d], 0), self.from_one.at[1], 5, s.xn)
-        self.put(halves(self.acc.at[self.q_d], 1), self.from_one.at[3], 7, s.yn)
-        self.add_core(1, self.q_x)
-        self.put(halves(self.acc.at[self.q_x], 0), self.from_one.at[0], 4, s.xn)
-        self.add_core(2, self.q_y)
-        self.put(halves(self.acc.at[self.q_y], 1), self.from_one.at[2], 6, s.yn)
-        self.add_core(3, self.q_own)
+        self.add_core(0)
+        self.put(halves(self.acc.at[self.q_d], 0), self.from_one.at[1], 1, s.xn)
+        self.put(halves(self.acc.at[self.q_d], 1), self.from_one.at[3], 3, s.yn)
+        self.add_core(1)
+        self.put(halves(self.acc.at[self.q_x], 0), self.from_one.at[0], 0, s.xn)
+        self.add_core(2)
+        self.put(halves(self.acc.at[self.q_y], 1), self.from_one.at[2], 2, s.yn)
+        self.add_core(3)
 
     def across_one(self):
         s = self.spot
-        self.got(self.from_one.at[1], 5)
+        self.got(self.from_one.at[1], 1)
         upper = halves(self.acc.at[self.q_y], 0)
-        upper[...] = (widen(upper[...]) + widen(self.from_one[1])).astype(BF16)
-        self.put(upper, self.from_two.at[0], 8, s.yn)
-        self.got(self.from_one.at[3], 7)
+        upper[...] = upper[...] + self.from_one[1]
+        self.put(upper, self.from_two.at[0], 4, s.yn)
+        self.got(self.from_one.at[3], 3)
         lower = halves(self.acc.at[self.q_x], 1)
-        lower[...] = (widen(lower[...]) + widen(self.from_one[3])).astype(BF16)
-        self.put(lower, self.from_two.at[1], 9, s.xn)
+        lower[...] = lower[...] + self.from_one[3]
+        self.put(lower, self.from_two.at[1], 5, s.xn)
 
     def total(self, out):
-        self.got(self.from_one.at[0], 4)
-        self.got(self.from_two.at[0], 8)
+        self.got(self.from_one.at[0], 0)
+        self.got(self.from_two.at[0], 4)
         own = self.acc.at[self.q_own]
         out[0:SPAN, :] = widen(own[0:SPAN, :]) + widen(self.from_one[0]) + widen(self.from_two[0])
-        self.got(self.from_one.at[2], 6)
-        self.got(self.from_two.at[1], 9)
+        self.got(self.from_one.at[2], 2)
+        self.got(self.from_two.at[1], 5)
         out[SPAN:TOKENS, :] = widen(own[SPAN:TOKENS, :]) + widen(self.from_one[2]) + widen(self.from_two[1])
 
     def finish(self):
@@ -1445,13 +1512,17 @@
 
 
 class GroupReduce:
-    def __init__(self, spot, theirs, ours, scratch):
+    def __init__(self, spot, here, there, arrived, scratch):
         acc, from_core, from_one, from_two, total, mate_send, mate_recv, send, recv, local, zs, zr = scratch
         self.total_ref, self.mate_send, self.mate_recv = total, mate_send, mate_recv
         parts = []
-        for which, part in enumerate((theirs, ours)):
+        for which, first in enumerate((4 * (1 - spot.half), 4 * spot.half)):
             buffers = (acc.at[which], from_core.at[which], from_one.at[which], from_two.at[which])
-            parts.append(PlaneReduce(spot, part, buffers, send.at[which], recv.at[which], local.at[which]))
+            parts.append(
+                PlaneReduce(
+                    spot, here, there, arrived, first, buffers, send.at[which], recv.at[which], local.at[which]
+                )
+            )
         self.theirs, self.ours = parts
         self.across = remote(mate_send, mate_recv, zs.at[0], zr.at[0], (spot.mate, spot.w))
 
@@ -1493,7 +1564,7 @@
         pltpu.VMEM((TOKENS, WIDTH), BF16),
         dma((2, PlaneReduce.COPIES)),
         dma((2, PlaneReduce.COPIES)),
-        dma((2, 4)),
+        dma((2, 8)),
         dma((1,)),
         dma((1,)),
     ]
@@ -1571,31 +1642,28 @@
 
 def backward_kernel(*refs):
     (
-        part_ref, y_ref, dgate_ref, h2_ref, w_out_ref, w_full_ref, h1_ref, qkv_ref, lse_ref, o_ref,
+        part_here, part_there, y_here, y_there, dgate_ref, h2_ref, w_out_ref, w_full_ref, h1_ref, qkv_ref, lse_ref, o_ref,
         angle_ref, mate_1, far_1, far_mate_1,
         x_ref, mid_ref, gate_ref, gain_ref, dy_ref, w_own, gain_col,
-    ) = refs[:21]
+    ) = refs[:23]
     (
         block_out, in_grad, q_grad, k_grad, v_grad, o_grad, router_grad, two_gains, load_out, *quarters_recv,
-    ) = refs[21:33]
+    ) = refs[23:35]
     (
         dgate_all, h2_own, dattn_all, dmid_ref, small_ref, small_all, small_sum, w_router, w_rows, w_full,
         h1, qkv, lse, outs, angle, dqkv_ref, dkv_ref, dq_ref, osum, og_ref, wg_ref,
-        dq_full, w_recv, o_recv, s_recv,
+        dq_full, w_recv, o_held, s_held, o_recv, s_recv,
         ts, tr, s0, r0, bs, br, qs, qr, ks, kr, ws, wr, os, orv, ss, sr, gs, gr, local,
-    ) = refs[33:77]
-    h2_sum_refs = refs[77 : 77 + REDUCE_REFS]
-    y_sum_refs = refs[77 + REDUCE_REFS :]
+    ) = refs[35:81]
+    h2_sum_refs = refs[81 : 81 + REDUCE_REFS]
+    y_sum_refs = refs[81 + REDUCE_REFS :]
 
     spot = Spot()
     everyone = NARROW * WIDE
+    h2_sum = GroupReduce(spot, part_here, part_there, True, h2_sum_refs)
+    y_sum = GroupReduce(spot, y_here, y_there, False, y_sum_refs)
+    h2_sum.begin()
     spot.greet(everyone)
-    base, mate_base = spot.half * WIDE, (1 - spot.half) * WIDE
-    h2_sum = GroupReduce(
-        spot, lambda who: part_ref.at[mate_base + who], lambda who: part_ref.at[base + who], h2_sum_refs
-    )
-    y_sum = GroupReduce(spot, lambda who: y_ref.at[mate_base + who], lambda who: y_ref.at[base + who], y_sum_refs)
-    h2_sum.begin()
 
     def tables(step, arriving):
         other = lax.rem(spot.slot + step, GROUP)
@@ -1625,9 +1693,11 @@
     ]
     loads = [pltpu.make_async_copy(src, dst, local.at[i]) for i, (src, dst) in enumerate(loads)]
     w_loads = [pltpu.make_async_copy(w_full_ref.at[who], w_full.at[who], local.at[10 + who]) for who in range(WIDE)]
-    h2_sum.across_core()
+    h2_sum.theirs.across_core()
     start_all(loads + w_loads)
     y_sum.begin()
+    h2_sum.theirs.across_one()
+    h2_sum.ours.across_core()
     far_plane = 2 - 4 * lax.div(spot.n, 2)
     quarter_copies = [
         remote(piece, quarters_recv[number], gs.at[number], gr.at[number], (plane, spot.w))
@@ -1635,8 +1705,9 @@
             ((mate_1, spot.mate), (far_1, spot.n + far_plane), (far_mate_1, spot.mate + far_plane))
         )
     ]
-    h2_sum.across_one()
     h2_sum.to_mate()
+    h2_sum.ours.across_one()
+    y_sum.across_core()
     h2_sum.finish()
     start_all(quarter_copies)
 
@@ -1719,10 +1790,10 @@
     gather.late()
     gather.got(sib_x, None, 7)
     back.chunk(0, order.q_x)
-    gather.last()
-    y_sum.across_core()
     back.chunk(1, order.q_x)
     send_queries((spot.xn, sib_x))
+    gather.last()
+    y_sum.across_one()
     gather.got(sib_y, None, 8)
     back.chunk(0, order.q_y)
     back.chunk(1, order.q_y)
@@ -1732,6 +1803,7 @@
     back.chunk(0, order.q_d)
     back.chunk(1, order.q_d)
     send_queries((spot.diag, sib_d))
+    y_sum.to_mate()
     for copy in gather.started:
         copy.wait_send()
     back.keys(0)
@@ -1776,46 +1848,55 @@
     for device in range(1, WIDE):
         lane_total = lane_total + small_all[device]
     small_sum[...] = lane_total
-    def output_copies(act_local, act_send, act_recv):
-        for i in range(4):
-            owner = 4 * spot.w + i
-            to = (lax.div(owner, WIDE), lax.rem(owner, WIDE))
-            source = og_ref.at[pl.ds(i * 32, 32)]
-            here = owner == spot.me
-
-            @pl.when(here)
-            def _():
-                act_local(pltpu.make_async_copy(source, o_recv.at[spot.n], local.at[3]))
-                act_local(pltpu.make_async_copy(small_sum, s_recv.at[spot.n], local.at[2]))
-
-            @pl.when(jnp.logical_not(here))
-            def _():
-                act_send(remote(source, o_recv.at[spot.n], os.at[i], orv.at[spot.n], to))
-                act_send(remote(small_sum, s_recv.at[spot.n], ss.at[i], sr.at[spot.n], to))
-
-        for plane in range(NARROW):
-            giver = lax.div(spot.me, 4)
-            here = (plane == spot.n) & (giver == spot.w)
-
-            @pl.when(jnp.logical_not(here))
-            def _():
-                place = o_recv.at[plane]
-                act_recv(remote(place, place, os.at[0], orv.at[plane], (plane, giver)))
-                small = s_recv.at[plane]
-                act_recv(remote(small, small, ss.at[0], sr.at[plane], (plane, giver)))
-
-    def nothing(copy):
-        return None
-
-    output_copies(lambda c: c.start(), lambda c: c.start(), nothing)
-    y_sum.across_one()
+    odd = 4 * lax.rem(spot.w, 2)
+
+    def first_hop(i, act_local, act_remote):
+        to = odd + i
+        source = og_ref.at[pl.ds(i * 32, 32)]
+        place = lax.div(spot.w, 2)
+
+        @pl.when(to == spot.w)
+        def _():
+            act_local(pltpu.make_async_copy(source, o_held.at[place], local.at[2]))
+            act_local(pltpu.make_async_copy(small_sum, s_held.at[place], local.at[3]))
+
+        @pl.when(to != spot.w)
+        def _():
+            act_remote(remote(source, o_held.at[place], os.at[i], orv.at[place], spot.wide(to)))
+            act_remote(remote(small_sum, s_held.at[place], ss.at[i], sr.at[place], spot.wide(to)))
+
+    def first_arrival(place, act):
+        giver = 2 * place + lax.div(spot.w, 4)
+
+        @pl.when(giver != spot.w)
+        def _():
+            held, small = o_held.at[place], s_held.at[place]
+            act(remote(held, held, os.at[0], orv.at[place], spot.wide(giver)))
+            act(remote(small, small, ss.at[0], sr.at[place], spot.wide(giver)))
+
+    def second_hop(step, arriving):
+        plane = lax.rem(spot.n + step, NARROW)
+        place = plane if arriving else spot.n
+        to = (plane, spot.w)
+        return (
+            remote(o_held.at[plane], o_recv.at[place], os.at[4 + step], orv.at[4 + place], to),
+            remote(s_held.at[plane], s_recv.at[place], ss.at[4 + step], sr.at[4 + place], to),
+        )
+
+    for i in range(4):
+        first_hop(i, lambda c: c.start(), lambda c: c.start())
 
     loads[8].wait()
     wg_ref[...] = (mm(h1[0], dqkv_ref[0], TN) + mm(h1[1], dqkv_ref[1], TN)).astype(BF16)
     lax.fori_loop(1, everyone, start_owner, 0)
     owner_mine = pltpu.make_async_copy(rows_of(wg_ref, spot.me), w_recv.at[spot.me], local.at[1])
     owner_mine.start()
-    y_sum.to_mate()
+    for i in range(4):
+        first_hop(i, lambda c: c.wait(), lambda c: c.wait_send())
+    for place in range(NARROW):
+        first_arrival(place, lambda c: c.wait_recv())
+    for step in range(1, NARROW):
+        start_all(second_hop(step, False))
 
     def wait_plane(step, carry):
         other = lax.rem(spot.w + step, WIDE)
@@ -1847,7 +1928,11 @@
 
     lax.fori_loop(1, everyone, wait_owner, 0)
     owner_mine.wait()
-    output_copies(lambda c: c.wait(), lambda c: c.wait_send(), lambda c: c.wait_recv())
+    for step in range(1, NARROW):
+        for copy in second_hop(step, False):
+            copy.wait_send()
+        for copy in second_hop(step, True):
+            copy.wait_recv()
     gain_total = jnp.zeros((32, 1), F32)
     for w in range(WIDE):
         total = widen(w_recv[w])
@@ -1858,6 +1943,8 @@
         v_grad[:, 64 * w : 64 * w + 64] = total[:, 192:256]
         gain_total += jnp.sum(total * widen(w_own[:, 256 * w : 256 * w + 256]), axis=1, keepdims=True)
     gain_total = gain_total / gain_col[...].astype(F32)
+    o_recv[spot.n] = o_held[spot.n]
+    s_recv[spot.n] = s_held[spot.n]
     total = widen(o_recv[0])
     for plane in range(1, NARROW):
         total = total + widen(o_recv[plane])
@@ -1901,7 +1988,7 @@
             jax.ShapeDtypeStruct((1, 32), jnp.int32),
         )
         + (QUARTER,) * 3,
-        in_specs=[IN_HBM] * 14 + [IN_VMEM] * 7,
+        in_specs=[IN_HBM] * 16 + [IN_VMEM] * 7,
         out_specs=(IN_VMEM,) * 9 + (IN_HBM,) * 3,
         scratch_shapes=[
             vmem((GROUP, 8, TOKENS), F32),
@@ -1929,6 +2016,8 @@
             vmem((everyone, 32, 256), BF16),
             vmem((NARROW, 32, WIDTH), BF16),
             vmem((NARROW, 40, 128), F32),
+            vmem((NARROW, 32, WIDTH), BF16),
+            vmem((NARROW, 40, 128), F32),
             dma((GROUP,)),
             dma((GROUP,)),
             dma((copies,)),
@@ -1941,10 +2030,10 @@
             dma((WIDE,)),
             dma((everyone,)),
             dma((everyone,)),
-            dma((4,)),
-            dma((NARROW,)),
-            dma((4,)),
-            dma((NARROW,)),
+            dma((8,)),
+            dma((8,)),
+            dma((8,)),
+            dma((8,)),
             dma((3,)),
             dma((3,)),
             dma((18,)),
@@ -1987,7 +2076,7 @@
     )
     (
         h1, qkv, lse, o_heads, angle, gain_rows, mid, gate, w_out, h2_all, dy_all, table_all,
-        mate_0, far_rest_0, far_mate_0, mate_1, far_1,
+        mate_0, far_rest_0, far_mate_0, mate_1, far_1, far_mate_early_1,
     ) = forward_call(
         x_all, w_all, g_all, seg_all, cos_table, sin_table, freq, wo_block, ids, dy_pair, w_gate_up, w_down
     )
@@ -1996,19 +2085,19 @@
     def send_grads(own, mate, far, far_mate):
         return own, swap(mate, 1), swap(far, 2), swap(far_mate, 3)
 
-    gated_0, dx_0, rows_1, grad_rows_1, dgate_0, *grads_0, far_mate_1 = expert_0_call(
+    gated_0, dx_0, rows_1, grad_rows_1, dgate_0, *grads_0, far_mate_rest_1 = expert_0_call(
         h2_all, dy_all, table_all, w_gate_up, w_down, (mate_0, far_early_0, far_rest_0, far_mate_0)
     )
     dgate_0, w_heads = lax.optimization_barrier((dgate_0, w_all))
     w_full = lax.all_gather(w_heads.reshape(WIDTH, 256), "wide", axis=0, tiled=False)
     grads_0 = send_grads(*grads_0)
-    y, part, dgate, *grads_1 = expert_1_call(
-        rows_1, grad_rows_1, gated_0, dx_0, dgate_0, table_all, w_gate_up, w_down, (mate_1, far_1, far_mate_1)
+    y_here, y_there, part_here, part_there, dgate, *grads_1 = expert_1_call(
+        rows_1, grad_rows_1, gated_0, dx_0, dgate_0, table_all, w_gate_up, w_down, (mate_1, far_1, far_mate_early_1, far_mate_rest_1)
     )
     (
         block_out, in_grad, q_grad, k_grad, v_grad, o_grad, router_grad, two_gains, load, *arrived_1,
     ) = backward_call(
-        part, y, dgate, h2_all, w_out, w_full, h1, qkv, lse, o_heads, angle, *grads_1[1:],
+        part_here, part_there, y_here, y_there, dgate, h2_all, w_out, w_full, h1, qkv, lse, o_heads, angle, *grads_1[1:],
         x_own, mid, gate, gain_rows, dy_own, w_own, attn_gain.reshape(32, 1),
     )
     (

time: 424 us -> 397 us (0.936)
  Pallas kernels: 381 us -> 366 us
  starting transfers between devices: 14.6 us -> 4.49 us
    pallas_call x1, Pallas kernels: 153 us -> 135 us  [backward_call(): pl.pallas_call(backward_kernel, name='backward', out_shape=(jax.ShapeDtyp...]
    ppermute x3, starting transfers between devices: 14.5 us -> 4.45 us  [swap(): lax.ppermute(values, 'narrow', [(i, i ^ distance) for i in range(NARROW)])]
  transfers between devices with their start and end apart: 4 -> 4, of which waited for: 1 -> 0; matrix products, arithmetic and copies ran while one was open for 0% -> 0% of each run, Pallas kernels for 44% -> 43%
where the time goes in v4:
time: 397 us; the launch traced here: 389 us
  Pallas kernels  366 us (92%)
  between operations  14.4 us (4%)
  starting transfers between devices  4.49 us (1%)
    pallas_call x1, Pallas kernels, backward_call(): pl.pallas_call(backward_kernel, name='backward', out_shape=(jax.ShapeDtyp...  135 us
    pallas_call x1, Pallas kernels, forward_call(): pl.pallas_call(forward_kernel, name='forward', out_shape=(jax.ShapeDtypeS...  116 us
    pallas_call x1, Pallas kernels, gather_call(): pl.pallas_call(gather_kernel, name='gather_inputs', out_shape=(jax.ShapeD...  47.2 us
    pallas_call x1, Pallas kernels, expert_1_call(): pl.pallas_call(expert_1_kernel, name='expert_1', grid=(STEPS,), out_shape...  31 us
    pallas_call x1, Pallas kernels, expert_0_call(): pl.pallas_call(expert_0_kernel, name='expert_0', grid=(STEPS,), out_shape...  29.3 us
  transfers between devices with their start and end apart: 4, of which 0 were waited for; matrix products, arithmetic and copies ran while one was open for 0% of the time, Pallas kernels for 43%

profile of v4, /device:TPU:0, one launch (start us, length us, event | category | flops | bytes accessed | tf_op | source)
XLA Modules:
  0.0 388.9 jit_solution(11490897955743648042)
XLA Ops:
  7.2 0.0 all-gather.2.cloned.1.call-start
  7.2 1.5 copy.30
  8.7 47.2 %gather_inputs.1 = (bf16[8,256,1024]{2,1,0:T(8,128)(2,1)}, bf16[32,32,256]{2,1,0:T(8,128)(2,1)}, f32[32,8,128]{2,1,0:T(8,128)}, s32[8,8,128]{2,1,0:T(8,128)}, bf...) custom-call(bf16[256,1024]{1,0:T(8,128)(2,1)} %bitcast.17, ...), custom_call_target="tpu_custom_call" | custom-call | flops 1000000000 | bytes 3600000 | tf_op jit(solution)/shard_map/gather_inputs/pallas_call | solution.py:696
  55.9 115.9 %forward.1 = (bf16[2,1024,1024]{2,1,0:T(8,128)(2,1)}, bf16[2,1024,256]{2,1,0:T(8,128)(2,1)}, f32[2,1024,128]{2,1,0:T(8,128)}, bf16[2,1024,128]{2,1,0:T(8,128)(2,...) custom-call(bf16[8,2,128,1024]{3,2,1,0:T(8,128)(2,1)} %bitcast.14, ...), custom_call_target="tpu_custom_call" | custom-call | flops 1000000000 | bytes 3600000 | tf_op jit(solution)/shard_map/forward/pallas_call | solution.py:1045
  171.8 0.0 copy-start.3
  171.8 29.3 %expert_0.1 = (bf16[4,320,1024]{2,1,0:T(8,128)(2,1)}, bf16[4,320,1024]{2,1,0:T(8,128)(2,1)}, bf16[4,320,1024]{2,1,0:T(8,128)(2,1)}, bf16[4,320,1024]{2,1,0:T(8,1...) custom-call(bf16[16,256,1024]{2,1,0:T(8,128)(2,1)} %get-tuple-elemen, ...), custom_call_target="tpu_custom_call" | custom-call | flops 1000000000 | bytes 3600000 | tf_op jit(solution)/shard_map/expert_0/pallas_call | solution.py:1320
  201.1 0.0 all-gather.2.cloned.1.call-update
  201.1 1.3 collective-permute-start
  202.5 1.3 collective-permute-start.1
  203.7 1.9 collective-permute-start.2
  205.6 0.0 copy-done.3
  205.6 0.7 copy.31.refs_22_
  206.3 31.0 %expert_1.1 = (bf16[8,256,1024]{2,1,0:T(8,128)(2,1)}, bf16[8,256,1024]{2,1,0:T(8,128)(2,1)}, bf16[8,256,1024]{2,1,0:T(8,128)(2,1)}, bf16[8,256,1024]{2,1,0:T(8,1...) custom-call(bf16[4,320,1024]{2,1,0:T(8,128)(2,1)} %get-tuple-element, ...), custom_call_target="tpu_custom_call" | custom-call | flops 1000000000 | bytes 3600000 | tf_op jit(solution)/shard_map/expert_1/pallas_call | solution.py:1338
  237.3 0.0 all-gather.2.cloned.1.call-done.refs_7_
  237.3 135.4 %backward.1 = (bf16[256,1024]{1,0:T(8,128)(2,1)}, bf16[256,1024]{1,0:T(8,128)(2,1)}, f32[32,1024]{1,0:T(8,128)}, f32[32,512]{1,0:T(8,128)}, f32[32,512]{1,0:T(8,...) custom-call(bf16[8,256,1024]{2,1,0:T(8,128)(2,1)} %get-tuple-element, ...), custom_call_target="tpu_custom_call" | custom-call | flops 1000000000 | bytes 3600000 | tf_op jit(solution)/shard_map/backward/pallas_call | solution.py:1976
  372.7 0.0 collective-permute-done.refs_1_
  372.7 0.0 copy-start
  372.7 0.0 collective-permute-done.1.refs_2_
  372.7 0.0 copy-start.1
  372.8 0.0 collective-permute-done.2.refs_3_
  372.8 0.0 copy-start.2
  372.8 0.8 copy-done
  373.6 0.3 copy-done.1
  373.9 0.3 copy-done.2
  374.2 7.6 %results.1 = (f32[4,256,1024]{2,1,0:T(8,128)}, f32[4,128,1024]{2,1,0:T(8,128)}, bf16[256,1024]{1,0:T(8,128)(2,1)}, bf16[256,1024]{1,0:T(8,128)(2,1)}, f32[32,102...) custom-call(bf16[384,1024]{1,0:T(8,128)(2,1)} %get-tuple-element.96., ...), custom_call_target="tpu_custom_call" | custom-call | flops 1000000000 | bytes 3600000 | tf_op jit(solution)/shard_map/results/pallas_call | solution.py:1403
Async XLA Ops:
  7.2 230.1 %all-gather.2.cloned.1.call-start = ((), (), s32[]{:S(2)}) async-start(), calls=%async_computation | async-start | bytes 4718592 | tf_op jit(solution)/shard_map/all_gather | solution.py:2092
  171.8 33.8 %copy-start.3 = (bf16[32]{0:T(256)(128)(2,1)S(1)}, bf16[32]{0:T(256)(128)(2,1)}, u32[]{:S(2)}) copy-start(bf16[32]{0:T(256)(128)(2,1)} %param.20) | copy-start | bytes 196
  201.1 171.6 %collective-permute-start = (bf16[384,1024]{1,0:T(8,128)(2,1)}, bf16[384,1024]{1,0:T(8,128)(2,1)S(1)}, u32[]{:S(2)}, u32[]{:S(2)}) collective-permute-start(bf16[384,1024]{1,0:T(8,128)(2,1)} %get-tuple-element.97), channel_id=1, source_target_pairs={{0,8},{8,0},{16,24},{24,16},{1,9},{9,1},{17,25},{25,17},{2,10},{10... | collective-permute-start | bytes 2359304 | tf_op jit(solution)/shard_map/ppermute | solution.py:2049
  202.5 170.3 %collective-permute-start.1 = (bf16[384,1024]{1,0:T(8,128)(2,1)}, bf16[384,1024]{1,0:T(8,128)(2,1)S(1)}, u32[]{:S(2)}, u32[]{:S(2)}) collective-permute-start(bf16[384,1024]{1,0:T(8,128)(2,1)} %get-tuple-element.98), channel_id=1, source_target_pairs={{0,16},{8,24},{16,0},{24,8},{1,17},{9,25},{17,1},{25,9},{2,18},{10... | collective-permute-start | bytes 2359304 | tf_op jit(solution)/shard_map/ppermute | solution.py:2049
  203.7 169.0 %collective-permute-start.2 = (bf16[384,1024]{1,0:T(8,128)(2,1)}, bf16[384,1024]{1,0:T(8,128)(2,1)S(1)}, u32[]{:S(2)}, u32[]{:S(2)}) collective-permute-start(bf16[384,1024]{1,0:T(8,128)(2,1)} %get-tuple-element.99), channel_id=1, source_target_pairs={{0,24},{8,16},{16,8},{24,0},{1,25},{9,17},{17,9},{25,1},{2,26},{10... | collective-permute-start | bytes 2359304 | tf_op jit(solution)/shard_map/ppermute | solution.py:2049
  372.7 0.9 copy-start
  372.7 1.2 copy-start.1
  372.8 1.4 copy-start.2
Sparse Core Ops, SparseCore 0:
  201.2 35.9 all-gather.1

commit v5 on v4

--- a/solution.py
+++ b/solution.py
@@ -441,7 +441,6 @@
 SEQ = 1024
 SLOTS = 80
 MINE = 2
-EARLY = 160
 MIDDLE = 96
 CHUNK = 4
 NT = (((1,), (1,)), ((), ()))
@@ -576,161 +575,6 @@
     return PlaneGather(
         spot, lambda half: part(own, half), lambda who, half: part(out.at[base + who], half), send, recv
     )
-
-
-def gather_kernel(
-    x_ref, dy_ref, seg_in, q_ref, k_ref, v_ref, o_ref, router_ref, gain_one_ref, gain_two_ref, gu_ref,
-    x_all, w_all, g_all, seg_all, wo_block, dy_pair, far_gu, w_ref,
-    g_ref, seg_ref, wo_ref, send, recv, local, ws, wr, gs, gr, ss, sr, zs, zr, ds, dr, es, er,
-):
-    spot = Spot()
-    for head in range(WIDE):
-        at = 256 * head
-        w_ref[:, at : at + 128] = q_ref[:, 128 * head : 128 * head + 128]
-        w_ref[:, at + 128 : at + 256] = jnp.concatenate(
-            [k_ref[:, 64 * head : 64 * head + 64], v_ref[:, 64 * head : 64 * head + 64]], axis=1
-        )
-    wo_ref[:, 0:WIDTH] = o_ref[...]
-    wo_ref[:, WIDTH : WIDTH + 128] = jnp.concatenate([router_ref[...], jnp.zeros((32, 96), BF16)], axis=1)
-    g_ref[...] = jnp.zeros_like(g_ref)
-    g_ref[0:1, 0:32] = gain_one_ref[...].astype(F32)
-    g_ref[1:2, 0:32] = gain_two_ref[...].astype(F32)
-    seg_ref[...] = jnp.zeros_like(seg_ref)
-    seg_ref[0:2, :] = seg_in[...]
-    spot.greet(NARROW * WIDE)
-    own = [
-        pltpu.make_async_copy(x_ref, x_all.at[spot.w], local.at[0]),
-        pltpu.make_async_copy(w_ref.at[:, pl.ds(pl.multiple_of(spot.w * 256, 256), 256)], w_all.at[spot.me], local.at[1]),
-        pltpu.make_async_copy(g_ref, g_all.at[spot.me], local.at[2]),
-        pltpu.make_async_copy(seg_ref, seg_all.at[spot.w], local.at[3]),
-        pltpu.make_async_copy(wo_ref, wo_block.at[spot.n], local.at[4]),
-        pltpu.make_async_copy(dy_ref, dy_pair.at[spot.half], local.at[5]),
-    ]
-    gather = gather_tokens(spot, x_ref, x_all, 0, send, recv)
-
-    def others(step):
-        other = lax.rem(spot.me + step, NARROW * WIDE)
-        return other, lax.div(other, WIDE), lax.rem(other, WIDE)
-
-    def weights(step, arriving):
-        other, o_n, o_w = others(step)
-        source = w_ref.at[:, pl.ds(pl.multiple_of(o_w * 256, 256), 256)]
-        place = other if arriving else spot.me
-        return (
-            remote(source, w_all.at[place], ws.at[other], wr.at[place], (o_n, o_w)),
-            remote(g_ref, g_all.at[place], gs.at[other], gr.at[place], (o_n, o_w)),
-        )
-
-    def documents(step, arriving):
-        other = lax.rem(spot.w + step, WIDE)
-        place = other if arriving else spot.w
-        return remote(seg_ref, seg_all.at[place], ss.at[other], sr.at[place], spot.wide(other))
-
-    def column(step, arriving):
-        other = lax.rem(spot.n + step, NARROW)
-        place = other if arriving else spot.n
-        return remote(wo_ref, wo_block.at[place], zs.at[other], zr.at[place], (other, spot.w))
-
-    def start(step, carry):
-        for copy in weights(step, False):
-            copy.start()
-        return carry
-
-    def start_column(step, carry):
-        column(step, False).start()
-        return carry
-
-    def start_documents(step, carry):
-        documents(step, False).start()
-        return carry
-
-    lax.fori_loop(1, WIDE, start_documents, 0)
-    lax.fori_loop(1, NARROW * WIDE, start, 0)
-    gather.begin()
-    lax.fori_loop(1, NARROW, start_column, 0)
-    for copy in own:
-        copy.start()
-    across = remote(dy_ref, dy_pair.at[spot.half], ds.at[0], dr.at[0], (spot.mate, spot.w))
-    across.start()
-    far = remote(
-        gu_ref.at[2 * spot.half, pl.ds(0, EARLY)], far_gu, es.at[0], er.at[0],
-        (spot.n + 2 - 4 * lax.div(spot.n, 2), spot.w),
-    )
-    far.start()
-    gather.middle()
-    gather.late()
-    gather.last()
-
-    def wait(step, carry):
-        for copy in weights(step, False):
-            copy.wait_send()
-        for copy in weights(step, True):
-            copy.wait_recv()
-        return carry
-
-    def wait_column(step, carry):
-        column(step, False).wait_send()
-        column(step, True).wait_recv()
-        return carry
-
-    def wait_documents(step, carry):
-        documents(step, False).wait_send()
-        documents(step, True).wait_recv()
-        return carry
-
-    lax.fori_loop(1, WIDE, wait_documents, 0)
-    lax.fori_loop(1, NARROW * WIDE, wait, 0)
-    lax.fori_loop(1, NARROW, wait_column, 0)
-    gather.finish()
-    across.wait_send()
-    arrived = dy_pair.at[1 - spot.half]
-    remote(arrived, arrived, ds.at[0], dr.at[0], (spot.mate, spot.w)).wait_recv()
-    for copy in own:
-        copy.wait()
-    far.wait_send()
-    far.wait_recv()
-
-
-def gather_call(*operands):
-    dma = pltpu.SemaphoreType.DMA
-    return pl.pallas_call(
-        gather_kernel,
-        name="gather_inputs",
-        out_shape=(
-            jax.ShapeDtypeStruct((WIDE, TOKENS, WIDTH), BF16),
-            jax.ShapeDtypeStruct((NARROW * WIDE, 32, 256), BF16),
-            jax.ShapeDtypeStruct((NARROW * WIDE, 8, 128), F32),
-            jax.ShapeDtypeStruct((WIDE, 8, 128), jnp.int32),
-            jax.ShapeDtypeStruct((NARROW, 32, WIDTH + 128), BF16),
-            jax.ShapeDtypeStruct((2, TOKENS, WIDTH), BF16),
-            jax.ShapeDtypeStruct((EARLY, WIDTH), BF16),
-            jax.ShapeDtypeStruct((32, 2 * WIDTH), BF16),
-        ),
-        in_specs=[IN_VMEM] * 10 + [IN_HBM],
-        out_specs=(IN_HBM,) * 7 + (IN_VMEM,),
-        scratch_shapes=[
-            pltpu.VMEM((8, 128), F32),
-            pltpu.VMEM((8, 128), jnp.int32),
-            pltpu.VMEM((32, WIDTH + 128), BF16),
-            dma((PlaneGather.COPIES,)),
-            dma((PlaneGather.COPIES,)),
-            dma((6,)),
-            dma((NARROW * WIDE,)),
-            dma((NARROW * WIDE,)),
-            dma((NARROW * WIDE,)),
-            dma((NARROW * WIDE,)),
-            dma((WIDE,)),
-            dma((WIDE,)),
-            dma((NARROW,)),
-            dma((NARROW,)),
-            dma((1,)),
-            dma((1,)),
-            dma((1,)),
-            dma((1,)),
-        ],
-        compiler_params=pltpu.CompilerParams(collective_id=1, has_side_effects=True),
-        cost_estimate=duration(1),
-    )(*operands)
 
 
 def lane_half():
@@ -858,14 +702,105 @@
 
 
 def forward_kernel(
-    x_ref, w_ref, g_ref, seg_ref, cos_ref, sin_ref, freq_ref, wo_ref, ids_ref, dy_ref, gu_ref, down_ref,
-    h1_out, qkv_ref, lse_ref, o_ref, angle_ref, gain_ref, mid_ref, gate_ref, w_all,
-    h2_all, dy_all, table_all, mate_0, far_rest_0, far_mate_0, mate_1, far_1, far_mate_early_1,
-    h1_ref, o_full, h2_own, table_own,
+    x_in, dy_ref, seg_in, wq_in, wk_in, wv_in, wo_in, router_in, gain_one_in, gain_two_in,
+    cos_ref, sin_ref, freq_ref, ids_ref, gu_ref, down_ref,
+    h1_out, qkv_ref, lse_ref, o_ref, angle_ref, gain_ref, mid_ref, gate_ref, w_all, w_ref, w_own,
+    h2_all, dy_all, table_all, mate_0, far_0, far_mate_0, mate_1, far_1, far_mate_early_1,
+    x_ref, g_ref, seg_ref, wo_ref, dy_mate, g_own, seg_own, wo_own, h1_ref, o_full, h2_own, table_own,
+    xs, xr, ws, wr, gs, gr, ss, sr, cs, cr, ds, dr, early,
     os, orv, w_send, w_recv, a_send, a_recv, b_send, b_recv, s0, r0, s1, r1, ts, tr, zs, zr, es, er, local,
 ):
     spot = Spot()
-    spot.greet(NARROW * WIDE)
+    everyone = NARROW * WIDE
+    for head in range(WIDE):
+        at = 256 * head
+        w_own[:, at : at + 128] = wq_in[:, 128 * head : 128 * head + 128]
+        w_own[:, at + 128 : at + 256] = jnp.concatenate(
+            [wk_in[:, 64 * head : 64 * head + 64], wv_in[:, 64 * head : 64 * head + 64]], axis=1
+        )
+    wo_own[:, 0:WIDTH] = wo_in[...]
+    wo_own[:, WIDTH : WIDTH + 128] = jnp.concatenate([router_in[...], jnp.zeros((32, 96), BF16)], axis=1)
+    g_own[...] = jnp.zeros_like(g_own)
+    g_own[0:1, 0:32] = gain_one_in[...].astype(F32)
+    g_own[1:2, 0:32] = gain_two_in[...].astype(F32)
+    seg_own[...] = jnp.zeros_like(seg_own)
+    seg_own[0:2, :] = seg_in[...]
+    spot.greet(everyone)
+
+    def others(step):
+        other = lax.rem(spot.me + step, everyone)
+        return other, lax.div(other, WIDE), lax.rem(other, WIDE)
+
+    def columns_of(o_w):
+        return w_own.at[:, pl.ds(pl.multiple_of(o_w * 256, 256), 256)]
+
+    def weights(step, arriving):
+        other, o_n, o_w = others(step)
+        place = other if arriving else spot.me
+        return (
+            remote(columns_of(o_w), w_ref.at[place], ws.at[other], wr.at[place], (o_n, o_w)),
+            remote(g_own, g_ref.at[place], gs.at[other], gr.at[place], (o_n, o_w)),
+        )
+
+    def documents(step, arriving):
+        other = lax.rem(spot.w + step, WIDE)
+        place = other if arriving else spot.w
+        return remote(seg_own, seg_ref.at[place], ss.at[other], sr.at[place], spot.wide(other))
+
+    def column(step, arriving):
+        other = lax.rem(spot.n + step, NARROW)
+        place = other if arriving else spot.n
+        return remote(wo_own, wo_ref.at[place], cs.at[other], cr.at[place], (other, spot.w))
+
+    def start_weights_out(step, carry):
+        start_all(weights(step, False))
+        return carry
+
+    def start_column(step, carry):
+        column(step, False).start()
+        return carry
+
+    def start_documents(step, carry):
+        documents(step, False).start()
+        return carry
+
+    def wait_weights(step, carry):
+        for copy in weights(step, False):
+            copy.wait_send()
+        for copy in weights(step, True):
+            copy.wait_recv()
+        return carry
+
+    def wait_column(step, carry):
+        column(step, False).wait_send()
+        column(step, True).wait_recv()
+        return carry
+
+    def wait_documents(step, carry):
+        documents(step, False).wait_send()
+        documents(step, True).wait_recv()
+        return carry
+
+    x_gather = PlaneGather(
+        spot,
+        lambda half: x_in if half is None else x_in.at[half],
+        lambda who, half: x_ref.at[who] if half is None else x_ref.at[who, half],
+        xs, xr,
+    )
+    lax.fori_loop(1, WIDE, start_documents, 0)
+    lax.fori_loop(1, everyone, start_weights_out, 0)
+    x_gather.begin()
+    lax.fori_loop(1, NARROW, start_column, 0)
+    dy_across = remote(dy_ref, dy_mate, ds.at[0], dr.at[0], (spot.mate, spot.w))
+    dy_across.start()
+    mine = [
+        pltpu.make_async_copy(x_in, x_ref.at[spot.w], early.at[0]),
+        pltpu.make_async_copy(columns_of(spot.w), w_ref.at[spot.me], early.at[1]),
+        pltpu.make_async_copy(g_own, g_ref.at[spot.me], early.at[2]),
+        pltpu.make_async_copy(seg_own, seg_ref.at[spot.w], early.at[3]),
+        pltpu.make_async_copy(wo_own, wo_ref.at[spot.n], early.at[4]),
+    ]
+    start_all(mine)
     mate_base = (1 - spot.half) * WIDE
     own_base = spot.half * WIDE
     mate_slot = mate_base + spot.w
@@ -877,19 +812,27 @@
         return w_all.at[:, who] if half is None else w_all.at[pl.ds(2 * half, 2), who]
 
     w_gather = PlaneGather(spot, w_source, w_place, w_send, w_recv)
-    dy_gather = gather_tokens(spot, dy_ref.at[spot.half], dy_all, own_base, a_send, a_recv)
-    mate_dy_gather = gather_tokens(spot, dy_ref.at[1 - spot.half], dy_all, mate_base, b_send, b_recv)
-    w_gather.begin()
-    dy_gather.begin()
-    first_expert = piece_copies(spot, gu_ref, down_ref, 0, 2, far_rest_0, es, er, 0, first=EARLY)
+    dy_gather = gather_tokens(spot, dy_ref, dy_all, own_base, a_send, a_recv)
+    mate_dy_gather = gather_tokens(spot, dy_mate, dy_all, mate_base, b_send, b_recv)
+    x_gather.middle()
+    first_expert = piece_copies(spot, gu_ref, down_ref, 0, 2, far_0, es, er, 0)
     first_expert += piece_copies(spot, gu_ref, down_ref, 0, 3, far_mate_0, es, er, 2)
     first_expert += piece_copies(spot, gu_ref, down_ref, 0, 1, mate_0, es, er, 4)
     start_all(first_expert)
-
+    x_gather.late()
+    x_gather.last()
+    lax.fori_loop(1, WIDE, wait_documents, 0)
+    lax.fori_loop(1, everyone, wait_weights, 0)
+    lax.fori_loop(1, NARROW, wait_column, 0)
+    for copy in mine:
+        copy.wait()
+    w_gather.begin()
+    dy_gather.begin()
+
+    x_gather.finish()
     keep = [
         pltpu.make_async_copy(wo_ref, w_place(spot.w, None), local.at[0]),
-        pltpu.make_async_copy(dy_ref.at[spot.half], dy_all.at[spot.slot], local.at[1]),
-        pltpu.make_async_copy(dy_ref.at[1 - spot.half], dy_all.at[mate_slot], local.at[2]),
+        pltpu.make_async_copy(dy_ref, dy_all.at[spot.slot], local.at[1]),
     ]
     for copy in keep:
         copy.start()
@@ -913,8 +856,7 @@
 
     expert = lax.broadcasted_iota(jnp.int32, (32, TOKENS), 0).astype(F32)
     named = jnp.zeros((32, TOKENS), F32)
-    ids = ids_ref[...].astype(F32)
-    ids = jnp.transpose(jnp.concatenate([ids, jnp.zeros((TOKENS, 128 - TOP), F32)], axis=1))
+    ids = jnp.concatenate([ids_ref[0], ids_ref[1]], axis=1).astype(F32)
     for k in range(TOP):
         named = jnp.where(expert == ids[k : k + 1, :], 1.0, named)
     before = lax.broadcasted_iota(jnp.int32, (TOKENS, TOKENS), 0) < lax.broadcasted_iota(
@@ -945,6 +887,10 @@
     h1_copy = pltpu.make_async_copy(h1_ref, h1_out, local.at[4])
     h1_copy.start()
     dy_gather.last()
+    dy_across.wait_send()
+    dy_across.wait_recv()
+    keep_mate = pltpu.make_async_copy(dy_mate, dy_all.at[mate_slot], local.at[2])
+    keep_mate.start()
     mate_dy_gather.begin()
     w_gather.finish()
     keep[0].wait()
@@ -1030,7 +976,7 @@
     second.finish()
     across.wait_send()
     keep[1].wait()
-    keep[2].wait()
+    keep_mate.wait()
     keep_own.wait()
     table_mine.wait()
     h1_copy.wait()
@@ -1039,9 +985,10 @@
         copy.wait_recv()
 
 
-def forward_call(x_all, w_all, g_all, seg_all, cos_table, sin_table, freq, wo_block, ids, dy_pair, w_gate_up, w_down):
+def forward_call(*operands):
     dma = pltpu.SemaphoreType.DMA
     copies = PlaneGather.COPIES
+    everyone = NARROW * WIDE
     return pl.pallas_call(
         forward_kernel,
         name="forward",
@@ -1055,26 +1002,40 @@
             jax.ShapeDtypeStruct((TOKENS, WIDTH), F32),
             jax.ShapeDtypeStruct((64, TOKENS), F32),
             jax.ShapeDtypeStruct((NARROW, WIDE, 32, WIDTH + 128), BF16),
+            jax.ShapeDtypeStruct((everyone, 32, 256), BF16),
+            jax.ShapeDtypeStruct((32, 2 * WIDTH), BF16),
             jax.ShapeDtypeStruct((GROUP, TOKENS, WIDTH), BF16),
             jax.ShapeDtypeStruct((GROUP, TOKENS, WIDTH), BF16),
             jax.ShapeDtypeStruct((GROUP, 8, TOKENS), F32),
         )
-        + tuple(jax.ShapeDtypeStruct((depth, WIDTH), BF16) for depth in (384, 384 - EARLY, 384, 384, 384, MIDDLE)),
-        in_specs=[IN_VMEM] * 7 + [IN_HBM, IN_VMEM, IN_VMEM, IN_HBM, IN_HBM],
-        out_specs=(IN_HBM,) + (IN_VMEM,) * 8 + (IN_HBM,) * 9,
+        + tuple(jax.ShapeDtypeStruct((depth, WIDTH), BF16) for depth in (384, 384, 384, 384, 384, MIDDLE)),
+        in_specs=[IN_VMEM] * 14 + [IN_HBM, IN_HBM],
+        out_specs=(IN_HBM,) + (IN_VMEM,) * 10 + (IN_HBM,) * 9,
         scratch_shapes=[
+            pltpu.VMEM((WIDE, 2, SPAN, WIDTH), BF16),
+            pltpu.VMEM((everyone, 8, 128), F32),
+            pltpu.VMEM((WIDE, 8, 128), jnp.int32),
+            pltpu.VMEM((NARROW, 32, WIDTH + 128), BF16),
+            pltpu.VMEM((TOKENS, WIDTH), BF16),
+            pltpu.VMEM((8, 128), F32),
+            pltpu.VMEM((8, 128), jnp.int32),
+            pltpu.VMEM((32, WIDTH + 128), BF16),
             pltpu.VMEM((2, SEQ, WIDTH), BF16),
             pltpu.VMEM((2, SPAN, WIDTH), BF16),
             pltpu.VMEM((TOKENS, WIDTH), BF16),
             pltpu.VMEM((GROUP, 8, TOKENS), F32),
-            dma((WIDE,)),
-            dma((WIDE,)),
+            dma((copies,)),
+            dma((copies,)),
         ]
+        + [dma((everyone,))] * 4
+        + [dma((WIDE,))] * 2
+        + [dma((NARROW,))] * 2
+        + [dma((1,)), dma((1,)), dma((5,)), dma((WIDE,)), dma((WIDE,))]
         + [dma((copies,))] * 10
         + [dma((GROUP,)), dma((GROUP,)), dma((1,)), dma((1,)), dma((12,)), dma((12,)), dma((7,))],
-        compiler_params=pltpu.CompilerParams(collective_id=2, has_side_effects=True, vmem_limit_bytes=VMEM_BYTES),
+        compiler_params=pltpu.CompilerParams(collective_id=1, has_side_effects=True, vmem_limit_bytes=VMEM_BYTES),
         cost_estimate=duration(1),
-    )(x_all.reshape(WIDE, 2, SPAN, WIDTH), w_all, g_all, seg_all, cos_table, sin_table, freq, wo_block, ids, dy_pair, w_gate_up, w_down)
+    )(*operands)
 
 
 def load_quarters(own, pieces, w_gu, w_down, sems):
@@ -1171,7 +1132,7 @@
 
 
 def expert_0_kernel(
-    h2_ref, dy_ref, table_ref, gu_ref, down_ref, w1, w2_early, w2_rest, w3,
+    h2_ref, dy_ref, table_ref, gu_ref, down_ref, w1, w2, w3,
     gated_ref, dx_ref, rows_ref, grad_rows_ref, dgate_ref, own, mate, far, far_mate, far_mate_1,
     w_gu, w_down, gu_sum, down_sum, sems, es, er,
 ):
@@ -1186,7 +1147,7 @@
         pl.semaphore_signal(barrier, inc=1, device_id=(plane, spot.w), device_id_type=MESH)
         pl.semaphore_wait(barrier, 1)
         start_all(second_expert)
-        start_weights(0, gu_ref, down_ref, (w1, (w2_early, w2_rest), w3), w_gu, w_down, gu_sum, down_sum, sems)
+        start_weights(0, gu_ref, down_ref, (w1, w2, w3), w_gu, w_down, gu_sum, down_sum, sems)
 
     masks = [[pick(table_ref, s, e) for s in range(CHUNK)] for e in range(MINE)]
     rows, grad_rows = [], []
@@ -1325,7 +1286,7 @@
         + (TABLES,)
         + (QUARTER,) * 4
         + (jax.ShapeDtypeStruct((384 - MIDDLE, WIDTH), BF16),),
-        in_specs=[block, block, small] + [IN_HBM] * 6,
+        in_specs=[block, block, small] + [IN_HBM] * 5,
         out_specs=(slots,) * 4 + (small,) + (quarter,) * 4 + (IN_HBM,),
         scratch_shapes=expert_scratch() + [pltpu.SemaphoreType.DMA((2,)), pltpu.SemaphoreType.DMA((2,))],
         compiler_params=pltpu.CompilerParams(collective_id=4, has_side_effects=True, vmem_limit_bytes=VMEM_BYTES),
@@ -2069,16 +2030,13 @@
 
     x_own = hidden_in.reshape(TOKENS, WIDTH)
     dy_own = out_grad.reshape(TOKENS, WIDTH)
-    ids = expert_ids.reshape(TOKENS, TOP)
-    x_all, w_all, g_all, seg_all, wo_block, dy_pair, far_early_0, w_own = gather_call(
-        x_own, dy_own, seg_ids, w_query, w_key, w_value, w_output, w_router,
-        attn_gain.reshape(1, 32), moe_gain.reshape(1, 32), w_gate_up,
-    )
     (
-        h1, qkv, lse, o_heads, angle, gain_rows, mid, gate, w_out, h2_all, dy_all, table_all,
-        mate_0, far_rest_0, far_mate_0, mate_1, far_1, far_mate_early_1,
+        h1, qkv, lse, o_heads, angle, gain_rows, mid, gate, w_out, w_heads, w_own, h2_all, dy_all, table_all,
+        mate_0, far_0, far_mate_0, mate_1, far_1, far_mate_early_1,
     ) = forward_call(
-        x_all, w_all, g_all, seg_all, cos_table, sin_table, freq, wo_block, ids, dy_pair, w_gate_up, w_down
+        hidden_in, dy_own, seg_ids, w_query, w_key, w_value, w_output, w_router,
+        attn_gain.reshape(1, 32), moe_gain.reshape(1, 32), cos_table, sin_table, freq,
+        jnp.transpose(expert_ids, (0, 2, 1)), w_gate_up, w_down,
     )
     w_out = w_out.reshape(WIDTH, WIDTH + 128)
 
@@ -2086,9 +2044,9 @@
         return own, swap(mate, 1), swap(far, 2), swap(far_mate, 3)
 
     gated_0, dx_0, rows_1, grad_rows_1, dgate_0, *grads_0, far_mate_rest_1 = expert_0_call(
-        h2_all, dy_all, table_all, w_gate_up, w_down, (mate_0, far_early_0, far_rest_0, far_mate_0)
-    )
-    dgate_0, w_heads = lax.optimization_barrier((dgate_0, w_all))
+        h2_all, dy_all, table_all, w_gate_up, w_down, (mate_0, far_0, far_mate_0)
+    )
+    dgate_0, w_heads = lax.optimization_barrier((dgate_0, w_heads))
     w_full = lax.all_gather(w_heads.reshape(WIDTH, 256), "wide", axis=0, tiled=False)
     grads_0 = send_grads(*grads_0)
     y_here, y_there, part_here, part_there, dgate, *grads_1 = expert_1_call(

time: 397 us -> 381 us (0.960)
  Pallas kernels: 366 us -> 350 us
    pallas_call x1 -> x0, Pallas kernels: 47.2 us -> none  [gather_call(): pl.pallas_call(gather_kernel, name='gather_inputs', out_shape=(jax.ShapeD...]
    pallas_call x1, Pallas kernels: 116 us -> 149 us  [forward_call(): pl.pallas_call(forward_kernel, name='forward', out_shape=(jax.ShapeDtypeS...]
  transfers between devices with their start and end apart: 4 -> 4, of which waited for: 0 -> 0; matrix products, arithmetic and copies ran while one was open for 0% -> 0% of each run, Pallas kernels for 43% -> 44%
where the time goes in v5:
time: 381 us; the launch traced here: 373 us
  Pallas kernels  350 us (92%)
  between operations  14.3 us (4%)
  starting transfers between devices  7.16 us (2%)
    pallas_call x1, Pallas kernels, forward_call(): pl.pallas_call(forward_kernel, name='forward', out_shape=(jax.ShapeDtypeS...  149 us
    pallas_call x1, Pallas kernels, backward_call(): pl.pallas_call(backward_kernel, name='backward', out_shape=(jax.ShapeDtyp...  135 us
    pallas_call x1, Pallas kernels, expert_1_call(): pl.pallas_call(expert_1_kernel, name='expert_1', grid=(STEPS,), out_shape...  30.6 us
    pallas_call x1, Pallas kernels, expert_0_call(): pl.pallas_call(expert_0_kernel, name='expert_0', grid=(STEPS,), out_shape...  27.5 us
    pallas_call x1, Pallas kernels, results_call(): pl.pallas_call(results_kernel, name='results', out_shape=(jax.ShapeDtypeS...  7.64 us
  transfers between devices with their start and end apart: 4, of which 0 were waited for; matrix products, arithmetic and copies ran while one was open for 0% of the time, Pallas kernels for 44%

profile of v5, /device:TPU:0, one launch (start us, length us, event | category | flops | bytes accessed | tf_op | source)
XLA Modules:
  0.0 373.3 jit_solution(10911236758629744316)
XLA Ops:
  7.2 0.0 all-gather.2.cloned.1.call-start
  7.2 149.4 %forward.1 = (bf16[2,1024,1024]{2,1,0:T(8,128)(2,1)}, bf16[2,1024,256]{2,1,0:T(8,128)(2,1)}, f32[2,1024,128]{2,1,0:T(8,128)}, bf16[2,1024,128]{2,1,0:T(8,128)(2,...) custom-call(bf16[2,128,1024]{2,1,0:T(8,128)(2,1)} %x_in.1, ...), custom_call_target="tpu_custom_call" | custom-call | flops 1000000000 | bytes 3600000 | tf_op jit(solution)/shard_map/forward/pallas_call | solution.py:992
  156.6 0.0 copy-start.3
  156.6 27.5 %expert_0.1 = (bf16[4,320,1024]{2,1,0:T(8,128)(2,1)}, bf16[4,320,1024]{2,1,0:T(8,128)(2,1)}, bf16[4,320,1024]{2,1,0:T(8,128)(2,1)}, bf16[4,320,1024]{2,1,0:T(8,1...) custom-call(bf16[16,256,1024]{2,1,0:T(8,128)(2,1)} %get-tuple-elemen, ...), custom_call_target="tpu_custom_call" | custom-call | flops 1000000000 | bytes 3600000 | tf_op jit(solution)/shard_map/expert_0/pallas_call | solution.py:1281
  184.1 0.0 all-gather.2.cloned.1.call-update
  184.1 4.7 %collective-permute-start = (bf16[384,1024]{1,0:T(8,128)(2,1)}, bf16[384,1024]{1,0:T(8,128)(2,1)S(1)}, u32[]{:S(2)}, u32[]{:S(2)}) collective-permute-start(bf16[384,1024]{1,0:T(8,128)(2,1)} %get-tuple-element.84), channel_id=1, source_target_pairs={{0,8},{8,0},{16,24},{24,16},{1,9},{9,1},{17,25},{25,17},{2,10},{10... | collective-permute-start | bytes 2359304 | tf_op jit(solution)/shard_map/ppermute | solution.py:2010
  188.8 0.3 collective-permute-start.1
  189.1 2.1 collective-permute-start.2
  191.2 0.0 copy-done.3
  191.2 0.7 copy.29.refs_22_
  191.9 30.6 %expert_1.1 = (bf16[8,256,1024]{2,1,0:T(8,128)(2,1)}, bf16[8,256,1024]{2,1,0:T(8,128)(2,1)}, bf16[8,256,1024]{2,1,0:T(8,128)(2,1)}, bf16[8,256,1024]{2,1,0:T(8,1...) custom-call(bf16[4,320,1024]{2,1,0:T(8,128)(2,1)} %get-tuple-element, ...), custom_call_target="tpu_custom_call" | custom-call | flops 1000000000 | bytes 3600000 | tf_op jit(solution)/shard_map/expert_1/pallas_call | solution.py:1299
  222.5 0.0 all-gather.2.cloned.1.call-done.refs_7_
  222.5 134.7 %backward.1 = (bf16[256,1024]{1,0:T(8,128)(2,1)}, bf16[256,1024]{1,0:T(8,128)(2,1)}, f32[32,1024]{1,0:T(8,128)}, f32[32,512]{1,0:T(8,128)}, f32[32,512]{1,0:T(8,...) custom-call(bf16[8,256,1024]{2,1,0:T(8,128)(2,1)} %get-tuple-element, ...), custom_call_target="tpu_custom_call" | custom-call | flops 1000000000 | bytes 3600000 | tf_op jit(solution)/shard_map/backward/pallas_call | solution.py:1937
  357.2 0.0 collective-permute-done.refs_1_
  357.2 0.0 copy-start
  357.2 0.0 collective-permute-done.1.refs_2_
  357.2 0.0 copy-start.1
  357.2 0.0 collective-permute-done.2.refs_3_
  357.3 0.0 copy-start.2
  357.3 0.8 copy-done
  358.1 0.3 copy-done.1
  358.4 0.3 copy-done.2
  358.7 7.6 %results.1 = (f32[4,256,1024]{2,1,0:T(8,128)}, f32[4,128,1024]{2,1,0:T(8,128)}, bf16[256,1024]{1,0:T(8,128)(2,1)}, bf16[256,1024]{1,0:T(8,128)(2,1)}, f32[32,102...) custom-call(bf16[384,1024]{1,0:T(8,128)(2,1)} %get-tuple-element.83., ...), custom_call_target="tpu_custom_call" | custom-call | flops 1000000000 | bytes 3600000 | tf_op jit(solution)/shard_map/results/pallas_call | solution.py:1364
Async XLA Ops:
  7.2 215.3 %all-gather.2.cloned.1.call-start = ((), (), s32[]{:S(2)}) async-start(), calls=%async_computation | async-start | bytes 4718592 | tf_op jit(solution)/shard_map/all_gather | solution.py:2050
  156.6 34.6 %copy-start.3 = (bf16[32]{0:T(256)(128)(2,1)S(1)}, bf16[32]{0:T(256)(128)(2,1)}, u32[]{:S(2)}) copy-start(bf16[32]{0:T(256)(128)(2,1)} %param.20) | copy-start | bytes 196
  184.1 173.1 %collective-permute-start = (bf16[384,1024]{1,0:T(8,128)(2,1)}, bf16[384,1024]{1,0:T(8,128)(2,1)S(1)}, u32[]{:S(2)}, u32[]{:S(2)}) collective-permute-start(bf16[384,1024]{1,0:T(8,128)(2,1)} %get-tuple-element.84), channel_id=1, source_target_pairs={{0,8},{8,0},{16,24},{24,16},{1,9},{9,1},{17,25},{25,17},{2,10},{10... | collective-permute-start | bytes 2359304 | tf_op jit(solution)/shard_map/ppermute | solution.py:2010
  188.8 168.4 %collective-permute-start.1 = (bf16[384,1024]{1,0:T(8,128)(2,1)}, bf16[384,1024]{1,0:T(8,128)(2,1)S(1)}, u32[]{:S(2)}, u32[]{:S(2)}) collective-permute-start(bf16[384,1024]{1,0:T(8,128)(2,1)} %get-tuple-element.85), channel_id=1, source_target_pairs={{0,16},{8,24},{16,0},{24,8},{1,17},{9,25},{17,1},{25,9},{2,18},{10... | collective-permute-start | bytes 2359304 | tf_op jit(solution)/shard_map/ppermute | solution.py:2010
  189.1 168.2 %collective-permute-start.2 = (bf16[384,1024]{1,0:T(8,128)(2,1)}, bf16[384,1024]{1,0:T(8,128)(2,1)S(1)}, u32[]{:S(2)}, u32[]{:S(2)}) collective-permute-start(bf16[384,1024]{1,0:T(8,128)(2,1)} %get-tuple-element.86), channel_id=1, source_target_pairs={{0,24},{8,16},{16,8},{24,0},{1,25},{9,17},{17,9},{25,1},{2,26},{10... | collective-permute-start | bytes 2359304 | tf_op jit(solution)/shard_map/ppermute | solution.py:2010
  357.2 0.9 copy-start
  357.2 1.1 copy-start.1
  357.3 1.4 copy-start.2
Sparse Core Ops, SparseCore 0:
  184.2 37.3 all-gather.1

commit v6 on v5

--- a/solution.py
+++ b/solution.py
@@ -1235,12 +1235,16 @@
     def _():
         finish(step - 2, slot)
 
-    for s in range(CHUNK):
-        at = slice(s * SLOTS, (s + 1) * SLOTS)
-        hot = jnp.concatenate([jnp.where(masks[e][s], 1.0, 0.0) for e in range(MINE)], axis=0).astype(BF16)
-        held[0, slot, s] = mm(hot, jnp.concatenate([gated_before[0, at, :], gated[at]], axis=0), TN).astype(BF16)
-        held[1, slot, s] = mm(hot, jnp.concatenate([dx_before[0, at, :], dx[at]], axis=0), TN).astype(BF16)
-    start_all(copies(step, slot))
+    hots = [
+        jnp.concatenate([jnp.where(masks[e][s], 1.0, 0.0) for e in range(MINE)], axis=0).astype(BF16)
+        for s in range(CHUNK)
+    ]
+    leaving = copies(step, slot)
+    for kind, before, now in ((1, dx_before, dx), (0, gated_before, gated)):
+        for s in range(CHUNK):
+            at = slice(s * SLOTS, (s + 1) * SLOTS)
+            held[kind, slot, s] = mm(hots[s], jnp.concatenate([before[0, at, :], now[at]], axis=0), TN).astype(BF16)
+        start_all(leaving[kind * CHUNK : (kind + 1) * CHUNK])
 
     @pl.when(step == STEPS - 1)
     def _():
@@ -1562,7 +1566,7 @@
             ],
             axis=0,
         )
-        query = self.stack(self.qkv[row, tokens, 0:128])
+        query = self.stack(self.qkv[row, tokens, 0:128]) * BF16(HEAD_DIM**-0.5)
         do = self.stack(do)
         log_total = jnp.concatenate([self.lse[row, tokens, 0:1], self.lse[row, tokens, 64:65]], axis=0)
         start = self.lse[row, tokens, 32:33]
@@ -1571,23 +1575,28 @@
         place_query = (jnp.concatenate([place, place], axis=0) + q * 256).astype(F32)
         self.dq[...] = jnp.zeros_like(self.dq)
 
-        def key_block(block, carry):
+        def key_block(block, diagonal):
             keys_at = pl.ds(pl.multiple_of(block * 256, 256), 256)
             keys = self.qkv[row, keys_at, 128:192]
             values = self.qkv[row, keys_at, 192:256]
             place_key = (lax.broadcasted_iota(jnp.int32, (1, 256), 1) + block * 256).astype(F32)
-            allowed = (place_key <= place_query) & (place_key >= start)
-            scores = jnp.where(allowed, mm(query, keys, NT) * (HEAD_DIM**-0.5), MASKED)
-            weights = jnp.exp(scores - log_total)
+            allowed = place_key >= start
+            if diagonal:
+                allowed = allowed & (place_key <= place_query)
+            weights = jnp.exp(jnp.where(allowed, mm(query, keys, NT), MASKED) - log_total)
             dp = mm(do, values, NT)
             ds = (weights * (dp - delta)).astype(BF16)
             self.dq[...] += mm(ds, keys)
-            dk = mm(ds, query, TN) * (HEAD_DIM**-0.5)
+            dk = mm(ds, query, TN)
             dv = mm(weights.astype(BF16), do, TN)
             self.dkv[row, keys_at, :] += jnp.concatenate([dk, dv], axis=1)
+
+        def below(block, carry):
+            key_block(block, False)
             return carry
 
-        lax.fori_loop(0, q + 1, key_block, 0)
+        lax.fori_loop(0, q, below, 0)
+        key_block(q, True)
         dq = jnp.concatenate([self.dq[0:256], self.dq[256:512]], axis=1) * (HEAD_DIM**-0.5)
         cosine = self.angle[row, tokens, 0:128]
         sine = self.angle[row, tokens, 128:256]
@@ -1605,7 +1614,7 @@
     (
         part_here, part_there, y_here, y_there, dgate_ref, h2_ref, w_out_ref, w_full_ref, h1_ref, qkv_ref, lse_ref, o_ref,
         angle_ref, mate_1, far_1, far_mate_1,
-        x_ref, mid_ref, gate_ref, gain_ref, dy_ref, w_own, gain_col,
+        x_ref, mid_ref, gate_ref, gain_ref, dy_ref, w_own, gain_own,
     ) = refs[:23]
     (
         block_out, in_grad, q_grad, k_grad, v_grad, o_grad, router_grad, two_gains, load_out, *quarters_recv,
@@ -1667,10 +1676,10 @@
         )
     ]
     h2_sum.to_mate()
+    start_all(quarter_copies)
     h2_sum.ours.across_one()
     y_sum.across_core()
     h2_sum.finish()
-    start_all(quarter_copies)
 
     def wait_table(step, carry):
         tables(step, False).wait_send()
@@ -1903,7 +1912,6 @@
         k_grad[:, 64 * w : 64 * w + 64] = total[:, 128:192]
         v_grad[:, 64 * w : 64 * w + 64] = total[:, 192:256]
         gain_total += jnp.sum(total * widen(w_own[:, 256 * w : 256 * w + 256]), axis=1, keepdims=True)
-    gain_total = gain_total / gain_col[...].astype(F32)
     o_recv[spot.n] = o_held[spot.n]
     s_recv[spot.n] = s_held[spot.n]
     total = widen(o_recv[0])
@@ -1922,7 +1930,8 @@
     square = jnp.concatenate([square, jnp.zeros((88, 128), F32)], axis=0)
     router_grad[...] = jnp.transpose(square)[0:32, 0:32]
     column = jnp.concatenate([jnp.broadcast_to(gain_total, (32, 128)), jnp.zeros((96, 128), F32)], axis=0)
-    two_gains[...] = jnp.concatenate([jnp.transpose(column)[0:1, 0:32], mine[32:33]], axis=0)
+    attn_gain_grad = jnp.transpose(column)[0:1, 0:32] / gain_own[...].astype(F32)
+    two_gains[...] = jnp.concatenate([attn_gain_grad, mine[32:33]], axis=0)
 
     for copy in quarter_copies:
         copy.wait_send()
@@ -2056,7 +2065,7 @@
         block_out, in_grad, q_grad, k_grad, v_grad, o_grad, router_grad, two_gains, load, *arrived_1,
     ) = backward_call(
         part_here, part_there, y_here, y_there, dgate, h2_all, w_out, w_full, h1, qkv, lse, o_heads, angle, *grads_1[1:],
-        x_own, mid, gate, gain_rows, dy_own, w_own, attn_gain.reshape(32, 1),
+        x_own, mid, gate, gain_rows, dy_own, w_own, attn_gain.reshape(1, 32),
     )
     (
         gate_up_sum, down_sum, block_out, in_grad, q_grad, k_grad, v_grad, o_grad,

time: 381 us -> 375 us (0.984)
  Pallas kernels: 350 us -> 345 us
    pallas_call x1, Pallas kernels: 135 us -> 130 us  [backward_call(): pl.pallas_call(backward_kernel, name='backward', out_shape=(jax.ShapeDtyp...]
where the time goes in v6:
time: 375 us; the launch traced here: 368 us
  Pallas kernels  345 us (92%)
  between operations  14.6 us (4%)
  starting transfers between devices  7.14 us (2%)
    pallas_call x1, Pallas kernels, forward_call(): pl.pallas_call(forward_kernel, name='forward', out_shape=(jax.ShapeDtypeS...  149 us
    pallas_call x1, Pallas kernels, backward_call(): pl.pallas_call(backward_kernel, name='backward', out_shape=(jax.ShapeDtyp...  130 us
    pallas_call x1, Pallas kernels, expert_1_call(): pl.pallas_call(expert_1_kernel, name='expert_1', grid=(STEPS,), out_shape...  30.6 us
    pallas_call x1, Pallas kernels, expert_0_call(): pl.pallas_call(expert_0_kernel, name='expert_0', grid=(STEPS,), out_shape...  27.5 us
    pallas_call x1, Pallas kernels, results_call(): pl.pallas_call(results_kernel, name='results', out_shape=(jax.ShapeDtypeS...  7.64 us
  transfers between devices with their start and end apart: 4, of which 0 were waited for; matrix products, arithmetic and copies ran while one was open for 0% of the time, Pallas kernels for 44%

profile of v6, /device:TPU:0, one launch (start us, length us, event | category | flops | bytes accessed | tf_op | source)
XLA Modules:
  0.0 367.8 jit_solution(18072688731724966183)
XLA Ops:
  7.2 0.0 all-gather.2.cloned.1.call-start
  7.2 149.4 %forward.1 = (bf16[2,1024,1024]{2,1,0:T(8,128)(2,1)}, bf16[2,1024,256]{2,1,0:T(8,128)(2,1)}, f32[2,1024,128]{2,1,0:T(8,128)}, bf16[2,1024,128]{2,1,0:T(8,128)(2,...) custom-call(bf16[2,128,1024]{2,1,0:T(8,128)(2,1)} %x_in.1, ...), custom_call_target="tpu_custom_call" | custom-call | flops 1000000000 | bytes 3600000 | tf_op jit(solution)/shard_map/forward/pallas_call | solution.py:992
  156.6 27.5 %expert_0.1 = (bf16[4,320,1024]{2,1,0:T(8,128)(2,1)}, bf16[4,320,1024]{2,1,0:T(8,128)(2,1)}, bf16[4,320,1024]{2,1,0:T(8,128)(2,1)}, bf16[4,320,1024]{2,1,0:T(8,1...) custom-call(bf16[16,256,1024]{2,1,0:T(8,128)(2,1)} %get-tuple-elemen, ...), custom_call_target="tpu_custom_call" | custom-call | flops 1000000000 | bytes 3600000 | tf_op jit(solution)/shard_map/expert_0/pallas_call | solution.py:1285
  184.1 0.0 all-gather.2.cloned.1.call-update
  184.1 4.7 %collective-permute-start = (bf16[384,1024]{1,0:T(8,128)(2,1)}, bf16[384,1024]{1,0:T(8,128)(2,1)S(1)}, u32[]{:S(2)}, u32[]{:S(2)}) collective-permute-start(bf16[384,1024]{1,0:T(8,128)(2,1)} %get-tuple-element.84), channel_id=1, source_target_pairs={{0,8},{8,0},{16,24},{24,16},{1,9},{9,1},{17,25},{25,17},{2,10},{10... | collective-permute-start | bytes 2359304 | tf_op jit(solution)/shard_map/ppermute | solution.py:2019
  188.8 0.3 collective-permute-start.1
  189.1 2.1 collective-permute-start.2
  191.2 30.6 %expert_1.1 = (bf16[8,256,1024]{2,1,0:T(8,128)(2,1)}, bf16[8,256,1024]{2,1,0:T(8,128)(2,1)}, bf16[8,256,1024]{2,1,0:T(8,128)(2,1)}, bf16[8,256,1024]{2,1,0:T(8,1...) custom-call(bf16[4,320,1024]{2,1,0:T(8,128)(2,1)} %get-tuple-element, ...), custom_call_target="tpu_custom_call" | custom-call | flops 1000000000 | bytes 3600000 | tf_op jit(solution)/shard_map/expert_1/pallas_call | solution.py:1303
  221.8 0.0 all-gather.2.cloned.1.call-done.refs_7_
  221.8 129.5 %backward.1 = (bf16[256,1024]{1,0:T(8,128)(2,1)}, bf16[256,1024]{1,0:T(8,128)(2,1)}, f32[32,1024]{1,0:T(8,128)}, f32[32,512]{1,0:T(8,128)}, f32[32,512]{1,0:T(8,...) custom-call(bf16[8,256,1024]{2,1,0:T(8,128)(2,1)} %get-tuple-element, ...), custom_call_target="tpu_custom_call" | custom-call | flops 1000000000 | bytes 3600000 | tf_op jit(solution)/shard_map/backward/pallas_call | solution.py:1946
  351.4 0.0 collective-permute-done.refs_1_
  351.4 0.0 copy-start
  351.4 0.0 collective-permute-done.1.refs_2_
  351.4 0.0 copy-start.1
  351.4 0.0 collective-permute-done.2.refs_3_
  351.4 0.0 copy-start.2
  351.5 0.9 copy-done
  352.3 0.3 copy-done.1
  352.6 0.3 copy-done.2
  352.8 7.6 %results.1 = (f32[4,256,1024]{2,1,0:T(8,128)}, f32[4,128,1024]{2,1,0:T(8,128)}, bf16[256,1024]{1,0:T(8,128)(2,1)}, bf16[256,1024]{1,0:T(8,128)(2,1)}, f32[32,102...) custom-call(bf16[384,1024]{1,0:T(8,128)(2,1)} %get-tuple-element.83., ...), custom_call_target="tpu_custom_call" | custom-call | flops 1000000000 | bytes 3600000 | tf_op jit(solution)/shard_map/results/pallas_call | solution.py:1368
Async XLA Ops:
  7.2 214.6 %all-gather.2.cloned.1.call-start = ((), (), s32[]{:S(2)}) async-start(), calls=%async_computation | async-start | bytes 4718592 | tf_op jit(solution)/shard_map/all_gather | solution.py:2059
  184.1 167.3 %collective-permute-start = (bf16[384,1024]{1,0:T(8,128)(2,1)}, bf16[384,1024]{1,0:T(8,128)(2,1)S(1)}, u32[]{:S(2)}, u32[]{:S(2)}) collective-permute-start(bf16[384,1024]{1,0:T(8,128)(2,1)} %get-tuple-element.84), channel_id=1, source_target_pairs={{0,8},{8,0},{16,24},{24,16},{1,9},{9,1},{17,25},{25,17},{2,10},{10... | collective-permute-start | bytes 2359304 | tf_op jit(solution)/shard_map/ppermute | solution.py:2019
  188.8 162.6 %collective-permute-start.1 = (bf16[384,1024]{1,0:T(8,128)(2,1)}, bf16[384,1024]{1,0:T(8,128)(2,1)S(1)}, u32[]{:S(2)}, u32[]{:S(2)}) collective-permute-start(bf16[384,1024]{1,0:T(8,128)(2,1)} %get-tuple-element.85), channel_id=1, source_target_pairs={{0,16},{8,24},{16,0},{24,8},{1,17},{9,25},{17,1},{25,9},{2,18},{10... | collective-permute-start | bytes 2359304 | tf_op jit(solution)/shard_map/ppermute | solution.py:2019
  189.1 162.3 %collective-permute-start.2 = (bf16[384,1024]{1,0:T(8,128)(2,1)}, bf16[384,1024]{1,0:T(8,128)(2,1)S(1)}, u32[]{:S(2)}, u32[]{:S(2)}) collective-permute-start(bf16[384,1024]{1,0:T(8,128)(2,1)} %get-tuple-element.86), channel_id=1, source_target_pairs={{0,24},{8,16},{16,8},{24,0},{1,25},{9,17},{17,9},{25,1},{2,26},{10... | collective-permute-start | bytes 2359304 | tf_op jit(solution)/shard_map/ppermute | solution.py:2019
  351.4 0.9 copy-start
  351.4 1.2 copy-start.1
  351.4 1.4 copy-start.2
Sparse Core Ops, SparseCore 0:
  184.2 37.3 all-gather.1
